TPU v7x, 32 devices: a whole 2x2x4 slice. The times are simulated.
32 devices in a mesh: head: 2 (over y), blk: 16 (over z, x, core).
Axes of the slice: x: 2, y: 2, z: 4, core: 2. Of those that a mesh axis runs over, the one named last changes fastest.
Arguments:
- tokens: bfloat16 [4096, 768], P(('head', 'blk')), may hold values from -6 to 6
- segments: int32 [2, 2048], P(None, 'blk'), may hold values from 0 to 98, as said below
- routes: int32 [2, 4096, 2], P(None, ('head', 'blk')), may hold values from 0 to 11, all different within a row; in each aligned block of 128 rows (0 to 127, 128 to 255, ..., all dimensions but the last counted through in order) at most 40 rows name the same one
- gates: float32 [2, 4096, 2], P(None, ('head', 'blk')), may hold values from 0.2 to 1
- w_qkv: bfloat16 [2, 768, 2304], P(None, ('head', 'blk')), may hold values from -0.21875 to 0.21875
- w_out: bfloat16 [2, 768, 768], P(None, ('head', 'blk')), may hold values from -0.625 to 0.625
- gain_attn: bfloat16 [2, 768], P(None, ('head', 'blk')), may hold values from 0.5 to 1.5
- gain_moe: bfloat16 [2, 768], P(None, ('head', 'blk')), may hold values from 0.5 to 1.5
- const_gate: bfloat16 [2, 768, 4], P(None, ('head', 'blk')), may hold values from -0.21875 to 0.21875
- const_vec: bfloat16 [2, 768, 2], P(None, ('head', 'blk')), may hold values from -6 to 6
- w_gate: bfloat16 [2, 16384, 768], P(None, 'blk', 'head'), may hold values from -0.21875 to 0.21875
- w_up: bfloat16 [2, 16384, 768], P(None, 'blk', 'head'), may hold values from -0.21875 to 0.21875
- w_down: bfloat16 [2, 16384, 768], P(None, 'blk', 'head'), may hold values from -0.125 to 0.125
- cotangent: bfloat16 [4096, 768], P(('head', 'blk')), may hold values from -6 to 6
Outputs:
- output: float32 [4096, 768], P(('head', 'blk'))
- input_grad: float32 [4096, 768], P(('head', 'blk'))
- grad_qkv: float32 [2, 768, 2304], P(None, ('head', 'blk'))
- grad_out: float32 [2, 768, 768], P(None, ('head', 'blk'))
- grad_gain_attn: float32 [2, 768], P(None, ('head', 'blk'))
- grad_gain_moe: float32 [2, 768], P(None, ('head', 'blk'))
- grad_const_gate: float32 [2, 768, 4], P(None, ('head', 'blk'))
- grad_const_vec: float32 [2, 768, 2], P(None, ('head', 'blk'))
- grad_gate: float32 [2, 16384, 768], P(None, 'blk', 'head')
- grad_up: float32 [2, 16384, 768], P(None, 'blk', 'head')
- grad_down: float32 [2, 16384, 768], P(None, 'blk', 'head')
Inputs may be any that keep to these rules, and one draw needn't show every extreme that they name: `routes`: each row names two different experts; in the 128 rows of one device no number is named by more than 40 rows. `segments`: never falling along the positions taken row after row; the first position holds 0 and the last the largest number.
All inputs are finite; a program needn't handle non-finite values.
Results may differ from a plain program's by a relative error of at most 0.04.
Values may be sent and summed in bfloat16 or wider, within the bound.
A program may use at most 384 MiB of HBM per device.

v0:
```python
from functools import partial

import jax
import jax.numpy as jnp
from jax import lax
from jax.sharding import PartitionSpec as P

HEADS = 12
NE = 8
LAYERS = 2
CAP = 40


NEGATIVE = -1e30
EPSILON = 1e-06
HIGHEST_PRECISION = lax.Precision.HIGHEST


def root_square_norm_forward(values, gain_vec):
    row_scale = lax.rsqrt(jnp.mean(values * values, axis=-1, keepdims=True) + EPSILON)
    normed = values * row_scale
    return (normed * gain_vec, normed, row_scale)


def root_square_norm_backward(upstream, normed, row_scale, gain_vec):
    through = upstream * gain_vec
    gain_grad = jnp.sum(upstream * normed, axis=0)
    inner_mean = jnp.mean(through * normed, axis=-1, keepdims=True)
    return (row_scale * (through - normed * inner_mean), gain_grad)


def keep_state(carry_state):
    return carry_state


def to_heads(values):
    arrived = lax.all_to_all(values, "head", split_axis=2, concat_axis=0, tiled=True)
    return arrived.reshape((values.shape[2], values.shape[0], values.shape[1], values.shape[3]))


def to_tokens(values):
    groups, token_rows, kind_count, features = values.shape
    arrived = lax.all_to_all(
        values.reshape((groups * token_rows, kind_count, 1, features)),
        "head",
        split_axis=0,
        concat_axis=2,
        tiled=True,
    )
    return arrived.reshape((token_rows, kind_count * groups * features))


def send_out(buffer, copies):
    experts, capacity, model_width = buffer.shape
    spread = jnp.broadcast_to(buffer[:, None], (experts, copies, capacity, model_width))
    return lax.all_to_all(
        spread.reshape((experts * copies, capacity, model_width)),
        "blk",
        split_axis=0,
        concat_axis=0,
        tiled=True,
    )


def send_home(pieces, experts):
    arrived = lax.all_to_all(pieces, "blk", split_axis=0, concat_axis=0, tiled=True)
    senders, capacity, model_width = arrived.shape
    summed = jnp.sum(
        arrived.reshape((experts, senders // experts, capacity, model_width)).astype(jnp.float32),
        axis=1,
    )
    summed = summed.reshape((experts * capacity, model_width))
    return jnp.concatenate([summed, jnp.zeros((1, model_width), jnp.float32)], axis=0)


def slot_index(route_ids, experts, capacity):
    token_rows = route_ids.shape[0]
    expert_ids = jnp.arange(experts, dtype=jnp.int32)
    matches = (
        (route_ids[:, :, None] == expert_ids[None, None, :])
        .astype(jnp.int32)
        .reshape((token_rows * 2, experts))
    )
    before = jnp.cumsum(matches, axis=0) - 1
    slot_pos = jnp.sum(matches * before, axis=1).reshape((token_rows, 2))
    return jnp.where(route_ids < experts, route_ids * capacity + slot_pos, experts * capacity)


def dispatch_rows(source, slot_ids, experts, capacity):
    token_rows, model_width = (source.shape[0], source.shape[-1])
    flat_rows = jnp.broadcast_to(
        source.reshape((token_rows, -1, model_width)), (token_rows, 2, model_width)
    ).reshape((token_rows * 2, model_width))
    buffer = (
        jnp.zeros((experts * capacity, model_width), source.dtype)
        .at[slot_ids.reshape(-1)]
        .set(flat_rows, mode="drop")
    )
    return buffer.reshape((experts, capacity, model_width))


def allowed_pairs(query_pos, query_seg, key_pos, key_seg):
    return (key_pos[None, :] <= query_pos[:, None]) & (key_seg[None, :] == query_seg[:, None])


def online_step(query_block, key_block, value_block, allowed, score_scale, carry_state):
    running_top, running_total, running_sum = carry_state
    scores = (
        jnp.einsum("qhd,khd->hqk", query_block, key_block, preferred_element_type=jnp.float32)
        * score_scale
    )
    scores = jnp.where(allowed[None], scores, NEGATIVE)
    new_top = jnp.maximum(running_top, jnp.max(scores, axis=-1))
    weights = jnp.exp(scores - new_top[:, :, None]) * allowed[None].astype(jnp.float32)
    shrink = jnp.exp(running_top - new_top)
    new_total = running_total * shrink + jnp.sum(weights, axis=-1)
    update = jnp.einsum(
        "hqk,khd->qhd",
        weights.astype(jnp.bfloat16),
        value_block,
        preferred_element_type=jnp.float32,
    )
    return (new_top, new_total, running_sum * shrink.T[:, :, None] + update)


def score_grads(
    query_block, grad_block, row_lse, row_delta, key_block, value_block, allowed, score_scale
):
    scores = (
        jnp.einsum("qhd,khd->hqk", query_block, key_block, preferred_element_type=jnp.float32)
        * score_scale
    )
    probability = jnp.exp(jnp.where(allowed[None], scores, NEGATIVE) - row_lse[:, :, None])
    prob_grad = jnp.einsum(
        "qhd,khd->hqk", grad_block, value_block, preferred_element_type=jnp.float32
    )
    score_grad = (probability * (prob_grad - row_delta[:, :, None])).astype(jnp.bfloat16)
    return (probability, score_grad)


def query_grad_step(
    query_block,
    grad_block,
    row_lse,
    row_delta,
    key_block,
    value_block,
    allowed,
    score_scale,
    carry_state,
):
    probability, score_grad = score_grads(
        query_block, grad_block, row_lse, row_delta, key_block, value_block, allowed, score_scale
    )
    return (
        carry_state
        + jnp.einsum("hqk,khd->qhd", score_grad, key_block, preferred_element_type=jnp.float32)
        * score_scale
    )


def key_grad_step(
    query_block,
    grad_block,
    row_lse,
    row_delta,
    key_block,
    value_block,
    allowed,
    score_scale,
    carry_state,
):
    probability, score_grad = score_grads(
        query_block, grad_block, row_lse, row_delta, key_block, value_block, allowed, score_scale
    )
    value_acc = jnp.einsum(
        "hqk,qhd->khd",
        probability.astype(jnp.bfloat16),
        grad_block,
        preferred_element_type=jnp.float32,
    )
    key_acc = (
        jnp.einsum("hqk,qhd->khd", score_grad, query_block, preferred_element_type=jnp.float32)
        * score_scale
    )
    return (key_acc, value_acc)


def per_device(
    tokens,
    segments,
    routes,
    gates,
    w_qkv,
    w_out,
    gain_attn,
    gain_moe,
    const_gate,
    const_vec,
    w_gate,
    w_up,
    w_down,
    cotangent,
):
    groups = lax.axis_size("head")
    blocks = lax.axis_size("blk")
    blk_index = lax.axis_index("blk")
    token_rows, model_width = tokens.shape
    local_heads = HEADS // groups
    head_dim = model_width // HEADS
    head_width = local_heads * head_dim
    score_scale = head_dim ** (-0.5)
    copies = blocks // NE
    half_length = blocks * token_rows
    query_count = groups * token_rows
    contract_last = (((1,), (1,)), ((), ()))
    contract_first = (((0,), (0,)), ((), ()))
    offsets = jnp.arange(token_rows, dtype=jnp.int32)
    pos_query = (
        (jnp.arange(groups, dtype=jnp.int32)[:, None] * blocks + blk_index) * token_rows
        + offsets[None, :]
    ).reshape(-1)
    seg_query = segments.reshape(-1)
    residual_state = tokens.astype(jnp.float32)
    kept_state = []
    for layer_index in range(LAYERS):
        layer_full = (
            lax.all_gather(w_qkv[layer_index], ("head", "blk"), axis=0, tiled=True),
            lax.all_gather(w_out[layer_index], ("head", "blk"), axis=0, tiled=True),
            lax.all_gather(gain_attn[layer_index], ("head", "blk"), axis=0, tiled=True),
            lax.all_gather(gain_moe[layer_index], ("head", "blk"), axis=0, tiled=True),
            lax.all_gather(const_gate[layer_index], ("head", "blk"), axis=0, tiled=True),
            lax.all_gather(const_vec[layer_index], ("head", "blk"), axis=0, tiled=True),
        )
        expert_full = (
            lax.all_gather(w_gate[layer_index], "head", axis=1, tiled=True),
            lax.all_gather(w_up[layer_index], "head", axis=1, tiled=True),
            lax.all_gather(w_down[layer_index], "head", axis=1, tiled=True),
        )
        qkv_full, out_full, attention_norm_gain, mixture_norm_gain, cgate_full, cvec_full = (
            layer_full
        )
        attention_norm_gain = attention_norm_gain.astype(jnp.float32)
        mixture_norm_gain = mixture_norm_gain.astype(jnp.float32)
        attention_normed_input, attention_unit_input, attention_inverse_scale = (
            root_square_norm_forward(residual_state, attention_norm_gain)
        )
        attn_in = attention_normed_input.astype(jnp.bfloat16)
        projected = jnp.dot(attn_in, qkv_full, preferred_element_type=jnp.float32).astype(
            jnp.bfloat16
        )
        head_parts = to_heads(projected.reshape((token_rows, 3, groups, head_width)))
        queries = head_parts[:, :, 0]
        key_heads = head_parts[:, :, 1]
        value_heads = head_parts[:, :, 2]
        query_rows = queries.reshape((query_count, local_heads, head_dim))
        start_state = (
            jnp.full((local_heads, query_count), NEGATIVE, jnp.float32),
            jnp.zeros((local_heads, query_count), jnp.float32),
            jnp.zeros((query_count, local_heads, head_dim), jnp.float32),
        )
        carry_state = start_state
        first_row = jnp.int32(0)
        key_piece = lax.all_gather(key_heads, "blk", axis=1, tiled=True)
        value_piece = lax.all_gather(value_heads, "blk", axis=1, tiled=True)
        seg_piece = lax.all_gather(segments, "blk", axis=1, tiled=True)
        piece_rows = key_piece.shape[1]
        for attend_half_index in range(key_piece.shape[0]):
            key_pos = (
                attend_half_index * half_length
                + first_row
                + jnp.arange(piece_rows, dtype=jnp.int32)
            )
            allowed = allowed_pairs(pos_query, seg_query, key_pos, seg_piece[attend_half_index])
            step_fn = partial(
                online_step,
                query_rows,
                key_piece[attend_half_index].reshape((piece_rows, local_heads, head_dim)),
                value_piece[attend_half_index].reshape((piece_rows, local_heads, head_dim)),
                allowed,
                score_scale,
            )
            carry_state = lax.cond(jnp.any(allowed), step_fn, keep_state, carry_state)
        row_top, row_total, row_sum = carry_state
        attn_full = row_sum / row_total.T[:, :, None]
        row_lse = row_top + jnp.log(row_total)
        attn_tok = to_tokens(
            attn_full.astype(jnp.bfloat16).reshape((groups, token_rows, 1, head_width))
        )
        residual_between = residual_state + jnp.dot(
            attn_tok, out_full, preferred_element_type=jnp.float32
        )
        mixture_normed_input, mixture_unit_input, mixture_inverse_scale = root_square_norm_forward(
            residual_between, mixture_norm_gain
        )
        moe_in = mixture_normed_input.astype(jnp.bfloat16)
        moe_float = moe_in.astype(jnp.float32)
        route_ids = routes[layer_index]
        gate_vals = gates[layer_index]
        slot_ids = slot_index(route_ids, NE, CAP)
        received = send_out(dispatch_rows(moe_in, slot_ids, NE, CAP), copies)
        flat_in = received.reshape((-1, model_width))
        gate_pre = lax.dot_general(
            flat_in, expert_full[0], contract_last, preferred_element_type=jnp.float32
        )
        up_pre = lax.dot_general(
            flat_in, expert_full[1], contract_last, preferred_element_type=jnp.float32
        )
        hidden = (jax.nn.silu(gate_pre) * up_pre).astype(jnp.bfloat16)
        part_out = (
            jnp.dot(hidden, expert_full[2], preferred_element_type=jnp.float32)
            .astype(jnp.bfloat16)
            .reshape(received.shape)
        )
        returned = send_home(part_out, NE)
        ffn_out = jnp.sum(gate_vals[:, :, None] * returned[slot_ids], axis=1)
        copy_weight = jnp.sum(jnp.where(route_ids == NE + 1, gate_vals, 0.0), axis=1)
        const_weight = jnp.stack(
            [
                jnp.sum(jnp.where(route_ids == NE + 2 + const_idx, gate_vals, 0.0), axis=1)
                for const_idx in range(2)
            ],
            axis=1,
        )
        mixing = jax.nn.softmax(
            jnp.dot(moe_in, cgate_full, preferred_element_type=jnp.float32).reshape(
                (token_rows, 2, 2)
            ),
            axis=-1,
        )
        vectors = cvec_full.astype(jnp.float32).T
        const_out = jnp.sum(
            const_weight[:, :, None]
            * (mixing[:, :, 0:1] * moe_float[:, None, :] + mixing[:, :, 1:2] * vectors[None]),
            axis=1,
        )
        residual_state = residual_between + ffn_out + copy_weight[:, None] * moe_float + const_out
        kept_state.append(
            (
                qkv_full,
                out_full,
                attention_norm_gain,
                mixture_norm_gain,
                cgate_full,
                expert_full,
                attention_unit_input,
                attention_inverse_scale,
                attn_in,
                queries,
                key_heads,
                value_heads,
                query_rows,
                attn_full,
                row_lse,
                attn_tok,
                mixture_unit_input,
                mixture_inverse_scale,
                moe_float,
                slot_ids,
                gate_vals,
                received,
                copy_weight,
                const_weight,
                mixing,
                vectors,
            )
        )
    upstream = cotangent.astype(jnp.float32)
    layer_results = [None] * LAYERS
    expert_results = [None] * LAYERS
    for layer_index in reversed(range(LAYERS)):
        (
            qkv_full,
            out_full,
            attention_norm_gain,
            mixture_norm_gain,
            cgate_full,
            expert_full,
            attention_unit_input,
            attention_inverse_scale,
            attn_in,
            queries,
            key_heads,
            value_heads,
            query_rows,
            attn_full,
            row_lse,
            attn_tok,
            mixture_unit_input,
            mixture_inverse_scale,
            moe_float,
            slot_ids,
            gate_vals,
            received,
            copy_weight,
            const_weight,
            mixing,
            vectors,
        ) = kept_state[layer_index]
        gate_full, up_full, down_full = expert_full
        mix_grad = const_weight[:, :, None] * upstream[:, None, :]
        alpha_grad = jnp.stack(
            [
                jnp.sum(mix_grad * moe_float[:, None, :], axis=-1),
                jnp.sum(mix_grad * vectors[None], axis=-1),
            ],
            axis=-1,
        )
        logit_grad = (
            mixing * (alpha_grad - jnp.sum(mixing * alpha_grad, axis=-1, keepdims=True))
        ).reshape((token_rows, 4))
        cgate_float = cgate_full.astype(jnp.float32)
        mixture_gradient = (
            copy_weight[:, None] * upstream
            + jnp.sum(mixing[:, :, 0:1] * mix_grad, axis=1)
            + jnp.dot(logit_grad, cgate_float.T, precision=HIGHEST_PRECISION)
        )
        cgate_grad = jnp.dot(moe_float.T, logit_grad, precision=HIGHEST_PRECISION)
        cvec_grad = jnp.sum(mixing[:, :, 1:2] * mix_grad, axis=0).T
        slot_grads = (gate_vals[:, :, None] * upstream[:, None, :]).astype(jnp.bfloat16)
        grad_arrived = send_out(dispatch_rows(slot_grads, slot_ids, NE, CAP), copies)
        flat_grad = grad_arrived.reshape((-1, model_width))
        flat_in = received.reshape((-1, model_width))
        gate_pre = lax.dot_general(
            flat_in, gate_full, contract_last, preferred_element_type=jnp.float32
        )
        up_pre = lax.dot_general(
            flat_in, up_full, contract_last, preferred_element_type=jnp.float32
        )
        sigmoid_gate = jax.nn.sigmoid(gate_pre)
        silu_gate = gate_pre * sigmoid_gate
        hidden = (silu_gate * up_pre).astype(jnp.bfloat16)
        hidden_grad = lax.dot_general(
            flat_grad, down_full, contract_last, preferred_element_type=jnp.float32
        )
        down_wgrad = lax.dot_general(
            hidden, flat_grad, contract_first, preferred_element_type=jnp.float32
        )
        gate_grad_pre = (
            hidden_grad * up_pre * sigmoid_gate * (1.0 + gate_pre * (1.0 - sigmoid_gate))
        ).astype(jnp.bfloat16)
        up_grad_pre = (hidden_grad * silu_gate).astype(jnp.bfloat16)
        gate_wgrad = lax.dot_general(
            gate_grad_pre, flat_in, contract_first, preferred_element_type=jnp.float32
        )
        up_wgrad = lax.dot_general(
            up_grad_pre, flat_in, contract_first, preferred_element_type=jnp.float32
        )
        input_part = (
            (
                jnp.dot(gate_grad_pre, gate_full, preferred_element_type=jnp.float32)
                + jnp.dot(up_grad_pre, up_full, preferred_element_type=jnp.float32)
            )
            .astype(jnp.bfloat16)
            .reshape(received.shape)
        )
        back_rows = send_home(input_part, NE)
        mixture_gradient = mixture_gradient + jnp.sum(back_rows[slot_ids], axis=1)
        middle_grad, gain_second_grad = root_square_norm_backward(
            mixture_gradient, mixture_unit_input, mixture_inverse_scale, mixture_norm_gain
        )
        middle_grad = middle_grad + upstream
        proj_grad = middle_grad.astype(jnp.bfloat16)
        out_wgrad = lax.dot_general(
            attn_tok, proj_grad, contract_first, preferred_element_type=jnp.float32
        )
        attn_grad_tok = lax.dot_general(
            proj_grad, out_full, contract_last, preferred_element_type=jnp.float32
        ).astype(jnp.bfloat16)
        attn_grad = to_heads(attn_grad_tok.reshape((token_rows, 1, groups, head_width)))[:, :, 0]
        grad_rows = attn_grad.reshape((query_count, local_heads, head_dim))
        row_delta = jnp.sum(grad_rows.astype(jnp.float32) * attn_full, axis=-1).T
        lse_rows = row_lse.T.reshape((groups, token_rows, local_heads))
        delta_rows = row_delta.T.reshape((groups, token_rows, local_heads))
        query_start = jnp.zeros((query_count, local_heads, head_dim), jnp.float32)
        key_start = tuple(
            (
                (
                    jnp.zeros((token_rows, local_heads, head_dim), jnp.float32),
                    jnp.zeros((token_rows, local_heads, head_dim), jnp.float32),
                )
                for half_index in range(groups)
            )
        )
        query_carry_state = query_start
        query_first_row = jnp.int32(0)
        query_key_piece = lax.all_gather(key_heads, "blk", axis=1, tiled=True)
        query_value_piece = lax.all_gather(value_heads, "blk", axis=1, tiled=True)
        query_seg_piece = lax.all_gather(segments, "blk", axis=1, tiled=True)
        query_piece_rows = query_key_piece.shape[1]
        for query_half_index in range(query_key_piece.shape[0]):
            query_key_pos = (
                query_half_index * half_length
                + query_first_row
                + jnp.arange(query_piece_rows, dtype=jnp.int32)
            )
            query_allowed = allowed_pairs(
                pos_query, seg_query, query_key_pos, query_seg_piece[query_half_index]
            )
            query_step_fn = partial(
                query_grad_step,
                query_rows,
                grad_rows,
                row_lse,
                row_delta,
                query_key_piece[query_half_index].reshape(
                    (query_piece_rows, local_heads, head_dim)
                ),
                query_value_piece[query_half_index].reshape(
                    (query_piece_rows, local_heads, head_dim)
                ),
                query_allowed,
                score_scale,
            )
            query_carry_state = lax.cond(
                jnp.any(query_allowed), query_step_fn, keep_state, query_carry_state
            )
        query_piece = lax.all_gather(queries, "blk", axis=1, tiled=True)
        grad_piece = lax.all_gather(attn_grad, "blk", axis=1, tiled=True)
        lse_piece = lax.all_gather(lse_rows.astype(jnp.bfloat16), "blk", axis=1, tiled=True).astype(
            jnp.float32
        )
        delta_piece = lax.all_gather(
            delta_rows.astype(jnp.bfloat16), "blk", axis=1, tiled=True
        ).astype(jnp.float32)
        key_seg_piece = lax.all_gather(segments, "blk", axis=1, tiled=True)
        piece_groups = query_piece.shape[0]
        key_piece_rows = query_piece.shape[1]
        piece_pos = (
            jnp.arange(piece_groups, dtype=jnp.int32)[:, None] * half_length
            + jnp.arange(key_piece_rows, dtype=jnp.int32)[None, :]
        ).reshape(-1)
        piece_query = query_piece.reshape((piece_groups * key_piece_rows, local_heads, head_dim))
        piece_grad = grad_piece.reshape((piece_groups * key_piece_rows, local_heads, head_dim))
        piece_lse = lse_piece.reshape((-1, local_heads)).T
        piece_delta = delta_piece.reshape((-1, local_heads)).T
        piece_seg = key_seg_piece.reshape(-1)
        updated = []
        for key_half_index in range(groups):
            own_pos = pos_query[key_half_index * token_rows : (key_half_index + 1) * token_rows]
            own_seg = seg_query[key_half_index * token_rows : (key_half_index + 1) * token_rows]
            key_allowed = allowed_pairs(piece_pos, piece_seg, own_pos, own_seg)
            key_step_fn = partial(
                key_grad_step,
                piece_query,
                piece_grad,
                piece_lse,
                piece_delta,
                key_heads[key_half_index].reshape((token_rows, local_heads, head_dim)),
                value_heads[key_half_index].reshape((token_rows, local_heads, head_dim)),
                key_allowed,
                score_scale,
            )
            updated.append(
                lax.cond(jnp.any(key_allowed), key_step_fn, keep_state, key_start[key_half_index])
            )
        key_grads = tuple(updated)
        key_grad = jnp.stack([pair_state[0] for pair_state in key_grads]).reshape(
            (groups, token_rows, head_width)
        )
        value_grad = jnp.stack([pair_state[1] for pair_state in key_grads]).reshape(
            (groups, token_rows, head_width)
        )
        qkv_grad = jnp.stack(
            [query_carry_state.reshape((groups, token_rows, head_width)), key_grad, value_grad],
            axis=2,
        ).astype(jnp.bfloat16)
        qkv_tok = to_tokens(qkv_grad)
        incoming_gradient = lax.dot_general(
            qkv_tok, qkv_full, contract_last, preferred_element_type=jnp.float32
        )
        qkv_wgrad = lax.dot_general(
            attn_in, qkv_tok, contract_first, preferred_element_type=jnp.float32
        )
        leading_gradient, attention_gain_gradient = root_square_norm_backward(
            incoming_gradient, attention_unit_input, attention_inverse_scale, attention_norm_gain
        )
        upstream = middle_grad + leading_gradient
        layer_results[layer_index] = (
            lax.psum_scatter(qkv_wgrad, ("head", "blk"), scatter_dimension=0, tiled=True),
            lax.psum_scatter(out_wgrad, ("head", "blk"), scatter_dimension=0, tiled=True),
            lax.psum_scatter(
                attention_gain_gradient, ("head", "blk"), scatter_dimension=0, tiled=True
            ),
            lax.psum_scatter(gain_second_grad, ("head", "blk"), scatter_dimension=0, tiled=True),
            lax.psum_scatter(cgate_grad, ("head", "blk"), scatter_dimension=0, tiled=True),
            lax.psum_scatter(cvec_grad, ("head", "blk"), scatter_dimension=0, tiled=True),
        )
        expert_results[layer_index] = (
            lax.psum_scatter(
                gate_wgrad.astype(jnp.bfloat16), "head", scatter_dimension=1, tiled=True
            ).astype(jnp.float32),
            lax.psum_scatter(
                up_wgrad.astype(jnp.bfloat16), "head", scatter_dimension=1, tiled=True
            ).astype(jnp.float32),
            lax.psum_scatter(
                down_wgrad.astype(jnp.bfloat16), "head", scatter_dimension=1, tiled=True
            ).astype(jnp.float32),
        )
    layer_stacks = [jnp.stack(list(grad_group)) for grad_group in zip(*layer_results)]
    expert_stacks = [jnp.stack(list(grad_group)) for grad_group in zip(*expert_results)]
    return (
        residual_state,
        upstream,
        layer_stacks[0],
        layer_stacks[1],
        layer_stacks[2],
        layer_stacks[3],
        layer_stacks[4],
        layer_stacks[5],
        expert_stacks[0],
        expert_stacks[1],
        expert_stacks[2],
    )


def solution(mesh):
    return jax.shard_map(
        per_device,
        mesh=mesh,
        in_specs=(
            P(("head", "blk"), None),
            P(None, "blk"),
            P(None, ("head", "blk"), None),
            P(None, ("head", "blk"), None),
            P(None, ("head", "blk"), None),
            P(None, ("head", "blk"), None),
            P(None, ("head", "blk")),
            P(None, ("head", "blk")),
            P(None, ("head", "blk"), None),
            P(None, ("head", "blk"), None),
            P(None, "blk", "head"),
            P(None, "blk", "head"),
            P(None, "blk", "head"),
            P(("head", "blk"), None),
        ),
        out_specs=(
            P(("head", "blk"), None),
            P(("head", "blk"), None),
            P(None, ("head", "blk"), None),
            P(None, ("head", "blk"), None),
            P(None, ("head", "blk")),
            P(None, ("head", "blk")),
            P(None, ("head", "blk"), None),
            P(None, ("head", "blk"), None),
            P(None, "blk", "head"),
            P(None, "blk", "head"),
            P(None, "blk", "head"),
        ),
        check_vma=False,
    )
```

profile of v0, /device:TPU:12, one launch (start us, length us, event | category | flops | bytes accessed | tf_op | source)
XLA Modules:
  0.0 1850.5 jit_solution(16088831605100327731)
XLA Ops:
  11.3 41.7 %all-reduce.17 = (bf16[768]{0:T(1024)(128)(2,1)S(1)}, bf16[768]{0:T(1024)(128)(2,1)S(1)}, bf16[768]{0:T(1024)(128)(2,1)S(1)}, bf16[768]{0:T(1024)(128)(2,1)}) all-reduce(bf16[768]{0:T(1024)(128)(2,1)S(1)} %dynamic-update-slice, bf16[768]{0:T(1024)(128)(2,1)S(1)} %dynamic-update-slice.1, ...), channel_id=2, replica_groups=mesh['head'=2,'blk'=16] {'head','blk'}, use_global_device_ids=true, to_apply=%add.4 | all-reduce | flops 3072 | bytes 12288
  138.5 44.2 %all-gather.49.cloned.1.call-done = bf16[2,2048,1,384]{1,3,2,0:T(8,128)(2,1)} async-done(((bf16[2,128,1,384]{1,3,2,0:T(8,128)(2,1)}), bf16[2,2048,1,384]{1,3,2,0:T(8,128)(2,1)}) %all-gather.49.cloned.1.call-update) | async-done | bytes 3145744 | tf_op jit(solution)/shard_map/all_gather | solution.py:265
  186.9 24.1 %conditional.12 = (f32[6,256]{1,0:T(8,128)}, f32[6,256]{1,0:T(8,128)S(1)}, f32[256,6,64]{0,2,1:T(8,128)S(1)}) conditional(s32[]{:T(128)} %convert_element_type.306, () %tuple.148, (pred[256,2048]{1,0:T(8,128)(4,1)S(1)}, bf16[256,6,64]{0,2,1:T(8,128)(2,1)S(1)}, bf16[2048,6,64]{0,2,1:T(8,128)(2,1)S(1)}, bf16[2048,6,64]{0,2,1:T(8,128)(2,1)}) %tuple.417), branch_computations={%region_3.4_spmd, %region_4.7_spmd} | conditional | flops 846829568 | bytes 49940504 | solution.py:283
  211.0 25.8 %conditional.13 = (f32[6,256]{1,0:T(8,128)S(1)}, f32[256,6,64]{0,2,1:T(8,128)S(1)}, f32[6,256]{1,0:T(8,128)}) conditional(s32[]{:T(128)} %convert_element_type.305, (f32[6,256]{1,0:T(8,128)}, f32[6,256]{1,0:T(8,128)S(1)}, f32[256,6,64]{0,2,1:T(8,128)S(1)}) %conditional.12, (pred[256,2048]{1,0:T(8,128)(4,1)S(1)}, ...), branch_computations={%region_7.8_spmd.clone, %region_8.11_spmd.clone} | conditional | flops 846926336 | bytes 50364440 | solution.py:283
  301.0 23.3 %all-gather.57.cloned.1.call-done = bf16[1,1024,768]{2,1,0:T(8,128)(2,1)} async-done(((bf16[1,1024,384]{2,1,0:T(8,128)(2,1)}), bf16[1,1024,768]{2,1,0:T(8,128)(2,1)}) %all-gather.57.cloned.1.call-update) | async-done | bytes 1572880 | tf_op jit(solution)/shard_map/all_gather | solution.py:238
  336.5 49.1 %all-gather.9 = bf16[1,768,4]{2,0,1:T(2,128)(2,1)S(1)} all-gather(bf16[1,24,4]{2,0,1:T(2,128)(2,1)S(1)} %copy.499), channel_id=11, replica_groups=mesh['head'=2,'blk'=16] {'head','blk'}, dimensions={1}, use_global_device_ids=true | all-gather | bytes 6336 | tf_op jit(solution)/shard_map/all_gather | solution.py:232
  386.6 39.5 %all-gather.10 = bf16[1,768,2]{2,0,1:T(2,128)(2,1)S(1)} all-gather(bf16[1,24,2]{2,0,1:T(2,128)(2,1)S(1)} %copy.500), channel_id=12, replica_groups=mesh['head'=2,'blk'=16] {'head','blk'}, dimensions={1}, use_global_device_ids=true | all-gather | bytes 3168 | tf_op jit(solution)/shard_map/all_gather | solution.py:233
  455.0 43.2 %all-gather.61.cloned.1.call-done = bf16[2,2048,1,384]{1,3,2,0:T(8,128)(2,1)} async-done(((bf16[2,128,1,384]{1,3,2,0:T(8,128)(2,1)}), bf16[2,2048,1,384]{1,3,2,0:T(8,128)(2,1)}) %all-gather.61.cloned.1.call-update) | async-done | bytes 3145744 | tf_op jit(solution)/shard_map/all_gather | solution.py:264
  502.2 44.0 %all-gather.63.cloned.1.call-done = bf16[2,2048,1,384]{1,3,2,0:T(8,128)(2,1)} async-done(((bf16[2,128,1,384]{1,3,2,0:T(8,128)(2,1)}), bf16[2,2048,1,384]{1,3,2,0:T(8,128)(2,1)}) %all-gather.63.cloned.1.call-update) | async-done | bytes 3145744 | tf_op jit(solution)/shard_map/all_gather | solution.py:265
  550.3 23.6 %conditional.14 = (f32[6,256]{1,0:T(8,128)}, f32[6,256]{1,0:T(8,128)S(1)}, f32[256,6,64]{0,2,1:T(8,128)S(1)}) conditional(s32[]{:T(128)} %convert_element_type.306, () %tuple.151, (pred[256,2048]{1,0:T(8,128)(4,1)S(1)}, bf16[256,6,64]{0,2,1:T(8,128)(2,1)S(1)}, bf16[2048,6,64]{0,2,1:T(8,128)(2,1)S(1)}, bf16[2048,6,64]{0,2,1:T(8,128)(2,1)}) %tuple.421), branch_computations={%region_25.26_spmd, %region_26.29_spmd} | conditional | flops 846829568 | bytes 49940504 | solution.py:283
  573.9 26.0 %conditional.15 = (f32[6,256]{1,0:T(8,128)S(1)}, f32[256,6,64]{0,2,1:T(8,128)S(1)}, f32[6,256]{1,0:T(8,128)}) conditional(s32[]{:T(128)} %convert_element_type.305, (f32[6,256]{1,0:T(8,128)}, f32[6,256]{1,0:T(8,128)S(1)}, f32[256,6,64]{0,2,1:T(8,128)S(1)}) %conditional.14, (pred[256,2048]{1,0:T(8,128)(4,1)S(1)}, ...), branch_computations={%region_29.30_spmd.clone, %region_30.33_spmd.clone} | conditional | flops 846926336 | bytes 50364440 | solution.py:283
  708.7 31.4 %all-to-all-done.9 = bf16[16,40,768]{2,1,0:T(8,128)(2,1)S(1)} async-done(((bf16[16,40,768]{2,1,0:T(8,128)(2,1)}), bf16[16,40,768]{2,1,0:T(8,128)(2,1)S(1)}, u32[]{:S(2)}, u32[]{:S(2)}) %all-to-all-start.9) | async-done | bytes 983072 | tf_op jit(solution)/shard_map/all_to_all | solution.py:66
  747.1 50.5 %all-gather.20 = bf16[1,768,4]{2,0,1:T(2,128)(2,1)} all-gather(bf16[1,24,4]{2,0,1:T(2,128)(2,1)S(1)} %copy.503), channel_id=22, replica_groups=mesh['head'=2,'blk'=16] {'head','blk'}, dimensions={1}, use_global_device_ids=true | all-gather | bytes 6336 | tf_op jit(solution)/shard_map/all_gather | solution.py:232
  798.9 38.1 %all-gather.21 = bf16[1,768,2]{2,0,1:T(2,128)(2,1)S(1)} all-gather(bf16[1,24,2]{2,0,1:T(2,128)(2,1)S(1)} %copy.504), channel_id=23, replica_groups=mesh['head'=2,'blk'=16] {'head','blk'}, dimensions={1}, use_global_device_ids=true | all-gather | bytes 3168 | tf_op jit(solution)/shard_map/all_gather | solution.py:233
  868.9 19.1 %all_gather.126 = bf16[2,2048,6]{1,0,2:T(2,128)(2,1)S(1)} all-gather(bf16[2,128,6]{1,0,2:T(2,128)(2,1)S(1)} %convert_element_type.344), channel_id=1, replica_groups=mesh['head'=2,'blk'=16] {'blk'}, dimensions={1}, use_global_device_ids=true | all-gather | bytes 52224 | tf_op jit(solution)/shard_map/all_gather | solution.py:520
  905.0 19.9 %conditional.16 = (f32[256,6,64]{0,2,1:T(8,128)}) conditional(s32[]{:T(128)} %convert_element_type.306, () %tuple.154, (pred[256,2048]{1,0:T(8,128)(4,1)}, bf16[256,6,64]{0,2,1:T(8,128)(2,1)}, bf16[2048,6,64]{0,2,1:T(8,128)(2,1)}, f32[6,256]{1,0:T(8,128)}, bf16[256,6,64]{0,2,1:T(8,128)(2,1)}, /*index=5*/bf16[2048,6,64]{0,2,1:T(8,128)(2,1)}, ...), branch_computations={%region_55.56_spmd, %region_56.57_spmd} | conditional | flops 1226932224 | bytes 31207432 | solution.py:515
  924.9 20.1 %conditional.17 = (f32[256,6,64]{0,2,1:T(8,128)}) conditional(s32[]{:T(128)} %convert_element_type.305, f32[256,6,64]{0,2,1:T(8,128)} %get-tuple-element.711, (pred[256,2048]{1,0:T(8,128)(4,1)}, bf16[256,6,64]{0,2,1:T(8,128)(2,1)}, bf16[2048,6,64]{0,2,1:T(8,128)(2,1)}, f32[6,256]{1,0:T(8,128)}, bf16[256,6,64]{0,2,1:T(8,128)(2,1)}, ...), branch_computations={%region_57.58_spmd, %region_58.59_spmd} | conditional | flops 1227030528 | bytes 31600648 | solution.py:515
  946.7 18.7 %all_gather.128 = bf16[2,2048,6]{1,0,2:T(2,128)(2,1)S(1)} all-gather(bf16[2,128,6]{1,0,2:T(2,128)(2,1)S(1)} %convert_element_type.346), channel_id=1, replica_groups=mesh['head'=2,'blk'=16] {'blk'}, dimensions={1}, use_global_device_ids=true | all-gather | bytes 52224 | tf_op jit(solution)/shard_map/all_gather | solution.py:523
  979.1 32.2 %conditional.18 = (bf16[1,128,1,384]{3,1,0,2:T(8,128)(2,1)}, bf16[1,128,1,384]{3,1,0,2:T(8,128)(2,1)}) conditional(s32[]{:T(128)} %convert_element_type.341, () %tuple.157, (pred[4096,128]{1,0:T(8,128)(4,1)}, bf16[2,128,3,384]{1,3,2,0:T(8,128)(2,1)}, bf16[4096,6,64]{0,2,1:T(8,128)(2,1)S(1)}, f32[6,4096]{1,0:T(8,128)}, ...), branch_computations={%region_60.61_spmd, %region_61.62_spmd} | conditional | flops 1642217472 | bytes 52854800 | solution.py:555
  1011.3 31.0 %conditional.19 = (bf16[1,128,1,384]{3,1,0,2:T(8,128)(2,1)}, bf16[1,128,1,384]{3,1,0,2:T(8,128)(2,1)}) conditional(s32[]{:T(128)} %convert_element_type.347, () %tuple.159, (pred[4096,128]{1,0:T(8,128)(4,1)}, bf16[2,128,3,384]{1,3,2,0:T(8,128)(2,1)}, bf16[4096,6,64]{0,2,1:T(8,128)(2,1)S(1)}, f32[6,4096]{1,0:T(8,128)}, ...), branch_computations={%region_63.64_spmd, %region_64.65_spmd} | conditional | flops 1642217472 | bytes 52854800 | solution.py:555
  1079.7 28.3 %all-to-all-done.12 = bf16[16,40,768]{2,1,0:T(8,128)(2,1)S(1)} async-done(((bf16[16,40,768]{2,1,0:T(8,128)(2,1)}), bf16[16,40,768]{2,1,0:T(8,128)(2,1)S(1)}, u32[]{:S(2)}, u32[]{:S(2)}) %all-to-all-start.12) | async-done | bytes 983072 | tf_op jit(solution)/shard_map/all_to_all | solution.py:56
  1125.0 26.0 %all-to-all-done.13 = bf16[16,40,768]{2,1,0:T(8,128)(2,1)S(1)} async-done(((bf16[16,40,768]{2,1,0:T(8,128)(2,1)}), bf16[16,40,768]{2,1,0:T(8,128)(2,1)S(1)}, u32[]{:S(2)}, u32[]{:S(2)}) %all-to-all-start.13) | async-done | bytes 983072 | tf_op jit(solution)/shard_map/all_to_all | solution.py:66
  1217.7 18.5 %all_gather.130 = bf16[2,2048,6]{1,0,2:T(2,128)(2,1)S(1)} all-gather(bf16[2,128,6]{1,0,2:T(2,128)(2,1)S(1)} %convert_element_type.359), channel_id=1, replica_groups=mesh['head'=2,'blk'=16] {'blk'}, dimensions={1}, use_global_device_ids=true | all-gather | bytes 52224 | tf_op jit(solution)/shard_map/all_gather | solution.py:520
  1251.7 19.7 %conditional.20 = (f32[256,6,64]{0,2,1:T(8,128)}) conditional(s32[]{:T(128)} %convert_element_type.306, () %tuple.161, (pred[256,2048]{1,0:T(8,128)(4,1)}, bf16[256,6,64]{0,2,1:T(8,128)(2,1)S(1)}, bf16[2048,6,64]{0,2,1:T(8,128)(2,1)}, f32[6,256]{1,0:T(8,128)}, bf16[256,6,64]{0,2,1:T(8,128)(2,1)S(1)}, /*index=5*/bf16[2048,6,64]{0,2,1:T(8,128)(2,1)}, ...), branch_computations={%region_75.76_spmd, %region_76.77_spmd} | conditional | flops 1226932224 | bytes 31207432 | solution.py:515
  1271.4 20.0 %conditional.21 = (f32[256,6,64]{0,2,1:T(8,128)}) conditional(s32[]{:T(128)} %convert_element_type.305, f32[256,6,64]{0,2,1:T(8,128)} %get-tuple-element.713, (pred[256,2048]{1,0:T(8,128)(4,1)}, bf16[256,6,64]{0,2,1:T(8,128)(2,1)S(1)}, bf16[2048,6,64]{0,2,1:T(8,128)(2,1)}, f32[6,256]{1,0:T(8,128)}, bf16[256,6,64]{0,2,1:T(8,128)(2,1)S(1)}, ...), branch_computations={%region_77.78_spmd, %region_78.79_spmd} | conditional | flops 1227030528 | bytes 31600648 | solution.py:515
  1323.8 33.9 %conditional.22 = (bf16[1,128,1,384]{3,1,0,2:T(8,128)(2,1)S(1)}, bf16[1,128,1,384]{3,1,0,2:T(8,128)(2,1)S(1)}) conditional(s32[]{:T(128)} %convert_element_type.341, () %tuple.164, (pred[4096,128]{1,0:T(8,128)(4,1)}, bf16[2,128,3,384]{1,3,2,0:T(8,128)(2,1)}, bf16[4096,6,64]{0,2,1:T(8,128)(2,1)S(1)}, f32[6,4096]{1,0:T(8,128)}, ...), branch_computations={%region_79.80_spmd, %region_80.81_spmd} | conditional | flops 1642217472 | bytes 53248044 | solution.py:555
  1357.7 31.2 %conditional.23 = (bf16[1,128,1,384]{3,1,0,2:T(8,128)(2,1)}, bf16[1,128,1,384]{3,1,0,2:T(8,128)(2,1)}) conditional(s32[]{:T(128)} %convert_element_type.347, () %tuple.166, (pred[4096,128]{1,0:T(8,128)(4,1)}, bf16[2,128,3,384]{1,3,2,0:T(8,128)(2,1)}, bf16[4096,6,64]{0,2,1:T(8,128)(2,1)S(1)}, f32[6,4096]{1,0:T(8,128)}, ...), branch_computations={%region_81.82_spmd, %region_82.83_spmd} | conditional | flops 1642217472 | bytes 52854800 | solution.py:555
  1429.0 59.6 %reduce-scatter.33.cloned.1.call-done = f32[24,768]{1,0:T(8,128)} async-done(((f32[768,768]{1,0:T(8,128)}), f32[24,768]{1,0:T(8,128)}) %reduce-scatter.33.cloned.1.call-update) | async-done | bytes 73744 | tf_op jit(solution)/shard_map/reduce_scatter | solution.py:581
  1488.6 104.1 %reduce-scatter.31.cloned.1.call-done = f32[24,768]{1,0:T(8,128)} async-done(((f32[768,768]{1,0:T(8,128)}), f32[24,768]{1,0:T(8,128)}) %reduce-scatter.31.cloned.1.call-update) | async-done | bytes 73744 | tf_op jit(solution)/shard_map/reduce_scatter | solution.py:581
  1598.0 41.2 %all-reduce.16 = (f32[768]{0:T(1024)S(1)}, f32[768]{0:T(1024)S(1)}, f32[768]{0:T(1024)S(1)}, f32[768]{0:T(1024)S(1)}, f32[768,4]{0,1:T(4,128)S(1)}, /*index=5*/f...) all-reduce(f32[768]{0:T(1024)} %get-tuple-element.523, ...), channel_id=33, replica_groups=mesh['head'=2,'blk'=16] {'head','blk'}, use_global_device_ids=true, to_apply=%region_91.92.clone | all-reduce | flops 12288 | bytes 98304
  1644.9 71.6 %reduce-scatter.29.cloned.1.call-done = f32[24,2304]{1,0:T(8,128)} async-done(((f32[768,2304]{1,0:T(8,128)}), f32[24,2304]{1,0:T(8,128)}) %reduce-scatter.29.cloned.1.call-update) | async-done | bytes 221200 | tf_op jit(solution)/shard_map/reduce_scatter | solution.py:580
  1716.5 125.1 %reduce-scatter.27.cloned.1.call-done = f32[24,2304]{1,0:T(8,128)} async-done(((f32[768,2304]{1,0:T(8,128)}), f32[24,2304]{1,0:T(8,128)}) %reduce-scatter.27.cloned.1.call-update) | async-done | bytes 221200 | tf_op jit(solution)/shard_map/reduce_scatter | solution.py:580
  (696 shorter events, 911.3 us)
Async XLA Ops:
  7.2 65.0 %all-gather.45.cloned.1.call-start = ((), (), s32[]{:S(2)}) async-start(), calls=%async_computation.30 | async-start | bytes 3649536 | tf_op jit(solution)/shard_map/all_gather | solution.py:228
  8.9 125.7 %all-gather.47.cloned.1.call-start = ((), (), s32[]{:S(2)}) async-start(), calls=%async_computation.31 | async-start | bytes 3342336 | tf_op jit(solution)/shard_map/all_gather | solution.py:264
  88.1 94.6 %all-gather.49.cloned.1.call-start = ((), (), s32[]{:S(2)}) async-start(), calls=%async_computation.32 | async-start | bytes 3342336 | tf_op jit(solution)/shard_map/all_gather | solution.py:265
  88.8 158.7 %all-gather.51.cloned.1.call-start = ((), (), s32[]{:S(2)}) async-start(), calls=%async_computation.33 | async-start | bytes 1216512 | tf_op jit(solution)/shard_map/all_gather | solution.py:229
  89.6 177.3 %all-gather.53.cloned.1.call-start = ((), (), s32[]{:S(2)}) async-start(), calls=%async_computation.34 | async-start | bytes 2359296 | tf_op jit(solution)/shard_map/all_gather | solution.py:236
  92.3 203.2 %all-gather.55.cloned.1.call-start = ((), (), s32[]{:S(2)}) async-start(), calls=%async_computation.35 | async-start | bytes 2359296 | tf_op jit(solution)/shard_map/all_gather | solution.py:237
  93.7 230.6 %all-gather.57.cloned.1.call-start = ((), (), s32[]{:S(2)}) async-start(), calls=%async_computation.36 | async-start | bytes 2359296 | tf_op jit(solution)/shard_map/all_gather | solution.py:238
  96.4 336.7 %all-gather.59.cloned.1.call-start = ((), (), s32[]{:S(2)}) async-start(), calls=%async_computation.37 | async-start | bytes 3649536 | tf_op jit(solution)/shard_map/all_gather | solution.py:228
  328.3 100.7 %all-to-all-start.3 = ((bf16[16,40,768]{2,1,0:T(8,128)(2,1)}), bf16[16,40,768]{2,1,0:T(8,128)(2,1)S(1)}, u32[]{:S(2)}, u32[]{:S(2)}) async-start(bf16[16,40,768]{2,1,0:T(8,128)(2,1)} %bitcast.625), calls=%async_computation.3 | async-start | bytes 1966080 | tf_op jit(solution)/shard_map/all_to_all | solution.py:66
  334.3 163.9 %all-gather.61.cloned.1.call-start = ((), (), s32[]{:S(2)}) async-start(), calls=%async_computation.38 | async-start | bytes 3342336 | tf_op jit(solution)/shard_map/all_gather | solution.py:264
  450.3 95.9 %all-gather.63.cloned.1.call-start = ((), (), s32[]{:S(2)}) async-start(), calls=%async_computation.39 | async-start | bytes 3342336 | tf_op jit(solution)/shard_map/all_gather | solution.py:265
  450.9 165.9 %all-gather.65.cloned.1.call-start = ((), (), s32[]{:S(2)}) async-start(), calls=%async_computation.40 | async-start | bytes 1216512 | tf_op jit(solution)/shard_map/all_gather | solution.py:229
  451.6 194.2 %all-gather.71.cloned.1.call-start = ((), (), s32[]{:S(2)}) async-start(), calls=%async_computation.43 | async-start | bytes 2359296 | tf_op jit(solution)/shard_map/all_gather | solution.py:238
  615.5 43.2 %all-gather.69.cloned.1.call-start = ((), (), s32[]{:S(2)}) async-start(), calls=%async_computation.42 | async-start | bytes 2359296 | tf_op jit(solution)/shard_map/all_gather | solution.py:237
  645.0 42.3 %all-gather.67.cloned.1.call-start = ((), (), s32[]{:S(2)}) async-start(), calls=%async_computation.41 | async-start | bytes 2359296 | tf_op jit(solution)/shard_map/all_gather | solution.py:236
  645.6 243.2 %all-gather.73.cloned.1.call-start = ((), (), s32[]{:S(2)}) async-start(), calls=%async_computation.44 | async-start | bytes 3342336 | tf_op jit(solution)/shard_map/all_gather | solution.py:518
  698.6 41.6 %all-to-all-start.9 = ((bf16[16,40,768]{2,1,0:T(8,128)(2,1)}), bf16[16,40,768]{2,1,0:T(8,128)(2,1)S(1)}, u32[]{:S(2)}, u32[]{:S(2)}) async-start(bf16[16,40,768]{2,1,0:T(8,128)(2,1)} %bitcast.627), calls=%async_computation.9 | async-start | bytes 1966080 | tf_op jit(solution)/shard_map/all_to_all | solution.py:66
  740.2 107.7 %all-to-all-start.7 = ((bf16[16,40,768]{2,1,0:T(8,128)(2,1)}), bf16[16,40,768]{2,1,0:T(8,128)(2,1)S(1)}, u32[]{:S(2)}, u32[]{:S(2)}) async-start(bf16[16,40,768]{2,1,0:T(8,128)(2,1)} %bitcast.624), calls=%async_computation.7 | async-start | bytes 1966080 | tf_op jit(solution)/shard_map/all_to_all | solution.py:66
  746.1 220.0 %all-gather.75.cloned.1.call-start = ((), (), s32[]{:S(2)}) async-start(), calls=%async_computation.45 | async-start | bytes 3342336 | tf_op jit(solution)/shard_map/all_gather | solution.py:519
  1072.4 35.6 %all-to-all-start.12 = ((bf16[16,40,768]{2,1,0:T(8,128)(2,1)}), bf16[16,40,768]{2,1,0:T(8,128)(2,1)S(1)}, u32[]{:S(2)}, u32[]{:S(2)}) async-start(bf16[16,40,768]{2,1,0:T(8,128)(2,1)} %bitcast.159), calls=%async_computation.12 | async-start | bytes 1966080 | tf_op jit(solution)/shard_map/all_to_all | solution.py:56
  1079.1 157.9 %all-gather.77.cloned.1.call-start = ((), (), s32[]{:S(2)}) async-start(), calls=%async_computation.46 | async-start | bytes 3342336 | tf_op jit(solution)/shard_map/all_gather | solution.py:518
  1123.7 187.2 %all-gather.79.cloned.1.call-start = ((), (), s32[]{:S(2)}) async-start(), calls=%async_computation.47 | async-start | bytes 3342336 | tf_op jit(solution)/shard_map/all_gather | solution.py:519
  1167.4 244.2 %reduce-scatter.45.cloned.1.call-start = ((), (), s32[]{:S(2)}) async-start(), calls=%async_computation.53 | async-start | bytes 2359296
  1174.4 238.8 %reduce-scatter.41.cloned.1.call-start = ((), (), s32[]{:S(2)}) async-start(), calls=%async_computation.51 | async-start | bytes 2359296
  1180.9 233.8 %reduce-scatter.37.cloned.1.call-start = ((), (), s32[]{:S(2)}) async-start(), calls=%async_computation.49 | async-start | bytes 2359296
  1187.6 230.2 %reduce-scatter.43.cloned.1.call-start = ((), (), s32[]{:S(2)}) async-start(), calls=%async_computation.52 | async-start | bytes 2359296
  1194.3 225.0 %reduce-scatter.39.cloned.1.call-start = ((), (), s32[]{:S(2)}) async-start(), calls=%async_computation.50 | async-start | bytes 2359296
  1201.0 219.9 %reduce-scatter.35.cloned.1.call-start = ((), (), s32[]{:S(2)}) async-start(), calls=%async_computation.48 | async-start | bytes 2359296
  1207.7 280.9 %reduce-scatter.33.cloned.1.call-start = ((), (), s32[]{:S(2)}) async-start(), calls=%async_computation.29 | async-start | bytes 2433024 | tf_op jit(solution)/shard_map/reduce_scatter | solution.py:581
  1209.6 383.0 %reduce-scatter.31.cloned.1.call-start = ((), (), s32[]{:S(2)}) async-start(), calls=%async_computation.28 | async-start | bytes 2433024 | tf_op jit(solution)/shard_map/reduce_scatter | solution.py:581
  1211.6 504.9 %reduce-scatter.29.cloned.1.call-start = ((), (), s32[]{:S(2)}) async-start(), calls=%async_computation.27 | async-start | bytes 7299072 | tf_op jit(solution)/shard_map/reduce_scatter | solution.py:580
  1215.7 626.0 %reduce-scatter.27.cloned.1.call-start = ((), (), s32[]{:S(2)}) async-start(), calls=%async_computation.26 | async-start | bytes 7299072 | tf_op jit(solution)/shard_map/reduce_scatter | solution.py:580
  (122 other events, 3579.1 us)
Sparse Core Ops, SparseCore 0:
  11.5 60.6 all-gather.44
  88.2 46.3 all-gather.46
  137.3 45.3 all-gather.48
  186.1 52.5 all-gather.50
  240.6 26.1 all-gather.52
  268.3 27.2 all-gather.54
  297.0 27.2 all-gather.56
  327.7 68.5 all-gather.58
  450.4 47.7 all-gather.60
  500.8 45.3 all-gather.62
  549.7 52.5 all-gather.64
  603.7 26.1 all-gather.70
  631.4 27.2 all-gather.68
  660.1 27.2 all-gather.66
  689.3 55.9 all-gather.72
  863.2 46.9 all-gather.74
  1081.8 55.0 all-gather.76
  1167.6 46.5 all-gather.78
  1216.4 24.6 reduce-scatter.44
  1243.3 26.0 reduce-scatter.40
  1272.2 26.0 reduce-scatter.36
  1300.7 26.0 reduce-scatter.42
  1329.0 26.0 reduce-scatter.38
  1357.4 26.0 reduce-scatter.34
  1388.8 99.7 reduce-scatter.32
  1494.6 98.0 reduce-scatter.30
  1598.2 118.2 reduce-scatter.28
  1723.1 118.4 reduce-scatter.26
where the time goes:
time: 1860 us; the launch traced here: 1850 us
  waiting for transfers between devices  731 us (39%)
  blocking collectives  404 us (22%)
  matrix products  356 us (19%)
  local copies, waits for them, and re-layouts  179 us (10%)
  other arithmetic  95.8 us (5%)
  starting transfers between devices  62.6 us (3%)
  between operations  19.3 us (1%)
    reduce_scatter x2, waiting for transfers between devices, per_device(): lax.psum_scatter(qkv_wgrad, ('head', 'blk'), scatter_dimension=0, tiled=T...  197 us
    reduce_scatter x2, waiting for transfers between devices, per_device(): lax.psum_scatter(out_wgrad, ('head', 'blk'), scatter_dimension=0, tiled=T...  164 us
    all_gather x2, blocking collectives, per_device(): lax.all_gather(const_gate[layer_index], ('head', 'blk'), axis=0, tiled=True)  99.7 us
    all_gather x2, waiting for transfers between devices, per_device(): value_piece = lax.all_gather(value_heads, 'blk', axis=1, tiled=True)  88.3 us
    unnamed x2, blocking collectives  82.8 us
    all_gather x2, blocking collectives, per_device(): lax.all_gather(const_vec[layer_index], ('head', 'blk'), axis=0, tiled=True)  77.5 us
    all_to_all x4, waiting for transfers between devices, send_out(): lax.all_to_all(spread.reshape((experts * copies, capacity, model_width)),...  67.5 us
    all_to_all x4, waiting for transfers between devices, send_home(): lax.all_to_all(pieces, 'blk', split_axis=0, concat_axis=0, tiled=True)  57.4 us
  transfers between devices with their start and end apart: 39, of which 23 were waited for; matrix products, arithmetic and copies ran while one was open for 28% of the time, Pallas kernels for 0%

commit v1 on v0

v1 whole, which is shorter than its diff:
```python
from functools import partial

import jax
import jax.numpy as jnp
from jax import lax
from jax.experimental import pallas as pl
from jax.experimental.pallas import tpu as pltpu
from jax.sharding import PartitionSpec as P

HEADS = 12
NE = 8
LAYERS = 2
CAP = 40
COLUMNS = 4
MESH = pl.DeviceIdType.MESH
ANY = pl.BlockSpec(memory_space=pl.ANY)
VMEM = pl.BlockSpec(memory_space=pltpu.VMEM)
DMA = pltpu.SemaphoreType.DMA
VMEM_BYTES = 48 * 1024 * 1024


def greet(peers):
    barrier = pltpu.get_barrier_semaphore()
    for peer in peers:
        pl.semaphore_signal(barrier, inc=1, device_id=peer, device_id_type=MESH)
    pl.semaphore_wait(barrier, len(peers))


def remote(src, dst, send_sem, recv_sem, peer):
    return pltpu.make_async_remote_copy(
        src_ref=src,
        dst_ref=dst,
        send_sem=send_sem,
        recv_sem=recv_sem,
        device_id=peer,
        device_id_type=MESH,
    )


def comm_params(collective_id):
    return pltpu.CompilerParams(
        collective_id=collective_id, has_side_effects=True, vmem_limit_bytes=VMEM_BYTES
    )


def column_exchange(values, blocks, gather, collective_id):
    span = blocks // COLUMNS
    slab = values.shape if gather else values.shape[1:]

    def body(src, dst, own_sem, send_sems, recv_sems):
        head, blk = lax.axis_index("head"), lax.axis_index("blk")
        plane, rest = lax.div(blk, span), lax.rem(blk, span)
        planes = [lax.rem(plane + d, COLUMNS) for d in range(COLUMNS)]
        peers = [(head, p * span + rest) for p in planes]
        greet(peers[1:])
        own = pltpu.make_async_copy(src if gather else src.at[plane], dst.at[plane], own_sem)
        own.start()
        copies = []
        for d in (2, 1, 3):
            copy = remote(
                src if gather else src.at[planes[d]],
                dst.at[plane],
                send_sems.at[d],
                recv_sems.at[d],
                peers[d],
            )
            copy.start()
            copies.append(copy)
        own.wait()
        for copy in copies:
            copy.wait()

    return pl.pallas_call(
        body,
        out_shape=jax.ShapeDtypeStruct((COLUMNS,) + tuple(slab), values.dtype),
        in_specs=[ANY],
        out_specs=ANY,
        scratch_shapes=[DMA, DMA((COLUMNS,)), DMA((COLUMNS,))],
        compiler_params=comm_params(collective_id),
    )(values)


def plane_gather(values, blocks, collective_id):
    span = blocks // COLUMNS
    width = span // 2
    half = values.shape[0] // 2
    links = 4 * (width - 1) + 2

    def body(src, dst, own_sem, send_sems, recv_sems, pass_sems, land_sems):
        head, blk = lax.axis_index("head"), lax.axis_index("blk")
        plane, rest = lax.div(blk, span), lax.rem(blk, span)
        x, core = lax.div(rest, 2), lax.rem(rest, 2)
        first = plane * span
        right = [lax.rem(x + d, width) for d in range(width)]
        left = [lax.rem(x - d + width, width) for d in range(width)]
        x_peers = [(head, first + right[d] * 2 + core) for d in range(width)]
        y_peer = (1 - head, blk)
        core_peer = (head, first + x * 2 + 1 - core)
        greet(x_peers[1:] + [y_peer, core_peer])

        def part(h):
            return src.at[pl.ds(h * half, half)]

        def place(h, dy, d):
            row = head if dy == 0 else 1 - head
            return dst.at[row, pl.ds(h * half, half), left[d] * 2 + core]

        sends = []

        def send(h, dy, d, peer, to_dy, to_d):
            copy = remote(
                part(h) if dy == 0 and d == 0 else place(h, dy, d),
                place(h, dy, d),
                send_sems.at[len(sends)],
                recv_sems.at[h, to_dy, to_d],
                peer,
            )
            copy.start()
            sends.append(copy)

        passes = []

        def hand_over(h, dy, d):
            copy = remote(
                part(h) if dy == 0 and d == 0 else place(h, dy, d),
                place(h, dy, d),
                pass_sems.at[h, dy, d],
                land_sems.at[h, dy, d],
                core_peer,
            )
            copy.start()
            passes.append(copy)

        def arrived(h, dy, d):
            remote(
                place(h, dy, d), place(h, dy, d), send_sems.at[0], recv_sems.at[h, dy, d], y_peer
            ).wait_recv()

        own = pltpu.make_async_copy(src, dst.at[head, :, rest], own_sem)
        own.start()
        for d in range(1, width):
            send(0, 0, 0, x_peers[d], 0, d)
        send(1, 0, 0, y_peer, 1, 0)
        send(0, 0, 0, y_peer, 1, 0)
        for d in range(1, width):
            send(1, 0, 0, x_peers[d], 0, d)
        hand_over(0, 0, 0)
        hand_over(1, 0, 0)
        for d in range(1, width):
            arrived(0, 0, d)
            send(0, 0, d, y_peer, 1, d)
            hand_over(0, 0, d)
        arrived(1, 1, 0)
        for d in range(1, width):
            send(1, 1, 0, x_peers[d], 1, d)
        hand_over(1, 1, 0)
        arrived(0, 1, 0)
        hand_over(0, 1, 0)
        for d in range(1, width):
            arrived(1, 0, d)
            hand_over(1, 0, d)
        for d in range(1, width):
            arrived(0, 1, d)
            hand_over(0, 1, d)
            arrived(1, 1, d)
            hand_over(1, 1, d)
        own.wait()
        for copy in passes:
            copy.wait()
        for copy in sends:
            copy.wait_send()

    return pl.pallas_call(
        body,
        out_shape=jax.ShapeDtypeStruct(
            (2, values.shape[0], span) + tuple(values.shape[1:]), values.dtype
        ),
        in_specs=[ANY],
        out_specs=ANY,
        scratch_shapes=[
            DMA,
            DMA((links,)),
            DMA((2, 2, width)),
            DMA((2, 2, width)),
            DMA((2, 2, width)),
        ],
        compiler_params=comm_params(collective_id),
    )(values)


def plane_reduce(values, blocks, collective_id):
    span = blocks // COLUMNS
    width = span // 2
    slabs, rows, cols = values.shape[1], values.shape[3], values.shape[4]
    half = slabs // 2
    kind = values.dtype

    def body(
        src,
        out,
        core_in,
        summed,
        xa_in,
        ya_out,
        ya_in,
        yb_in,
        xb_out,
        xb_in,
        core_send,
        core_recv,
        link_send,
        link_recv,
    ):
        head, blk = lax.axis_index("head"), lax.axis_index("blk")
        plane, rest = lax.div(blk, span), lax.rem(blk, span)
        x, core = lax.div(rest, 2), lax.rem(rest, 2)
        first = plane * span
        right = [lax.rem(x + d, width) for d in range(width)]
        x_peers = [(head, first + right[d] * 2 + core) for d in range(width)]
        y_peer = (1 - head, blk)
        core_peer = (head, first + x * 2 + 1 - core)
        greet(x_peers[1:] + [y_peer, core_peer])

        def wide(ref, *at):
            return ref[at].astype(jnp.float32)

        starts = []
        for h in range(2):
            copy = remote(
                src.at[:, pl.ds(h * half, half), :, 1 - core],
                core_in.at[:, pl.ds(h * half, half)],
                core_send.at[h],
                core_recv.at[h],
                core_peer,
            )
            copy.start()
            starts.append(copy)

        def core_sum(h):
            def step(i, _):
                yy = lax.div(i, half * width)
                zz = lax.div(lax.rem(i, half * width), width) + h * half
                xx = lax.rem(i, width)
                total = wide(src, yy, zz, xx, core) + wide(core_in, yy, zz, xx)
                summed[yy, zz, xx] = total.astype(kind)
                return 0

            lax.fori_loop(0, 2 * half * width, step, 0)

        sends = []
        starts[0].wait_recv()
        core_sum(0)
        for d in range(1, width):
            copy = remote(
                summed.at[:, pl.ds(0, half), right[d]],
                xa_in.at[d],
                link_send.at[0, d],
                link_recv.at[0, d],
                x_peers[d],
            )
            copy.start()
            sends.append(copy)
        starts[1].wait_recv()
        core_sum(1)
        yb = remote(
            summed.at[1 - head, pl.ds(half, half)],
            yb_in,
            link_send.at[1, 0],
            link_recv.at[1, 0],
            y_peer,
        )
        yb.start()
        for copy in sends:
            copy.wait_recv()

        def a_step(zz, _):
            total = wide(summed, 1 - head, zz, x)
            for d in range(1, width):
                total = total + wide(xa_in, d, 1 - head, zz)
            ya_out[zz] = total.astype(kind)
            return 0

        lax.fori_loop(0, half, a_step, 0)
        ya = remote(ya_out, ya_in, link_send.at[0, 0], link_recv.at[0, 0], y_peer)
        ya.start()
        yb.wait_recv()
        xb_sends = []
        for d in range(1, width):

            def b_step(zz, _):
                total = wide(summed, head, half + zz, right[d]) + wide(yb_in, zz, right[d])
                xb_out[d, zz] = total.astype(kind)
                return 0

            lax.fori_loop(0, half, b_step, 0)
            copy = remote(
                xb_out.at[d], xb_in.at[d], link_send.at[1, d], link_recv.at[1, d], x_peers[d]
            )
            copy.start()
            xb_sends.append(copy)
        ya.wait_recv()

        def a_last(zz, _):
            total = wide(summed, head, zz, x) + wide(ya_in, zz)
            for d in range(1, width):
                total = total + wide(xa_in, d, head, zz)
            out[zz] = total.astype(kind)
            return 0

        lax.fori_loop(0, half, a_last, 0)
        for copy in xb_sends:
            copy.wait_recv()

        def b_last(zz, _):
            total = wide(summed, head, half + zz, x) + wide(yb_in, zz, x)
            for d in range(1, width):
                total = total + wide(xb_in, d, zz)
            out[half + zz] = total.astype(kind)
            return 0

        lax.fori_loop(0, half, b_last, 0)
        for copy in starts + sends + [yb, ya] + xb_sends:
            copy.wait_send()

    tile = (rows, cols)
    return pl.pallas_call(
        body,
        out_shape=jax.ShapeDtypeStruct((slabs,) + tile, kind),
        in_specs=[VMEM],
        out_specs=VMEM,
        scratch_shapes=[
            pltpu.VMEM((2, slabs, width) + tile, kind),
            pltpu.VMEM((2, slabs, width) + tile, kind),
            pltpu.VMEM((width, 2, half) + tile, kind),
            pltpu.VMEM((half,) + tile, kind),
            pltpu.VMEM((half,) + tile, kind),
            pltpu.VMEM((half, width) + tile, kind),
            pltpu.VMEM((width, half) + tile, kind),
            pltpu.VMEM((width, half) + tile, kind),
            DMA((2,)),
            DMA((2,)),
            DMA((2, width)),
            DMA((2, width)),
        ],
        compiler_params=comm_params(collective_id),
    )(values.reshape((2, slabs, width, 2) + tile))


def expert_dispatch(buffer, blocks, collective_id):
    copies = blocks // NE
    tile = tuple(buffer.shape[1:])

    def body(src, dst, own_sem, send_sems, recv_sems, pass_sems, land_sems):
        head, blk = lax.axis_index("head"), lax.axis_index("blk")
        expert, piece = lax.div(blk, copies), lax.rem(blk, copies)
        ahead = [lax.rem(expert + d, NE) for d in range(NE)]
        behind = [lax.rem(expert - d + NE, NE) for d in range(NE)]
        peers = [(head, ahead[d] * copies + piece) for d in range(NE)]
        siblings = [
            (head, expert * copies + lax.rem(piece + k, copies)) for k in range(copies)
        ]
        greet(peers[1:] + siblings[1:])
        own = pltpu.make_async_copy(src.at[expert], dst.at[piece, expert], own_sem)
        own.start()
        sends, passes = [], []
        for d in (4, 3, 5, 2, 6, 1, 7):
            copy = remote(
                src.at[ahead[d]],
                dst.at[piece, expert],
                send_sems.at[d],
                recv_sems.at[d],
                peers[d],
            )
            copy.start()
            sends.append(copy)
        for d in (0, 1, 7, 2, 6, 3, 5, 4):
            place = dst.at[piece, behind[d]]
            if d > 0:
                remote(place, place, send_sems.at[d], recv_sems.at[d], peers[d]).wait_recv()
            for k in range(1, copies):
                copy = remote(
                    place if d > 0 else src.at[expert],
                    place,
                    pass_sems.at[k, d],
                    land_sems.at[k, d],
                    siblings[k],
                )
                copy.start()
                passes.append(copy)
        own.wait()
        for copy in passes:
            copy.wait()
        for copy in sends:
            copy.wait_send()

    return pl.pallas_call(
        body,
        out_shape=jax.ShapeDtypeStruct((copies, NE) + tile, buffer.dtype),
        in_specs=[ANY],
        out_specs=ANY,
        scratch_shapes=[DMA, DMA((NE,)), DMA((NE,)), DMA((copies, NE)), DMA((copies, NE))],
        compiler_params=comm_params(collective_id),
    )(buffer)


def expert_return(parts, blocks, collective_id):
    copies = blocks // NE
    tile = tuple(parts.shape[2:])
    kind = parts.dtype

    def body(src, dst, sib_in, total, own_sem, send_sems, recv_sems, pass_sems, land_sems):
        head, blk = lax.axis_index("head"), lax.axis_index("blk")
        expert, piece = lax.div(blk, copies), lax.rem(blk, copies)
        ahead = [lax.rem(expert + d, NE) for d in range(NE)]
        peers = [(head, ahead[d] * copies + piece) for d in range(NE)]
        places = [lax.rem(piece + k, copies) for k in range(copies)]
        siblings = [(head, expert * copies + places[k]) for k in range(copies)]
        greet(peers[1:] + siblings[1:])
        order = (4, 3, 5, 2, 6, 1, 7, 0)
        passes, sends = {}, []
        for d in order:
            for k in range(1, copies):
                copy = remote(
                    src.at[places[k], ahead[d]],
                    sib_in.at[k, ahead[d]],
                    pass_sems.at[k, d],
                    land_sems.at[k, d],
                    siblings[k],
                )
                copy.start()
                passes[k, d] = copy
        for d in order:
            value = src[piece, ahead[d]].astype(jnp.float32)
            for k in range(1, copies):
                passes[k, d].wait_recv()
                value = value + sib_in[k, ahead[d]].astype(jnp.float32)
            total[ahead[d]] = value.astype(kind)
            if d > 0:
                copy = remote(
                    total.at[ahead[d]],
                    dst.at[expert],
                    send_sems.at[d],
                    recv_sems.at[d],
                    peers[d],
                )
                copy.start()
                sends.append(copy)
        own = pltpu.make_async_copy(total.at[expert], dst.at[expert], own_sem)
        own.start()
        own.wait()
        for copy in sends:
            copy.wait()
        for copy in passes.values():
            copy.wait_send()

    return pl.pallas_call(
        body,
        out_shape=jax.ShapeDtypeStruct((NE,) + tile, kind),
        in_specs=[VMEM],
        out_specs=ANY,
        scratch_shapes=[
            pltpu.VMEM((copies, NE) + tile, kind),
            pltpu.VMEM((NE,) + tile, kind),
            DMA,
            DMA((NE,)),
            DMA((NE,)),
            DMA((copies, NE)),
            DMA((copies, NE)),
        ],
        compiler_params=comm_params(collective_id),
    )(parts)


NEGATIVE = -1e30
EPSILON = 1e-06
HIGHEST = lax.Precision.HIGHEST
KEYS = 512
LANES = 128
LAST = (((1,), (1,)), ((), ()))
FIRST = (((0,), (0,)), ((), ()))


def dot32(a, b, dims=(((1,), (0,)), ((), ()))):
    return lax.dot_general(a, b, dims, preferred_element_type=jnp.float32)


def visible(key_base, query_base, keys, queries, starts):
    key_pos = key_base + lax.broadcasted_iota(jnp.int32, (keys, queries), 0)
    query_pos = query_base + lax.broadcasted_iota(jnp.int32, (keys, queries), 1)
    return (key_pos <= query_pos) & (key_pos >= starts)


def attend(bounds, queries, kv_all, starts):
    count, rows, width = queries.shape
    heads = width // LANES

    def body(bounds_ref, q_ref, kv_ref, start_ref, out_ref):
        i = pl.program_id(0)
        low, high, base = bounds_ref[i, 0], bounds_ref[i, 1], bounds_ref[i, 2]
        start_row = start_ref[0]
        q = [q_ref[0, :, h * LANES : (h + 1) * LANES] for h in range(heads)]

        def step(t, carry):
            chunk = high - t
            at = pl.multiple_of(chunk * KEYS, KEYS)
            ok = visible(chunk * KEYS, base, KEYS, rows, start_row)
            new = []
            for h in range(heads):
                top, total, acc = carry[h]
                kv = kv_ref[pl.ds(at, KEYS), h * LANES : (h + 1) * LANES]
                score = jnp.where(ok, dot32(kv, q[h], LAST), NEGATIVE)
                new_top = jnp.maximum(top, jnp.max(score, axis=0, keepdims=True))
                weight = jnp.exp(score - new_top)
                shrink = jnp.exp(top - new_top)
                total = total * shrink + jnp.sum(weight, axis=0, keepdims=True)
                acc = acc * shrink + dot32(kv, weight.astype(jnp.bfloat16), FIRST)
                new.append((new_top, total, acc))
            return tuple(new)

        empty = tuple(
            (
                jnp.full((1, rows), NEGATIVE, jnp.float32),
                jnp.zeros((1, rows), jnp.float32),
                jnp.zeros((LANES, rows), jnp.float32),
            )
            for h in range(heads)
        )
        done = lax.fori_loop(0, high - low + 1, step, empty)
        lane = lax.broadcasted_iota(jnp.int32, (LANES, rows), 0)
        for h in range(heads):
            top, total, acc = done[h]
            value = jnp.where(lane < LANES // 2, top + jnp.log(total), acc / total)
            out_ref[0, :, h * LANES : (h + 1) * LANES] = value.T

    return pl.pallas_call(
        body,
        out_shape=jax.ShapeDtypeStruct((count, rows, width), jnp.float32),
        grid_spec=pltpu.PrefetchScalarGridSpec(
            num_scalar_prefetch=1,
            grid=(count,),
            in_specs=[
                pl.BlockSpec((1, rows, width), lambda i, b: (i, 0, 0)),
                pl.BlockSpec(kv_all.shape, lambda i, b: (0, 0)),
                pl.BlockSpec((1, 1, rows), lambda i, b: (i, 0, 0)),
            ],
            out_specs=pl.BlockSpec((1, rows, width), lambda i, b: (i, 0, 0)),
        ),
        compiler_params=pltpu.CompilerParams(vmem_limit_bytes=VMEM_BYTES),
        cost_estimate=pl.CostEstimate(
            flops=2 * count * rows * kv_all.shape[0] * width,
            bytes_accessed=kv_all.size * 2,
            transcendentals=count * rows * kv_all.shape[0],
        ),
    )(bounds, queries, kv_all, starts)


def attend_back(bounds, queries, grads, kept, kv_all, starts, scale):
    count, rows, width = queries.shape
    total_keys = kv_all.shape[0]
    heads = width // LANES
    if total_keys * width * 14 > VMEM_BYTES:
        heads = 1
    wide = heads * LANES

    def body(bounds_ref, q_ref, g_ref, kept_ref, kv_ref, start_ref, dq_ref, dkv_ref, acc_ref):
        i = pl.program_id(1)
        low, high, base = bounds_ref[i, 0], bounds_ref[i, 1], bounds_ref[i, 2]
        start_row = start_ref[0]

        @pl.when(i == 0)
        def _():
            def clear(c, _):
                acc_ref[pl.ds(pl.multiple_of(c * KEYS, KEYS), KEYS), :] = jnp.zeros(
                    (KEYS, wide), jnp.float32
                )
                return 0

            lax.fori_loop(0, total_keys // KEYS, clear, 0)

        q = [q_ref[0, :, h * LANES : (h + 1) * LANES] for h in range(heads)]
        g = [g_ref[0, :, h * LANES : (h + 1) * LANES] for h in range(heads)]
        lse, delta = [], []
        for h in range(heads):
            kept_t = kept_ref[0, :, h * LANES : (h + 1) * LANES].T
            lse.append(kept_t[0:1])
            delta.append(jnp.sum(kept_t * g[h].astype(jnp.float32).T, axis=0, keepdims=True))

        def step(t, carry):
            chunk = high - t
            at = pl.multiple_of(chunk * KEYS, KEYS)
            ok = visible(chunk * KEYS, base, KEYS, rows, start_row)
            new = []
            for h in range(heads):
                lanes = slice(h * LANES, (h + 1) * LANES)
                kv = kv_ref[pl.ds(at, KEYS), lanes]
                score = jnp.where(ok, dot32(kv, q[h], LAST), NEGATIVE)
                prob = jnp.exp(score - lse[h])
                dscore = (prob * (dot32(kv, g[h], LAST) - delta[h])).astype(jnp.bfloat16)
                acc_ref[pl.ds(at, KEYS), lanes] += dot32(dscore, q[h]) + dot32(
                    prob.astype(jnp.bfloat16), g[h]
                )
                new.append(carry[h] + dot32(kv, dscore, FIRST))
            return tuple(new)

        done = lax.fori_loop(
            0,
            high - low + 1,
            step,
            tuple(jnp.zeros((LANES, rows), jnp.float32) for h in range(heads)),
        )
        lane = lax.broadcasted_iota(jnp.int32, (LANES, rows), 0)
        for h in range(heads):
            value = jnp.where(lane < LANES // 2, done[h] * scale, 0.0)
            dq_ref[0, :, h * LANES : (h + 1) * LANES] = value.T.astype(jnp.bfloat16)

        @pl.when(i == count - 1)
        def _():
            def store(c, _):
                at = pl.ds(pl.multiple_of(c * KEYS, KEYS), KEYS)
                dkv_ref[at, :] = acc_ref[at, :].astype(jnp.bfloat16)
                return 0

            lax.fori_loop(0, total_keys // KEYS, store, 0)

    block = pl.BlockSpec((1, rows, wide), lambda h, i, b: (i, 0, h))
    whole = pl.BlockSpec((total_keys, wide), lambda h, i, b: (0, h))
    return pl.pallas_call(
        body,
        out_shape=(
            jax.ShapeDtypeStruct((count, rows, width), jnp.bfloat16),
            jax.ShapeDtypeStruct(kv_all.shape, jnp.bfloat16),
        ),
        grid_spec=pltpu.PrefetchScalarGridSpec(
            num_scalar_prefetch=1,
            grid=(width // wide, count),
            in_specs=[
                block,
                block,
                block,
                whole,
                pl.BlockSpec((1, 1, rows), lambda h, i, b: (i, 0, 0)),
            ],
            out_specs=(block, whole),
            scratch_shapes=[pltpu.VMEM((total_keys, wide), jnp.float32)],
        ),
        compiler_params=pltpu.CompilerParams(vmem_limit_bytes=VMEM_BYTES),
        cost_estimate=pl.CostEstimate(
            flops=5 * count * rows * total_keys * width,
            bytes_accessed=kv_all.size * 4,
            transcendentals=count * rows * total_keys,
        ),
    )(bounds, queries, grads, kept, kv_all, starts)


def norm_forward(values, gain_vec):
    row_scale = lax.rsqrt(jnp.mean(values * values, axis=-1, keepdims=True) + EPSILON)
    normed = values * row_scale
    return normed * gain_vec, normed, row_scale


def norm_backward(upstream, normed, row_scale, gain_vec):
    through = upstream * gain_vec
    gain_grad = jnp.sum(upstream * normed, axis=0)
    inner_mean = jnp.mean(through * normed, axis=-1, keepdims=True)
    return row_scale * (through - normed * inner_mean), gain_grad


def slot_index(route_ids):
    token_rows = route_ids.shape[0]
    expert_ids = jnp.arange(NE, dtype=jnp.int32)
    matches = (
        (route_ids[:, :, None] == expert_ids[None, None, :])
        .astype(jnp.int32)
        .reshape((token_rows * 2, NE))
    )
    before = jnp.cumsum(matches, axis=0) - 1
    slot_pos = jnp.sum(matches * before, axis=1).reshape((token_rows, 2))
    return jnp.where(route_ids < NE, route_ids * CAP + slot_pos, NE * CAP)


def per_device(
    tokens,
    segments,
    routes,
    gates,
    w_qkv,
    w_out,
    gain_attn,
    gain_moe,
    const_gate,
    const_vec,
    w_gate,
    w_up,
    w_down,
    cotangent,
):
    blocks = lax.axis_size("blk")
    head_index, blk_index = lax.axis_index("head"), lax.axis_index("blk")
    span = blocks // COLUMNS
    plane, rest = lax.div(blk_index, span), lax.rem(blk_index, span)
    shards = 2 * blocks
    token_rows, width = tokens.shape
    shard_rows = width // shards
    head_dim = width // HEADS
    heads = HEADS // COLUMNS
    scale = head_dim ** (-0.5)
    half_length = blocks * token_rows
    positions = 2 * half_length
    features = w_gate.shape[2]
    hidden_rows = w_gate.shape[1]
    copies = blocks // NE
    own_qkv = heads * 3 * head_dim
    own_out = heads * head_dim

    swap = [(0, 1), (1, 0)]
    ready = [
        [lax.ppermute(w[layer], "head", swap) for w in (w_gate, w_up, w_down)]
        for layer in range(LAYERS)
    ]

    def whole_features(own, other):
        return jnp.concatenate(
            [
                jnp.where(head_index == 0, own, other),
                jnp.where(head_index == 0, other, own),
            ],
            axis=1,
        )

    qkv_slabs = w_qkv.reshape((LAYERS, shard_rows, 3, COLUMNS, heads, head_dim))
    qkv_slabs = qkv_slabs.transpose((3, 0, 1, 4, 2, 5)).reshape(
        (COLUMNS, LAYERS, shard_rows, own_qkv)
    )
    small = jnp.concatenate(
        [gain_attn[..., None], gain_moe[..., None], const_gate, const_vec], axis=2
    )
    seg_own = lax.dynamic_index_in_dim(segments, head_index, 0, keepdims=False)
    seg_parts = jnp.concatenate([lax.rem(seg_own, 128), lax.div(seg_own, 128)]).astype(
        jnp.bfloat16
    )
    seg_columns = -(-seg_parts.shape[0] // shard_rows)
    seg_parts = jnp.pad(seg_parts, (0, seg_columns * shard_rows - seg_parts.shape[0]))
    seg_parts = jnp.broadcast_to(
        seg_parts.reshape((1, shard_rows, seg_columns)), (LAYERS, shard_rows, seg_columns)
    )
    side = jnp.concatenate([w_out, small, seg_parts], axis=2)
    side = jnp.pad(side, ((0, 0), (0, 0), (0, -(own_qkv + side.shape[2]) % LANES)))
    slabs = jnp.concatenate(
        [qkv_slabs, jnp.broadcast_to(side[None], (COLUMNS,) + side.shape)], axis=3
    )
    weights = plane_gather(column_exchange(slabs, blocks, False, 1), blocks, 2)
    weights = weights.reshape((shards, LAYERS, shard_rows, -1))

    seg_all = weights[:, 0, :, own_qkv + width + 8 : own_qkv + width + 8 + seg_columns]
    seg_all = seg_all.reshape((shards, -1))[:, : 2 * token_rows].astype(jnp.int32)
    seg_all = seg_all[:, :token_rows] + 128 * seg_all[:, token_rows:]
    seg_query = lax.dynamic_index_in_dim(
        seg_all.reshape((2, COLUMNS, span, token_rows)), head_index, 0, keepdims=False
    )
    seg_query = lax.dynamic_index_in_dim(seg_query, rest, 1, keepdims=False)
    starts = jnp.sum(
        (seg_all.reshape((1, 1, -1)) < seg_query[:, :, None]).astype(jnp.int32), axis=2
    )
    bases = (
        head_index * half_length
        + (jnp.arange(COLUMNS, dtype=jnp.int32) * span + rest) * token_rows
    )
    bounds = jnp.stack(
        [lax.div(starts[:, 0], KEYS), lax.div(bases + token_rows - 1, KEYS), bases], axis=1
    )
    starts = starts[:, None, :]

    layers = []
    for layer in range(LAYERS):
        rows = weights[:, layer]
        qkv = rows[:, :, :own_qkv].reshape((width, heads, 3, head_dim))
        query_w = jnp.pad(qkv[:, :, 0], ((0, 0), (0, 0), (0, LANES - head_dim)))
        query_w = query_w.reshape((width, heads * LANES))
        kv_w = qkv[:, :, 1:].reshape((width, heads * LANES))
        out_w = rows[:, :, own_qkv : own_qkv + width].reshape((width, width))
        small_w = rows[:, :, own_qkv + width : own_qkv + width + 8].reshape((width, 8))
        layers.append((query_w, kv_w, out_w, small_w))

    residual = tokens.astype(jnp.float32)
    kept = []
    for layer in range(LAYERS):
        query_w, kv_w, out_w, small_w = layers[layer]
        attn_gain = small_w[:, 0].astype(jnp.float32)
        moe_gain = small_w[:, 1].astype(jnp.float32)
        gate_w = small_w[:, 2:6]
        vectors = small_w[:, 6:8].astype(jnp.float32).T
        normed_in, unit_in, scale_in = norm_forward(residual, attn_gain)
        column = column_exchange(normed_in.astype(jnp.bfloat16), blocks, True, 3)
        column = column.reshape((COLUMNS * token_rows, width))
        queries = (
            dot32(column, query_w).astype(jnp.bfloat16).astype(jnp.float32) * scale
        ).astype(jnp.bfloat16)
        queries = queries.reshape((COLUMNS, token_rows, heads * LANES))
        kv_own = dot32(column, kv_w).astype(jnp.bfloat16)
        kv_all = plane_gather(kv_own.reshape((COLUMNS, token_rows, heads * LANES)), blocks, 4)
        kv_all = kv_all.reshape((positions, heads * LANES))
        attended = attend(bounds, queries, kv_all, starts)
        attn_col = (
            attended.reshape((COLUMNS, token_rows, heads, LANES))[..., head_dim:]
            .reshape((COLUMNS, token_rows, own_out))
            .astype(jnp.bfloat16)
        )
        attn = column_exchange(attn_col, blocks, False, 5)
        attn = attn.transpose((1, 0, 2)).reshape((token_rows, width))
        middle = residual + dot32(attn, out_w)
        normed_mid, unit_mid, scale_mid = norm_forward(middle, moe_gain)
        moe_in = normed_mid.astype(jnp.bfloat16)
        moe_float = moe_in.astype(jnp.float32)
        route_ids, gate_vals = routes[layer], gates[layer]
        slots = slot_index(route_ids)
        named = slots[:, :, None] == jnp.arange(NE * CAP, dtype=jnp.int32)[None, None, :]
        picks = jnp.any(named, axis=1)
        pick_gates = jnp.sum(jnp.where(named, gate_vals[:, :, None], 0.0), axis=1)
        sent = dot32(picks.astype(jnp.bfloat16), moe_in, FIRST).astype(jnp.bfloat16)
        arrived = expert_dispatch(sent.reshape((NE, CAP, width)), blocks, 6)
        flat_in = arrived.reshape((-1, width))
        expert_w = [
            whole_features(w[layer], other)
            for w, other in zip((w_gate, w_up, w_down), ready[layer])
        ]
        gate_pre = dot32(flat_in, expert_w[0], LAST)
        up_pre = dot32(flat_in, expert_w[1], LAST)
        hidden = (jax.nn.silu(gate_pre) * up_pre).astype(jnp.bfloat16)
        parts = dot32(hidden, expert_w[2]).astype(jnp.bfloat16)
        back = expert_return(parts.reshape((copies, NE, CAP, width)), blocks, 7)
        back = back.reshape((NE * CAP, width)).astype(jnp.float32)
        ffn_out = jnp.dot(pick_gates, back, precision=HIGHEST)
        copy_weight = jnp.sum(jnp.where(route_ids == NE + 1, gate_vals, 0.0), axis=1)
        const_weight = jnp.stack(
            [
                jnp.sum(jnp.where(route_ids == NE + 2 + c, gate_vals, 0.0), axis=1)
                for c in range(2)
            ],
            axis=1,
        )
        mixing = jax.nn.softmax(dot32(moe_in, gate_w).reshape((token_rows, 2, 2)), axis=-1)
        const_out = jnp.sum(
            const_weight[:, :, None]
            * (mixing[:, :, 0:1] * moe_float[:, None, :] + mixing[:, :, 1:2] * vectors[None]),
            axis=1,
        )
        residual = middle + ffn_out + copy_weight[:, None] * moe_float + const_out
        kept.append(
            (
                unit_in,
                scale_in,
                column,
                queries,
                kv_all,
                attended,
                attn_col,
                unit_mid,
                scale_mid,
                moe_float,
                picks,
                pick_gates,
                flat_in,
                expert_w,
                gate_pre,
                up_pre,
                hidden,
                copy_weight,
                const_weight,
                mixing,
            )
        )
    output = residual

    upstream = cotangent.astype(jnp.float32)
    shared_grads = [None] * LAYERS
    expert_grads = [None] * LAYERS
    for layer in reversed(range(LAYERS)):
        query_w, kv_w, out_w, small_w = layers[layer]
        attn_gain = small_w[:, 0].astype(jnp.float32)
        moe_gain = small_w[:, 1].astype(jnp.float32)
        gate_w = small_w[:, 2:6].astype(jnp.float32)
        vectors = small_w[:, 6:8].astype(jnp.float32).T
        (
            unit_in,
            scale_in,
            column,
            queries,
            kv_all,
            attended,
            attn_col,
            unit_mid,
            scale_mid,
            moe_float,
            picks,
            pick_gates,
            flat_in,
            expert_w,
            gate_pre,
            up_pre,
            hidden,
            copy_weight,
            const_weight,
            mixing,
        ) = kept[layer]
        picked = jnp.dot(picks.astype(jnp.float32).T, upstream, precision=HIGHEST)
        dz = (jnp.sum(pick_gates, axis=0)[:, None] * picked).astype(jnp.bfloat16)
        dz_in = expert_dispatch(dz.reshape((NE, CAP, width)), blocks, 6).reshape((-1, width))

        mix_grad = const_weight[:, :, None] * upstream[:, None, :]
        alpha_grad = jnp.stack(
            [
                jnp.sum(mix_grad * moe_float[:, None, :], axis=-1),
                jnp.sum(mix_grad * vectors[None], axis=-1),
            ],
            axis=-1,
        )
        logit_grad = (
            mixing * (alpha_grad - jnp.sum(mixing * alpha_grad, axis=-1, keepdims=True))
        ).reshape((token_rows, 4))
        hn_grad = (
            copy_weight[:, None] * upstream
            + jnp.sum(mixing[:, :, 0:1] * mix_grad, axis=1)
            + jnp.dot(logit_grad, gate_w.T, precision=HIGHEST)
        )
        cgate_grad = jnp.dot(moe_float.T, logit_grad, precision=HIGHEST)
        cvec_grad = jnp.sum(mixing[:, :, 1:2] * mix_grad, axis=0).T

        sigmoid = jax.nn.sigmoid(gate_pre)
        silu = gate_pre * sigmoid
        hidden_grad = dot32(dz_in, expert_w[2], LAST)
        dgate = (hidden_grad * up_pre * sigmoid * (1.0 + gate_pre * (1.0 - sigmoid))).astype(
            jnp.bfloat16
        )
        dup = (hidden_grad * silu).astype(jnp.bfloat16)
        dparts = (dot32(dgate, expert_w[0]) + dot32(dup, expert_w[1])).astype(jnp.bfloat16)
        dback = expert_return(dparts.reshape((copies, NE, CAP, width)), blocks, 7)
        weight_grads = [dot32(a, b, FIRST) for a, b in ((dgate, flat_in), (dup, flat_in), (hidden, dz_in))]
        summed = []
        for grad in weight_grads:
            away = lax.dynamic_slice_in_dim(grad, (1 - head_index) * features, features, 1)
            own = lax.dynamic_slice_in_dim(grad, head_index * features, features, 1)
            got = lax.ppermute(away.astype(jnp.bfloat16), "head", swap)
            summed.append(own + got.astype(jnp.float32))
        expert_grads[layer] = summed

        hn_grad = hn_grad + dot32(
            picks.astype(jnp.bfloat16), dback.reshape((NE * CAP, width))
        )
        middle_grad, moe_gain_grad = norm_backward(hn_grad, unit_mid, scale_mid, moe_gain)
        middle_grad = middle_grad + upstream
        dy = column_exchange(middle_grad.astype(jnp.bfloat16), blocks, True, 3)
        dy = dy.reshape((COLUMNS * token_rows, width))
        out_rows = lax.dynamic_slice_in_dim(out_w, plane * own_out, own_out, 0)
        out_rows = jnp.pad(
            out_rows.reshape((heads, head_dim, width)), ((0, 0), (LANES - head_dim, 0), (0, 0))
        ).reshape((heads * LANES, width))
        dattn = dot32(dy, out_rows, LAST).astype(jnp.bfloat16)
        dattn = dattn.reshape((COLUMNS, token_rows, heads * LANES))
        out_grad = dot32(attn_col.reshape((-1, own_out)), dy, FIRST)
        dq, dkv_all = attend_back(bounds, queries, dattn, attended, kv_all, starts, scale)
        dkv = plane_reduce(
            dkv_all.reshape((2, COLUMNS, span, token_rows, heads * LANES)), blocks, 8
        )
        dq = dq.reshape((-1, heads * LANES))
        dkv = dkv.reshape((-1, heads * LANES))
        dxn = (dot32(dq, query_w, LAST) + dot32(dkv, kv_w, LAST)).astype(jnp.bfloat16)
        dxn = column_exchange(dxn.reshape((COLUMNS, token_rows, width)), blocks, False, 9)
        dxn = jnp.sum(dxn.astype(jnp.float32), axis=0)
        query_grad = dot32(column, dq, FIRST).reshape((width, heads, LANES))[:, :, :head_dim]
        kv_grad = dot32(column, dkv, FIRST).reshape((width, heads, LANES))
        lead_grad, attn_gain_grad = norm_backward(dxn, unit_in, scale_in, attn_gain)
        upstream = middle_grad + lead_grad

        qkv_part = jnp.concatenate([query_grad, kv_grad], axis=2).reshape(
            (2, COLUMNS, span, shard_rows, own_qkv)
        )
        out_part = out_grad.reshape((2, span, shard_rows, COLUMNS, own_out)).transpose(
            (0, 3, 1, 2, 4)
        )
        small_part = jnp.concatenate(
            [attn_gain_grad[:, None], moe_gain_grad[:, None], cgate_grad, cvec_grad], axis=1
        ).reshape((2, COLUMNS, span, shard_rows, 8))
        shared_grads[layer] = jnp.concatenate(
            [
                qkv_part.astype(jnp.bfloat16),
                out_part.astype(jnp.bfloat16),
                small_part.astype(jnp.bfloat16),
            ],
            axis=4,
        )

    packed = jnp.concatenate(shared_grads, axis=3)
    packed = jnp.pad(packed, ((0, 0),) * 4 + ((0, -packed.shape[4] % LANES),))
    reduced = plane_reduce(packed, blocks, 10)
    from_planes = column_exchange(reduced, blocks, False, 11).astype(jnp.float32)
    from_planes = from_planes.reshape((COLUMNS, LAYERS, shard_rows, -1))
    qkv_out = from_planes[..., :own_qkv].reshape(
        (COLUMNS, LAYERS, shard_rows, heads, 3, head_dim)
    )
    qkv_out = qkv_out.transpose((1, 2, 4, 0, 3, 5)).reshape((LAYERS, shard_rows, 3 * width))
    small_out = jnp.sum(from_planes[..., own_qkv + own_out : own_qkv + own_out + 8], axis=0)
    out_rows = reduced[..., own_qkv : own_qkv + own_out].reshape(
        (COLUMNS, LAYERS, shard_rows, own_out)
    )
    out_rows = out_rows.transpose((1, 2, 0, 3)).reshape((LAYERS, shard_rows, width))
    owners = [
        (y * blocks + z * span + r, (z * 2 + y) * span + r)
        for y in range(2)
        for z in range(COLUMNS)
        for r in range(span)
    ]
    out_rows = lax.ppermute(out_rows, ("head", "blk"), owners).astype(jnp.float32)
    stacked = [jnp.stack(group) for group in zip(*expert_grads)]
    return (
        output,
        upstream,
        qkv_out,
        out_rows,
        small_out[..., 0],
        small_out[..., 1],
        small_out[..., 2:6],
        small_out[..., 6:8],
        stacked[0],
        stacked[1],
        stacked[2],
    )


def solution(mesh):
    tokens = P(("head", "blk"), None)
    by_layer = P(None, ("head", "blk"), None)
    gains = P(None, ("head", "blk"))
    experts = P(None, "blk", "head")
    return jax.shard_map(
        per_device,
        mesh=mesh,
        in_specs=(
            tokens,
            P(None, "blk"),
            by_layer,
            by_layer,
            by_layer,
            by_layer,
            gains,
            gains,
            by_layer,
            by_layer,
            experts,
            experts,
            experts,
            tokens,
        ),
        out_specs=(
            tokens,
            tokens,
            by_layer,
            by_layer,
            gains,
            gains,
            by_layer,
            by_layer,
            experts,
            experts,
            experts,
        ),
        check_vma=False,
    )
```

time: 1860 us -> 870 us (0.47)
  waiting for transfers between devices: 731 us -> 84.7 us
  Pallas kernels: 0 us -> 533 us
  blocking collectives: 404 us -> 0 us
  matrix products: 356 us -> 66.7 us
  other arithmetic: 95.8 us -> 36.6 us
  local copies, waits for them, and re-layouts: 179 us -> 122 us
  starting transfers between devices: 62.6 us -> 16 us
    pallas_call x0 -> x28, Pallas kernels: none -> 533 us  [the longest x10 157 us: column_exchange(): pl.pallas_call(body, out_shape=jax.ShapeDtypeStruct((COLUMNS,) + tuple(sl...]
    reduce_scatter x4 -> x0, waiting for transfers between devices: 360 us -> none  [the longest x2 197 us: per_device(): lax.psum_scatter(qkv_wgrad, ('head', 'blk'), scatter_dimension=0, tiled=T...]
    dot_general x64 -> x50, matrix products: 356 us -> 66.7 us  [the longest x42 62.1 us: dot32(): return lax.dot_general(a, b, dims, preferred_element_type=jnp.float32)]
    all_gather x9 -> x0, blocking collectives: 269 us -> none  [the longest x2 99.7 us: per_device(): lax.all_gather(const_gate[layer_index], ('head', 'blk'), axis=0, tiled=True)]
    all_gather x18 -> x0, waiting for transfers between devices: 228 us -> none  [the longest x2 88.3 us: per_device(): value_piece = lax.all_gather(value_heads, 'blk', axis=1, tiled=True)]
    all_to_all x11 -> x0, waiting for transfers between devices: 139 us -> none  [the longest x4 67.5 us: send_out(): lax.all_to_all(spread.reshape((experts * copies, capacity, model_width)),...]
    ppermute x0 -> x13, waiting for transfers between devices: none -> 84.7 us  [the longest x6 69.9 us: per_device(): got = lax.ppermute(away.astype(jnp.bfloat16), 'head', swap)]
    unnamed x2 -> x0, blocking collectives: 82.8 us -> none
  transfers between devices with their start and end apart: 39 -> 13, of which waited for: 23 -> 6; matrix products, arithmetic and copies ran while one was open for 28% -> 11% of each run, Pallas kernels for 0% -> 22%
where the time goes in v1:
time: 870 us; the launch traced here: 863 us
  Pallas kernels  533 us (61%)
  local copies, waits for them, and re-layouts  122 us (14%)
  waiting for transfers between devices  84.7 us (10%)
  matrix products  66.7 us (8%)
  other arithmetic  36.6 us (4%)
  starting transfers between devices  16 us (2%)
    pallas_call x10, Pallas kernels, column_exchange(): pl.pallas_call(body, out_shape=jax.ShapeDtypeStruct((COLUMNS,) + tuple(sl...  157 us
    pallas_call x3, Pallas kernels, plane_gather(): pl.pallas_call(body, out_shape=jax.ShapeDtypeStruct((2, values.shape[0],...  116 us
    ppermute x6, waiting for transfers between devices, per_device(): got = lax.ppermute(away.astype(jnp.bfloat16), 'head', swap)  69.9 us
    dot_general x42, matrix products, dot32(): return lax.dot_general(a, b, dims, preferred_element_type=jnp.float32)  62.1 us
    pallas_call x4, Pallas kernels, expert_return(): pl.pallas_call(body, out_shape=jax.ShapeDtypeStruct((NE,) + tile, kind),...  60.5 us
    pallas_call x4, Pallas kernels, expert_dispatch(): pl.pallas_call(body, out_shape=jax.ShapeDtypeStruct((copies, NE) + tile,...  59.5 us
    pallas_call x3, Pallas kernels, plane_reduce(): pl.pallas_call(body, out_shape=jax.ShapeDtypeStruct((slabs,) + tile, kind...  57.7 us
    pallas_call x2, Pallas kernels, attend_back(): pl.pallas_call(body, out_shape=(jax.ShapeDtypeStruct((count, rows, width)...  47.5 us
  transfers between devices with their start and end apart: 13, of which 6 were waited for; matrix products, arithmetic and copies ran while one was open for 11% of the time, Pallas kernels for 22%

profile of v1, /device:TPU:12, one launch (start us, length us, event | category | flops | bytes accessed | tf_op | source)
XLA Modules:
  0.0 863.3 jit_solution(2696361549348195379)
XLA Ops:
  13.8 14.5 %shard_map.221.src = bf16[4,2,24,1408]{3,2,1,0:T(8,128)(2,1)S(1)} custom-call(bf16[4,2,24,1408]{3,2,1,0:T(8,128)(2,1)S(1)} %pad_maximum_fusion.23.src), custom_call_target="tpu_custom_call" | custom-call | tf_op jit(solution)/shard_map/pallas_call | solution.py:73
  28.3 81.3 %shard_map.222 = bf16[2,4,4,2,24,1408]{5,4,3,2,1,0:T(8,128)(2,1)S(1)} custom-call(bf16[4,2,24,1408]{3,2,1,0:T(8,128)(2,1)S(1)} %shard_map.221.src), custom_call_target="tpu_custom_call" | custom-call | tf_op jit(solution)/shard_map/pallas_call | solution.py:173
  144.9 16.7 %shard_map.235 = bf16[2,8,40,768]{3,2,1,0:T(8,128)(2,1)S(1)} custom-call(bf16[8,40,768]{2,1,0:T(8,128)(2,1)S(1)} %bitcast.401), custom_call_target="tpu_custom_call" | custom-call | tf_op jit(solution)/shard_map/pallas_call | solution.py:396
  166.0 20.8 %shard_map.223 = bf16[4,128,768]{2,1,0:T(8,128)(2,1)S(1)} custom-call(bf16[128,768]{1,0:T(8,128)(2,1)S(1)} %fusion.41.src), custom_call_target="tpu_custom_call" | custom-call | tf_op jit(solution)/shard_map/pallas_call | solution.py:73
  206.7 17.1 %shard_map.224 = bf16[2,4,4,128,384]{4,3,2,1,0:T(8,128)(2,1)S(1)} custom-call(bf16[4,128,384]{2,1,0:T(8,128)(2,1)S(1)} %bitcast.426), custom_call_target="tpu_custom_call" | custom-call | tf_op jit(solution)/shard_map/pallas_call | solution.py:173
  223.8 17.5 %shard_map.225.kept_ref = f32[4,128,384]{2,1,0:T(8,128)S(1)} custom-call(s32[4,3]{1,0:T(4,128)S(1)} %pad_add_fusion.bounds_ref, bf16[4,128,384]{2,1,0:T(8,128)(2,1)S(1)} %bitcast.431, bf16[4096,384]{1,0:T(8,128)(2,1)S(1)} %bitcast.383, s32[4,1,128]{2,1,0:T(1,128)S(1)} %bitcast.427), custom_call_target="tpu_custom_call" | custom-call | flops 1610612736 | bytes 3145728 | tf_op jit(solution)/shard_map/pallas_call | solution.py:535
  254.3 13.8 %shard_map.227 = bf16[2,8,40,768]{3,2,1,0:T(8,128)(2,1)S(1)} custom-call(bf16[8,40,768]{2,1,0:T(8,128)(2,1)S(1)} %bitcast.402), custom_call_target="tpu_custom_call" | custom-call | tf_op jit(solution)/shard_map/pallas_call | solution.py:396
  275.0 14.8 %collective-permute-done.2 = bf16[1024,384]{1,0:T(8,128)(2,1)S(1)} collective-permute-done((bf16[1024,384]{1,0:T(8,128)(2,1)}, bf16[1024,384]{1,0:T(8,128)(2,1)S(1)}, u32[]{:S(2)}, u32[]{:S(2)}) %collective-permute-start.2) | collective-permute-done | bytes 786464 | tf_op jit(solution)/shard_map/ppermute | solution.py:717
  297.6 14.6 %shard_map.228 = bf16[8,40,768]{2,1,0:T(8,128)(2,1)S(1)} custom-call(bf16[2,8,40,768]{3,2,1,0:T(8,128)(2,1)S(1)} %bitcast.424), custom_call_target="tpu_custom_call" | custom-call | tf_op jit(solution)/shard_map/pallas_call | solution.py:456
  313.1 21.0 %shard_map.229 = bf16[4,128,768]{2,1,0:T(8,128)(2,1)S(1)} custom-call(bf16[128,768]{1,0:T(8,128)(2,1)S(1)} %multiply_convert_fusion.7.src), custom_call_target="tpu_custom_call" | custom-call | tf_op jit(solution)/shard_map/pallas_call | solution.py:73
  335.3 17.3 %shard_map.230 = bf16[2,4,4,128,384]{4,3,2,1,0:T(8,128)(2,1)S(1)} custom-call(bf16[4,128,384]{2,1,0:T(8,128)(2,1)S(1)} %bitcast.425), custom_call_target="tpu_custom_call" | custom-call | tf_op jit(solution)/shard_map/pallas_call | solution.py:173
  352.7 17.5 %shard_map.231.kept_ref = f32[4,128,384]{2,1,0:T(8,128)S(1)} custom-call(s32[4,3]{1,0:T(4,128)S(1)} %pad_add_fusion.bounds_ref, bf16[4,128,384]{2,1,0:T(8,128)(2,1)S(1)} %bitcast.433, bf16[4096,384]{1,0:T(8,128)(2,1)S(1)} %bitcast.385, s32[4,1,128]{2,1,0:T(1,128)S(1)} %bitcast.428), custom_call_target="tpu_custom_call" | custom-call | flops 1610612736 | bytes 3145728 | tf_op jit(solution)/shard_map/pallas_call | solution.py:535
  391.4 13.8 %shard_map.233 = bf16[2,8,40,768]{3,2,1,0:T(8,128)(2,1)S(1)} custom-call(bf16[8,40,768]{2,1,0:T(8,128)(2,1)S(1)} %bitcast.400), custom_call_target="tpu_custom_call" | custom-call | tf_op jit(solution)/shard_map/pallas_call | solution.py:396
  415.8 15.9 %shard_map.236 = bf16[8,40,768]{2,1,0:T(8,128)(2,1)S(1)} custom-call(bf16[2,8,40,768]{3,2,1,0:T(8,128)(2,1)S(1)} %bitcast.422), custom_call_target="tpu_custom_call" | custom-call | tf_op jit(solution)/shard_map/pallas_call | solution.py:456
  434.0 20.1 %shard_map.237 = bf16[4,128,768]{2,1,0:T(8,128)(2,1)S(1)} custom-call(bf16[128,768]{1,0:T(8,128)(2,1)S(1)} %fusion.87.src), custom_call_target="tpu_custom_call" | custom-call | tf_op jit(solution)/shard_map/pallas_call | solution.py:73
  455.9 23.7 %shard_map.238 = (bf16[4,128,384]{2,1,0:T(8,128)(2,1)S(1)}, bf16[4096,384]{1,0:T(8,128)(2,1)S(1)}) custom-call(s32[4,3]{1,0:T(4,128)S(1)} %pad_add_fusion.bounds_ref, bf16[4,128,384]{2,1,0:T(8,128)(2,1)S(1)} %bitcast.434, bf16[4,128,384]{2,1,0:T(8,128)(2,1)S(1)} %bitcast.436, f32[4,128,384]{2,1,0:T(8,128)S(1)} %copy-done.11, bf16[4096,384]{1,0:T(8,128)(2,1)} %bitcast.386, ...), custom_call_target="tpu_custom_call" | custom-call | flops 4026531840 | bytes 6291456 | tf_op jit(solution)/shard_map/pallas_call | solution.py:627
  479.5 18.8 %shard_map.239 = bf16[4,128,384]{2,1,0:T(8,128)(2,1)S(1)} custom-call(bf16[2,4,2,2,128,384]{5,4,3,2,1,0:T(8,128)(2,1)S(1)} %bitcast.388), custom_call_target="tpu_custom_call" | custom-call | tf_op jit(solution)/shard_map/pallas_call | solution.py:326
  514.4 18.7 %shard_map.240 = bf16[4,128,768]{2,1,0:T(8,128)(2,1)S(1)} custom-call(bf16[4,128,768]{2,1,0:T(8,128)(2,1)S(1)} %bitcast.393), custom_call_target="tpu_custom_call" | custom-call | tf_op jit(solution)/shard_map/pallas_call | solution.py:73
  538.3 15.2 %shard_map.241 = bf16[2,8,40,768]{3,2,1,0:T(8,128)(2,1)S(1)} custom-call(bf16[8,40,768]{2,1,0:T(8,128)(2,1)S(1)} %bitcast.398), custom_call_target="tpu_custom_call" | custom-call | tf_op jit(solution)/shard_map/pallas_call | solution.py:396
  564.0 16.0 %shard_map.242 = bf16[8,40,768]{2,1,0:T(8,128)(2,1)S(1)} custom-call(bf16[2,8,40,768]{3,2,1,0:T(8,128)(2,1)S(1)} %bitcast.423), custom_call_target="tpu_custom_call" | custom-call | tf_op jit(solution)/shard_map/pallas_call | solution.py:456
  583.0 20.4 %shard_map.243 = bf16[4,128,768]{2,1,0:T(8,128)(2,1)S(1)} custom-call(bf16[128,768]{1,0:T(8,128)(2,1)S(1)} %get-tuple-element.92.src), custom_call_target="tpu_custom_call" | custom-call | tf_op jit(solution)/shard_map/pallas_call | solution.py:73
  605.1 23.8 %shard_map.244 = (bf16[4,128,384]{2,1,0:T(8,128)(2,1)S(1)}, bf16[4096,384]{1,0:T(8,128)(2,1)S(1)}) custom-call(s32[4,3]{1,0:T(4,128)S(1)} %pad_add_fusion.bounds_ref, bf16[4,128,384]{2,1,0:T(8,128)(2,1)S(1)} %bitcast.432, bf16[4,128,384]{2,1,0:T(8,128)(2,1)S(1)} %bitcast.435, f32[4,128,384]{2,1,0:T(8,128)S(1)} %copy-done.9, bf16[4096,384]{1,0:T(8,128)(2,1)} %bitcast.384, ...), custom_call_target="tpu_custom_call" | custom-call | flops 4026531840 | bytes 6291456 | tf_op jit(solution)/shard_map/pallas_call | solution.py:627
  628.9 18.8 %shard_map.245 = bf16[4,128,384]{2,1,0:T(8,128)(2,1)S(1)} custom-call(bf16[2,4,2,2,128,384]{5,4,3,2,1,0:T(8,128)(2,1)S(1)} %bitcast.387), custom_call_target="tpu_custom_call" | custom-call | tf_op jit(solution)/shard_map/pallas_call | solution.py:326
  663.4 18.7 %shard_map.246 = bf16[4,128,768]{2,1,0:T(8,128)(2,1)S(1)} custom-call(bf16[4,128,768]{2,1,0:T(8,128)(2,1)S(1)} %bitcast.394), custom_call_target="tpu_custom_call" | custom-call | tf_op jit(solution)/shard_map/pallas_call | solution.py:73
  691.7 20.2 %shard_map.247.src = bf16[4,48,896]{2,1,0:T(8,128)(2,1)S(1)} custom-call(bf16[2,4,2,2,48,896]{5,4,3,2,1,0:T(8,128)(2,1)S(1)} %bitcast.368), custom_call_target="tpu_custom_call" | custom-call | tf_op jit(solution)/shard_map/pallas_call | solution.py:326
  712.1 9.9 %shard_map.248 = bf16[4,48,896]{2,1,0:T(8,128)(2,1)S(1)} custom-call(bf16[4,48,896]{2,1,0:T(8,128)(2,1)S(1)} %shard_map.247.src), custom_call_target="tpu_custom_call" | custom-call | tf_op jit(solution)/shard_map/pallas_call | solution.py:73
  739.9 14.0 %shard_map.234 = bf16[8,40,768]{2,1,0:T(8,128)(2,1)S(1)} custom-call(bf16[2,8,40,768]{3,2,1,0:T(8,128)(2,1)S(1)} %bitcast.421), custom_call_target="tpu_custom_call" | custom-call | tf_op jit(solution)/shard_map/pallas_call | solution.py:456
  781.8 12.0 %collective-permute-done.7 = bf16[1024,384]{1,0:T(8,128)(2,1)S(1)} collective-permute-done((bf16[1024,384]{1,0:T(8,128)(2,1)S(1)}, bf16[1024,384]{1,0:T(8,128)(2,1)S(1)}, u32[]{:S(2)}, u32[]{:S(2)}) %collective-permute-start.7) | collective-permute-done | bytes 786464 | tf_op jit(solution)/shard_map/ppermute | solution.py:942
  796.5 14.2 %collective-permute-done.9 = bf16[1024,384]{1,0:T(8,128)(2,1)S(1)} collective-permute-done((bf16[1024,384]{1,0:T(8,128)(2,1)S(1)}, bf16[1024,384]{1,0:T(8,128)(2,1)S(1)}, u32[]{:S(2)}, u32[]{:S(2)}) %collective-permute-start.9) | collective-permute-done | bytes 786464 | tf_op jit(solution)/shard_map/ppermute | solution.py:942
  810.9 16.7 %collective-permute-done.8 = bf16[1024,384]{1,0:T(8,128)(2,1)S(1)} collective-permute-done((bf16[1024,384]{1,0:T(8,128)(2,1)S(1)}, bf16[1024,384]{1,0:T(8,128)(2,1)S(1)}, u32[]{:S(2)}, u32[]{:S(2)}) %collective-permute-start.8) | collective-permute-done | bytes 786464 | tf_op jit(solution)/shard_map/ppermute | solution.py:942
  829.6 14.8 %collective-permute-done.10 = bf16[1024,384]{1,0:T(8,128)(2,1)S(1)} collective-permute-done((bf16[1024,384]{1,0:T(8,128)(2,1)S(1)}, bf16[1024,384]{1,0:T(8,128)(2,1)S(1)}, u32[]{:S(2)}, u32[]{:S(2)}) %collective-permute-start.10) | collective-permute-done | bytes 786464 | tf_op jit(solution)/shard_map/ppermute | solution.py:942
  848.9 12.1 %collective-permute-done.12 = bf16[1024,384]{1,0:T(8,128)(2,1)S(1)} collective-permute-done((bf16[1024,384]{1,0:T(8,128)(2,1)S(1)}, bf16[1024,384]{1,0:T(8,128)(2,1)S(1)}, u32[]{:S(2)}, u32[]{:S(2)}) %collective-permute-start.12) | collective-permute-done | bytes 786464 | tf_op jit(solution)/shard_map/ppermute | solution.py:942
  (605 shorter events, 254.9 us)
Async XLA Ops:
  3.5 266.2 %collective-permute-start.3 = (bf16[1024,384]{1,0:T(8,128)(2,1)}, bf16[1024,384]{1,0:T(8,128)(2,1)}, u32[]{:S(2)}, u32[]{:S(2)}) collective-permute-start(bf16[1024,384]{1,0:T(8,128)(2,1)} %get-tuple-element.123), channel_id=1, source_target_pairs={{0,16},{16,0},{1,17},{17,1},{2,18},{18,2},{3,19},{19,3},{4,20},{20... | collective-permute-start | bytes 2359304 | tf_op jit(solution)/shard_map/ppermute | solution.py:717
  4.0 266.4 %collective-permute-start = (bf16[1024,384]{1,0:T(8,128)(2,1)}, bf16[1024,384]{1,0:T(8,128)(2,1)}, u32[]{:S(2)}, u32[]{:S(2)}) collective-permute-start(bf16[1024,384]{1,0:T(8,128)(2,1)} %get-tuple-element.124), channel_id=1, source_target_pairs={{0,16},{16,0},{1,17},{17,1},{2,18},{18,2},{3,19},{19,3},{4,20},{20... | collective-permute-start | bytes 2359304 | tf_op jit(solution)/shard_map/ppermute | solution.py:717
  6.9 268.1 %collective-permute-start.4 = (bf16[1024,384]{1,0:T(8,128)(2,1)}, bf16[1024,384]{1,0:T(8,128)(2,1)}, u32[]{:S(2)}, u32[]{:S(2)}) collective-permute-start(bf16[1024,384]{1,0:T(8,128)(2,1)} %get-tuple-element.127), channel_id=1, source_target_pairs={{0,16},{16,0},{1,17},{17,1},{2,18},{18,2},{3,19},{19,3},{4,20},{20... | collective-permute-start | bytes 2359304 | tf_op jit(solution)/shard_map/ppermute | solution.py:717
  7.4 267.6 %collective-permute-start.1 = (bf16[1024,384]{1,0:T(8,128)(2,1)}, bf16[1024,384]{1,0:T(8,128)(2,1)}, u32[]{:S(2)}, u32[]{:S(2)}) collective-permute-start(bf16[1024,384]{1,0:T(8,128)(2,1)} %get-tuple-element.128), channel_id=1, source_target_pairs={{0,16},{16,0},{1,17},{17,1},{2,18},{18,2},{3,19},{19,3},{4,20},{20... | collective-permute-start | bytes 2359304 | tf_op jit(solution)/shard_map/ppermute | solution.py:717
  10.4 264.6 %collective-permute-start.5 = (bf16[1024,384]{1,0:T(8,128)(2,1)}, bf16[1024,384]{1,0:T(8,128)(2,1)}, u32[]{:S(2)}, u32[]{:S(2)}) collective-permute-start(bf16[1024,384]{1,0:T(8,128)(2,1)} %get-tuple-element.119), channel_id=1, source_target_pairs={{0,16},{16,0},{1,17},{17,1},{2,18},{18,2},{3,19},{19,3},{4,20},{20... | collective-permute-start | bytes 2359304 | tf_op jit(solution)/shard_map/ppermute | solution.py:717
  113.8 139.9 %copy-start.25 = (bf16[32,24,8]{2,1,0:T(8,128)(2,1)}, bf16[32,24,8]{2,1,0:T(8,128)(2,1)S(1)}, u32[]{:S(2)}) copy-start(bf16[32,24,8]{2,1,0:T(8,128)(2,1)S(1)} %slice.241) | copy-start | bytes 36868
  137.4 28.5 %copy-start.123 = (f32[128]{0:T(128)}, f32[128]{0:T(128)S(1)}, u32[]{:S(2)}) copy-start(f32[128]{0:T(128)S(1)} %add_rsqrt_fusion.3) | copy-start | bytes 1540
  139.5 22.0 %copy-start.90 = (pred[128,320]{0,1:T(8,128)(4,1)}, pred[128,320]{0,1:T(8,128)(4,1)S(1)}, u32[]{:S(2)}) copy-start(pred[128,320]{0,1:T(8,128)(4,1)S(1)} %fusion.48) | copy-start | bytes 122884
  161.5 243.7 %copy-start.2 = (bf16[2,8,40,768]{3,2,1,0:T(8,128)(2,1)}, bf16[2,8,40,768]{3,2,1,0:T(8,128)(2,1)S(1)}, u32[]{:S(2)}) copy-start(bf16[2,8,40,768]{3,2,1,0:T(8,128)(2,1)S(1)} %shard_map.235) | copy-start | bytes 2949124
  165.7 23.1 %copy-start.97 = (f32[768]{0:T(1024)}, f32[768]{0:T(1024)S(1)}, u32[]{:S(2)}) copy-start(f32[768]{0:T(1024)S(1)} %convert_reduce_fusion.6) | copy-start | bytes 9220
  165.9 86.9 %copy-start.99 = (f32[768]{0:T(1024)}, f32[768]{0:T(1024)S(1)}, u32[]{:S(2)}) copy-start(f32[768]{0:T(1024)S(1)} %convert_reduce_fusion.5) | copy-start | bytes 9220
  252.7 59.5 %copy-start.22 = (f32[128,768]{1,0:T(8,128)}, f32[128,768]{1,0:T(8,128)S(1)}, u32[]{:S(2)}) copy-start(f32[128,768]{1,0:T(8,128)S(1)} %get-tuple-element.144) | copy-start | bytes 1179652
  253.7 58.5 %copy-start.35 = (bf16[128,768]{1,0:T(8,128)(2,1)}, bf16[128,768]{1,0:T(8,128)(2,1)S(1)}, u32[]{:S(2)}) copy-start(bf16[128,768]{1,0:T(8,128)(2,1)S(1)} %get-tuple-element.97) | copy-start | bytes 589828
  268.1 25.4 %copy-start.4 = (bf16[2,8,40,768]{3,2,1,0:T(8,128)(2,1)}, bf16[2,8,40,768]{3,2,1,0:T(8,128)(2,1)S(1)}, u32[]{:S(2)}) copy-start(bf16[2,8,40,768]{3,2,1,0:T(8,128)(2,1)S(1)} %shard_map.227) | copy-start | bytes 2949124
  268.2 44.8 %copy-start.101 = (f32[768]{0:T(1024)}, f32[768]{0:T(1024)S(1)}, u32[]{:S(2)}) copy-start(f32[768]{0:T(1024)S(1)} %get-tuple-element.162) | copy-start | bytes 9220
  269.7 20.1 %collective-permute-start.2 = (bf16[1024,384]{1,0:T(8,128)(2,1)}, bf16[1024,384]{1,0:T(8,128)(2,1)S(1)}, u32[]{:S(2)}, u32[]{:S(2)}) collective-permute-start(bf16[1024,384]{1,0:T(8,128)(2,1)} %get-tuple-element.120), channel_id=1, source_target_pairs={{0,16},{16,0},{1,17},{17,1},{2,18},{18,2},{3,19},{19,3},{4,20},{20... | collective-permute-start | bytes 2359304 | tf_op jit(solution)/shard_map/ppermute | solution.py:717
  312.2 21.9 %copy-start.45 = (bf16[768,3,2,64]{0,3,2,1:T(8,128)(2,1)S(1)}, bf16[768,3,2,64]{0,3,2,1:T(8,128)(2,1)}, u32[]{:S(2)}) copy-start(bf16[768,3,2,64]{0,3,2,1:T(8,128)(2,1)} %copy.352) | copy-start | bytes 1769476
  384.6 49.3 %copy-start.119 = (f32[128]{0:T(128)}, f32[128]{0:T(128)S(1)}, u32[]{:S(2)}) copy-start(f32[128]{0:T(128)S(1)} %add_rsqrt_fusion) | copy-start | bytes 1540
  434.0 21.8 %copy-start.11 = (f32[4,128,384]{2,1,0:T(8,128)S(1)}, f32[4,128,384]{2,1,0:T(8,128)}, u32[]{:S(2)}) copy-start(f32[4,128,384]{2,1,0:T(8,128)} %copy-done.10) | copy-start | bytes 2359300
  434.0 21.8 %copy-start.15 = (bf16[512,384]{1,0:T(8,128)(2,1)S(1)}, bf16[512,384]{1,0:T(8,128)(2,1)}, u32[]{:S(2)}) copy-start(bf16[512,384]{1,0:T(8,128)(2,1)} %copy-done.14) | copy-start | bytes 1179652
  583.0 22.1 %copy-start.9 = (f32[4,128,384]{2,1,0:T(8,128)S(1)}, f32[4,128,384]{2,1,0:T(8,128)}, u32[]{:S(2)}) copy-start(f32[4,128,384]{2,1,0:T(8,128)} %copy-done.8) | copy-start | bytes 2359300
  583.0 22.1 %copy-start.13 = (bf16[512,384]{1,0:T(8,128)(2,1)S(1)}, bf16[512,384]{1,0:T(8,128)(2,1)}, u32[]{:S(2)}) copy-start(bf16[512,384]{1,0:T(8,128)(2,1)} %copy-done.12) | copy-start | bytes 1179652
  756.4 90.1 %collective-permute-start.11 = (bf16[1024,384]{1,0:T(8,128)(2,1)}, bf16[1024,384]{1,0:T(8,128)(2,1)}, u32[]{:S(2)}, u32[]{:S(2)}) collective-permute-start(bf16[1024,384]{1,0:T(8,128)(2,1)} %dynamic-slice_convert_fusion.1), channel_id=1, source_target_pairs={{0,16},{16,0},{1,17},{17,1},{2,18},{18,2},{3,19},{19,3},{4,20},{20... | collective-permute-start | bytes 2359304 | tf_op jit(solution)/shard_map/ppermute | solution.py:942
  758.1 23.1 %collective-permute-start.6 = (bf16[2,24,768]{2,1,0:T(8,128)(2,1)}, bf16[2,24,768]{2,1,0:T(8,128)(2,1)S(1)}, u32[]{:S(2)}, u32[]{:S(2)}) collective-permute-start(bf16[2,24,768]{2,1,0:T(8,128)(2,1)} %reshape.586), channel_id=1, source_target_pairs={{0,0},{1,1},{2,2},{3,3},{4,8},{5,9},{6,10},{7,11},{8,16},{9,17},{1... | collective-permute-start | bytes 221192 | tf_op jit(solution)/shard_map/ppermute | solution.py:1012
  769.3 24.6 %collective-permute-start.7 = (bf16[1024,384]{1,0:T(8,128)(2,1)S(1)}, bf16[1024,384]{1,0:T(8,128)(2,1)S(1)}, u32[]{:S(2)}, u32[]{:S(2)}) collective-permute-start(bf16[1024,384]{1,0:T(8,128)(2,1)S(1)} %dynamic-slice_convert_fusion.5), channel_id=1, source_target_pairs={{0,16},{16,0},{1,17},{17,1},{2,18},{18,2},{3,19},{19,3},{4,20},{20... | collective-permute-start | bytes 2359304 | tf_op jit(solution)/shard_map/ppermute | solution.py:942
  774.1 36.6 %collective-permute-start.9 = (bf16[1024,384]{1,0:T(8,128)(2,1)S(1)}, bf16[1024,384]{1,0:T(8,128)(2,1)S(1)}, u32[]{:S(2)}, u32[]{:S(2)}) collective-permute-start(bf16[1024,384]{1,0:T(8,128)(2,1)S(1)} %dynamic-slice_convert_fusion.3), channel_id=1, source_target_pairs={{0,16},{16,0},{1,17},{17,1},{2,18},{18,2},{3,19},{19,3},{4,20},{20... | collective-permute-start | bytes 2359304 | tf_op jit(solution)/shard_map/ppermute | solution.py:942
  774.2 22.1 %copy-start.57 = (f32[1024,768]{1,0:T(8,128)S(1)}, f32[1024,768]{1,0:T(8,128)}, u32[]{:S(2)}) copy-start(f32[1024,768]{1,0:T(8,128)} %fusion.101) | copy-start | bytes 9437188
  775.9 51.6 %collective-permute-start.8 = (bf16[1024,384]{1,0:T(8,128)(2,1)S(1)}, bf16[1024,384]{1,0:T(8,128)(2,1)S(1)}, u32[]{:S(2)}, u32[]{:S(2)}) collective-permute-start(bf16[1024,384]{1,0:T(8,128)(2,1)S(1)} %dynamic-slice_convert_fusion.4), channel_id=1, source_target_pairs={{0,16},{16,0},{1,17},{17,1},{2,18},{18,2},{3,19},{19,3},{4,20},{20... | collective-permute-start | bytes 2359304 | tf_op jit(solution)/shard_map/ppermute | solution.py:942
  781.1 63.3 %collective-permute-start.10 = (bf16[1024,384]{1,0:T(8,128)(2,1)S(1)}, bf16[1024,384]{1,0:T(8,128)(2,1)S(1)}, u32[]{:S(2)}, u32[]{:S(2)}) collective-permute-start(bf16[1024,384]{1,0:T(8,128)(2,1)S(1)} %dynamic-slice_convert_fusion.2), channel_id=1, source_target_pairs={{0,16},{16,0},{1,17},{17,1},{2,18},{18,2},{3,19},{19,3},{4,20},{20... | collective-permute-start | bytes 2359304 | tf_op jit(solution)/shard_map/ppermute | solution.py:942
  781.8 28.9 %copy-start.56 = (f32[1024,768]{1,0:T(8,128)S(1)}, f32[1024,768]{1,0:T(8,128)}, u32[]{:S(2)}) copy-start(f32[1024,768]{1,0:T(8,128)} %fusion.103) | copy-start | bytes 9437188
  793.8 67.2 %collective-permute-start.12 = (bf16[1024,384]{1,0:T(8,128)(2,1)S(1)}, bf16[1024,384]{1,0:T(8,128)(2,1)S(1)}, u32[]{:S(2)}, u32[]{:S(2)}) collective-permute-start(bf16[1024,384]{1,0:T(8,128)(2,1)S(1)} %dynamic-slice_convert_fusion), channel_id=1, source_target_pairs={{0,16},{16,0},{1,17},{17,1},{2,18},{18,2},{3,19},{19,3},{4,20},{20... | collective-permute-start | bytes 2359304 | tf_op jit(solution)/shard_map/ppermute | solution.py:942
  796.4 31.1 %copy-start.55 = (f32[1024,768]{1,0:T(8,128)S(1)}, f32[1024,768]{1,0:T(8,128)}, u32[]{:S(2)}) copy-start(f32[1024,768]{1,0:T(8,128)} %fusion.102) | copy-start | bytes 9437188
  (139 other events, 1100.5 us)

commit v2 on v1

--- a/solution.py
+++ b/solution.py
@@ -43,50 +43,74 @@
     )
 
 
-def column_exchange(values, blocks, gather, collective_id):
+def lasting(microseconds):
+    return pl.CostEstimate(
+        flops=0, bytes_accessed=int(microseconds * 3_500_000), transcendentals=0
+    )
+
+
+def column_exchange(arrays, gathers, blocks, collective_id, cost=16):
     span = blocks // COLUMNS
-    slab = values.shape if gather else values.shape[1:]
-
-    def body(src, dst, own_sem, send_sems, recv_sems):
+    count = len(arrays)
+    slabs = [
+        tuple(values.shape if gather else values.shape[1:])
+        for values, gather in zip(arrays, gathers)
+    ]
+
+    def body(*refs):
+        srcs, dsts = refs[:count], refs[count : 2 * count]
+        own_sems, send_sems, recv_sems = refs[2 * count :]
         head, blk = lax.axis_index("head"), lax.axis_index("blk")
         plane, rest = lax.div(blk, span), lax.rem(blk, span)
         planes = [lax.rem(plane + d, COLUMNS) for d in range(COLUMNS)]
         peers = [(head, p * span + rest) for p in planes]
         greet(peers[1:])
-        own = pltpu.make_async_copy(src if gather else src.at[plane], dst.at[plane], own_sem)
-        own.start()
-        copies = []
-        for d in (2, 1, 3):
-            copy = remote(
-                src if gather else src.at[planes[d]],
-                dst.at[plane],
-                send_sems.at[d],
-                recv_sems.at[d],
-                peers[d],
+        waits, copies = [], []
+        for n in range(count):
+            own = pltpu.make_async_copy(
+                srcs[n] if gathers[n] else srcs[n].at[plane], dsts[n].at[plane], own_sems.at[n]
             )
-            copy.start()
-            copies.append(copy)
-        own.wait()
+            own.start()
+            waits.append(own)
+        for n in range(count):
+            for d in (2, 1, 3):
+                copy = remote(
+                    srcs[n] if gathers[n] else srcs[n].at[planes[d]],
+                    dsts[n].at[plane],
+                    send_sems.at[n, d],
+                    recv_sems.at[n, d],
+                    peers[d],
+                )
+                copy.start()
+                copies.append(copy)
+        for own in waits:
+            own.wait()
         for copy in copies:
             copy.wait()
 
     return pl.pallas_call(
         body,
-        out_shape=jax.ShapeDtypeStruct((COLUMNS,) + tuple(slab), values.dtype),
-        in_specs=[ANY],
-        out_specs=ANY,
-        scratch_shapes=[DMA, DMA((COLUMNS,)), DMA((COLUMNS,))],
+        out_shape=[
+            jax.ShapeDtypeStruct((COLUMNS,) + slab, values.dtype)
+            for values, slab in zip(arrays, slabs)
+        ],
+        in_specs=[ANY] * count,
+        out_specs=[ANY] * count,
+        scratch_shapes=[DMA((count,)), DMA((count, COLUMNS)), DMA((count, COLUMNS))],
         compiler_params=comm_params(collective_id),
-    )(values)
-
-
-def plane_gather(values, blocks, collective_id):
+        cost_estimate=lasting(cost),
+    )(*arrays)
+
+
+def plane_gather(arrays, blocks, collective_id, cost=16):
     span = blocks // COLUMNS
     width = span // 2
-    half = values.shape[0] // 2
+    count = len(arrays)
     links = 4 * (width - 1) + 2
 
-    def body(src, dst, own_sem, send_sems, recv_sems, pass_sems, land_sems):
+    def body(*refs):
+        srcs, dsts = refs[:count], refs[count : 2 * count]
+        own_sems, send_sems, recv_sems, pass_sems, land_sems = refs[2 * count :]
         head, blk = lax.axis_index("head"), lax.axis_index("blk")
         plane, rest = lax.div(blk, span), lax.rem(blk, span)
         x, core = lax.div(rest, 2), lax.rem(rest, 2)
@@ -97,74 +121,79 @@
         y_peer = (1 - head, blk)
         core_peer = (head, first + x * 2 + 1 - core)
         greet(x_peers[1:] + [y_peer, core_peer])
-
-        def part(h):
-            return src.at[pl.ds(h * half, half)]
-
-        def place(h, dy, d):
+        sends, passes = [], []
+
+        def place(n, h, dy, d):
+            half = srcs[n].shape[0] // 2
             row = head if dy == 0 else 1 - head
-            return dst.at[row, pl.ds(h * half, half), left[d] * 2 + core]
-
-        sends = []
-
-        def send(h, dy, d, peer, to_dy, to_d):
+            return dsts[n].at[row, pl.ds(h * half, half), left[d] * 2 + core]
+
+        def held(n, h, dy, d):
+            half = srcs[n].shape[0] // 2
+            return srcs[n].at[pl.ds(h * half, half)] if dy == 0 and d == 0 else place(n, h, dy, d)
+
+        def send(n, h, dy, d, peer, to_dy, to_d):
             copy = remote(
-                part(h) if dy == 0 and d == 0 else place(h, dy, d),
-                place(h, dy, d),
+                held(n, h, dy, d),
+                place(n, h, dy, d),
                 send_sems.at[len(sends)],
-                recv_sems.at[h, to_dy, to_d],
+                recv_sems.at[n, h, to_dy, to_d],
                 peer,
             )
             copy.start()
             sends.append(copy)
 
-        passes = []
-
-        def hand_over(h, dy, d):
+        def hand_over(n, h, dy, d):
             copy = remote(
-                part(h) if dy == 0 and d == 0 else place(h, dy, d),
-                place(h, dy, d),
-                pass_sems.at[h, dy, d],
-                land_sems.at[h, dy, d],
+                held(n, h, dy, d),
+                place(n, h, dy, d),
+                pass_sems.at[n, h, dy, d],
+                land_sems.at[n, h, dy, d],
                 core_peer,
             )
             copy.start()
             passes.append(copy)
 
-        def arrived(h, dy, d):
-            remote(
-                place(h, dy, d), place(h, dy, d), send_sems.at[0], recv_sems.at[h, dy, d], y_peer
-            ).wait_recv()
-
-        own = pltpu.make_async_copy(src, dst.at[head, :, rest], own_sem)
-        own.start()
-        for d in range(1, width):
-            send(0, 0, 0, x_peers[d], 0, d)
-        send(1, 0, 0, y_peer, 1, 0)
-        send(0, 0, 0, y_peer, 1, 0)
-        for d in range(1, width):
-            send(1, 0, 0, x_peers[d], 0, d)
-        hand_over(0, 0, 0)
-        hand_over(1, 0, 0)
-        for d in range(1, width):
-            arrived(0, 0, d)
-            send(0, 0, d, y_peer, 1, d)
-            hand_over(0, 0, d)
-        arrived(1, 1, 0)
-        for d in range(1, width):
-            send(1, 1, 0, x_peers[d], 1, d)
-        hand_over(1, 1, 0)
-        arrived(0, 1, 0)
-        hand_over(0, 1, 0)
-        for d in range(1, width):
-            arrived(1, 0, d)
-            hand_over(1, 0, d)
-        for d in range(1, width):
-            arrived(0, 1, d)
-            hand_over(0, 1, d)
-            arrived(1, 1, d)
-            hand_over(1, 1, d)
-        own.wait()
+        def arrived(n, h, dy, d):
+            at = place(n, h, dy, d)
+            remote(at, at, send_sems.at[0], recv_sems.at[n, h, dy, d], y_peer).wait_recv()
+
+        owns = []
+        for n in range(count):
+            own = pltpu.make_async_copy(srcs[n], dsts[n].at[head, :, rest], own_sems.at[n])
+            own.start()
+            owns.append(own)
+        for n in range(count):
+            for d in range(1, width):
+                send(n, 0, 0, 0, x_peers[d], 0, d)
+            send(n, 1, 0, 0, y_peer, 1, 0)
+            send(n, 0, 0, 0, y_peer, 1, 0)
+            for d in range(1, width):
+                send(n, 1, 0, 0, x_peers[d], 0, d)
+            hand_over(n, 0, 0, 0)
+            hand_over(n, 1, 0, 0)
+        for n in range(count):
+            for d in range(1, width):
+                arrived(n, 0, 0, d)
+                send(n, 0, 0, d, y_peer, 1, d)
+                hand_over(n, 0, 0, d)
+            arrived(n, 1, 1, 0)
+            for d in range(1, width):
+                send(n, 1, 1, 0, x_peers[d], 1, d)
+            hand_over(n, 1, 1, 0)
+        for n in range(count):
+            arrived(n, 0, 1, 0)
+            hand_over(n, 0, 1, 0)
+            for d in range(1, width):
+                arrived(n, 1, 0, d)
+                hand_over(n, 1, 0, d)
+            for d in range(1, width):
+                arrived(n, 0, 1, d)
+                hand_over(n, 0, 1, d)
+                arrived(n, 1, 1, d)
+                hand_over(n, 1, 1, d)
+        for own in owns:
+            own.wait()
         for copy in passes:
             copy.wait()
         for copy in sends:
@@ -172,20 +201,24 @@
 
     return pl.pallas_call(
         body,
-        out_shape=jax.ShapeDtypeStruct(
-            (2, values.shape[0], span) + tuple(values.shape[1:]), values.dtype
-        ),
-        in_specs=[ANY],
-        out_specs=ANY,
+        out_shape=[
+            jax.ShapeDtypeStruct(
+                (2, values.shape[0], span) + tuple(values.shape[1:]), values.dtype
+            )
+            for values in arrays
+        ],
+        in_specs=[ANY] * count,
+        out_specs=[ANY] * count,
         scratch_shapes=[
-            DMA,
-            DMA((links,)),
-            DMA((2, 2, width)),
-            DMA((2, 2, width)),
-            DMA((2, 2, width)),
+            DMA((count,)),
+            DMA((count * links,)),
+            DMA((count, 2, 2, width)),
+            DMA((count, 2, 2, width)),
+            DMA((count, 2, 2, width)),
         ],
         compiler_params=comm_params(collective_id),
-    )(values)
+        cost_estimate=lasting(cost),
+    )(*arrays)
 
 
 def plane_reduce(values, blocks, collective_id):
@@ -343,6 +376,7 @@
             DMA((2, width)),
         ],
         compiler_params=comm_params(collective_id),
+        cost_estimate=lasting(25),
     )(values.reshape((2, slabs, width, 2) + tile))
 
 
@@ -400,6 +434,7 @@
         out_specs=ANY,
         scratch_shapes=[DMA, DMA((NE,)), DMA((NE,)), DMA((copies, NE)), DMA((copies, NE))],
         compiler_params=comm_params(collective_id),
+        cost_estimate=lasting(15),
     )(buffer)
 
 
@@ -468,6 +503,7 @@
             DMA((copies, NE)),
         ],
         compiler_params=comm_params(collective_id),
+        cost_estimate=lasting(15),
     )(parts)
 
 
@@ -650,6 +686,114 @@
             transcendentals=count * rows * total_keys,
         ),
     )(bounds, queries, grads, kept, kv_all, starts)
+
+
+def expert_forward(head, rows_in, own, other):
+    count, width = rows_in.shape
+    hidden, features = own[0].shape
+    tile = min(hidden, 256)
+    steps = hidden // tile
+
+    def body(head_ref, x_ref, go, gx, uo, ux, do, dx, out_ref, acc_ref):
+        i = pl.program_id(0)
+        mine = pl.ds(pl.multiple_of(head_ref[0] * features, LANES), features)
+        rest = pl.ds(pl.multiple_of((1 - head_ref[0]) * features, LANES), features)
+        xo, xx = x_ref[:, mine], x_ref[:, rest]
+        gate = dot32(xo, go[...], LAST) + dot32(xx, gx[...], LAST)
+        up = dot32(xo, uo[...], LAST) + dot32(xx, ux[...], LAST)
+        act = (jax.nn.silu(gate) * up).astype(jnp.bfloat16)
+
+        @pl.when(i == 0)
+        def _():
+            acc_ref[...] = jnp.zeros_like(acc_ref)
+
+        acc_ref[:, mine] += dot32(act, do[...])
+        acc_ref[:, rest] += dot32(act, dx[...])
+
+        @pl.when(i == steps - 1)
+        def _():
+            out_ref[...] = acc_ref[...].astype(jnp.bfloat16)
+
+    whole = pl.BlockSpec((count, width), lambda i, h: (0, 0))
+    piece = pl.BlockSpec((tile, features), lambda i, h: (i, 0))
+    weights = [w for pair in zip(own, other) for w in pair]
+    return pl.pallas_call(
+        body,
+        out_shape=jax.ShapeDtypeStruct((count, width), jnp.bfloat16),
+        grid_spec=pltpu.PrefetchScalarGridSpec(
+            num_scalar_prefetch=1,
+            grid=(steps,),
+            in_specs=[whole] + [piece] * 6,
+            out_specs=whole,
+            scratch_shapes=[pltpu.VMEM((count, width), jnp.float32)],
+        ),
+        compiler_params=pltpu.CompilerParams(vmem_limit_bytes=VMEM_BYTES),
+        cost_estimate=pl.CostEstimate(
+            flops=6 * count * width * hidden,
+            bytes_accessed=6 * hidden * features * 2 + 4 * count * width,
+            transcendentals=count * hidden,
+        ),
+    )(head, rows_in, *weights)
+
+
+def expert_backward(head, rows_in, grads_in, own, other):
+    count, width = rows_in.shape
+    hidden, features = own[0].shape
+    tile = min(hidden, 256)
+    steps = hidden // tile
+
+    def body(head_ref, x_ref, z_ref, go, gx, uo, ux, do, dx, *outs):
+        keeps, sends, out_ref, acc_ref = outs[:3], outs[3:6], outs[6], outs[7]
+        i = pl.program_id(0)
+        mine = pl.ds(pl.multiple_of(head_ref[0] * features, LANES), features)
+        rest = pl.ds(pl.multiple_of((1 - head_ref[0]) * features, LANES), features)
+        xo, xx = x_ref[:, mine], x_ref[:, rest]
+        zo, zx = z_ref[:, mine], z_ref[:, rest]
+        gate = dot32(xo, go[...], LAST) + dot32(xx, gx[...], LAST)
+        up = dot32(xo, uo[...], LAST) + dot32(xx, ux[...], LAST)
+        dact = dot32(zo, do[...], LAST) + dot32(zx, dx[...], LAST)
+        sigmoid = jax.nn.sigmoid(gate)
+        silu = gate * sigmoid
+        act = (silu * up).astype(jnp.bfloat16)
+        dgate = (dact * up * sigmoid * (1.0 + gate * (1.0 - sigmoid))).astype(jnp.bfloat16)
+        dup = (dact * silu).astype(jnp.bfloat16)
+
+        @pl.when(i == 0)
+        def _():
+            acc_ref[...] = jnp.zeros_like(acc_ref)
+
+        acc_ref[:, mine] += dot32(dgate, go[...]) + dot32(dup, uo[...])
+        acc_ref[:, rest] += dot32(dgate, gx[...]) + dot32(dup, ux[...])
+        for n, (left, mine_in, rest_in) in enumerate(((dgate, xo, xx), (dup, xo, xx), (act, zo, zx))):
+            keeps[n][...] = dot32(left, mine_in, FIRST)
+            sends[n][...] = dot32(left, rest_in, FIRST).astype(jnp.bfloat16)
+
+        @pl.when(i == steps - 1)
+        def _():
+            out_ref[...] = acc_ref[...].astype(jnp.bfloat16)
+
+    whole = pl.BlockSpec((count, width), lambda i, h: (0, 0))
+    piece = pl.BlockSpec((tile, features), lambda i, h: (i, 0))
+    weights = [w for pair in zip(own, other) for w in pair]
+    return pl.pallas_call(
+        body,
+        out_shape=[jax.ShapeDtypeStruct((hidden, features), jnp.float32)] * 3
+        + [jax.ShapeDtypeStruct((hidden, features), jnp.bfloat16)] * 3
+        + [jax.ShapeDtypeStruct((count, width), jnp.bfloat16)],
+        grid_spec=pltpu.PrefetchScalarGridSpec(
+            num_scalar_prefetch=1,
+            grid=(steps,),
+            in_specs=[whole, whole] + [piece] * 6,
+            out_specs=[piece] * 6 + [whole],
+            scratch_shapes=[pltpu.VMEM((count, width), jnp.float32)],
+        ),
+        compiler_params=pltpu.CompilerParams(vmem_limit_bytes=VMEM_BYTES),
+        cost_estimate=pl.CostEstimate(
+            flops=22 * count * width * hidden,
+            bytes_accessed=15 * hidden * features * 2 + 8 * count * width,
+            transcendentals=count * hidden,
+        ),
+    )(head, rows_in, grads_in, *weights)
 
 
 def norm_forward(values, gain_vec):
@@ -713,45 +857,59 @@
     own_out = heads * head_dim
 
     swap = [(0, 1), (1, 0)]
-    ready = [
-        [lax.ppermute(w[layer], "head", swap) for w in (w_gate, w_up, w_down)]
-        for layer in range(LAYERS)
-    ]
-
-    def whole_features(own, other):
-        return jnp.concatenate(
-            [
-                jnp.where(head_index == 0, own, other),
-                jnp.where(head_index == 0, other, own),
-            ],
-            axis=1,
-        )
-
-    qkv_slabs = w_qkv.reshape((LAYERS, shard_rows, 3, COLUMNS, heads, head_dim))
-    qkv_slabs = qkv_slabs.transpose((3, 0, 1, 4, 2, 5)).reshape(
-        (COLUMNS, LAYERS, shard_rows, own_qkv)
-    )
-    small = jnp.concatenate(
-        [gain_attn[..., None], gain_moe[..., None], const_gate, const_vec], axis=2
-    )
+    head_scalar = head_index.reshape((1,)).astype(jnp.int32)
+
     seg_own = lax.dynamic_index_in_dim(segments, head_index, 0, keepdims=False)
     seg_parts = jnp.concatenate([lax.rem(seg_own, 128), lax.div(seg_own, 128)]).astype(
         jnp.bfloat16
     )
     seg_columns = -(-seg_parts.shape[0] // shard_rows)
     seg_parts = jnp.pad(seg_parts, (0, seg_columns * shard_rows - seg_parts.shape[0]))
-    seg_parts = jnp.broadcast_to(
-        seg_parts.reshape((1, shard_rows, seg_columns)), (LAYERS, shard_rows, seg_columns)
-    )
-    side = jnp.concatenate([w_out, small, seg_parts], axis=2)
-    side = jnp.pad(side, ((0, 0), (0, 0), (0, -(own_qkv + side.shape[2]) % LANES)))
-    slabs = jnp.concatenate(
-        [qkv_slabs, jnp.broadcast_to(side[None], (COLUMNS,) + side.shape)], axis=3
-    )
-    weights = plane_gather(column_exchange(slabs, blocks, False, 1), blocks, 2)
-    weights = weights.reshape((shards, LAYERS, shard_rows, -1))
-
-    seg_all = weights[:, 0, :, own_qkv + width + 8 : own_qkv + width + 8 + seg_columns]
+    seg_parts = seg_parts.reshape((shard_rows, seg_columns))
+    packs = []
+    for layer in range(LAYERS):
+        split = w_qkv[layer].reshape((shard_rows, 3, COLUMNS, heads, head_dim))
+        query_part = jnp.pad(split[:, 0], ((0, 0),) * 3 + ((0, LANES - head_dim),))
+        kv_part = jnp.concatenate([split[:, 1], split[:, 2]], axis=3)
+        side = jnp.concatenate(
+            [
+                w_out[layer],
+                gain_attn[layer][:, None],
+                gain_moe[layer][:, None],
+                const_gate[layer],
+                const_vec[layer],
+                seg_parts,
+            ],
+            axis=1,
+        )
+        side = jnp.pad(side, ((0, 0), (0, -side.shape[1] % LANES)))
+        pack = jnp.concatenate(
+            [
+                query_part.transpose((1, 0, 2, 3)).reshape((COLUMNS, shard_rows, heads * LANES)),
+                kv_part.transpose((1, 0, 2, 3)).reshape((COLUMNS, shard_rows, heads * LANES)),
+                jnp.broadcast_to(side[None], (COLUMNS,) + side.shape),
+            ],
+            axis=2,
+        )
+        packs.append(pack)
+    *packs, column_tokens = column_exchange(
+        packs + [tokens], [False] * LAYERS + [True], blocks, 1, 14
+    )
+    weights = plane_gather(packs, blocks, 2, 24)
+    weights = [pack.reshape((shards, shard_rows, -1)) for pack in weights]
+    out_at = 2 * heads * LANES
+    small_at = out_at + width
+
+    def send_experts(layer, after):
+        held = lax.optimization_barrier(
+            tuple(w[layer] for w in (w_gate, w_up, w_down)) + (after,)
+        )[:3]
+        return held, [lax.ppermute(w, "head", swap) for w in held]
+
+    own_experts, other_experts = [None] * LAYERS, [None] * LAYERS
+    own_experts[0], other_experts[0] = send_experts(0, weights[0])
+
+    seg_all = weights[0][:, :, small_at + 8 : small_at + 8 + seg_columns]
     seg_all = seg_all.reshape((shards, -1))[:, : 2 * token_rows].astype(jnp.int32)
     seg_all = seg_all[:, :token_rows] + 128 * seg_all[:, token_rows:]
     seg_query = lax.dynamic_index_in_dim(
@@ -771,14 +929,12 @@
     starts = starts[:, None, :]
 
     layers = []
-    for layer in range(LAYERS):
-        rows = weights[:, layer]
-        qkv = rows[:, :, :own_qkv].reshape((width, heads, 3, head_dim))
-        query_w = jnp.pad(qkv[:, :, 0], ((0, 0), (0, 0), (0, LANES - head_dim)))
-        query_w = query_w.reshape((width, heads * LANES))
-        kv_w = qkv[:, :, 1:].reshape((width, heads * LANES))
-        out_w = rows[:, :, own_qkv : own_qkv + width].reshape((width, width))
-        small_w = rows[:, :, own_qkv + width : own_qkv + width + 8].reshape((width, 8))
+    for pack in weights:
+        rows = pack.reshape((width, -1))
+        query_w = rows[:, : heads * LANES]
+        kv_w = rows[:, heads * LANES : out_at]
+        out_w = rows[:, out_at:small_at]
+        small_w = rows[:, small_at : small_at + 8]
         layers.append((query_w, kv_w, out_w, small_w))
 
     residual = tokens.astype(jnp.float32)
@@ -790,14 +946,20 @@
         gate_w = small_w[:, 2:6]
         vectors = small_w[:, 6:8].astype(jnp.float32).T
         normed_in, unit_in, scale_in = norm_forward(residual, attn_gain)
-        column = column_exchange(normed_in.astype(jnp.bfloat16), blocks, True, 3)
+        if layer == 0:
+            column = norm_forward(column_tokens.astype(jnp.float32), attn_gain)[0]
+            column = column.astype(jnp.bfloat16)
+        else:
+            (column,) = column_exchange([normed_in.astype(jnp.bfloat16)], [True], blocks, 3)
         column = column.reshape((COLUMNS * token_rows, width))
         queries = (
             dot32(column, query_w).astype(jnp.bfloat16).astype(jnp.float32) * scale
         ).astype(jnp.bfloat16)
         queries = queries.reshape((COLUMNS, token_rows, heads * LANES))
         kv_own = dot32(column, kv_w).astype(jnp.bfloat16)
-        kv_all = plane_gather(kv_own.reshape((COLUMNS, token_rows, heads * LANES)), blocks, 4)
+        (kv_all,) = plane_gather(
+            [kv_own.reshape((COLUMNS, token_rows, heads * LANES))], blocks, 4
+        )
         kv_all = kv_all.reshape((positions, heads * LANES))
         attended = attend(bounds, queries, kv_all, starts)
         attn_col = (
@@ -805,7 +967,7 @@
             .reshape((COLUMNS, token_rows, own_out))
             .astype(jnp.bfloat16)
         )
-        attn = column_exchange(attn_col, blocks, False, 5)
+        (attn,) = column_exchange([attn_col], [False], blocks, 5, 9)
         attn = attn.transpose((1, 0, 2)).reshape((token_rows, width))
         middle = residual + dot32(attn, out_w)
         normed_mid, unit_mid, scale_mid = norm_forward(middle, moe_gain)
@@ -819,14 +981,9 @@
         sent = dot32(picks.astype(jnp.bfloat16), moe_in, FIRST).astype(jnp.bfloat16)
         arrived = expert_dispatch(sent.reshape((NE, CAP, width)), blocks, 6)
         flat_in = arrived.reshape((-1, width))
-        expert_w = [
-            whole_features(w[layer], other)
-            for w, other in zip((w_gate, w_up, w_down), ready[layer])
-        ]
-        gate_pre = dot32(flat_in, expert_w[0], LAST)
-        up_pre = dot32(flat_in, expert_w[1], LAST)
-        hidden = (jax.nn.silu(gate_pre) * up_pre).astype(jnp.bfloat16)
-        parts = dot32(hidden, expert_w[2]).astype(jnp.bfloat16)
+        if layer + 1 < LAYERS:
+            own_experts[layer + 1], other_experts[layer + 1] = send_experts(layer + 1, flat_in)
+        parts = expert_forward(head_scalar, flat_in, own_experts[layer], other_experts[layer])
         back = expert_return(parts.reshape((copies, NE, CAP, width)), blocks, 7)
         back = back.reshape((NE * CAP, width)).astype(jnp.float32)
         ffn_out = jnp.dot(pick_gates, back, precision=HIGHEST)
@@ -860,10 +1017,6 @@
                 picks,
                 pick_gates,
                 flat_in,
-                expert_w,
-                gate_pre,
-                up_pre,
-                hidden,
                 copy_weight,
                 const_weight,
                 mixing,
@@ -894,10 +1047,6 @@
             picks,
             pick_gates,
             flat_in,
-            expert_w,
-            gate_pre,
-            up_pre,
-            hidden,
             copy_weight,
             const_weight,
             mixing,
@@ -925,30 +1074,18 @@
         cgate_grad = jnp.dot(moe_float.T, logit_grad, precision=HIGHEST)
         cvec_grad = jnp.sum(mixing[:, :, 1:2] * mix_grad, axis=0).T
 
-        sigmoid = jax.nn.sigmoid(gate_pre)
-        silu = gate_pre * sigmoid
-        hidden_grad = dot32(dz_in, expert_w[2], LAST)
-        dgate = (hidden_grad * up_pre * sigmoid * (1.0 + gate_pre * (1.0 - sigmoid))).astype(
-            jnp.bfloat16
-        )
-        dup = (hidden_grad * silu).astype(jnp.bfloat16)
-        dparts = (dot32(dgate, expert_w[0]) + dot32(dup, expert_w[1])).astype(jnp.bfloat16)
+        *wgrads, dparts = expert_backward(
+            head_scalar, flat_in, dz_in, own_experts[layer], other_experts[layer]
+        )
         dback = expert_return(dparts.reshape((copies, NE, CAP, width)), blocks, 7)
-        weight_grads = [dot32(a, b, FIRST) for a, b in ((dgate, flat_in), (dup, flat_in), (hidden, dz_in))]
-        summed = []
-        for grad in weight_grads:
-            away = lax.dynamic_slice_in_dim(grad, (1 - head_index) * features, features, 1)
-            own = lax.dynamic_slice_in_dim(grad, head_index * features, features, 1)
-            got = lax.ppermute(away.astype(jnp.bfloat16), "head", swap)
-            summed.append(own + got.astype(jnp.float32))
-        expert_grads[layer] = summed
+        got = [lax.ppermute(away, "head", swap) for away in wgrads[3:]]
 
         hn_grad = hn_grad + dot32(
             picks.astype(jnp.bfloat16), dback.reshape((NE * CAP, width))
         )
         middle_grad, moe_gain_grad = norm_backward(hn_grad, unit_mid, scale_mid, moe_gain)
         middle_grad = middle_grad + upstream
-        dy = column_exchange(middle_grad.astype(jnp.bfloat16), blocks, True, 3)
+        (dy,) = column_exchange([middle_grad.astype(jnp.bfloat16)], [True], blocks, 3)
         dy = dy.reshape((COLUMNS * token_rows, width))
         out_rows = lax.dynamic_slice_in_dim(out_w, plane * own_out, own_out, 0)
         out_rows = jnp.pad(
@@ -964,12 +1101,19 @@
         dq = dq.reshape((-1, heads * LANES))
         dkv = dkv.reshape((-1, heads * LANES))
         dxn = (dot32(dq, query_w, LAST) + dot32(dkv, kv_w, LAST)).astype(jnp.bfloat16)
-        dxn = column_exchange(dxn.reshape((COLUMNS, token_rows, width)), blocks, False, 9)
+        (dxn,) = column_exchange(
+            [dxn.reshape((COLUMNS, token_rows, width))], [False], blocks, 9
+        )
         dxn = jnp.sum(dxn.astype(jnp.float32), axis=0)
         query_grad = dot32(column, dq, FIRST).reshape((width, heads, LANES))[:, :, :head_dim]
         kv_grad = dot32(column, dkv, FIRST).reshape((width, heads, LANES))
         lead_grad, attn_gain_grad = norm_backward(dxn, unit_in, scale_in, attn_gain)
         upstream = middle_grad + lead_grad
+        if layer > 0:
+            upstream, *got = lax.optimization_barrier((upstream, *got))
+        expert_grads[layer] = [
+            own + other.astype(jnp.float32) for own, other in zip(wgrads[:3], got)
+        ]
 
         qkv_part = jnp.concatenate([query_grad, kv_grad], axis=2).reshape(
             (2, COLUMNS, span, shard_rows, own_qkv)
@@ -992,7 +1136,8 @@
     packed = jnp.concatenate(shared_grads, axis=3)
     packed = jnp.pad(packed, ((0, 0),) * 4 + ((0, -packed.shape[4] % LANES),))
     reduced = plane_reduce(packed, blocks, 10)
-    from_planes = column_exchange(reduced, blocks, False, 11).astype(jnp.float32)
+    (from_planes,) = column_exchange([reduced], [False], blocks, 11, 10)
+    from_planes = from_planes.astype(jnp.float32)
     from_planes = from_planes.reshape((COLUMNS, LAYERS, shard_rows, -1))
     qkv_out = from_planes[..., :own_qkv].reshape(
         (COLUMNS, LAYERS, shard_rows, heads, 3, head_dim)

time: 870 us -> 823 us (0.946)
  waiting for transfers between devices: 84.7 us -> 38 us
  matrix products: 66.7 us -> 29.8 us
  Pallas kernels: 533 us -> 569 us
  local copies, waits for them, and re-layouts: 122 us -> 111 us
    ppermute x12, waiting for transfers between devices: 84.7 us -> 38 us  [the longest x6 38 us: per_device(): got = [lax.ppermute(away, 'head', swap) for away in wgrads[3:]]]
    dot_general x42 -> x24, matrix products: 62.1 us -> 23.2 us  [dot32(): return lax.dot_general(a, b, dims, preferred_element_type=jnp.float32)]
    pallas_call x13 -> x16, Pallas kernels: 273 us -> 307 us  [the longest x9 156 us: column_exchange(): pl.pallas_call(body, out_shape=[jax.ShapeDtypeStruct((COLUMNS,) + slab, v...]
    slice x16 -> x5, local copies, waits for them, and re-layouts: 29.5 us -> 5.47 us  [the longest x2 3.48 us: per_device(): out_w = rows[:, out_at:small_at]]
    unnamed x332 -> x306, local copies, waits for them, and re-layouts: 14.1 us -> 28.5 us
  transfers between devices with their start and end apart: 13 -> 13, of which waited for: 6 -> 3; matrix products, arithmetic and copies ran while one was open for 11% -> 15% of each run, Pallas kernels for 22% -> 28%
where the time goes in v2:
time: 823 us; the launch traced here: 810 us
  Pallas kernels  569 us (69%)
  local copies, waits for them, and re-layouts  111 us (13%)
  other arithmetic  43.2 us (5%)
  waiting for transfers between devices  38 us (5%)
  matrix products  29.8 us (4%)
  starting transfers between devices  15.6 us (2%)
    pallas_call x9, Pallas kernels, column_exchange(): pl.pallas_call(body, out_shape=[jax.ShapeDtypeStruct((COLUMNS,) + slab, v...  156 us
    pallas_call x3, Pallas kernels, plane_gather(): pl.pallas_call(body, out_shape=[jax.ShapeDtypeStruct((2, values.shape[0],...  95.1 us
    pallas_call x4, Pallas kernels, expert_return(): pl.pallas_call(body, out_shape=jax.ShapeDtypeStruct((NE,) + tile, kind),...  62.7 us
    pallas_call x4, Pallas kernels, expert_dispatch(): pl.pallas_call(body, out_shape=jax.ShapeDtypeStruct((copies, NE) + tile,...  59.1 us
    pallas_call x3, Pallas kernels, plane_reduce(): pl.pallas_call(body, out_shape=jax.ShapeDtypeStruct((slabs,) + tile, kind...  57.7 us
    pallas_call x2, Pallas kernels, attend_back(): pl.pallas_call(body, out_shape=(jax.ShapeDtypeStruct((count, rows, width)...  47.5 us
    pallas_call x2, Pallas kernels, expert_backward(): pl.pallas_call(body, out_shape=[jax.ShapeDtypeStruct((hidden, features),...  40.1 us
    ppermute x6, waiting for transfers between devices, per_device(): got = [lax.ppermute(away, 'head', swap) for away in wgrads[3:]]  38 us
  transfers between devices with their start and end apart: 13, of which 3 were waited for; matrix products, arithmetic and copies ran while one was open for 15% of the time, Pallas kernels for 28%

profile of v2, /device:TPU:12, one launch (start us, length us, event | category | flops | bytes accessed | tf_op | source)
XLA Modules:
  0.0 810.0 jit_solution(4779076892415256205)
XLA Ops:
  10.8 34.6 %shard_map.221 = (bf16[4,24,1664]{2,1,0:T(8,128)(2,1)S(1)}, bf16[4,24,1664]{2,1,0:T(8,128)(2,1)S(1)}, bf16[4,128,768]{2,1,0:T(8,128)(2,1)S(1)}) custom-call(bf16[4,24,1664]{2,1,0:T(8,128)(2,1)S(1)} %pad_maximum_fusion.5.refs_0_, bf16[4,24,1664]{2,1,0:T(8,128)(2,1)S(1)} %pad_maximum_fusion.6.refs_1_, bf16[128,768]{1,0:T(8,128)(2,1)S(1)} %copy-done.2), custom_call_target="tpu_custom_call" | custom-call | bytes 49000000 | tf_op jit(solution)/shard_map/pallas_call | solution.py:91
  45.5 25.1 %shard_map.222 = (bf16[2,4,4,24,1664]{4,3,2,1,0:T(8,128)(2,1)S(1)}, bf16[2,4,4,24,1664]{4,3,2,1,0:T(8,128)(2,1)S(1)}) custom-call(bf16[4,24,1664]{2,1,0:T(8,128)(2,1)S(1)} %get-tuple-element.44.refs_0_, bf16[4,24,1664]{2,1,0:T(8,128)(2,1)S(1)} %get-tuple-element.45.refs_1_), custom_call_target="tpu_custom_call" | custom-call | bytes 84000000 | tf_op jit(solution)/shard_map/pallas_call | solution.py:202
  89.0 52.1 %shard_map.223 = bf16[2,4,4,128,384]{4,3,2,1,0:T(8,128)(2,1)S(1)} custom-call(bf16[4,128,384]{2,1,0:T(8,128)(2,1)S(1)} %bitcast.410), custom_call_target="tpu_custom_call" | custom-call | bytes 56000000 | tf_op jit(solution)/shard_map/pallas_call | solution.py:202
  141.2 17.5 %shard_map.224.kept_ref = f32[4,128,384]{2,1,0:T(8,128)S(1)} custom-call(s32[4,3]{1,0:T(4,128)S(1)} %pad_add_fusion.bounds_ref, bf16[4,128,384]{2,1,0:T(8,128)(2,1)S(1)} %bitcast.416, bf16[4096,384]{1,0:T(8,128)(2,1)S(1)} %bitcast.374, s32[4,1,128]{2,1,0:T(1,128)S(1)} %bitcast.412), custom_call_target="tpu_custom_call" | custom-call | flops 1610612736 | bytes 3145728 | tf_op jit(solution)/shard_map/pallas_call | solution.py:571
  175.8 13.9 %shard_map.226 = bf16[2,8,40,768]{3,2,1,0:T(8,128)(2,1)S(1)} custom-call(bf16[8,40,768]{2,1,0:T(8,128)(2,1)S(1)} %bitcast.392), custom_call_target="tpu_custom_call" | custom-call | bytes 52500000 | tf_op jit(solution)/shard_map/pallas_call | solution.py:430
  221.8 15.7 %shard_map.236 = bf16[2,8,40,768]{3,2,1,0:T(8,128)(2,1)S(1)} custom-call(bf16[8,40,768]{2,1,0:T(8,128)(2,1)S(1)} %bitcast.391), custom_call_target="tpu_custom_call" | custom-call | bytes 52500000 | tf_op jit(solution)/shard_map/pallas_call | solution.py:430
  245.7 8.1 shard_map.227
  253.9 15.6 %shard_map.228 = bf16[8,40,768]{2,1,0:T(8,128)(2,1)S(1)} custom-call(bf16[2,8,40,768]{3,2,1,0:T(8,128)(2,1)S(1)} %bitcast.409), custom_call_target="tpu_custom_call" | custom-call | bytes 52500000 | tf_op jit(solution)/shard_map/pallas_call | solution.py:491
  271.1 20.8 %shard_map.229 = bf16[4,128,768]{2,1,0:T(8,128)(2,1)S(1)} custom-call(bf16[128,768]{1,0:T(8,128)(2,1)S(1)} %multiply_convert_fusion.1.refs_0_), custom_call_target="tpu_custom_call" | custom-call | bytes 56000000 | tf_op jit(solution)/shard_map/pallas_call | solution.py:91
  295.3 17.8 %shard_map.230 = bf16[2,4,4,128,384]{4,3,2,1,0:T(8,128)(2,1)S(1)} custom-call(bf16[4,128,384]{2,1,0:T(8,128)(2,1)S(1)} %bitcast.411), custom_call_target="tpu_custom_call" | custom-call | bytes 56000000 | tf_op jit(solution)/shard_map/pallas_call | solution.py:202
  313.2 17.5 %shard_map.231.kept_ref = f32[4,128,384]{2,1,0:T(8,128)S(1)} custom-call(s32[4,3]{1,0:T(4,128)S(1)} %pad_add_fusion.bounds_ref, bf16[4,128,384]{2,1,0:T(8,128)(2,1)S(1)} %bitcast.418, bf16[4096,384]{1,0:T(8,128)(2,1)S(1)} %bitcast.376, s32[4,1,128]{2,1,0:T(1,128)S(1)} %bitcast.413), custom_call_target="tpu_custom_call" | custom-call | flops 1610612736 | bytes 3145728 | tf_op jit(solution)/shard_map/pallas_call | solution.py:571
  357.9 13.8 %shard_map.233 = bf16[2,8,40,768]{3,2,1,0:T(8,128)(2,1)S(1)} custom-call(bf16[8,40,768]{2,1,0:T(8,128)(2,1)S(1)} %bitcast.393), custom_call_target="tpu_custom_call" | custom-call | bytes 52500000 | tf_op jit(solution)/shard_map/pallas_call | solution.py:430
  372.8 20.1 %shard_map.237 = (f32[1024,384]{1,0:T(8,128)}, f32[1024,384]{1,0:T(8,128)}, f32[1024,384]{1,0:T(8,128)}, bf16[1024,384]{1,0:T(8,128)(2,1)}, bf16[1024,384]{1,0:T...) custom-call(s32[1]{0:T(128)} %bitcast.40.head_ref, bf16[640,768]{1,0:T(8,128)(2,1)} %bitcast.402, ...), custom_call_target="tpu_custom_call" | custom-call | flops 11072962560 | bytes 15728640 | tf_op jit(solution)/shard_map/pallas_call | solution.py:778
  394.1 15.8 %shard_map.238 = bf16[8,40,768]{2,1,0:T(8,128)(2,1)S(1)} custom-call(bf16[2,8,40,768]{3,2,1,0:T(8,128)(2,1)S(1)} %bitcast.408), custom_call_target="tpu_custom_call" | custom-call | bytes 52500000 | tf_op jit(solution)/shard_map/pallas_call | solution.py:491
  414.6 20.1 %shard_map.239 = bf16[4,128,768]{2,1,0:T(8,128)(2,1)S(1)} custom-call(bf16[128,768]{1,0:T(8,128)(2,1)S(1)} %fusion.78.refs_0_), custom_call_target="tpu_custom_call" | custom-call | bytes 56000000 | tf_op jit(solution)/shard_map/pallas_call | solution.py:91
  435.5 23.8 %shard_map.240 = (bf16[4,128,384]{2,1,0:T(8,128)(2,1)S(1)}, bf16[4096,384]{1,0:T(8,128)(2,1)S(1)}) custom-call(s32[4,3]{1,0:T(4,128)S(1)} %pad_add_fusion.bounds_ref, bf16[4,128,384]{2,1,0:T(8,128)(2,1)S(1)} %bitcast.419, bf16[4,128,384]{2,1,0:T(8,128)(2,1)S(1)} %bitcast.421, f32[4,128,384]{2,1,0:T(8,128)S(1)} %copy-done.21, bf16[4096,384]{1,0:T(8,128)(2,1)} %bitcast.377, ...), custom_call_target="tpu_custom_call" | custom-call | flops 4026531840 | bytes 6291456 | tf_op jit(solution)/shard_map/pallas_call | solution.py:663
  460.0 18.8 %shard_map.241 = bf16[4,128,384]{2,1,0:T(8,128)(2,1)S(1)} custom-call(bf16[2,4,2,2,128,384]{5,4,3,2,1,0:T(8,128)(2,1)S(1)} %bitcast.379), custom_call_target="tpu_custom_call" | custom-call | bytes 87500000 | tf_op jit(solution)/shard_map/pallas_call | solution.py:359
  479.5 18.6 %shard_map.242 = bf16[4,128,768]{2,1,0:T(8,128)(2,1)S(1)} custom-call(bf16[4,128,768]{2,1,0:T(8,128)(2,1)S(1)} %bitcast.384), custom_call_target="tpu_custom_call" | custom-call | bytes 56000000 | tf_op jit(solution)/shard_map/pallas_call | solution.py:91
  514.1 7.8 shard_map.234
  522.9 15.0 %shard_map.235 = bf16[8,40,768]{2,1,0:T(8,128)(2,1)S(1)} custom-call(bf16[2,8,40,768]{3,2,1,0:T(8,128)(2,1)S(1)} %bitcast.407), custom_call_target="tpu_custom_call" | custom-call | bytes 52500000 | tf_op jit(solution)/shard_map/pallas_call | solution.py:491
  561.0 15.6 %shard_map.243 = bf16[2,8,40,768]{3,2,1,0:T(8,128)(2,1)S(1)} custom-call(bf16[8,40,768]{2,1,0:T(8,128)(2,1)S(1)} %bitcast.388), custom_call_target="tpu_custom_call" | custom-call | bytes 52500000 | tf_op jit(solution)/shard_map/pallas_call | solution.py:430
  577.5 20.0 %shard_map.244 = (f32[1024,384]{1,0:T(8,128)}, f32[1024,384]{1,0:T(8,128)}, f32[1024,384]{1,0:T(8,128)}, bf16[1024,384]{1,0:T(8,128)(2,1)S(1)}, bf16[1024,384]{1...) custom-call(s32[1]{0:T(128)} %bitcast.40.head_ref, bf16[640,768]{1,0:T(8,128)(2,1)} %bitcast.401, ...), custom_call_target="tpu_custom_call" | custom-call | flops 11072962560 | bytes 15728640 | tf_op jit(solution)/shard_map/pallas_call | solution.py:778
  599.5 16.3 %shard_map.245 = bf16[8,40,768]{2,1,0:T(8,128)(2,1)S(1)} custom-call(bf16[2,8,40,768]{3,2,1,0:T(8,128)(2,1)S(1)} %bitcast.406), custom_call_target="tpu_custom_call" | custom-call | bytes 52500000 | tf_op jit(solution)/shard_map/pallas_call | solution.py:491
  617.7 20.4 %shard_map.246 = bf16[4,128,768]{2,1,0:T(8,128)(2,1)S(1)} custom-call(bf16[128,768]{1,0:T(8,128)(2,1)S(1)} %get-tuple-element.150.refs_0_), custom_call_target="tpu_custom_call" | custom-call | bytes 56000000 | tf_op jit(solution)/shard_map/pallas_call | solution.py:91
  639.1 23.7 %shard_map.247 = (bf16[4,128,384]{2,1,0:T(8,128)(2,1)S(1)}, bf16[4096,384]{1,0:T(8,128)(2,1)S(1)}) custom-call(s32[4,3]{1,0:T(4,128)S(1)} %pad_add_fusion.bounds_ref, bf16[4,128,384]{2,1,0:T(8,128)(2,1)S(1)} %bitcast.417, bf16[4,128,384]{2,1,0:T(8,128)(2,1)S(1)} %bitcast.420, f32[4,128,384]{2,1,0:T(8,128)S(1)} %copy-done.19, bf16[4096,384]{1,0:T(8,128)(2,1)} %bitcast.375, ...), custom_call_target="tpu_custom_call" | custom-call | flops 4026531840 | bytes 6291456 | tf_op jit(solution)/shard_map/pallas_call | solution.py:663
  663.4 18.8 %shard_map.248 = bf16[4,128,384]{2,1,0:T(8,128)(2,1)S(1)} custom-call(bf16[2,4,2,2,128,384]{5,4,3,2,1,0:T(8,128)(2,1)S(1)} %bitcast.378), custom_call_target="tpu_custom_call" | custom-call | bytes 87500000 | tf_op jit(solution)/shard_map/pallas_call | solution.py:359
  682.7 18.7 %shard_map.249 = bf16[4,128,768]{2,1,0:T(8,128)(2,1)S(1)} custom-call(bf16[4,128,768]{2,1,0:T(8,128)(2,1)S(1)} %bitcast.385), custom_call_target="tpu_custom_call" | custom-call | bytes 56000000 | tf_op jit(solution)/shard_map/pallas_call | solution.py:91
  715.6 20.2 %shard_map.250.refs_0_ = bf16[4,48,896]{2,1,0:T(8,128)(2,1)S(1)} custom-call(bf16[2,4,2,2,48,896]{5,4,3,2,1,0:T(8,128)(2,1)S(1)} %bitcast.342), custom_call_target="tpu_custom_call" | custom-call | bytes 87500000 | tf_op jit(solution)/shard_map/pallas_call | solution.py:359
  735.8 9.9 %shard_map.251 = bf16[4,48,896]{2,1,0:T(8,128)(2,1)S(1)} custom-call(bf16[4,48,896]{2,1,0:T(8,128)(2,1)S(1)} %shard_map.250.refs_0_), custom_call_target="tpu_custom_call" | custom-call | bytes 35000000 | tf_op jit(solution)/shard_map/pallas_call | solution.py:91
  765.6 10.4 %collective-permute-done.10 = bf16[1024,384]{1,0:T(8,128)(2,1)S(1)} collective-permute-done((bf16[1024,384]{1,0:T(8,128)(2,1)S(1)}, bf16[1024,384]{1,0:T(8,128)(2,1)S(1)}, u32[]{:S(2)}, u32[]{:S(2)}) %collective-permute-start.10) | collective-permute-done | bytes 786464 | tf_op jit(solution)/shard_map/ppermute | solution.py:1081
  778.0 14.8 %collective-permute-done.11 = bf16[1024,384]{1,0:T(8,128)(2,1)S(1)} collective-permute-done((bf16[1024,384]{1,0:T(8,128)(2,1)S(1)}, bf16[1024,384]{1,0:T(8,128)(2,1)S(1)}, u32[]{:S(2)}, u32[]{:S(2)}) %collective-permute-start.11) | collective-permute-done | bytes 786464 | tf_op jit(solution)/shard_map/ppermute | solution.py:1081
  794.8 12.8 %collective-permute-done.12 = bf16[1024,384]{1,0:T(8,128)(2,1)S(1)} collective-permute-done((bf16[1024,384]{1,0:T(8,128)(2,1)S(1)}, bf16[1024,384]{1,0:T(8,128)(2,1)S(1)}, u32[]{:S(2)}, u32[]{:S(2)}) %collective-permute-start.12) | collective-permute-done | bytes 786464 | tf_op jit(solution)/shard_map/ppermute | solution.py:1081
  (571 shorter events, 212.5 us)
Async XLA Ops:
  8.5 62.1 %copy-start.70 = (bf16[2,1024,384]{2,1,0:T(8,128)(2,1)S(1)}, bf16[2,1024,384]{2,1,0:T(8,128)(2,1)}, u32[]{:S(2)}) copy-start(bf16[2,1024,384]{2,1,0:T(8,128)(2,1)} %param.25) | copy-start | bytes 4718596
  9.9 60.7 %copy-start.69 = (bf16[2,1024,384]{2,1,0:T(8,128)(2,1)S(1)}, bf16[2,1024,384]{2,1,0:T(8,128)(2,1)}, u32[]{:S(2)}) copy-start(bf16[2,1024,384]{2,1,0:T(8,128)(2,1)} %param.26) | copy-start | bytes 4718596
  73.1 172.3 %collective-permute-start = (bf16[1024,384]{1,0:T(8,128)(2,1)}, bf16[1024,384]{1,0:T(8,128)(2,1)}, u32[]{:S(2)}, u32[]{:S(2)}) collective-permute-start(bf16[1024,384]{1,0:T(8,128)(2,1)} %get-tuple-element.48.go), channel_id=1, source_target_pairs={{0,16},{16,0},{1,17},{17,1},{2,18},{18,2},{3,19},{19,3},{4,20},{20... | collective-permute-start | bytes 2359304 | tf_op jit(solution)/shard_map/ppermute | solution.py:907
  74.6 171.1 %collective-permute-start.1 = (bf16[1024,384]{1,0:T(8,128)(2,1)}, bf16[1024,384]{1,0:T(8,128)(2,1)}, u32[]{:S(2)}, u32[]{:S(2)}) collective-permute-start(bf16[1024,384]{1,0:T(8,128)(2,1)} %get-tuple-element.49.uo), channel_id=1, source_target_pairs={{0,16},{16,0},{1,17},{17,1},{2,18},{18,2},{3,19},{19,3},{4,20},{20... | collective-permute-start | bytes 2359304 | tf_op jit(solution)/shard_map/ppermute | solution.py:907
  75.1 170.6 %collective-permute-start.2 = (bf16[1024,384]{1,0:T(8,128)(2,1)}, bf16[1024,384]{1,0:T(8,128)(2,1)}, u32[]{:S(2)}, u32[]{:S(2)}) collective-permute-start(bf16[1024,384]{1,0:T(8,128)(2,1)} %get-tuple-element.50.do), channel_id=1, source_target_pairs={{0,16},{16,0},{1,17},{17,1},{2,18},{18,2},{3,19},{19,3},{4,20},{20... | collective-permute-start | bytes 2359304 | tf_op jit(solution)/shard_map/ppermute | solution.py:907
  86.2 54.9 %copy-start.62 = (s32[1,128,2]{2,1,0:T(8,128)}, s32[1,128,2]{2,1,0:T(8,128)S(1)}, u32[]{:S(2)}) copy-start(s32[1,128,2]{2,1,0:T(8,128)S(1)} %copy.459) | copy-start | bytes 3076
  87.2 87.4 %copy-start.91 = (f32[768]{0:T(1024)}, f32[768]{0:T(1024)S(1)}, u32[]{:S(2)}) copy-start(f32[768]{0:T(1024)S(1)} %convert_reduce_fusion.5) | copy-start | bytes 9220
  88.9 52.3 %copy-start.28 = (bf16[512,384]{1,0:T(8,128)(2,1)S(1)}, bf16[512,384]{1,0:T(8,128)(2,1)}, u32[]{:S(2)}) copy-start(bf16[512,384]{1,0:T(8,128)(2,1)} %fusion.13) | copy-start | bytes 1179652
  172.8 96.7 %copy-start.38 = (f32[128,768]{1,0:T(8,128)}, f32[128,768]{1,0:T(8,128)S(1)}, u32[]{:S(2)}) copy-start(f32[128,768]{1,0:T(8,128)S(1)} %get-tuple-element.195) | copy-start | bytes 1179652
  175.8 21.9 %copy-start.133 = (s32[1,128,2]{1,2,0:T(2,128)S(1)}, s32[1,128,2]{1,2,0:T(2,128)}, u32[]{:S(2)}) copy-start(s32[1,128,2]{1,2,0:T(2,128)} %get-tuple-element.180) | copy-start | bytes 3076
  190.8 181.9 %collective-permute-start.3 = (bf16[1024,384]{1,0:T(8,128)(2,1)}, bf16[1024,384]{1,0:T(8,128)(2,1)}, u32[]{:S(2)}, u32[]{:S(2)}) collective-permute-start(bf16[1024,384]{1,0:T(8,128)(2,1)} %get-tuple-element.52.go), channel_id=1, source_target_pairs={{0,16},{16,0},{1,17},{17,1},{2,18},{18,2},{3,19},{19,3},{4,20},{20... | collective-permute-start | bytes 2359304 | tf_op jit(solution)/shard_map/ppermute | solution.py:907
  190.8 181.9 %collective-permute-start.4 = (bf16[1024,384]{1,0:T(8,128)(2,1)}, bf16[1024,384]{1,0:T(8,128)(2,1)}, u32[]{:S(2)}, u32[]{:S(2)}) collective-permute-start(bf16[1024,384]{1,0:T(8,128)(2,1)} %get-tuple-element.53.uo), channel_id=1, source_target_pairs={{0,16},{16,0},{1,17},{17,1},{2,18},{18,2},{3,19},{19,3},{4,20},{20... | collective-permute-start | bytes 2359304 | tf_op jit(solution)/shard_map/ppermute | solution.py:907
  245.4 127.3 %collective-permute-start.5 = (bf16[1024,384]{1,0:T(8,128)(2,1)}, bf16[1024,384]{1,0:T(8,128)(2,1)}, u32[]{:S(2)}, u32[]{:S(2)}) collective-permute-start(bf16[1024,384]{1,0:T(8,128)(2,1)} %get-tuple-element.54.do), channel_id=1, source_target_pairs={{0,16},{16,0},{1,17},{17,1},{2,18},{18,2},{3,19},{19,3},{4,20},{20... | collective-permute-start | bytes 2359304 | tf_op jit(solution)/shard_map/ppermute | solution.py:907
  245.7 23.8 %copy-start.125 = (f32[128]{0:T(128)S(1)}, f32[128]{0:T(128)}, u32[]{:S(2)}) copy-start(f32[128]{0:T(128)} %get-tuple-element.141) | copy-start | bytes 1540
  372.7 37.2 %copy-start.82 = (pred[128,320]{0,1:T(8,128)(4,1)S(1)}, pred[128,320]{0,1:T(8,128)(4,1)}, u32[]{:S(2)}) copy-start(pred[128,320]{0,1:T(8,128)(4,1)} %copy-done.81) | copy-start | bytes 122884
  372.7 37.6 %copy-start.66 = (f32[128,768]{1,0:T(8,128)S(1)}, f32[128,768]{1,0:T(8,128)}, u32[]{:S(2)}) copy-start(f32[128,768]{1,0:T(8,128)} %get-tuple-element.152) | copy-start | bytes 1179652
  372.8 37.6 %copy-start.68 = (f32[128,768]{1,0:T(8,128)S(1)}, f32[128,768]{1,0:T(8,128)}, u32[]{:S(2)}) copy-start(f32[128,768]{1,0:T(8,128)} %convert_element_type.273) | copy-start | bytes 1179652
  372.8 37.6 %copy-start.102 = (f32[2,768]{1,0:T(2,128)S(1)}, f32[2,768]{1,0:T(2,128)}, u32[]{:S(2)}) copy-start(f32[2,768]{1,0:T(2,128)} %copy.411) | copy-start | bytes 18436
  499.1 59.0 %collective-permute-start.6 = (bf16[1024,384]{1,0:T(8,128)(2,1)}, bf16[1024,384]{1,0:T(8,128)(2,1)}, u32[]{:S(2)}, u32[]{:S(2)}) collective-permute-start(bf16[1024,384]{1,0:T(8,128)(2,1)} %get-tuple-element.58), channel_id=1, source_target_pairs={{0,16},{16,0},{1,17},{17,1},{2,18},{18,2},{3,19},{19,3},{4,20},{20... | collective-permute-start | bytes 2359304 | tf_op jit(solution)/shard_map/ppermute | solution.py:1081
  500.8 57.3 %collective-permute-start.7 = (bf16[1024,384]{1,0:T(8,128)(2,1)}, bf16[1024,384]{1,0:T(8,128)(2,1)}, u32[]{:S(2)}, u32[]{:S(2)}) collective-permute-start(bf16[1024,384]{1,0:T(8,128)(2,1)} %get-tuple-element.59), channel_id=1, source_target_pairs={{0,16},{16,0},{1,17},{17,1},{2,18},{18,2},{3,19},{19,3},{4,20},{20... | collective-permute-start | bytes 2359304 | tf_op jit(solution)/shard_map/ppermute | solution.py:1081
  501.1 57.0 %collective-permute-start.8 = (bf16[1024,384]{1,0:T(8,128)(2,1)}, bf16[1024,384]{1,0:T(8,128)(2,1)}, u32[]{:S(2)}, u32[]{:S(2)}) collective-permute-start(bf16[1024,384]{1,0:T(8,128)(2,1)} %get-tuple-element.60), channel_id=1, source_target_pairs={{0,16},{16,0},{1,17},{17,1},{2,18},{18,2},{3,19},{19,3},{4,20},{20... | collective-permute-start | bytes 2359304 | tf_op jit(solution)/shard_map/ppermute | solution.py:1081
  577.5 38.3 %copy-start.39 = (f32[128,768]{1,0:T(8,128)S(1)}, f32[128,768]{1,0:T(8,128)}, u32[]{:S(2)}) copy-start(f32[128,768]{1,0:T(8,128)} %copy-done.38) | copy-start | bytes 1179652
  577.5 38.3 %copy-start.92 = (f32[768]{0:T(1024)S(1)}, f32[768]{0:T(1024)}, u32[]{:S(2)}) copy-start(f32[768]{0:T(1024)} %copy-done.91) | copy-start | bytes 9220
  577.5 38.3 %copy-start.124 = (f32[128]{0:T(128)S(1)}, f32[128]{0:T(128)}, u32[]{:S(2)}) copy-start(f32[128]{0:T(128)} %copy-done.123) | copy-start | bytes 1540
  577.5 38.3 %copy-start.126 = (f32[128]{0:T(128)S(1)}, f32[128]{0:T(128)}, u32[]{:S(2)}) copy-start(f32[128]{0:T(128)} %get-tuple-element.141) | copy-start | bytes 1540
  616.8 21.4 %copy-start.86 = (bf16[3,128,768]{2,1,0:T(8,128)(2,1)S(1)}, bf16[3,128,768]{2,1,0:T(8,128)(2,1)}, u32[]{:S(2)}) copy-start(bf16[3,128,768]{2,1,0:T(8,128)(2,1)} %pad.35) | copy-start | bytes 1769476
  617.7 21.3 %copy-start.19 = (f32[4,128,384]{2,1,0:T(8,128)S(1)}, f32[4,128,384]{2,1,0:T(8,128)}, u32[]{:S(2)}) copy-start(f32[4,128,384]{2,1,0:T(8,128)} %copy-done.18) | copy-start | bytes 2359300
  617.7 21.3 %copy-start.29 = (bf16[512,384]{1,0:T(8,128)(2,1)S(1)}, bf16[512,384]{1,0:T(8,128)(2,1)}, u32[]{:S(2)}) copy-start(bf16[512,384]{1,0:T(8,128)(2,1)} %fusion.13) | copy-start | bytes 1179652
  750.7 14.2 %collective-permute-start.9 = (bf16[2,24,768]{2,1,0:T(8,128)(2,1)S(1)}, bf16[2,24,768]{2,1,0:T(8,128)(2,1)S(1)}, u32[]{:S(2)}, u32[]{:S(2)}) collective-permute-start(bf16[2,24,768]{2,1,0:T(8,128)(2,1)S(1)} %reshape.578), channel_id=1, source_target_pairs={{0,0},{1,1},{2,2},{3,3},{4,8},{5,9},{6,10},{7,11},{8,16},{9,17},{1... | collective-permute-start | bytes 221192 | tf_op jit(solution)/shard_map/ppermute | solution.py:1157
  755.5 20.5 %collective-permute-start.10 = (bf16[1024,384]{1,0:T(8,128)(2,1)S(1)}, bf16[1024,384]{1,0:T(8,128)(2,1)S(1)}, u32[]{:S(2)}, u32[]{:S(2)}) collective-permute-start(bf16[1024,384]{1,0:T(8,128)(2,1)S(1)} %copy-done.27), channel_id=1, source_target_pairs={{0,16},{16,0},{1,17},{17,1},{2,18},{18,2},{3,19},{19,3},{4,20},{20... | collective-permute-start | bytes 2359304 | tf_op jit(solution)/shard_map/ppermute | solution.py:1081
  756.0 36.8 %collective-permute-start.11 = (bf16[1024,384]{1,0:T(8,128)(2,1)S(1)}, bf16[1024,384]{1,0:T(8,128)(2,1)S(1)}, u32[]{:S(2)}, u32[]{:S(2)}) collective-permute-start(bf16[1024,384]{1,0:T(8,128)(2,1)S(1)} %copy-done.25), channel_id=1, source_target_pairs={{0,16},{16,0},{1,17},{17,1},{2,18},{18,2},{3,19},{19,3},{4,20},{20... | collective-permute-start | bytes 2359304 | tf_op jit(solution)/shard_map/ppermute | solution.py:1081
  757.5 50.1 %collective-permute-start.12 = (bf16[1024,384]{1,0:T(8,128)(2,1)S(1)}, bf16[1024,384]{1,0:T(8,128)(2,1)S(1)}, u32[]{:S(2)}, u32[]{:S(2)}) collective-permute-start(bf16[1024,384]{1,0:T(8,128)(2,1)S(1)} %copy-done.23), channel_id=1, source_target_pairs={{0,16},{16,0},{1,17},{17,1},{2,18},{18,2},{3,19},{19,3},{4,20},{20... | collective-permute-start | bytes 2359304 | tf_op jit(solution)/shard_map/ppermute | solution.py:1081
  (129 other events, 774.2 us)

commit v3 on v2

v3 whole, which is shorter than its diff:
```python
from functools import partial

import jax
import jax.numpy as jnp
from jax import lax
from jax.experimental import pallas as pl
from jax.experimental.pallas import tpu as pltpu
from jax.sharding import PartitionSpec as P

HEADS = 12
NE = 8
LAYERS = 2
CAP = 40
COLUMNS = 4
MESH = pl.DeviceIdType.MESH
ANY = pl.BlockSpec(memory_space=pl.ANY)
VMEM = pl.BlockSpec(memory_space=pltpu.VMEM)
DMA = pltpu.SemaphoreType.DMA
VMEM_BYTES = 48 * 1024 * 1024


def greet(peers):
    barrier = pltpu.get_barrier_semaphore()
    for peer in peers:
        pl.semaphore_signal(barrier, inc=1, device_id=peer, device_id_type=MESH)
    pl.semaphore_wait(barrier, len(peers))


def remote(src, dst, send_sem, recv_sem, peer):
    return pltpu.make_async_remote_copy(
        src_ref=src,
        dst_ref=dst,
        send_sem=send_sem,
        recv_sem=recv_sem,
        device_id=peer,
        device_id_type=MESH,
    )


def comm_params(collective_id):
    return pltpu.CompilerParams(
        collective_id=collective_id, has_side_effects=True, vmem_limit_bytes=VMEM_BYTES
    )


def lasting(microseconds):
    return pl.CostEstimate(
        flops=0, bytes_accessed=int(microseconds * 3_500_000), transcendentals=0
    )


def column_place(blocks):
    span = blocks // COLUMNS
    head, blk = lax.axis_index("head"), lax.axis_index("blk")
    plane, rest = lax.div(blk, span), lax.rem(blk, span)
    planes = [lax.rem(plane + d, COLUMNS) for d in range(COLUMNS)]
    return plane, planes, [(head, p * span + rest) for p in planes]


def column_start(src, gather, dst, own_sem, send_sems, recv_sems, where):
    plane, planes, peers = where
    own = pltpu.make_async_copy(src if gather else src.at[plane], dst.at[plane], own_sem)
    own.start()
    copies = [own]
    for d in (2, 1, 3):
        copy = remote(
            src if gather else src.at[planes[d]],
            dst.at[plane],
            send_sems.at[d],
            recv_sems.at[d],
            peers[d],
        )
        copy.start()
        copies.append(copy)
    return copies


def column_exchange(arrays, gathers, blocks, collective_id, cost=16):
    count = len(arrays)
    slabs = [
        tuple(values.shape if gather else values.shape[1:])
        for values, gather in zip(arrays, gathers)
    ]

    def body(*refs):
        srcs, dsts = refs[:count], refs[count : 2 * count]
        own_sems, send_sems, recv_sems = refs[2 * count :]
        where = column_place(blocks)
        greet(where[2][1:])
        copies = []
        for n in range(count):
            copies += column_start(
                srcs[n],
                gathers[n],
                dsts[n],
                own_sems.at[n],
                send_sems.at[n],
                recv_sems.at[n],
                where,
            )
        for copy in copies:
            copy.wait()

    return pl.pallas_call(
        body,
        out_shape=[
            jax.ShapeDtypeStruct((COLUMNS,) + slab, values.dtype)
            for values, slab in zip(arrays, slabs)
        ],
        in_specs=[ANY] * count,
        out_specs=[ANY] * count,
        scratch_shapes=[DMA((count,)), DMA((count, COLUMNS)), DMA((count, COLUMNS))],
        compiler_params=comm_params(collective_id),
        cost_estimate=lasting(cost),
    )(*arrays)


def plane_place(blocks):
    span = blocks // COLUMNS
    width = span // 2
    head, blk = lax.axis_index("head"), lax.axis_index("blk")
    plane, rest = lax.div(blk, span), lax.rem(blk, span)
    x, core = lax.div(rest, 2), lax.rem(rest, 2)
    first = plane * span
    right = [lax.rem(x + d, width) for d in range(width)]
    left = [lax.rem(x - d + width, width) for d in range(width)]
    x_peers = [(head, first + right[d] * 2 + core) for d in range(width)]
    y_peer = (1 - head, blk)
    core_peer = (head, first + x * 2 + 1 - core)
    return head, rest, core, left, x_peers, y_peer, core_peer


def plane_run(srcs, dsts, own_sems, send_sems, recv_sems, pass_sems, land_sems, where):
    head, rest, core, left, x_peers, y_peer, core_peer = where
    width, count = len(x_peers), len(srcs)
    sends, passes = [], []

    def place(n, h, dy, d):
        half = srcs[n].shape[0] // 2
        row = head if dy == 0 else 1 - head
        return dsts[n].at[row, pl.ds(h * half, half), left[d] * 2 + core]

    def held(n, h, dy, d):
        half = srcs[n].shape[0] // 2
        return srcs[n].at[pl.ds(h * half, half)] if dy == 0 and d == 0 else place(n, h, dy, d)

    def send(n, h, dy, d, peer, to_dy, to_d):
        copy = remote(
            held(n, h, dy, d),
            place(n, h, dy, d),
            send_sems.at[len(sends)],
            recv_sems.at[n, h, to_dy, to_d],
            peer,
        )
        copy.start()
        sends.append(copy)

    def hand_over(n, h, dy, d):
        copy = remote(
            held(n, h, dy, d),
            place(n, h, dy, d),
            pass_sems.at[n, h, dy, d],
            land_sems.at[n, h, dy, d],
            core_peer,
        )
        copy.start()
        passes.append(copy)

    def arrived(n, h, dy, d):
        at = place(n, h, dy, d)
        remote(at, at, send_sems.at[0], recv_sems.at[n, h, dy, d], y_peer).wait_recv()

    owns = []
    for n in range(count):
        own = pltpu.make_async_copy(srcs[n], dsts[n].at[head, :, rest], own_sems.at[n])
        own.start()
        owns.append(own)
    for n in range(count):
        for d in range(1, width):
            send(n, 0, 0, 0, x_peers[d], 0, d)
        send(n, 1, 0, 0, y_peer, 1, 0)
        send(n, 0, 0, 0, y_peer, 1, 0)
        for d in range(1, width):
            send(n, 1, 0, 0, x_peers[d], 0, d)
        hand_over(n, 0, 0, 0)
        hand_over(n, 1, 0, 0)
    for n in range(count):
        for d in range(1, width):
            arrived(n, 0, 0, d)
            send(n, 0, 0, d, y_peer, 1, d)
            hand_over(n, 0, 0, d)
        arrived(n, 1, 1, 0)
        for d in range(1, width):
            send(n, 1, 1, 0, x_peers[d], 1, d)
        hand_over(n, 1, 1, 0)
    for n in range(count):
        arrived(n, 0, 1, 0)
        hand_over(n, 0, 1, 0)
        for d in range(1, width):
            arrived(n, 1, 0, d)
            hand_over(n, 1, 0, d)
        for d in range(1, width):
            arrived(n, 0, 1, d)
            hand_over(n, 0, 1, d)
            arrived(n, 1, 1, d)
            hand_over(n, 1, 1, d)
    for own in owns:
        own.wait()
    for copy in passes:
        copy.wait()
    for copy in sends:
        copy.wait_send()


def plane_scratch(count, blocks):
    width = blocks // COLUMNS // 2
    links = 4 * (width - 1) + 2
    return [DMA((count,)), DMA((count * links,))] + [DMA((count, 2, 2, width))] * 3


def plane_shapes(arrays, blocks):
    return [
        jax.ShapeDtypeStruct(
            (2, values.shape[0], blocks // COLUMNS) + tuple(values.shape[1:]), values.dtype
        )
        for values in arrays
    ]


def plane_gather(arrays, blocks, collective_id, cost=16):
    count = len(arrays)

    def body(*refs):
        srcs, dsts, sems = refs[:count], refs[count : 2 * count], refs[2 * count :]
        where = plane_place(blocks)
        greet(where[4][1:] + [where[5], where[6]])
        plane_run(srcs, dsts, *sems, where)

    return pl.pallas_call(
        body,
        out_shape=plane_shapes(arrays, blocks),
        in_specs=[ANY] * count,
        out_specs=[ANY] * count,
        scratch_shapes=plane_scratch(count, blocks),
        compiler_params=comm_params(collective_id),
        cost_estimate=lasting(cost),
    )(*arrays)


def start_gather(packs, tokens, blocks, collective_id, cost=35):
    count = len(packs)

    def body(*refs):
        srcs, refs = refs[: count + 1], refs[count + 1 :]
        wholes, refs = refs[:count], refs[count:]
        columns, refs = refs[: count + 1], refs[count + 1 :]
        own_sems, send_sems, recv_sems, *plane_sems = refs
        column, plane = column_place(blocks), plane_place(blocks)
        greet(column[2][1:] + plane[4][1:] + [plane[5], plane[6]])
        waits = [
            column_start(
                srcs[n],
                n == count,
                columns[n],
                own_sems.at[n],
                send_sems.at[n],
                recv_sems.at[n],
                column,
            )
            for n in range(count + 1)
        ]
        for n in range(count):
            for copy in waits[n]:
                copy.wait()
        plane_run(columns[:count], wholes, *plane_sems, plane)
        for copy in waits[count]:
            copy.wait()

    results = pl.pallas_call(
        body,
        out_shape=plane_shapes(packs, blocks)
        + [jax.ShapeDtypeStruct(pack.shape, pack.dtype) for pack in packs]
        + [jax.ShapeDtypeStruct((COLUMNS,) + tokens.shape, tokens.dtype)],
        in_specs=[ANY] * (count + 1),
        out_specs=[ANY] * (2 * count + 1),
        scratch_shapes=[
            DMA((count + 1,)),
            DMA((count + 1, COLUMNS)),
            DMA((count + 1, COLUMNS)),
        ]
        + plane_scratch(count, blocks),
        compiler_params=comm_params(collective_id),
        cost_estimate=lasting(cost),
    )(*packs, tokens)
    return results[:count], results[-1]


def plane_reduce(arrays, blocks, collective_id, cost=25):
    span = blocks // COLUMNS
    width = span // 2
    count = len(arrays)
    shapes = [(values.shape[1],) + tuple(values.shape[3:]) for values in arrays]

    def body(*refs):
        srcs, outs, refs = refs[:count], refs[count : 2 * count], refs[2 * count :]
        scratch = [refs[8 * n : 8 * n + 8] for n in range(count)]
        core_send, core_recv, link_send, link_recv = refs[8 * count :]
        head, blk = lax.axis_index("head"), lax.axis_index("blk")
        plane, rest = lax.div(blk, span), lax.rem(blk, span)
        x, core = lax.div(rest, 2), lax.rem(rest, 2)
        first = plane * span
        right = [lax.rem(x + d, width) for d in range(width)]
        x_peers = [(head, first + right[d] * 2 + core) for d in range(width)]
        y_peer = (1 - head, blk)
        core_peer = (head, first + x * 2 + 1 - core)
        greet(x_peers[1:] + [y_peer, core_peer])

        def wide(ref, *at):
            return ref[at].astype(jnp.float32)

        starts = {}
        for n in range(count):
            half = shapes[n][0] // 2
            for h in range(2):
                copy = remote(
                    srcs[n].at[:, pl.ds(h * half, half), :, 1 - core],
                    scratch[n][0].at[:, pl.ds(h * half, half)],
                    core_send.at[n, h],
                    core_recv.at[n, h],
                    core_peer,
                )
                copy.start()
                starts[n, h] = copy

        sends, yas, ybs, xbs = {}, {}, {}, {}
        for n in range(count):
            src, half, kind = srcs[n], shapes[n][0] // 2, arrays[n].dtype
            core_in, summed, xa_in, _, _, yb_in, _, _ = scratch[n]

            def core_sum(h):
                def step(i, _):
                    yy = lax.div(i, half * width)
                    zz = lax.div(lax.rem(i, half * width), width) + h * half
                    xx = lax.rem(i, width)
                    total = wide(src, yy, zz, xx, core) + wide(core_in, yy, zz, xx)
                    summed[yy, zz, xx] = total.astype(kind)
                    return 0

                lax.fori_loop(0, 2 * half * width, step, 0)

            starts[n, 0].wait_recv()
            core_sum(0)
            for d in range(1, width):
                copy = remote(
                    summed.at[:, pl.ds(0, half), right[d]],
                    xa_in.at[d],
                    link_send.at[n, 0, d],
                    link_recv.at[n, 0, d],
                    x_peers[d],
                )
                copy.start()
                sends[n, d] = copy
            starts[n, 1].wait_recv()
            core_sum(1)
            ybs[n] = remote(
                summed.at[1 - head, pl.ds(half, half)],
                yb_in,
                link_send.at[n, 1, 0],
                link_recv.at[n, 1, 0],
                y_peer,
            )
            ybs[n].start()
        for n in range(count):
            half, kind = shapes[n][0] // 2, arrays[n].dtype
            _, summed, xa_in, ya_out, ya_in, yb_in, xb_out, xb_in = scratch[n]
            for d in range(1, width):
                sends[n, d].wait_recv()

            def a_step(zz, _):
                total = wide(summed, 1 - head, zz, x)
                for d in range(1, width):
                    total = total + wide(xa_in, d, 1 - head, zz)
                ya_out[zz] = total.astype(kind)
                return 0

            lax.fori_loop(0, half, a_step, 0)
            yas[n] = remote(
                ya_out, ya_in, link_send.at[n, 0, 0], link_recv.at[n, 0, 0], y_peer
            )
            yas[n].start()
            ybs[n].wait_recv()
            for d in range(1, width):

                def b_step(zz, _):
                    total = wide(summed, head, half + zz, right[d]) + wide(yb_in, zz, right[d])
                    xb_out[d, zz] = total.astype(kind)
                    return 0

                lax.fori_loop(0, half, b_step, 0)
                xbs[n, d] = remote(
                    xb_out.at[d],
                    xb_in.at[d],
                    link_send.at[n, 1, d],
                    link_recv.at[n, 1, d],
                    x_peers[d],
                )
                xbs[n, d].start()
        for n in range(count):
            out, half, kind = outs[n], shapes[n][0] // 2, arrays[n].dtype
            _, summed, xa_in, _, ya_in, yb_in, _, xb_in = scratch[n]
            yas[n].wait_recv()

            def a_last(zz, _):
                total = wide(summed, head, zz, x) + wide(ya_in, zz)
                for d in range(1, width):
                    total = total + wide(xa_in, d, head, zz)
                out[zz] = total.astype(kind)
                return 0

            lax.fori_loop(0, half, a_last, 0)
            for d in range(1, width):
                xbs[n, d].wait_recv()

            def b_last(zz, _):
                total = wide(summed, head, half + zz, x) + wide(yb_in, zz, x)
                for d in range(1, width):
                    total = total + wide(xb_in, d, zz)
                out[half + zz] = total.astype(kind)
                return 0

            lax.fori_loop(0, half, b_last, 0)
        for group in (starts, sends, yas, ybs, xbs):
            for copy in group.values():
                copy.wait_send()

    scratch = []
    for (slabs, *tile), values in zip(shapes, arrays):
        tile, half, kind = tuple(tile), slabs // 2, values.dtype
        scratch += [
            pltpu.VMEM((2, slabs, width) + tile, kind),
            pltpu.VMEM((2, slabs, width) + tile, kind),
            pltpu.VMEM((width, 2, half) + tile, kind),
            pltpu.VMEM((half,) + tile, kind),
            pltpu.VMEM((half,) + tile, kind),
            pltpu.VMEM((half, width) + tile, kind),
            pltpu.VMEM((width, half) + tile, kind),
            pltpu.VMEM((width, half) + tile, kind),
        ]
    return pl.pallas_call(
        body,
        out_shape=[
            jax.ShapeDtypeStruct(shape, values.dtype) for shape, values in zip(shapes, arrays)
        ],
        in_specs=[VMEM] * count,
        out_specs=[VMEM] * count,
        scratch_shapes=scratch
        + [DMA((count, 2)), DMA((count, 2)), DMA((count, 2, width)), DMA((count, 2, width))],
        compiler_params=comm_params(collective_id),
        cost_estimate=lasting(cost),
    )(
        *[
            values.reshape((2, values.shape[1], width, 2) + tuple(values.shape[3:]))
            for values in arrays
        ]
    )


def expert_dispatch(buffers, blocks, collective_id, cost=15):
    copies = blocks // NE
    count = len(buffers)

    def body(*refs):
        srcs, dsts = refs[:count], refs[count : 2 * count]
        own_sems, send_sems, recv_sems, pass_sems, land_sems = refs[2 * count :]
        head, blk = lax.axis_index("head"), lax.axis_index("blk")
        expert, piece = lax.div(blk, copies), lax.rem(blk, copies)
        ahead = [lax.rem(expert + d, NE) for d in range(NE)]
        behind = [lax.rem(expert - d + NE, NE) for d in range(NE)]
        peers = [(head, ahead[d] * copies + piece) for d in range(NE)]
        siblings = [(head, expert * copies + lax.rem(piece + k, copies)) for k in range(copies)]
        greet(peers[1:] + siblings[1:])
        sends, passes = [], []
        for n in range(count):
            own = pltpu.make_async_copy(
                srcs[n].at[expert], dsts[n].at[piece, expert], own_sems.at[n]
            )
            own.start()
            passes.append(own)
        for n in range(count):
            for d in (4, 3, 5, 2, 6, 1, 7):
                copy = remote(
                    srcs[n].at[ahead[d]],
                    dsts[n].at[piece, expert],
                    send_sems.at[n, d],
                    recv_sems.at[n, d],
                    peers[d],
                )
                copy.start()
                sends.append(copy)
        for n in range(count):
            for d in (0, 1, 7, 2, 6, 3, 5, 4):
                place = dsts[n].at[piece, behind[d]]
                if d > 0:
                    remote(
                        place, place, send_sems.at[n, d], recv_sems.at[n, d], peers[d]
                    ).wait_recv()
                for k in range(1, copies):
                    copy = remote(
                        place if d > 0 else srcs[n].at[expert],
                        place,
                        pass_sems.at[n, k, d],
                        land_sems.at[n, k, d],
                        siblings[k],
                    )
                    copy.start()
                    passes.append(copy)
        for copy in passes:
            copy.wait()
        for copy in sends:
            copy.wait_send()

    return pl.pallas_call(
        body,
        out_shape=[
            jax.ShapeDtypeStruct((copies,) + tuple(b.shape), b.dtype) for b in buffers
        ],
        in_specs=[ANY] * count,
        out_specs=[ANY] * count,
        scratch_shapes=[DMA((count,))]
        + [DMA((count, NE))] * 2
        + [DMA((count, copies, NE))] * 2,
        compiler_params=comm_params(collective_id),
        cost_estimate=lasting(cost),
    )(*buffers)


def expert_return(arrays, blocks, collective_id, cost=15):
    copies = blocks // NE
    count = len(arrays)

    def body(*refs):
        srcs, dsts = refs[:count], refs[count : 2 * count]
        sib_ins, totals = refs[2 * count : 3 * count], refs[3 * count : 4 * count]
        own_sems, send_sems, recv_sems, pass_sems, land_sems = refs[4 * count :]
        head, blk = lax.axis_index("head"), lax.axis_index("blk")
        expert, piece = lax.div(blk, copies), lax.rem(blk, copies)
        ahead = [lax.rem(expert + d, NE) for d in range(NE)]
        peers = [(head, ahead[d] * copies + piece) for d in range(NE)]
        places = [lax.rem(piece + k, copies) for k in range(copies)]
        siblings = [(head, expert * copies + places[k]) for k in range(copies)]
        greet(peers[1:] + siblings[1:])
        order = (4, 3, 5, 2, 6, 1, 7, 0)
        passes, sends = {}, []
        for n in range(count):
            for d in order:
                for k in range(1, copies):
                    copy = remote(
                        srcs[n].at[places[k], ahead[d]],
                        sib_ins[n].at[k, ahead[d]],
                        pass_sems.at[n, k, d],
                        land_sems.at[n, k, d],
                        siblings[k],
                    )
                    copy.start()
                    passes[n, k, d] = copy
        for n in range(count):
            for d in order:
                value = srcs[n][piece, ahead[d]].astype(jnp.float32)
                for k in range(1, copies):
                    passes[n, k, d].wait_recv()
                    value = value + sib_ins[n][k, ahead[d]].astype(jnp.float32)
                totals[n][ahead[d]] = value.astype(arrays[n].dtype)
                if d > 0:
                    copy = remote(
                        totals[n].at[ahead[d]],
                        dsts[n].at[expert],
                        send_sems.at[n, d],
                        recv_sems.at[n, d],
                        peers[d],
                    )
                else:
                    copy = pltpu.make_async_copy(
                        totals[n].at[expert], dsts[n].at[expert], own_sems.at[n]
                    )
                copy.start()
                sends.append(copy)
        for copy in sends:
            copy.wait()
        for copy in passes.values():
            copy.wait_send()

    return pl.pallas_call(
        body,
        out_shape=[jax.ShapeDtypeStruct(a.shape[1:], a.dtype) for a in arrays],
        in_specs=[VMEM] * count,
        out_specs=[ANY] * count,
        scratch_shapes=[pltpu.VMEM(a.shape, a.dtype) for a in arrays]
        + [pltpu.VMEM(a.shape[1:], a.dtype) for a in arrays]
        + [DMA((count,))]
        + [DMA((count, NE))] * 2
        + [DMA((count, copies, NE))] * 2,
        compiler_params=comm_params(collective_id),
        cost_estimate=lasting(cost),
    )(*arrays)


NEGATIVE = -1e30
EPSILON = 1e-06
HIGHEST = lax.Precision.HIGHEST
KEYS = 512
LANES = 128
LAST = (((1,), (1,)), ((), ()))
FIRST = (((0,), (0,)), ((), ()))


def dot32(a, b, dims=(((1,), (0,)), ((), ()))):
    return lax.dot_general(a, b, dims, preferred_element_type=jnp.float32)


def visible(key_base, query_base, keys, queries, starts):
    key_pos = key_base + lax.broadcasted_iota(jnp.int32, (keys, queries), 0)
    query_pos = query_base + lax.broadcasted_iota(jnp.int32, (keys, queries), 1)
    return (key_pos <= query_pos) & (key_pos >= starts)


def attend(bounds, queries, kv_all, starts):
    count, rows, width = queries.shape
    heads = width // LANES

    def body(bounds_ref, q_ref, kv_ref, start_ref, out_ref):
        i = pl.program_id(0)
        low, high, base = bounds_ref[i, 0], bounds_ref[i, 1], bounds_ref[i, 2]
        start_row = start_ref[0]
        q = [q_ref[0, :, h * LANES : (h + 1) * LANES] for h in range(heads)]

        def step(t, carry):
            chunk = high - t
            at = pl.multiple_of(chunk * KEYS, KEYS)
            ok = visible(chunk * KEYS, base, KEYS, rows, start_row)
            new = []
            for h in range(heads):
                top, total, acc = carry[h]
                kv = kv_ref[pl.ds(at, KEYS), h * LANES : (h + 1) * LANES]
                score = jnp.where(ok, dot32(kv, q[h], LAST), NEGATIVE)
                new_top = jnp.maximum(top, jnp.max(score, axis=0, keepdims=True))
                weight = jnp.exp(score - new_top)
                shrink = jnp.exp(top - new_top)
                total = total * shrink + jnp.sum(weight, axis=0, keepdims=True)
                acc = acc * shrink + dot32(kv, weight.astype(jnp.bfloat16), FIRST)
                new.append((new_top, total, acc))
            return tuple(new)

        empty = tuple(
            (
                jnp.full((1, rows), NEGATIVE, jnp.float32),
                jnp.zeros((1, rows), jnp.float32),
                jnp.zeros((LANES, rows), jnp.float32),
            )
            for h in range(heads)
        )
        done = lax.fori_loop(0, high - low + 1, step, empty)
        lane = lax.broadcasted_iota(jnp.int32, (LANES, rows), 0)
        for h in range(heads):
            top, total, acc = done[h]
            value = jnp.where(lane < LANES // 2, top + jnp.log(total), acc / total)
            out_ref[0, :, h * LANES : (h + 1) * LANES] = value.T

    return pl.pallas_call(
        body,
        out_shape=jax.ShapeDtypeStruct((count, rows, width), jnp.float32),
        grid_spec=pltpu.PrefetchScalarGridSpec(
            num_scalar_prefetch=1,
            grid=(count,),
            in_specs=[
                pl.BlockSpec((1, rows, width), lambda i, b: (i, 0, 0)),
                pl.BlockSpec(kv_all.shape, lambda i, b: (0, 0)),
                pl.BlockSpec((1, 1, rows), lambda i, b: (i, 0, 0)),
            ],
            out_specs=pl.BlockSpec((1, rows, width), lambda i, b: (i, 0, 0)),
        ),
        compiler_params=pltpu.CompilerParams(vmem_limit_bytes=VMEM_BYTES),
        cost_estimate=pl.CostEstimate(
            flops=2 * count * rows * kv_all.shape[0] * width,
            bytes_accessed=kv_all.size * 2,
            transcendentals=count * rows * kv_all.shape[0],
        ),
    )(bounds, queries, kv_all, starts)


def attend_back(bounds, queries, grads, kept, kv_all, starts, scale):
    count, rows, width = queries.shape
    total_keys = kv_all.shape[0]
    heads = width // LANES
    if total_keys * width * 14 > VMEM_BYTES:
        heads = 1
    wide = heads * LANES

    def body(bounds_ref, q_ref, g_ref, kept_ref, kv_ref, start_ref, dq_ref, dkv_ref, acc_ref):
        i = pl.program_id(1)
        low, high, base = bounds_ref[i, 0], bounds_ref[i, 1], bounds_ref[i, 2]
        start_row = start_ref[0]

        @pl.when(i == 0)
        def _():
            def clear(c, _):
                acc_ref[pl.ds(pl.multiple_of(c * KEYS, KEYS), KEYS), :] = jnp.zeros(
                    (KEYS, wide), jnp.float32
                )
                return 0

            lax.fori_loop(0, total_keys // KEYS, clear, 0)

        q = [q_ref[0, :, h * LANES : (h + 1) * LANES] for h in range(heads)]
        g = [g_ref[0, :, h * LANES : (h + 1) * LANES] for h in range(heads)]
        lse, delta = [], []
        for h in range(heads):
            kept_t = kept_ref[0, :, h * LANES : (h + 1) * LANES].T
            lse.append(kept_t[0:1])
            delta.append(jnp.sum(kept_t * g[h].astype(jnp.float32).T, axis=0, keepdims=True))

        def step(t, carry):
            chunk = high - t
            at = pl.multiple_of(chunk * KEYS, KEYS)
            ok = visible(chunk * KEYS, base, KEYS, rows, start_row)
            new = []
            for h in range(heads):
                lanes = slice(h * LANES, (h + 1) * LANES)
                kv = kv_ref[pl.ds(at, KEYS), lanes]
                score = jnp.where(ok, dot32(kv, q[h], LAST), NEGATIVE)
                prob = jnp.exp(score - lse[h])
                dscore = (prob * (dot32(kv, g[h], LAST) - delta[h])).astype(jnp.bfloat16)
                acc_ref[pl.ds(at, KEYS), lanes] += dot32(dscore, q[h]) + dot32(
                    prob.astype(jnp.bfloat16), g[h]
                )
                new.append(carry[h] + dot32(kv, dscore, FIRST))
            return tuple(new)

        done = lax.fori_loop(
            0,
            high - low + 1,
            step,
            tuple(jnp.zeros((LANES, rows), jnp.float32) for h in range(heads)),
        )
        lane = lax.broadcasted_iota(jnp.int32, (LANES, rows), 0)
        for h in range(heads):
            value = jnp.where(lane < LANES // 2, done[h] * scale, 0.0)
            dq_ref[0, :, h * LANES : (h + 1) * LANES] = value.T.astype(jnp.bfloat16)

        @pl.when(i == count - 1)
        def _():
            def store(c, _):
                at = pl.ds(pl.multiple_of(c * KEYS, KEYS), KEYS)
                dkv_ref[at, :] = acc_ref[at, :].astype(jnp.bfloat16)
                return 0

            lax.fori_loop(0, total_keys // KEYS, store, 0)

    block = pl.BlockSpec((1, rows, wide), lambda h, i, b: (i, 0, h))
    whole = pl.BlockSpec((total_keys, wide), lambda h, i, b: (0, h))
    return pl.pallas_call(
        body,
        out_shape=(
            jax.ShapeDtypeStruct((count, rows, width), jnp.bfloat16),
            jax.ShapeDtypeStruct(kv_all.shape, jnp.bfloat16),
        ),
        grid_spec=pltpu.PrefetchScalarGridSpec(
            num_scalar_prefetch=1,
            grid=(width // wide, count),
            in_specs=[
                block,
                block,
                block,
                whole,
                pl.BlockSpec((1, 1, rows), lambda h, i, b: (i, 0, 0)),
            ],
            out_specs=(block, whole),
            scratch_shapes=[pltpu.VMEM((total_keys, wide), jnp.float32)],
        ),
        compiler_params=pltpu.CompilerParams(vmem_limit_bytes=VMEM_BYTES),
        cost_estimate=pl.CostEstimate(
            flops=5 * count * rows * total_keys * width,
            bytes_accessed=kv_all.size * 4,
            transcendentals=count * rows * total_keys,
        ),
    )(bounds, queries, grads, kept, kv_all, starts)


def expert_forward(head, rows_in, own, other):
    count, width = rows_in.shape
    hidden, features = own[0].shape
    tile = min(hidden, 256)
    steps = hidden // tile

    def body(head_ref, x_ref, go, gx, uo, ux, do, dx, out_ref, acc_ref):
        i = pl.program_id(0)
        mine = pl.ds(pl.multiple_of(head_ref[0] * features, LANES), features)
        rest = pl.ds(pl.multiple_of((1 - head_ref[0]) * features, LANES), features)
        xo, xx = x_ref[:, mine], x_ref[:, rest]
        gate = dot32(xo, go[...], LAST) + dot32(xx, gx[...], LAST)
        up = dot32(xo, uo[...], LAST) + dot32(xx, ux[...], LAST)
        act = (jax.nn.silu(gate) * up).astype(jnp.bfloat16)

        @pl.when(i == 0)
        def _():
            acc_ref[...] = jnp.zeros_like(acc_ref)

        acc_ref[:, mine] += dot32(act, do[...])
        acc_ref[:, rest] += dot32(act, dx[...])

        @pl.when(i == steps - 1)
        def _():
            out_ref[...] = acc_ref[...].astype(jnp.bfloat16)

    whole = pl.BlockSpec((count, width), lambda i, h: (0, 0))
    piece = pl.BlockSpec((tile, features), lambda i, h: (i, 0))
    weights = [w for pair in zip(own, other) for w in pair]
    return pl.pallas_call(
        body,
        out_shape=jax.ShapeDtypeStruct((count, width), jnp.bfloat16),
        grid_spec=pltpu.PrefetchScalarGridSpec(
            num_scalar_prefetch=1,
            grid=(steps,),
            in_specs=[whole] + [piece] * 6,
            out_specs=whole,
            scratch_shapes=[pltpu.VMEM((count, width), jnp.float32)],
        ),
        compiler_params=pltpu.CompilerParams(vmem_limit_bytes=VMEM_BYTES),
        cost_estimate=pl.CostEstimate(
            flops=6 * count * width * hidden,
            bytes_accessed=6 * hidden * features * 2 + 4 * count * width,
            transcendentals=count * hidden,
        ),
    )(head, rows_in, *weights)


def expert_backward(head, rows_in, grads_in, own, other, with_parts):
    count, width = rows_in.shape
    hidden, features = own[0].shape
    tile = min(hidden, 256)
    steps = hidden // tile
    sums = 2 if with_parts else 1

    def body(head_ref, x_ref, z_ref, go, gx, uo, ux, do, dx, *outs):
        keeps, sends, totals, accs = outs[:3], outs[3:6], outs[6 : 6 + sums], outs[6 + sums :]
        i = pl.program_id(0)
        mine = pl.ds(pl.multiple_of(head_ref[0] * features, LANES), features)
        rest = pl.ds(pl.multiple_of((1 - head_ref[0]) * features, LANES), features)
        xo, xx = x_ref[:, mine], x_ref[:, rest]
        zo, zx = z_ref[:, mine], z_ref[:, rest]
        gate = dot32(xo, go[...], LAST) + dot32(xx, gx[...], LAST)
        up = dot32(xo, uo[...], LAST) + dot32(xx, ux[...], LAST)
        dact = dot32(zo, do[...], LAST) + dot32(zx, dx[...], LAST)
        sigmoid = jax.nn.sigmoid(gate)
        silu = gate * sigmoid
        act = (silu * up).astype(jnp.bfloat16)
        dgate = (dact * up * sigmoid * (1.0 + gate * (1.0 - sigmoid))).astype(jnp.bfloat16)
        dup = (dact * silu).astype(jnp.bfloat16)

        @pl.when(i == 0)
        def _():
            for acc in accs:
                acc[...] = jnp.zeros_like(acc)

        accs[0][:, mine] += dot32(dgate, go[...]) + dot32(dup, uo[...])
        accs[0][:, rest] += dot32(dgate, gx[...]) + dot32(dup, ux[...])
        if with_parts:
            accs[1][:, mine] += dot32(act, do[...])
            accs[1][:, rest] += dot32(act, dx[...])
        for n, (left, mine_in, rest_in) in enumerate(
            ((dgate, xo, xx), (dup, xo, xx), (act, zo, zx))
        ):
            keeps[n][...] = dot32(left, mine_in, FIRST)
            sends[n][...] = dot32(left, rest_in, FIRST).astype(jnp.bfloat16)

        @pl.when(i == steps - 1)
        def _():
            for total, acc in zip(totals, accs):
                total[...] = acc[...].astype(jnp.bfloat16)

    whole = pl.BlockSpec((count, width), lambda i, h: (0, 0))
    piece = pl.BlockSpec((tile, features), lambda i, h: (i, 0))
    weights = [w for pair in zip(own, other) for w in pair]
    return pl.pallas_call(
        body,
        out_shape=[jax.ShapeDtypeStruct((hidden, features), jnp.float32)] * 3
        + [jax.ShapeDtypeStruct((hidden, features), jnp.bfloat16)] * 3
        + [jax.ShapeDtypeStruct((count, width), jnp.bfloat16)] * sums,
        grid_spec=pltpu.PrefetchScalarGridSpec(
            num_scalar_prefetch=1,
            grid=(steps,),
            in_specs=[whole, whole] + [piece] * 6,
            out_specs=[piece] * 6 + [whole] * sums,
            scratch_shapes=[pltpu.VMEM((count, width), jnp.float32)] * sums,
        ),
        compiler_params=pltpu.CompilerParams(vmem_limit_bytes=VMEM_BYTES),
        cost_estimate=pl.CostEstimate(
            flops=22 * count * width * hidden,
            bytes_accessed=15 * hidden * features * 2 + 8 * count * width,
            transcendentals=count * hidden,
        ),
    )(head, rows_in, grads_in, *weights)


def pack_grads(column, dq, dkv, attn, dy, small, compact):
    width = column.shape[1]
    kv_cols, own_out = dkv.shape[1], attn.shape[1]
    small_cols = small.shape[1]
    rows, cols = own_out // 2, width // 2

    def body(column_ref, dq_ref, dkv_ref, attn_ref, dy_ref, small_ref, compact_ref, one, two):
        one[:, :kv_cols] = dot32(column_ref[...], dkv_ref[...], FIRST).astype(jnp.bfloat16)
        narrow = dot32(dq_ref[...], compact_ref[...]).astype(jnp.bfloat16)
        one[:, kv_cols:] = (
            dot32(column_ref[...], narrow, FIRST) + small_ref[...]
        ).astype(jnp.bfloat16)
        out = dot32(attn_ref[...], dy_ref[...], FIRST).astype(jnp.bfloat16)
        for a in range(2):
            for b in range(2):
                two[a, b] = out[a * rows : (a + 1) * rows, b * cols : (b + 1) * cols]

    return pl.pallas_call(
        body,
        out_shape=[
            jax.ShapeDtypeStruct((width, kv_cols + small_cols), jnp.bfloat16),
            jax.ShapeDtypeStruct((2, 2, rows, cols), jnp.bfloat16),
        ],
        compiler_params=pltpu.CompilerParams(vmem_limit_bytes=VMEM_BYTES),
        cost_estimate=lasting(4),
    )(column, dq, dkv, attn, dy, small, compact)


def norm_forward(values, gain_vec):
    row_scale = lax.rsqrt(jnp.mean(values * values, axis=-1, keepdims=True) + EPSILON)
    normed = values * row_scale
    return normed * gain_vec, normed, row_scale


def norm_backward(upstream, normed, row_scale, gain_vec):
    through = upstream * gain_vec
    gain_grad = jnp.sum(upstream * normed, axis=0)
    inner_mean = jnp.mean(through * normed, axis=-1, keepdims=True)
    return row_scale * (through - normed * inner_mean), gain_grad


def slot_index(route_ids):
    token_rows = route_ids.shape[0]
    expert_ids = jnp.arange(NE, dtype=jnp.int32)
    matches = (
        (route_ids[:, :, None] == expert_ids[None, None, :])
        .astype(jnp.int32)
        .reshape((token_rows * 2, NE))
    )
    before = jnp.cumsum(matches, axis=0) - 1
    slot_pos = jnp.sum(matches * before, axis=1).reshape((token_rows, 2))
    return jnp.where(route_ids < NE, route_ids * CAP + slot_pos, NE * CAP)


def per_device(
    tokens,
    segments,
    routes,
    gates,
    w_qkv,
    w_out,
    gain_attn,
    gain_moe,
    const_gate,
    const_vec,
    w_gate,
    w_up,
    w_down,
    cotangent,
):
    blocks = lax.axis_size("blk")
    head_index, blk_index = lax.axis_index("head"), lax.axis_index("blk")
    span = blocks // COLUMNS
    plane, rest = lax.div(blk_index, span), lax.rem(blk_index, span)
    shards = 2 * blocks
    token_rows, width = tokens.shape
    shard_rows = width // shards
    head_dim = width // HEADS
    heads = HEADS // COLUMNS
    scale = head_dim ** (-0.5)
    half_length = blocks * token_rows
    positions = 2 * half_length
    features = w_gate.shape[2]
    hidden_rows = w_gate.shape[1]
    copies = blocks // NE
    own_out = heads * head_dim

    swap = [(0, 1), (1, 0)]
    head_scalar = head_index.reshape((1,)).astype(jnp.int32)

    seg_own = lax.dynamic_index_in_dim(segments, head_index, 0, keepdims=False)
    seg_parts = jnp.concatenate([lax.rem(seg_own, 128), lax.div(seg_own, 128)]).astype(
        jnp.bfloat16
    )
    seg_columns = -(-seg_parts.shape[0] // shard_rows)
    seg_parts = jnp.pad(seg_parts, (0, seg_columns * shard_rows - seg_parts.shape[0]))
    seg_parts = seg_parts.reshape((shard_rows, seg_columns))
    packs = []
    for layer in range(LAYERS):
        split = w_qkv[layer].reshape((shard_rows, 3, COLUMNS, heads, head_dim))
        kv_part = jnp.concatenate([split[:, 1], split[:, 2]], axis=3)
        kv_part = kv_part.transpose((1, 0, 2, 3)).reshape((COLUMNS, shard_rows, heads * LANES))
        query_part = split[:, 0].transpose((1, 0, 2, 3)).reshape((COLUMNS, shard_rows, own_out))
        side = [
            gain_attn[layer][:, None],
            gain_moe[layer][:, None],
            const_gate[layer],
            const_vec[layer],
            seg_parts,
        ]
        filled = own_out + 8 + seg_columns
        side.append(jnp.zeros((shard_rows, -filled % LANES), jnp.bfloat16))
        side = jnp.concatenate(side, axis=1)
        packs.append(
            jnp.concatenate(
                [
                    kv_part,
                    jnp.broadcast_to(w_out[layer][None], (COLUMNS, shard_rows, width)),
                    query_part,
                    jnp.broadcast_to(side[None], (COLUMNS,) + side.shape),
                ],
                axis=2,
            )
        )
    weights, column_tokens = start_gather(packs, tokens, blocks, 1)
    weights = [pack.reshape((shards, shard_rows, -1)) for pack in weights]
    out_at = heads * LANES
    query_at = out_at + width
    small_at = query_at + own_out

    place = jnp.arange(own_out, dtype=jnp.int32)
    place = lax.div(place, head_dim) * LANES + lax.rem(place, head_dim)
    wide_place = jnp.arange(heads * LANES, dtype=jnp.int32)
    to_low = (place[:, None] == wide_place[None, :]).astype(jnp.bfloat16)
    to_high = (place[:, None] + head_dim == wide_place[None, :]).astype(jnp.bfloat16)
    small_cols = own_out + LANES - own_out % LANES
    compact = jnp.pad(to_low.T, ((0, 0), (0, small_cols - own_out)))

    def send_experts(layer, after):
        held = lax.optimization_barrier(
            tuple(w[layer] for w in (w_gate, w_up, w_down)) + (after,)
        )[:3]
        return held, [lax.ppermute(w, "head", swap) for w in held]

    own_experts, other_experts = [None] * LAYERS, [None] * LAYERS

    seg_all = weights[0][:, :, small_at + 8 : small_at + 8 + seg_columns]
    seg_all = seg_all.reshape((shards, -1))[:, : 2 * token_rows].astype(jnp.int32)
    seg_all = seg_all[:, :token_rows] + 128 * seg_all[:, token_rows:]
    seg_query = lax.dynamic_index_in_dim(
        seg_all.reshape((2, COLUMNS, span, token_rows)), head_index, 0, keepdims=False
    )
    seg_query = lax.dynamic_index_in_dim(seg_query, rest, 1, keepdims=False)
    starts = jnp.sum(
        (seg_all.reshape((1, 1, -1)) < seg_query[:, :, None]).astype(jnp.int32), axis=2
    )
    bases = (
        head_index * half_length
        + (jnp.arange(COLUMNS, dtype=jnp.int32) * span + rest) * token_rows
    )
    bounds = jnp.stack(
        [lax.div(starts[:, 0], KEYS), lax.div(bases + token_rows - 1, KEYS), bases], axis=1
    )
    starts = starts[:, None, :]

    layers = []
    for pack in weights:
        rows = pack.reshape((width, -1))
        kv_w = rows[:, :out_at]
        out_w = rows[:, out_at:query_at]
        query_w = dot32(rows[:, query_at:small_at], to_low).astype(jnp.bfloat16)
        small_w = rows[:, small_at : small_at + 8]
        out_rows = lax.dynamic_slice_in_dim(out_w, plane * own_out, own_out, 0)
        out_rows = dot32(to_high, out_rows, FIRST).astype(jnp.bfloat16)
        layers.append((query_w, kv_w, out_w, small_w, out_rows))

    def expert_buffers(layer):
        route_ids, gate_vals = routes[layer], gates[layer]
        slots = slot_index(route_ids)
        named = slots[:, :, None] == jnp.arange(NE * CAP, dtype=jnp.int32)[None, None, :]
        picks = jnp.any(named, axis=1)
        pick_gates = jnp.sum(jnp.where(named, gate_vals[:, :, None], 0.0), axis=1)
        return picks, pick_gates

    def gated_rows(picks, pick_gates, upstream):
        picked = jnp.dot(picks.astype(jnp.float32).T, upstream, precision=HIGHEST)
        dz = (jnp.sum(pick_gates, axis=0)[:, None] * picked).astype(jnp.bfloat16)
        return dz.reshape((NE, CAP, width))

    upstream = cotangent.astype(jnp.float32)
    residual = tokens.astype(jnp.float32)
    kept = []
    for layer in range(LAYERS):
        query_w, kv_w, out_w, small_w, out_rows = layers[layer]
        attn_gain = small_w[:, 0].astype(jnp.float32)
        moe_gain = small_w[:, 1].astype(jnp.float32)
        gate_w = small_w[:, 2:6]
        vectors = small_w[:, 6:8].astype(jnp.float32).T
        normed_in, unit_in, scale_in = norm_forward(residual, attn_gain)
        if layer == 0:
            column = norm_forward(column_tokens.astype(jnp.float32), attn_gain)[0]
            column = column.astype(jnp.bfloat16)
        else:
            (column,) = column_exchange([normed_in.astype(jnp.bfloat16)], [True], blocks, 3)
        column = column.reshape((COLUMNS * token_rows, width))
        queries = (
            dot32(column, query_w).astype(jnp.bfloat16).astype(jnp.float32) * scale
        ).astype(jnp.bfloat16)
        queries = queries.reshape((COLUMNS, token_rows, heads * LANES))
        kv_own = dot32(column, kv_w).astype(jnp.bfloat16)
        (kv_all,) = plane_gather(
            [kv_own.reshape((COLUMNS, token_rows, heads * LANES))], blocks, 4
        )
        kv_all = kv_all.reshape((positions, heads * LANES))
        if layer == 0:
            own_experts[0], other_experts[0] = send_experts(0, kv_all)
        attended = attend(bounds, queries, kv_all, starts)
        attn_col = dot32(
            attended.astype(jnp.bfloat16).reshape((-1, heads * LANES)), to_high, LAST
        ).astype(jnp.bfloat16)
        (attn,) = column_exchange(
            [attn_col.reshape((COLUMNS, token_rows, own_out))], [False], blocks, 5, 9
        )
        attn = attn.transpose((1, 0, 2)).reshape((token_rows, width))
        middle = residual + dot32(attn, out_w)
        normed_mid, unit_mid, scale_mid = norm_forward(middle, moe_gain)
        moe_in = normed_mid.astype(jnp.bfloat16)
        moe_float = moe_in.astype(jnp.float32)
        route_ids, gate_vals = routes[layer], gates[layer]
        picks, pick_gates = expert_buffers(layer)
        sent = dot32(picks.astype(jnp.bfloat16), moe_in, FIRST).astype(jnp.bfloat16)
        sent = [sent.reshape((NE, CAP, width))]
        last = layer + 1 == LAYERS
        if last:
            sent.append(gated_rows(picks, pick_gates, upstream))
        arrived = expert_dispatch(sent, blocks, 7 if last else 6, 24 if last else 15)
        flat_in, *dz_in = [rows.reshape((-1, width)) for rows in arrived]
        if last:
            *wgrads, dparts, parts = expert_backward(
                head_scalar, flat_in, dz_in[0], own_experts[layer], other_experts[layer], True
            )
            back, dback = expert_return(
                [rows.reshape((copies, NE, CAP, width)) for rows in (parts, dparts)],
                blocks,
                9,
                24,
            )
            last_grads = wgrads, dback
        else:
            own_experts[layer + 1], other_experts[layer + 1] = send_experts(layer + 1, flat_in)
            parts = expert_forward(
                head_scalar, flat_in, own_experts[layer], other_experts[layer]
            )
            (back,) = expert_return([parts.reshape((copies, NE, CAP, width))], blocks, 8)
        back = back.reshape((NE * CAP, width)).astype(jnp.float32)
        ffn_out = jnp.dot(pick_gates, back, precision=HIGHEST)
        copy_weight = jnp.sum(jnp.where(route_ids == NE + 1, gate_vals, 0.0), axis=1)
        const_weight = jnp.stack(
            [
                jnp.sum(jnp.where(route_ids == NE + 2 + c, gate_vals, 0.0), axis=1)
                for c in range(2)
            ],
            axis=1,
        )
        mixing = jax.nn.softmax(dot32(moe_in, gate_w).reshape((token_rows, 2, 2)), axis=-1)
        const_out = jnp.sum(
            const_weight[:, :, None]
            * (mixing[:, :, 0:1] * moe_float[:, None, :] + mixing[:, :, 1:2] * vectors[None]),
            axis=1,
        )
        residual = middle + ffn_out + copy_weight[:, None] * moe_float + const_out
        kept.append(
            (
                unit_in,
                scale_in,
                column,
                queries,
                kv_all,
                attended,
                attn_col,
                unit_mid,
                scale_mid,
                moe_float,
                picks,
                pick_gates,
                flat_in,
                copy_weight,
                const_weight,
                mixing,
            )
        )
    output = residual

    shared_grads = [None] * LAYERS
    expert_grads = [None] * LAYERS
    for layer in reversed(range(LAYERS)):
        query_w, kv_w, out_w, small_w, out_rows = layers[layer]
        attn_gain = small_w[:, 0].astype(jnp.float32)
        moe_gain = small_w[:, 1].astype(jnp.float32)
        gate_w = small_w[:, 2:6].astype(jnp.float32)
        vectors = small_w[:, 6:8].astype(jnp.float32).T
        (
            unit_in,
            scale_in,
            column,
            queries,
            kv_all,
            attended,
            attn_col,
            unit_mid,
            scale_mid,
            moe_float,
            picks,
            pick_gates,
            flat_in,
            copy_weight,
            const_weight,
            mixing,
        ) = kept[layer]
        mix_grad = const_weight[:, :, None] * upstream[:, None, :]
        alpha_grad = jnp.stack(
            [
                jnp.sum(mix_grad * moe_float[:, None, :], axis=-1),
                jnp.sum(mix_grad * vectors[None], axis=-1),
            ],
            axis=-1,
        )
        logit_grad = (
            mixing * (alpha_grad - jnp.sum(mixing * alpha_grad, axis=-1, keepdims=True))
        ).reshape((token_rows, 4))
        hn_grad = (
            copy_weight[:, None] * upstream
            + jnp.sum(mixing[:, :, 0:1] * mix_grad, axis=1)
            + jnp.dot(logit_grad, gate_w.T, precision=HIGHEST)
        )
        cgate_grad = jnp.dot(moe_float.T, logit_grad, precision=HIGHEST)
        cvec_grad = jnp.sum(mixing[:, :, 1:2] * mix_grad, axis=0).T

        if layer + 1 == LAYERS:
            wgrads, dback = last_grads
        else:
            (dz_in,) = expert_dispatch([gated_rows(picks, pick_gates, upstream)], blocks, 6)
            *wgrads, dparts = expert_backward(
                head_scalar,
                flat_in,
                dz_in.reshape((-1, width)),
                own_experts[layer],
                other_experts[layer],
                False,
            )
            (dback,) = expert_return([dparts.reshape((copies, NE, CAP, width))], blocks, 8)
        got = [lax.ppermute(away, "head", swap) for away in wgrads[3:]]
        dback, got[0] = lax.optimization_barrier((dback, got[0]))
        hn_grad = hn_grad + dot32(
            picks.astype(jnp.bfloat16), dback.reshape((NE * CAP, width))
        )
        middle_grad, moe_gain_grad = norm_backward(hn_grad, unit_mid, scale_mid, moe_gain)
        middle_grad = middle_grad + upstream
        (dy,) = column_exchange([middle_grad.astype(jnp.bfloat16)], [True], blocks, 3)
        dy, got[1] = lax.optimization_barrier((dy, got[1]))
        dy = dy.reshape((COLUMNS * token_rows, width))
        dattn = dot32(dy, out_rows, LAST).astype(jnp.bfloat16)
        dattn = dattn.reshape((COLUMNS, token_rows, heads * LANES))
        dq, dkv_all = attend_back(bounds, queries, dattn, attended, kv_all, starts, scale)
        dkv_all, got[2] = lax.optimization_barrier((dkv_all, got[2]))
        (dkv,) = plane_reduce(
            [dkv_all.reshape((2, COLUMNS, span, token_rows, heads * LANES))], blocks, 10
        )
        dq = dq.reshape((-1, heads * LANES))
        dkv = dkv.reshape((-1, heads * LANES))
        dxn = (dot32(dq, query_w, LAST) + dot32(dkv, kv_w, LAST)).astype(jnp.bfloat16)
        (dxn,) = column_exchange(
            [dxn.reshape((COLUMNS, token_rows, width))], [False], blocks, 11
        )
        dxn = jnp.sum(dxn.astype(jnp.float32), axis=0)
        lead_grad, attn_gain_grad = norm_backward(dxn, unit_in, scale_in, attn_gain)
        upstream = middle_grad + lead_grad
        expert_grads[layer] = [
            own + other.astype(jnp.float32) for own, other in zip(wgrads[:3], got)
        ]

        small_part = jnp.concatenate(
            [
                jnp.zeros((width, own_out), jnp.float32),
                attn_gain_grad[:, None],
                moe_gain_grad[:, None],
                cgate_grad,
                cvec_grad,
                jnp.zeros((width, small_cols - own_out - 8), jnp.float32),
            ],
            axis=1,
        )
        qkv_part, out_part = pack_grads(column, dq, dkv, attn_col, dy, small_part, compact)
        shared_grads[layer] = [
            qkv_part.reshape((2, COLUMNS, span, shard_rows, -1)),
            out_part.reshape((2, 2, span, shard_rows, width // 2)),
        ]

    packed = [part for layer in range(LAYERS) for part in shared_grads[layer]]
    reduced = plane_reduce(packed, blocks, 12, 20)
    from_planes = column_exchange(reduced[::2], [False] * LAYERS, blocks, 13, 10)
    from_planes = jnp.stack(from_planes, axis=1).astype(jnp.float32)
    kv_out = from_planes[..., : heads * LANES].reshape(
        (COLUMNS, LAYERS, shard_rows, heads, 2, head_dim)
    )
    query_out = from_planes[..., heads * LANES : heads * LANES + own_out].reshape(
        (COLUMNS, LAYERS, shard_rows, heads, 1, head_dim)
    )
    qkv_out = jnp.concatenate([query_out, kv_out], axis=4)
    qkv_out = qkv_out.transpose((1, 2, 4, 0, 3, 5)).reshape((LAYERS, shard_rows, 3 * width))
    small_out = heads * LANES + own_out
    small_out = jnp.sum(from_planes[..., small_out : small_out + 8], axis=0)
    out_grads = jnp.stack(reduced[1::2]).transpose((0, 2, 1, 3))
    out_grads = out_grads.reshape((LAYERS, shard_rows, width))
    owners = [
        (y * blocks + z * span + r, (z * 2 + y) * span + r)
        for y in range(2)
        for z in range(COLUMNS)
        for r in range(span)
    ]
    out_grads = lax.ppermute(out_grads, ("head", "blk"), owners).astype(jnp.float32)
    stacked = [jnp.stack(group) for group in zip(*expert_grads)]
    return (
        output,
        upstream,
        qkv_out,
        out_grads,
        small_out[..., 0],
        small_out[..., 1],
        small_out[..., 2:6],
        small_out[..., 6:8],
        stacked[0],
        stacked[1],
        stacked[2],
    )


def solution(mesh):
    tokens = P(("head", "blk"), None)
    by_layer = P(None, ("head", "blk"), None)
    gains = P(None, ("head", "blk"))
    experts = P(None, "blk", "head")
    return jax.shard_map(
        per_device,
        mesh=mesh,
        in_specs=(
            tokens,
            P(None, "blk"),
            by_layer,
            by_layer,
            by_layer,
            by_layer,
            gains,
            gains,
            by_layer,
            by_layer,
            experts,
            experts,
            experts,
            tokens,
        ),
        out_specs=(
            tokens,
            tokens,
            by_layer,
            by_layer,
            gains,
            gains,
            by_layer,
            by_layer,
            experts,
            experts,
            experts,
        ),
        check_vma=False,
    )
```

time: 823 us -> 681 us (0.83)
  Pallas kernels: 569 us -> 501 us
  local copies, waits for them, and re-layouts: 111 us -> 70.1 us
  waiting for transfers between devices: 38 us -> 0.03 us
    ppermute x6, waiting for transfers between devices: 38 us -> 0.02 us  [per_device(): got = [lax.ppermute(away, 'head', swap) for away in wgrads[3:]]]
    pallas_call x9 -> x8, Pallas kernels: 156 us -> 121 us  [column_exchange(): pl.pallas_call(body, out_shape=[jax.ShapeDtypeStruct((COLUMNS,) + slab, v...]
    pallas_call x14, Pallas kernels: 275 us -> 247 us  [the longest x3 56 us: expert_return(): pl.pallas_call(body, out_shape=[jax.ShapeDtypeStruct(a.shape[1:], a.dtype...]
    convert_element_type x8 -> x0, local copies, waits for them, and re-layouts: 13.4 us -> none  [the longest x2 6.35 us: per_device(): qkv_part.astype(jnp.bfloat16)]
    concatenate x14 -> x6, local copies, waits for them, and re-layouts: 18.2 us -> 5.48 us  [the longest x2 4.38 us: per_device(): jnp.concatenate([jnp.zeros((width, own_out), jnp.float32), attn_gain_grad...]
    dot_general x24 -> x22, matrix products: 23.2 us -> 22.7 us  [dot32(): return lax.dot_general(a, b, dims, preferred_element_type=jnp.float32)]
  transfers between devices with their start and end apart: 13 -> 13, of which waited for: 3 -> 0; matrix products, arithmetic and copies ran while one was open for 15% -> 14% of each run, Pallas kernels for 28% -> 42%
where the time goes in v3:
time: 681 us; the launch traced here: 669 us
  Pallas kernels  501 us (74%)
  local copies, waits for them, and re-layouts  70.1 us (10%)
  other arithmetic  48.9 us (7%)
  matrix products  31.3 us (5%)
  starting transfers between devices  15.2 us (2%)
    pallas_call x8, Pallas kernels, column_exchange(): pl.pallas_call(body, out_shape=[jax.ShapeDtypeStruct((COLUMNS,) + slab, v...  121 us
    pallas_call x3, Pallas kernels, expert_return(): pl.pallas_call(body, out_shape=[jax.ShapeDtypeStruct(a.shape[1:], a.dtype...  56 us
    pallas_call x3, Pallas kernels, expert_dispatch(): pl.pallas_call(body, out_shape=[jax.ShapeDtypeStruct((copies,) + tuple(b....  54 us
    pallas_call x3, Pallas kernels, plane_reduce(): pl.pallas_call(body, out_shape=[jax.ShapeDtypeStruct(shape, values.dtype)...  53.6 us
    pallas_call x2, Pallas kernels, attend_back(): pl.pallas_call(body, out_shape=(jax.ShapeDtypeStruct((count, rows, width)...  47.3 us
    pallas_call x1, Pallas kernels, start_gather(): pl.pallas_call(body, out_shape=plane_shapes(packs, blocks) + [jax.ShapeDt...  45.6 us
    pallas_call x2, Pallas kernels, expert_backward(): pl.pallas_call(body, out_shape=[jax.ShapeDtypeStruct((hidden, features),...  42.5 us
    pallas_call x2, Pallas kernels, plane_gather(): pl.pallas_call(body, out_shape=plane_shapes(arrays, blocks), in_specs=[AN...  35.4 us
  transfers between devices with their start and end apart: 13, of which 0 were waited for; matrix products, arithmetic and copies ran while one was open for 14% of the time, Pallas kernels for 42%

profile of v3, /device:TPU:12, one launch (start us, length us, event | category | flops | bytes accessed | tf_op | source)
XLA Modules:
  0.0 669.4 jit_solution(14117359474017516229)
XLA Ops:
  9.7 45.6 %shard_map.221 = (bf16[2,4,4,24,1408]{4,3,2,1,0:T(8,128)(2,1)S(1)}, bf16[2,4,4,24,1408]{4,3,2,1,0:T(8,128)(2,1)}, bf16[4,24,1408]{2,1,0:T(8,128)(2,1)}, bf16[4,2...) custom-call(bf16[4,24,1408]{2,1,0:T(8,128)(2,1)S(1)} %copy-done.19, bf16[4,24,1408]{2,1,0:T(8,128)(2,1)S(1)} %concatenate.37.refs_1_, ...), custom_call_target="tpu_custom_call" | custom-call | bytes 122500000 | tf_op jit(solution)/shard_map/pallas_call | solution.py:279
  58.6 17.5 %shard_map.222 = bf16[2,4,4,128,384]{4,3,2,1,0:T(8,128)(2,1)S(1)} custom-call(bf16[4,128,384]{2,1,0:T(8,128)(2,1)S(1)} %bitcast.334), custom_call_target="tpu_custom_call" | custom-call | bytes 56000000 | tf_op jit(solution)/shard_map/pallas_call | solution.py:239
  93.0 17.5 %shard_map.223.kept_ref = f32[4,128,384]{2,1,0:T(8,128)S(1)} custom-call(s32[4,3]{1,0:T(4,128)S(1)} %pad_add_fusion.bounds_ref, bf16[4,128,384]{2,1,0:T(8,128)(2,1)S(1)} %bitcast.346, bf16[4096,384]{1,0:T(8,128)(2,1)S(1)} %bitcast.291, s32[4,1,128]{2,1,0:T(1,128)S(1)} %bitcast.340), custom_call_target="tpu_custom_call" | custom-call | flops 1610612736 | bytes 3145728 | tf_op jit(solution)/shard_map/pallas_call | solution.py:668
  111.0 6.5 shard_map.224
  121.5 13.8 %shard_map.225 = bf16[2,8,40,768]{3,2,1,0:T(8,128)(2,1)S(1)} custom-call(bf16[8,40,768]{2,1,0:T(8,128)(2,1)S(1)} %bitcast.310), custom_call_target="tpu_custom_call" | custom-call | bytes 52500000 | tf_op jit(solution)/shard_map/pallas_call | solution.py:522
  164.1 7.9 %shard_map.226 = bf16[640,768]{1,0:T(8,128)(2,1)S(1)} custom-call(s32[1]{0:T(128)} %bitcast.40.head_ref, bf16[640,768]{1,0:T(8,128)(2,1)} %bitcast.319, bf16[1024,384]{1,0:T(8,128)(2,1)} %get-tuple-element.67.go, bf16[1024,384]{1,0:T(8,128)(2,1)} %collective-permute-done.gx, bf16[1024,384]{1,0:T(8,128)(2,1)} %get-tuple-element.68.uo, ...), custom_call_target="tpu_custom_call" | custom-call | flops 3019898880 | bytes 6684672 | tf_op jit(solution)/shard_map/pallas_call | solution.py:817
  172.1 15.0 %shard_map.227 = bf16[8,40,768]{2,1,0:T(8,128)(2,1)S(1)} custom-call(bf16[2,8,40,768]{3,2,1,0:T(8,128)(2,1)S(1)} %bitcast.327), custom_call_target="tpu_custom_call" | custom-call | bytes 52500000 | tf_op jit(solution)/shard_map/pallas_call | solution.py:592
  187.9 21.0 %shard_map.228 = bf16[4,128,768]{2,1,0:T(8,128)(2,1)S(1)} custom-call(bf16[128,768]{1,0:T(8,128)(2,1)S(1)} %multiply_convert_fusion.1.refs_0_), custom_call_target="tpu_custom_call" | custom-call | bytes 56000000 | tf_op jit(solution)/shard_map/pallas_call | solution.py:104
  210.9 17.9 %shard_map.229 = bf16[2,4,4,128,384]{4,3,2,1,0:T(8,128)(2,1)S(1)} custom-call(bf16[4,128,384]{2,1,0:T(8,128)(2,1)S(1)} %bitcast.335), custom_call_target="tpu_custom_call" | custom-call | bytes 56000000 | tf_op jit(solution)/shard_map/pallas_call | solution.py:239
  229.5 17.5 %shard_map.230.kept_ref = f32[4,128,384]{2,1,0:T(8,128)S(1)} custom-call(s32[4,3]{1,0:T(4,128)S(1)} %pad_add_fusion.bounds_ref, bf16[4,128,384]{2,1,0:T(8,128)(2,1)S(1)} %bitcast.348, bf16[4096,384]{1,0:T(8,128)(2,1)S(1)} %bitcast.292, s32[4,1,128]{2,1,0:T(1,128)S(1)} %bitcast.341), custom_call_target="tpu_custom_call" | custom-call | flops 1610612736 | bytes 3145728 | tf_op jit(solution)/shard_map/pallas_call | solution.py:668
  247.4 6.5 shard_map.231
  257.9 24.9 %shard_map.232 = (bf16[2,8,40,768]{3,2,1,0:T(8,128)(2,1)S(1)}, bf16[2,8,40,768]{3,2,1,0:T(8,128)(2,1)S(1)}) custom-call(bf16[8,40,768]{2,1,0:T(8,128)(2,1)S(1)} %bitcast.309, bf16[8,40,768]{2,1,0:T(8,128)(2,1)S(1)} %bitcast.307), custom_call_target="tpu_custom_call" | custom-call | bytes 84000000 | tf_op jit(solution)/shard_map/pallas_call | solution.py:522
  286.5 22.1 %shard_map.233 = (f32[1024,384]{1,0:T(8,128)}, f32[1024,384]{1,0:T(8,128)}, f32[1024,384]{1,0:T(8,128)}, bf16[1024,384]{1,0:T(8,128)(2,1)}, bf16[1024,384]{1,0:T...) custom-call(s32[1]{0:T(128)} %bitcast.40.head_ref, ...), custom_call_target="tpu_custom_call" | custom-call | flops 11072962560 | bytes 15728640 | tf_op jit(solution)/shard_map/pallas_call | solution.py:883
  319.3 26.0 %shard_map.234 = (bf16[8,40,768]{2,1,0:T(8,128)(2,1)S(1)}, bf16[8,40,768]{2,1,0:T(8,128)(2,1)S(1)}) custom-call(bf16[2,8,40,768]{3,2,1,0:T(8,128)(2,1)S(1)} %bitcast.323, bf16[2,8,40,768]{3,2,1,0:T(8,128)(2,1)S(1)} %bitcast.322), custom_call_target="tpu_custom_call" | custom-call | bytes 84000000 | tf_op jit(solution)/shard_map/pallas_call | solution.py:592
  354.9 20.4 %shard_map.235 = bf16[4,128,768]{2,1,0:T(8,128)(2,1)S(1)} custom-call(bf16[128,768]{1,0:T(8,128)(2,1)S(1)} %fusion.89.refs_0_), custom_call_target="tpu_custom_call" | custom-call | bytes 56000000 | tf_op jit(solution)/shard_map/pallas_call | solution.py:104
  375.4 2.9 fusion.6
  380.4 23.7 %shard_map.236 = (bf16[4,128,384]{2,1,0:T(8,128)(2,1)S(1)}, bf16[4096,384]{1,0:T(8,128)(2,1)S(1)}) custom-call(s32[4,3]{1,0:T(4,128)S(1)} %pad_add_fusion.bounds_ref, bf16[4,128,384]{2,1,0:T(8,128)(2,1)S(1)} %bitcast.349, bf16[4,128,384]{2,1,0:T(8,128)(2,1)S(1)} %bitcast.351, f32[4,128,384]{2,1,0:T(8,128)S(1)} %copy-done.34, bf16[4096,384]{1,0:T(8,128)(2,1)} %bitcast.293, ...), custom_call_target="tpu_custom_call" | custom-call | flops 4026531840 | bytes 6291456 | tf_op jit(solution)/shard_map/pallas_call | solution.py:760
  404.1 18.8 %shard_map.237 = bf16[4,128,384]{2,1,0:T(8,128)(2,1)S(1)} custom-call(bf16[2,4,2,2,128,384]{5,4,3,2,1,0:T(8,128)(2,1)S(1)} %bitcast.295), custom_call_target="tpu_custom_call" | custom-call | bytes 87500000 | tf_op jit(solution)/shard_map/pallas_call | solution.py:449
  425.2 18.7 %shard_map.238 = bf16[4,128,768]{2,1,0:T(8,128)(2,1)S(1)} custom-call(bf16[4,128,768]{2,1,0:T(8,128)(2,1)S(1)} %bitcast.303), custom_call_target="tpu_custom_call" | custom-call | bytes 56000000 | tf_op jit(solution)/shard_map/pallas_call | solution.py:104
  446.1 15.3 %shard_map.239 = bf16[2,8,40,768]{3,2,1,0:T(8,128)(2,1)S(1)} custom-call(bf16[8,40,768]{2,1,0:T(8,128)(2,1)S(1)} %bitcast.306), custom_call_target="tpu_custom_call" | custom-call | bytes 52500000 | tf_op jit(solution)/shard_map/pallas_call | solution.py:522
  462.3 20.4 %shard_map.240 = (f32[1024,384]{1,0:T(8,128)}, f32[1024,384]{1,0:T(8,128)}, f32[1024,384]{1,0:T(8,128)}, bf16[1024,384]{1,0:T(8,128)(2,1)}, bf16[1024,384]{1,0:T...) custom-call(s32[1]{0:T(128)} %bitcast.40.head_ref, bf16[640,768]{1,0:T(8,128)(2,1)} %bitcast.320, ...), custom_call_target="tpu_custom_call" | custom-call | flops 11072962560 | bytes 15728640 | tf_op jit(solution)/shard_map/pallas_call | solution.py:883
  484.9 2.6 add_bitcast_fusion
  487.6 2.6 add_bitcast_fusion.2
  495.0 15.1 %shard_map.241 = bf16[8,40,768]{2,1,0:T(8,128)(2,1)S(1)} custom-call(bf16[2,8,40,768]{3,2,1,0:T(8,128)(2,1)S(1)} %bitcast.324), custom_call_target="tpu_custom_call" | custom-call | bytes 52500000 | tf_op jit(solution)/shard_map/pallas_call | solution.py:592
  527.6 20.6 %shard_map.242 = bf16[4,128,768]{2,1,0:T(8,128)(2,1)S(1)} custom-call(bf16[128,768]{1,0:T(8,128)(2,1)S(1)} %get-tuple-element.192.refs_0_), custom_call_target="tpu_custom_call" | custom-call | bytes 56000000 | tf_op jit(solution)/shard_map/pallas_call | solution.py:104
  548.2 2.6 fusion.8
  553.0 23.7 %shard_map.243 = (bf16[4,128,384]{2,1,0:T(8,128)(2,1)S(1)}, bf16[4096,384]{1,0:T(8,128)(2,1)S(1)}) custom-call(s32[4,3]{1,0:T(4,128)S(1)} %pad_add_fusion.bounds_ref, bf16[4,128,384]{2,1,0:T(8,128)(2,1)S(1)} %bitcast.347, bf16[4,128,384]{2,1,0:T(8,128)(2,1)S(1)} %bitcast.350, f32[4,128,384]{2,1,0:T(8,128)S(1)} %copy-done.32, bf16[4096,384]{1,0:T(8,128)(2,1)} %bitcast.290, ...), custom_call_target="tpu_custom_call" | custom-call | flops 4026531840 | bytes 6291456 | tf_op jit(solution)/shard_map/pallas_call | solution.py:760
  576.7 18.8 %shard_map.244 = bf16[4,128,384]{2,1,0:T(8,128)(2,1)S(1)} custom-call(bf16[2,4,2,2,128,384]{5,4,3,2,1,0:T(8,128)(2,1)S(1)} %bitcast.294), custom_call_target="tpu_custom_call" | custom-call | bytes 87500000 | tf_op jit(solution)/shard_map/pallas_call | solution.py:449
  596.7 18.7 %shard_map.245 = bf16[4,128,768]{2,1,0:T(8,128)(2,1)S(1)} custom-call(bf16[4,128,768]{2,1,0:T(8,128)(2,1)S(1)} %bitcast.304), custom_call_target="tpu_custom_call" | custom-call | bytes 56000000 | tf_op jit(solution)/shard_map/pallas_call | solution.py:104
  622.8 16.1 %shard_map.248 = (bf16[4,24,640]{2,1,0:T(8,128)(2,1)S(1)}, bf16[2,24,384]{2,1,0:T(8,128)(2,1)S(1)}, bf16[4,24,640]{2,1,0:T(8,128)(2,1)S(1)}, bf16[2,24,384]{2,1,0:T(8,128)(2,1)S(1)}) custom-call(bf16[2,4,2,2,24,640]{5,4,3,2,1,0:T(8,128)(2,1)S(1)} %bitcast.326, bf16[2,2,2,2,24,384]{5,4,3,2,1,0:T(8,128)(2,1)S(1)} %bitcast.337, ...), custom_call_target="tpu_custom_call" | custom-call | bytes 70000000 | tf_op jit(solution)/shard_map/pallas_call | solution.py:449
  638.9 8.0 %shard_map.249 = (bf16[4,24,640]{2,1,0:T(8,128)(2,1)S(1)}, bf16[4,24,640]{2,1,0:T(8,128)(2,1)S(1)}) custom-call(bf16[4,24,640]{2,1,0:T(8,128)(2,1)S(1)} %get-tuple-element.101.refs_0_, bf16[4,24,640]{2,1,0:T(8,128)(2,1)S(1)} %get-tuple-element.102.refs_1_), custom_call_target="tpu_custom_call" | custom-call | bytes 35000000 | tf_op jit(solution)/shard_map/pallas_call | solution.py:104
  648.6 4.8 collective-permute-start.12
  (545 shorter events, 152.9 us)
Async XLA Ops:
  58.0 29.8 %copy-start.1 = (bf16[4,128,768]{2,1,0:T(8,128)(2,1)}, bf16[4,128,768]{2,1,0:T(8,128)(2,1)S(1)}, u32[]{:S(2)}) copy-start(bf16[4,128,768]{2,1,0:T(8,128)(2,1)S(1)} %fusion.2) | copy-start | bytes 2359300
  81.5 82.5 %collective-permute-start = (bf16[1024,384]{1,0:T(8,128)(2,1)}, bf16[1024,384]{1,0:T(8,128)(2,1)}, u32[]{:S(2)}, u32[]{:S(2)}) collective-permute-start(bf16[1024,384]{1,0:T(8,128)(2,1)} %get-tuple-element.67.go), channel_id=1, source_target_pairs={{0,16},{16,0},{1,17},{17,1},{2,18},{18,2},{3,19},{19,3},{4,20},{20... | collective-permute-start | bytes 2359304 | tf_op jit(solution)/shard_map/ppermute | solution.py:1046
  81.7 82.4 %collective-permute-start.1 = (bf16[1024,384]{1,0:T(8,128)(2,1)}, bf16[1024,384]{1,0:T(8,128)(2,1)}, u32[]{:S(2)}, u32[]{:S(2)}) collective-permute-start(bf16[1024,384]{1,0:T(8,128)(2,1)} %get-tuple-element.68.uo), channel_id=1, source_target_pairs={{0,16},{16,0},{1,17},{17,1},{2,18},{18,2},{3,19},{19,3},{4,20},{20... | collective-permute-start | bytes 2359304 | tf_op jit(solution)/shard_map/ppermute | solution.py:1046
  83.5 80.6 %collective-permute-start.2 = (bf16[1024,384]{1,0:T(8,128)(2,1)}, bf16[1024,384]{1,0:T(8,128)(2,1)}, u32[]{:S(2)}, u32[]{:S(2)}) collective-permute-start(bf16[1024,384]{1,0:T(8,128)(2,1)} %get-tuple-element.69.do), channel_id=1, source_target_pairs={{0,16},{16,0},{1,17},{17,1},{2,18},{18,2},{3,19},{19,3},{4,20},{20... | collective-permute-start | bytes 2359304 | tf_op jit(solution)/shard_map/ppermute | solution.py:1046
  121.2 65.8 %copy-start.61 = (bf16[128,768]{1,0:T(8,128)(2,1)}, bf16[128,768]{1,0:T(8,128)(2,1)S(1)}, u32[]{:S(2)}) copy-start(bf16[128,768]{1,0:T(8,128)(2,1)S(1)} %get-tuple-element.197) | copy-start | bytes 589828
  136.3 150.2 %collective-permute-start.3 = (bf16[1024,384]{1,0:T(8,128)(2,1)}, bf16[1024,384]{1,0:T(8,128)(2,1)}, u32[]{:S(2)}, u32[]{:S(2)}) collective-permute-start(bf16[1024,384]{1,0:T(8,128)(2,1)} %get-tuple-element.73.go), channel_id=1, source_target_pairs={{0,16},{16,0},{1,17},{17,1},{2,18},{18,2},{3,19},{19,3},{4,20},{20... | collective-permute-start | bytes 2359304 | tf_op jit(solution)/shard_map/ppermute | solution.py:1046
  136.3 150.2 %collective-permute-start.4 = (bf16[1024,384]{1,0:T(8,128)(2,1)}, bf16[1024,384]{1,0:T(8,128)(2,1)}, u32[]{:S(2)}, u32[]{:S(2)}) collective-permute-start(bf16[1024,384]{1,0:T(8,128)(2,1)} %get-tuple-element.74.uo), channel_id=1, source_target_pairs={{0,16},{16,0},{1,17},{17,1},{2,18},{18,2},{3,19},{19,3},{4,20},{20... | collective-permute-start | bytes 2359304 | tf_op jit(solution)/shard_map/ppermute | solution.py:1046
  160.8 27.0 %copy-start.104 = (f32[768]{0:T(1024)}, f32[768]{0:T(1024)S(1)}, u32[]{:S(2)}) copy-start(f32[768]{0:T(1024)S(1)} %get-tuple-element.249) | copy-start | bytes 9220
  164.0 64.8 %copy-start.75 = (bf16[768,384]{1,0:T(8,128)(2,1)}, bf16[768,384]{1,0:T(8,128)(2,1)S(1)}, u32[]{:S(2)}) copy-start(bf16[768,384]{1,0:T(8,128)(2,1)S(1)} %convolution_convert_fusion.2) | copy-start | bytes 1769476
  164.0 122.5 %collective-permute-start.5 = (bf16[1024,384]{1,0:T(8,128)(2,1)}, bf16[1024,384]{1,0:T(8,128)(2,1)}, u32[]{:S(2)}, u32[]{:S(2)}) collective-permute-start(bf16[1024,384]{1,0:T(8,128)(2,1)} %get-tuple-element.75.do), channel_id=1, source_target_pairs={{0,16},{16,0},{1,17},{17,1},{2,18},{18,2},{3,19},{19,3},{4,20},{20... | collective-permute-start | bytes 2359304 | tf_op jit(solution)/shard_map/ppermute | solution.py:1046
  164.1 23.0 %copy-start.130 = (f32[128]{0:T(128)S(1)}, f32[128]{0:T(128)}, u32[]{:S(2)}) copy-start(f32[128]{0:T(128)} %get-tuple-element.183) | copy-start | bytes 1540
  187.8 23.2 %copy-start.51 = (f32[128,768]{1,0:T(8,128)}, f32[128,768]{1,0:T(8,128)S(1)}, u32[]{:S(2)}) copy-start(f32[128,768]{1,0:T(8,128)S(1)} %get-tuple-element.239) | copy-start | bytes 1179652
  187.8 23.1 %copy-start.133 = (f32[128]{0:T(128)}, f32[128]{0:T(128)S(1)}, u32[]{:S(2)}) copy-start(f32[128]{0:T(128)S(1)} %add_rsqrt_fusion.3) | copy-start | bytes 1540
  256.7 29.9 %copy-start.47 = (f32[128,768]{1,0:T(8,128)}, f32[128,768]{1,0:T(8,128)S(1)}, u32[]{:S(2)}) copy-start(f32[128,768]{1,0:T(8,128)S(1)} %get-tuple-element.241) | copy-start | bytes 1179652
  256.7 29.8 %copy-start.124 = (f32[128]{0:T(128)}, f32[128]{0:T(128)S(1)}, u32[]{:S(2)}) copy-start(f32[128]{0:T(128)S(1)} %add_rsqrt_fusion.2) | copy-start | bytes 1540
  309.5 42.2 %collective-permute-start.6 = (bf16[1024,384]{1,0:T(8,128)(2,1)}, bf16[1024,384]{1,0:T(8,128)(2,1)}, u32[]{:S(2)}, u32[]{:S(2)}) collective-permute-start(bf16[1024,384]{1,0:T(8,128)(2,1)} %get-tuple-element.80), channel_id=1, source_target_pairs={{0,16},{16,0},{1,17},{17,1},{2,18},{18,2},{3,19},{19,3},{4,20},{20... | collective-permute-start | bytes 2359304 | tf_op jit(solution)/shard_map/ppermute | solution.py:1255
  312.3 33.0 %copy-start.64 = (bf16[128,768]{1,0:T(8,128)(2,1)S(1)}, bf16[128,768]{1,0:T(8,128)(2,1)}, u32[]{:S(2)}) copy-start(bf16[128,768]{1,0:T(8,128)(2,1)} %param.27) | copy-start | bytes 589828
  312.3 33.0 %copy-start.132 = (f32[128]{0:T(128)S(1)}, f32[128]{0:T(128)}, u32[]{:S(2)}) copy-start(f32[128]{0:T(128)} %get-tuple-element.180) | copy-start | bytes 1540
  315.4 59.9 %collective-permute-start.7 = (bf16[1024,384]{1,0:T(8,128)(2,1)}, bf16[1024,384]{1,0:T(8,128)(2,1)}, u32[]{:S(2)}, u32[]{:S(2)}) collective-permute-start(bf16[1024,384]{1,0:T(8,128)(2,1)} %copy-done.40), channel_id=1, source_target_pairs={{0,16},{16,0},{1,17},{17,1},{2,18},{18,2},{3,19},{19,3},{4,20},{20... | collective-permute-start | bytes 2359304 | tf_op jit(solution)/shard_map/ppermute | solution.py:1255
  319.3 28.3 %copy-start.48 = (f32[128,768]{1,0:T(8,128)S(1)}, f32[128,768]{1,0:T(8,128)}, u32[]{:S(2)}) copy-start(f32[128,768]{1,0:T(8,128)} %copy-done.47) | copy-start | bytes 1179652
  319.3 28.3 %copy-start.96 = (f32[128,320]{0,1:T(8,128)S(1)}, f32[128,320]{0,1:T(8,128)}, u32[]{:S(2)}) copy-start(f32[128,320]{0,1:T(8,128)} %get-tuple-element.191) | copy-start | bytes 491524
  350.1 53.9 %collective-permute-start.8 = (bf16[1024,384]{1,0:T(8,128)(2,1)}, bf16[1024,384]{1,0:T(8,128)(2,1)}, u32[]{:S(2)}, u32[]{:S(2)}) collective-permute-start(bf16[1024,384]{1,0:T(8,128)(2,1)} %get-tuple-element.86), channel_id=1, source_target_pairs={{0,16},{16,0},{1,17},{17,1},{2,18},{18,2},{3,19},{19,3},{4,20},{20... | collective-permute-start | bytes 2359304 | tf_op jit(solution)/shard_map/ppermute | solution.py:1255
  354.9 23.3 %copy-start.44 = (bf16[512,384]{1,0:T(8,128)(2,1)S(1)}, bf16[512,384]{1,0:T(8,128)(2,1)}, u32[]{:S(2)}) copy-start(bf16[512,384]{1,0:T(8,128)(2,1)} %copy-done.43) | copy-start | bytes 1179652
  375.3 28.7 %copy-start.8 = (bf16[4,128,768]{2,1,0:T(8,128)(2,1)}, bf16[4,128,768]{2,1,0:T(8,128)(2,1)S(1)}, u32[]{:S(2)}) copy-start(bf16[4,128,768]{2,1,0:T(8,128)(2,1)S(1)} %shard_map.235) | copy-start | bytes 2359300
  445.1 45.1 %copy-start.56 = (f32[128,768]{1,0:T(8,128)}, f32[128,768]{1,0:T(8,128)S(1)}, u32[]{:S(2)}) copy-start(f32[128,768]{1,0:T(8,128)S(1)} %multiply_add_fusion.1) | copy-start | bytes 1179652
  462.3 22.6 %copy-start.87 = (f32[1024,384]{1,0:T(8,128)S(1)}, f32[1024,384]{1,0:T(8,128)}, u32[]{:S(2)}) copy-start(f32[1024,384]{1,0:T(8,128)} %get-tuple-element.117) | copy-start | bytes 4718596
  482.7 42.7 %collective-permute-start.9 = (bf16[1024,384]{1,0:T(8,128)(2,1)}, bf16[1024,384]{1,0:T(8,128)(2,1)}, u32[]{:S(2)}, u32[]{:S(2)}) collective-permute-start(bf16[1024,384]{1,0:T(8,128)(2,1)} %get-tuple-element.89), channel_id=1, source_target_pairs={{0,16},{16,0},{1,17},{17,1},{2,18},{18,2},{3,19},{19,3},{4,20},{20... | collective-permute-start | bytes 2359304 | tf_op jit(solution)/shard_map/ppermute | solution.py:1255
  484.1 64.1 %collective-permute-start.10 = (bf16[1024,384]{1,0:T(8,128)(2,1)}, bf16[1024,384]{1,0:T(8,128)(2,1)}, u32[]{:S(2)}, u32[]{:S(2)}) collective-permute-start(bf16[1024,384]{1,0:T(8,128)(2,1)} %get-tuple-element.91), channel_id=1, source_target_pairs={{0,16},{16,0},{1,17},{17,1},{2,18},{18,2},{3,19},{19,3},{4,20},{20... | collective-permute-start | bytes 2359304 | tf_op jit(solution)/shard_map/ppermute | solution.py:1255
  510.9 65.7 %collective-permute-start.11 = (bf16[1024,384]{1,0:T(8,128)(2,1)}, bf16[1024,384]{1,0:T(8,128)(2,1)}, u32[]{:S(2)}, u32[]{:S(2)}) collective-permute-start(bf16[1024,384]{1,0:T(8,128)(2,1)} %get-tuple-element.95), channel_id=1, source_target_pairs={{0,16},{16,0},{1,17},{17,1},{2,18},{18,2},{3,19},{19,3},{4,20},{20... | collective-permute-start | bytes 2359304 | tf_op jit(solution)/shard_map/ppermute | solution.py:1255
  525.9 22.3 %copy-start.147 = (s32[192]{0:T(256)S(1)}, s32[192]{0:T(256)}, u32[]{:S(2)}) copy-start(s32[192]{0:T(256)} %broadcast_add_fusion) | copy-start | bytes 2308
  527.6 23.3 %copy-start.42 = (bf16[512,384]{1,0:T(8,128)(2,1)S(1)}, bf16[512,384]{1,0:T(8,128)(2,1)}, u32[]{:S(2)}) copy-start(bf16[512,384]{1,0:T(8,128)(2,1)} %copy-done.41) | copy-start | bytes 1179652
  648.6 19.9 %collective-permute-start.12 = (bf16[2,24,768]{2,1,0:T(8,128)(2,1)S(1)}, bf16[2,24,768]{2,1,0:T(8,128)(2,1)S(1)}, u32[]{:S(2)}, u32[]{:S(2)}) collective-permute-start(bf16[2,24,768]{2,1,0:T(8,128)(2,1)S(1)} %bitcast.377), channel_id=1, source_target_pairs={{0,0},{1,1},{2,2},{3,3},{4,8},{5,9},{6,10},{7,11},{8,16},{9,17},{1... | collective-permute-start | bytes 221192 | tf_op jit(solution)/shard_map/ppermute | solution.py:1324
  (129 other events, 908.9 us)

commit v4 on v3

--- a/solution.py
+++ b/solution.py
@@ -1,5 +1,3 @@
-from functools import partial
-
 import jax
 import jax.numpy as jnp
 from jax import lax
@@ -606,8 +604,7 @@
 
 NEGATIVE = -1e30
 EPSILON = 1e-06
-HIGHEST = lax.Precision.HIGHEST
-KEYS = 512
+KEYS = 1024
 LANES = 128
 LAST = (((1,), (1,)), ((), ()))
 FIRST = (((0,), (0,)), ((), ()))
@@ -623,32 +620,60 @@
     return (key_pos <= query_pos) & (key_pos >= starts)
 
 
+def block_bounds(starts, bases, rows):
+    return jnp.stack(
+        [
+            lax.div(starts[:, 0], KEYS),
+            lax.div(bases + rows - 1, KEYS),
+            bases,
+            lax.div(starts[:, rows - 1], KEYS),
+        ],
+        axis=1,
+    )
+
+
+def over_chunks(bounds_ref, i, step, carry):
+    low, high, edge = bounds_ref[i, 0], bounds_ref[i, 1], bounds_ref[i, 3]
+    carry = step(high, True, carry)
+    inner = jnp.maximum(high - 1 - edge, 0)
+    carry = lax.fori_loop(0, inner, lambda t, c: step(high - 1 - t, False, c), carry)
+    below = high - 1 - inner
+    return lax.fori_loop(0, below - low + 1, lambda t, c: step(below - t, True, c), carry)
+
+
 def attend(bounds, queries, kv_all, starts):
     count, rows, width = queries.shape
     heads = width // LANES
 
-    def body(bounds_ref, q_ref, kv_ref, start_ref, out_ref):
+    def body(bounds_ref, q_ref, kv_ref, start_ref, out_ref, attn_ref):
         i = pl.program_id(0)
-        low, high, base = bounds_ref[i, 0], bounds_ref[i, 1], bounds_ref[i, 2]
+        base = bounds_ref[i, 2]
         start_row = start_ref[0]
         q = [q_ref[0, :, h * LANES : (h + 1) * LANES] for h in range(heads)]
 
-        def step(t, carry):
-            chunk = high - t
+        def step(chunk, masked, carry):
             at = pl.multiple_of(chunk * KEYS, KEYS)
-            ok = visible(chunk * KEYS, base, KEYS, rows, start_row)
-            new = []
-            for h in range(heads):
-                top, total, acc = carry[h]
-                kv = kv_ref[pl.ds(at, KEYS), h * LANES : (h + 1) * LANES]
-                score = jnp.where(ok, dot32(kv, q[h], LAST), NEGATIVE)
-                new_top = jnp.maximum(top, jnp.max(score, axis=0, keepdims=True))
-                weight = jnp.exp(score - new_top)
-                shrink = jnp.exp(top - new_top)
-                total = total * shrink + jnp.sum(weight, axis=0, keepdims=True)
-                acc = acc * shrink + dot32(kv, weight.astype(jnp.bfloat16), FIRST)
-                new.append((new_top, total, acc))
-            return tuple(new)
+            if masked:
+                ok = visible(chunk * KEYS, base, KEYS, rows, start_row)
+            kvs = [kv_ref[pl.ds(at, KEYS), h * LANES : (h + 1) * LANES] for h in range(heads)]
+            scores = [dot32(kvs[h], q[h], LAST) for h in range(heads)]
+            if masked:
+                scores = [jnp.where(ok, s, NEGATIVE) for s in scores]
+            tops = [
+                jnp.maximum(carry[h][0], jnp.max(scores[h], axis=0, keepdims=True))
+                for h in range(heads)
+            ]
+            weights = [jnp.exp(scores[h] - tops[h]) for h in range(heads)]
+            shrinks = [jnp.exp(carry[h][0] - tops[h]) for h in range(heads)]
+            totals = [
+                carry[h][1] * shrinks[h] + jnp.sum(weights[h], axis=0, keepdims=True)
+                for h in range(heads)
+            ]
+            accs = [
+                carry[h][2] * shrinks[h] + dot32(kvs[h], weights[h].astype(jnp.bfloat16), FIRST)
+                for h in range(heads)
+            ]
+            return tuple(zip(tops, totals, accs))
 
         empty = tuple(
             (
@@ -658,16 +683,22 @@
             )
             for h in range(heads)
         )
-        done = lax.fori_loop(0, high - low + 1, step, empty)
+        done = over_chunks(bounds_ref, i, step, empty)
         lane = lax.broadcasted_iota(jnp.int32, (LANES, rows), 0)
+        narrow = []
         for h in range(heads):
             top, total, acc = done[h]
             value = jnp.where(lane < LANES // 2, top + jnp.log(total), acc / total)
             out_ref[0, :, h * LANES : (h + 1) * LANES] = value.T
+            narrow.append(value[LANES // 2 :])
+        attn_ref[0] = jnp.concatenate(narrow, axis=0).T.astype(jnp.bfloat16)
 
     return pl.pallas_call(
         body,
-        out_shape=jax.ShapeDtypeStruct((count, rows, width), jnp.float32),
+        out_shape=(
+            jax.ShapeDtypeStruct((count, rows, width), jnp.float32),
+            jax.ShapeDtypeStruct((count, rows, width // 2), jnp.bfloat16),
+        ),
         grid_spec=pltpu.PrefetchScalarGridSpec(
             num_scalar_prefetch=1,
             grid=(count,),
@@ -676,18 +707,17 @@
                 pl.BlockSpec(kv_all.shape, lambda i, b: (0, 0)),
                 pl.BlockSpec((1, 1, rows), lambda i, b: (i, 0, 0)),
             ],
-            out_specs=pl.BlockSpec((1, rows, width), lambda i, b: (i, 0, 0)),
+            out_specs=(
+                pl.BlockSpec((1, rows, width), lambda i, b: (i, 0, 0)),
+                pl.BlockSpec((1, rows, width // 2), lambda i, b: (i, 0, 0)),
+            ),
         ),
         compiler_params=pltpu.CompilerParams(vmem_limit_bytes=VMEM_BYTES),
-        cost_estimate=pl.CostEstimate(
-            flops=2 * count * rows * kv_all.shape[0] * width,
-            bytes_accessed=kv_all.size * 2,
-            transcendentals=count * rows * kv_all.shape[0],
-        ),
+        cost_estimate=lasting(13),
     )(bounds, queries, kv_all, starts)
 
 
-def attend_back(bounds, queries, grads, kept, kv_all, starts, scale):
+def attend_back(bounds, queries, dy, out_rows, kept, kv_all, starts, scale):
     count, rows, width = queries.shape
     total_keys = kv_all.shape[0]
     heads = width // LANES
@@ -695,9 +725,9 @@
         heads = 1
     wide = heads * LANES
 
-    def body(bounds_ref, q_ref, g_ref, kept_ref, kv_ref, start_ref, dq_ref, dkv_ref, acc_ref):
+    def body(bounds_ref, q_ref, dy_ref, w_ref, kept_ref, kv_ref, start_ref, dq_ref, dkv_ref, acc_ref):
         i = pl.program_id(1)
-        low, high, base = bounds_ref[i, 0], bounds_ref[i, 1], bounds_ref[i, 2]
+        base = bounds_ref[i, 2]
         start_row = start_ref[0]
 
         @pl.when(i == 0)
@@ -711,33 +741,41 @@
             lax.fori_loop(0, total_keys // KEYS, clear, 0)
 
         q = [q_ref[0, :, h * LANES : (h + 1) * LANES] for h in range(heads)]
-        g = [g_ref[0, :, h * LANES : (h + 1) * LANES] for h in range(heads)]
+        grads = dot32(dy_ref[0], w_ref[...], LAST).astype(jnp.bfloat16)
+        g = [grads[:, h * LANES : (h + 1) * LANES] for h in range(heads)]
+        qg = [jnp.concatenate([q[h], g[h]], axis=0) for h in range(heads)]
         lse, delta = [], []
         for h in range(heads):
             kept_t = kept_ref[0, :, h * LANES : (h + 1) * LANES].T
             lse.append(kept_t[0:1])
             delta.append(jnp.sum(kept_t * g[h].astype(jnp.float32).T, axis=0, keepdims=True))
 
-        def step(t, carry):
-            chunk = high - t
+        def step(chunk, masked, carry):
             at = pl.multiple_of(chunk * KEYS, KEYS)
-            ok = visible(chunk * KEYS, base, KEYS, rows, start_row)
-            new = []
+            if masked:
+                ok = visible(chunk * KEYS, base, KEYS, rows, start_row)
+            lanes = [slice(h * LANES, (h + 1) * LANES) for h in range(heads)]
+            kvs = [kv_ref[pl.ds(at, KEYS), lanes[h]] for h in range(heads)]
+            pairs = [dot32(kvs[h], qg[h], LAST) for h in range(heads)]
+            scores = [p[:, :rows] for p in pairs]
+            dprobs = [p[:, rows:] for p in pairs]
+            if masked:
+                scores = [jnp.where(ok, s, NEGATIVE) for s in scores]
+            probs = [jnp.exp(scores[h] - lse[h]) for h in range(heads)]
+            dscores = [
+                (probs[h] * (dprobs[h] - delta[h])).astype(jnp.bfloat16) for h in range(heads)
+            ]
+            both = [
+                jnp.concatenate([dscores[h], probs[h].astype(jnp.bfloat16)], axis=1)
+                for h in range(heads)
+            ]
             for h in range(heads):
-                lanes = slice(h * LANES, (h + 1) * LANES)
-                kv = kv_ref[pl.ds(at, KEYS), lanes]
-                score = jnp.where(ok, dot32(kv, q[h], LAST), NEGATIVE)
-                prob = jnp.exp(score - lse[h])
-                dscore = (prob * (dot32(kv, g[h], LAST) - delta[h])).astype(jnp.bfloat16)
-                acc_ref[pl.ds(at, KEYS), lanes] += dot32(dscore, q[h]) + dot32(
-                    prob.astype(jnp.bfloat16), g[h]
-                )
-                new.append(carry[h] + dot32(kv, dscore, FIRST))
-            return tuple(new)
-
-        done = lax.fori_loop(
-            0,
-            high - low + 1,
+                acc_ref[pl.ds(at, KEYS), lanes[h]] += dot32(both[h], qg[h])
+            return tuple(carry[h] + dot32(kvs[h], dscores[h], FIRST) for h in range(heads))
+
+        done = over_chunks(
+            bounds_ref,
+            i,
             step,
             tuple(jnp.zeros((LANES, rows), jnp.float32) for h in range(heads)),
         )
@@ -768,7 +806,8 @@
             grid=(width // wide, count),
             in_specs=[
                 block,
-                block,
+                pl.BlockSpec((1,) + tuple(dy.shape[1:]), lambda h, i, b: (i, 0, 0)),
+                pl.BlockSpec((wide, out_rows.shape[1]), lambda h, i, b: (h, 0)),
                 block,
                 whole,
                 pl.BlockSpec((1, 1, rows), lambda h, i, b: (i, 0, 0)),
@@ -777,12 +816,8 @@
             scratch_shapes=[pltpu.VMEM((total_keys, wide), jnp.float32)],
         ),
         compiler_params=pltpu.CompilerParams(vmem_limit_bytes=VMEM_BYTES),
-        cost_estimate=pl.CostEstimate(
-            flops=5 * count * rows * total_keys * width,
-            bytes_accessed=kv_all.size * 4,
-            transcendentals=count * rows * total_keys,
-        ),
-    )(bounds, queries, grads, kept, kv_all, starts)
+        cost_estimate=lasting(20),
+    )(bounds, queries, dy, out_rows, kept, kv_all, starts)
 
 
 def expert_forward(head, rows_in, own, other):
@@ -901,58 +936,350 @@
     )(head, rows_in, grads_in, *weights)
 
 
-def pack_grads(column, dq, dkv, attn, dy, small, compact):
+def split(values, terms=2):
+    parts = []
+    for _ in range(terms):
+        part = values.astype(jnp.bfloat16)
+        parts.append(part)
+        values = values - part.astype(jnp.float32)
+    return parts
+
+
+def exact_dot(pieces, values, dims):
+    total = dot32(pieces[0], values, dims)
+    for piece in pieces[1:]:
+        total = total + dot32(piece, values, dims)
+    return total
+
+
+def unit_scale(values):
+    return lax.rsqrt(jnp.mean(values * values, axis=-1, keepdims=True) + EPSILON)
+
+
+def alone(body, out_shape, cost, *operands, scalars=0):
+    specs = [pl.BlockSpec(memory_space=pltpu.SMEM)] * scalars + [VMEM] * (len(operands) - scalars)
+    results = pl.pallas_call(
+        body,
+        out_shape=out_shape,
+        in_specs=specs,
+        out_specs=jax.tree.map(lambda _: VMEM, out_shape),
+        compiler_params=pltpu.CompilerParams(vmem_limit_bytes=VMEM_BYTES),
+        cost_estimate=lasting(cost),
+    )(*operands)
+    return list(results) if isinstance(out_shape, (list, tuple)) else results
+
+
+def make(shape, kind=jnp.float32):
+    return jax.ShapeDtypeStruct(tuple(shape), kind)
+
+
+def route_tables(routes, gates):
+    count, rows, _ = routes.shape
+    slots = NE * CAP
+
+    def body(routes_ref, gates_ref, picks_ref, weights_ref, slot_ref, other_ref):
+        row = lax.broadcasted_iota(jnp.int32, (rows, rows), 0)
+        col = lax.broadcasted_iota(jnp.int32, (rows, rows), 1)
+        before = (col < row).astype(jnp.bfloat16)
+        expert = lax.broadcasted_iota(jnp.int32, (rows, LANES), 1)
+        slot = lax.broadcasted_iota(jnp.int32, (rows, slots), 1)
+        source = lax.broadcasted_iota(jnp.int32, (LANES, slots), 0)
+        target = lax.broadcasted_iota(jnp.int32, (LANES, slots), 1)
+        spread = (
+            (target >= source * CAP) & (target < source * CAP + CAP) & (source < NE)
+        ).astype(jnp.bfloat16)
+        ones = jnp.ones((rows, LANES), jnp.bfloat16)
+        for n in range(count):
+            gate = jnp.zeros((rows, LANES), jnp.float32)
+            named = jnp.zeros((rows, LANES), jnp.float32)
+            for k in range(2):
+                hit = routes_ref[n, :, k : k + 1] == expert
+                named = named + jnp.where(hit, 1.0, 0.0)
+                gate = gate + jnp.where(hit, gates_ref[n, :, k : k + 1], 0.0)
+            rank = dot32(before, named.astype(jnp.bfloat16)) + expert.astype(jnp.float32) * CAP
+            rank = jnp.where(expert < NE, rank, 0.0)
+            goal = exact_dot(split(rank, 2), spread, (((1,), (0,)), ((), ())))
+            member = dot32(named.astype(jnp.bfloat16), spread)
+            pick = jnp.where(goal == slot.astype(jnp.float32), member, 0.0)
+            weight = pick * exact_dot(split(gate, 3), spread, (((1,), (0,)), ((), ())))
+            picks_ref[n] = pick.astype(jnp.bfloat16)
+            weights_ref[n] = weight
+            slot_ref[n] = exact_dot(split(weight, 3), ones, FIRST)
+            other_ref[n] = gate
+
+    return alone(
+        body,
+        (
+            make((count, rows, slots), jnp.bfloat16),
+            make((count, rows, slots)),
+            make((count, slots, LANES)),
+            make((count, rows, LANES)),
+        ),
+        3,
+        routes,
+        gates,
+    )
+
+
+def gate_slots(slot_gates, picks, grads):
+    picked = dot32(picks, grads[0], FIRST)
+    for part in grads[1:]:
+        picked = picked + dot32(picks, part, FIRST)
+    lanes = [
+        (picked[:, at : at + LANES] * slot_gates).astype(jnp.bfloat16)
+        for at in range(0, picked.shape[1], LANES)
+    ]
+    return jnp.concatenate(lanes, axis=1)
+
+
+def const_alphas(hn, smalls, base):
+    logits = dot32(hn, smalls[base + 2 : base + 6].astype(jnp.bfloat16), LAST)
+    alphas = []
+    for c in range(2):
+        first, second = logits[:, 2 * c : 2 * c + 1], logits[:, 2 * c + 1 : 2 * c + 2]
+        top = jnp.maximum(first, second)
+        first, second = jnp.exp(first - top), jnp.exp(second - top)
+        total = first + second
+        alphas.append((first / total, second / total))
+    return alphas
+
+
+def project(column, pack, smalls, plane, heads, scale, normed):
+    count, rows, width = column.shape
+    own_out = pack.shape[1] - width - heads * LANES - LANES + LANES // 2
+    kv_at, tail_at = width, width + heads * LANES
+    wide = heads * LANES
+    small_rows = 8 * LAYERS
+
+    def body(plane_ref, column_ref, pack_ref, *refs):
+        if normed:
+            smalls_in, query_ref, kv_ref, query_w_ref, out_w_ref = refs
+        else:
+            xn_ref, query_ref, kv_ref, query_w_ref, out_w_ref, small_ref = refs
+        tail = pack_ref[:, tail_at:]
+        source = lax.broadcasted_iota(jnp.int32, (tail.shape[1], wide), 0)
+        target = lax.broadcasted_iota(jnp.int32, (tail.shape[1], wide), 1)
+        dim = LANES // 2
+        goal = lax.div(source, dim) * LANES + lax.rem(source, dim)
+        to_low = ((goal == target) & (source < own_out)).astype(jnp.bfloat16)
+        query_w = dot32(tail, to_low).astype(jnp.bfloat16)
+        query_w_ref[...] = query_w
+        out_rows = pack_ref[pl.ds(pl.multiple_of(plane_ref[0] * own_out, 64), own_out), :width]
+        pieces = []
+        for h in range(heads):
+            pieces += [jnp.zeros((dim, width), jnp.bfloat16), out_rows[h * dim : (h + 1) * dim]]
+        out_w_ref[...] = jnp.concatenate(pieces, axis=0)
+        if normed:
+            xn = column_ref[...].reshape((count * rows, width))
+        else:
+            small = tail[:, tail.shape[1] - LANES :].astype(jnp.float32).T
+            first = own_out - (tail.shape[1] - LANES)
+            small = small[first : first + small_rows]
+            small_ref[...] = small
+            x = column_ref[...].reshape((count * rows, width)).astype(jnp.float32)
+            xn = (x * unit_scale(x) * small[0:1]).astype(jnp.bfloat16)
+            xn_ref[...] = xn.reshape((count, rows, width))
+        query = dot32(xn, query_w).astype(jnp.bfloat16).astype(jnp.float32) * scale
+        query_ref[...] = query.astype(jnp.bfloat16).reshape((count, rows, wide))
+        kv = dot32(xn, pack_ref[:, kv_at:tail_at]).astype(jnp.bfloat16)
+        kv_ref[...] = kv.reshape((count, rows, wide))
+
+    outs = [
+        make((count, rows, wide), jnp.bfloat16),
+        make((count, rows, wide), jnp.bfloat16),
+        make((width, wide), jnp.bfloat16),
+        make((wide, width), jnp.bfloat16),
+    ]
+    if normed:
+        return [column] + alone(body, outs, 4, plane, column, pack, smalls, scalars=1) + [smalls]
+    outs = [make(column.shape, jnp.bfloat16)] + outs + [make((small_rows, width))]
+    return alone(body, outs, 4, plane, column, pack, scalars=1)
+
+
+def middle(attn, x, pack, smalls, base, picks, slot_gates, grads):
+    planes, rows, part = attn.shape
+    width = x.shape[1]
+    slots = picks.shape[1]
+
+    def body(attn_ref, x_ref, w_ref, small_ref, picks_ref, gates_ref, *refs):
+        total = x_ref[...].astype(jnp.float32)
+        for z in range(planes):
+            total = total + dot32(attn_ref[z], w_ref[z * part : (z + 1) * part, :width])
+        mid_ref, sent_ref = refs[-2:] if grads is None else refs[-3:-1]
+        mid_ref[...] = total
+        hn = (total * unit_scale(total) * small_ref[base + 1 : base + 2]).astype(jnp.bfloat16)
+        sent_ref[...] = dot32(picks_ref[...], hn, FIRST).astype(jnp.bfloat16)
+        if grads is not None:
+            refs[-1][...] = gate_slots(gates_ref[...], picks_ref[...], [refs[0][...]])
+
+    outs = [make((rows, width)), make((slots, width), jnp.bfloat16)]
+    more = []
+    if grads is not None:
+        outs.append(make((slots, width), jnp.bfloat16))
+        more.append(grads)
+    return alone(body, outs, 3, attn, x, pack, smalls, picks, slot_gates, *more)
+
+
+def combine(back, weights, mid, other, smalls, base, following):
+    rows, width = mid.shape
+
+    def body(back_ref, weights_ref, mid_ref, other_ref, small_ref, x_ref, *refs):
+        mid_value, gate = mid_ref[...], other_ref[...]
+        hn = (mid_value * unit_scale(mid_value) * small_ref[base + 1 : base + 2]).astype(
+            jnp.bfloat16
+        )
+        alphas = const_alphas(hn, small_ref, base)
+        wide = hn.astype(jnp.float32)
+        total = mid_value + exact_dot(
+            split(weights_ref[...]), back_ref[...], (((1,), (0,)), ((), ()))
+        )
+        factor = gate[:, NE + 1 : NE + 2]
+        for c in range(2):
+            weight = gate[:, NE + 2 + c : NE + 3 + c]
+            factor = factor + weight * alphas[c][0]
+            total = total + (weight * alphas[c][1]) * small_ref[base + 6 + c : base + 7 + c]
+        total = total + factor * wide
+        x_ref[...] = total
+        if following:
+            refs[0][...] = (total * unit_scale(total) * small_ref[base + 8 : base + 9]).astype(
+                jnp.bfloat16
+            )
+
+    outs = [make((rows, width))]
+    if following:
+        outs.append(make((rows, width), jnp.bfloat16))
+    return alone(body, outs, 3, back, weights, mid, other, smalls)
+
+
+def experts_back(dback, picks, upstream, mid, other, smalls, base):
+    rows, width = mid.shape
+
+    def body(dback_ref, picks_ref, up_ref, mid_ref, other_ref, small_ref, dmid_ref, dy_ref, row_ref):
+        mid_value, gate = mid_ref[...], other_ref[...]
+        g = up_ref[...].astype(jnp.float32)
+        scale = unit_scale(mid_value)
+        unit = mid_value * scale
+        gain = small_ref[base + 1 : base + 2]
+        hn = (unit * gain).astype(jnp.bfloat16)
+        alphas = const_alphas(hn, small_ref, base)
+        wide = hn.astype(jnp.float32)
+        dhn = dot32(picks_ref[...], dback_ref[...])
+        g_hn = jnp.sum(g * wide, axis=1, keepdims=True)
+        factor = gate[:, NE + 1 : NE + 2]
+        row_ref[0:1] = jnp.zeros((1, width), jnp.float32)
+        for c in range(2):
+            weight = gate[:, NE + 2 + c : NE + 3 + c]
+            vector = small_ref[base + 6 + c : base + 7 + c]
+            first, second = alphas[c]
+            factor = factor + weight * first
+            row_ref[6 + c : 7 + c] = jnp.sum((weight * second) * g, axis=0, keepdims=True)
+            da_first = weight * g_hn
+            da_second = weight * jnp.sum(g * vector, axis=1, keepdims=True)
+            mean = first * da_first + second * da_second
+            for j, dlog in enumerate((first * (da_first - mean), second * (da_second - mean))):
+                at = 2 + 2 * c + j
+                dhn = dhn + dlog * small_ref[base + at : base + at + 1]
+                row_ref[at : at + 1] = jnp.sum(dlog * wide, axis=0, keepdims=True)
+        dhn = dhn + factor * g
+        row_ref[1:2] = jnp.sum(dhn * unit, axis=0, keepdims=True)
+        through = dhn * gain
+        inner = jnp.mean(through * unit, axis=1, keepdims=True)
+        dmid = g + scale * (through - unit * inner)
+        dmid_ref[...] = dmid
+        dy_ref[...] = dmid.astype(jnp.bfloat16)
+
+    return alone(
+        body,
+        [make((rows, width)), make((rows, width), jnp.bfloat16), make((8, width))],
+        4,
+        dback,
+        picks,
+        upstream,
+        mid,
+        other,
+        smalls,
+    )
+
+
+def finish(dxn, x, dmid, rows_in, smalls, base, picks, slot_gates):
+    planes, rows, width = dxn.shape
+
+    def body(dxn_ref, x_ref, dmid_ref, row_ref, small_ref, *refs):
+        grad = dxn_ref[0].astype(jnp.float32)
+        for z in range(1, planes):
+            grad = grad + dxn_ref[z].astype(jnp.float32)
+        value = x_ref[...].astype(jnp.float32)
+        scale = unit_scale(value)
+        unit = value * scale
+        out_rows = refs[-1 if picks is None else -2]
+        out_rows[...] = row_ref[...]
+        out_rows[0:1] = jnp.sum(grad * unit, axis=0, keepdims=True)
+        through = grad * small_ref[base : base + 1]
+        inner = jnp.mean(through * unit, axis=1, keepdims=True)
+        g = dmid_ref[...] + scale * (through - unit * inner)
+        refs[-2 if picks is None else -3][...] = g
+        if picks is not None:
+            refs[-1][...] = gate_slots(refs[1][...], refs[0][...], split(g))
+
+    outs = [make((rows, width)), make((8, width))]
+    more = []
+    if picks is not None:
+        outs.append(make((picks.shape[1], width), jnp.bfloat16))
+        more = [picks, slot_gates]
+    return alone(body, outs, 3, dxn, x, dmid, rows_in, smalls, *more)
+
+
+def column_parts(dq, dkv, query_w, pack, width):
+    rows, wide = dq.shape
+
+    def body(dq_ref, dkv_ref, w_ref, pack_ref, out_ref):
+        out_ref[...] = (
+            dot32(dq_ref[...], w_ref[...], LAST)
+            + dot32(dkv_ref[...], pack_ref[:, width : width + wide], LAST)
+        ).astype(jnp.bfloat16)
+
+    return alone(body, make((rows, width), jnp.bfloat16), 2, dq, dkv, query_w, pack)
+
+
+def pack_grads(column, dq, dkv, attn, dy, small):
     width = column.shape[1]
     kv_cols, own_out = dkv.shape[1], attn.shape[1]
-    small_cols = small.shape[1]
+    tail = own_out + LANES // 2
     rows, cols = own_out // 2, width // 2
 
-    def body(column_ref, dq_ref, dkv_ref, attn_ref, dy_ref, small_ref, compact_ref, one, two):
+    def body(column_ref, dq_ref, dkv_ref, attn_ref, dy_ref, small_ref, one, two):
         one[:, :kv_cols] = dot32(column_ref[...], dkv_ref[...], FIRST).astype(jnp.bfloat16)
-        narrow = dot32(dq_ref[...], compact_ref[...]).astype(jnp.bfloat16)
-        one[:, kv_cols:] = (
-            dot32(column_ref[...], narrow, FIRST) + small_ref[...]
-        ).astype(jnp.bfloat16)
+        source = lax.broadcasted_iota(jnp.int32, (kv_cols, tail), 0)
+        target = lax.broadcasted_iota(jnp.int32, (kv_cols, tail), 1)
+        dim = LANES // 2
+        goal = lax.div(target, dim) * LANES + lax.rem(target, dim)
+        compact = ((goal == source) & (target < own_out)).astype(jnp.bfloat16)
+        narrow = dot32(dq_ref[...], compact).astype(jnp.bfloat16)
+        placed = jnp.concatenate(
+            [
+                jnp.zeros((own_out, width), jnp.float32),
+                small_ref[...],
+                jnp.zeros((tail - own_out - 8, width), jnp.float32),
+            ],
+            axis=0,
+        ).T
+        one[:, kv_cols:] = (dot32(column_ref[...], narrow, FIRST) + placed).astype(jnp.bfloat16)
         out = dot32(attn_ref[...], dy_ref[...], FIRST).astype(jnp.bfloat16)
         for a in range(2):
             for b in range(2):
                 two[a, b] = out[a * rows : (a + 1) * rows, b * cols : (b + 1) * cols]
 
-    return pl.pallas_call(
+    return alone(
         body,
-        out_shape=[
-            jax.ShapeDtypeStruct((width, kv_cols + small_cols), jnp.bfloat16),
-            jax.ShapeDtypeStruct((2, 2, rows, cols), jnp.bfloat16),
-        ],
-        compiler_params=pltpu.CompilerParams(vmem_limit_bytes=VMEM_BYTES),
-        cost_estimate=lasting(4),
-    )(column, dq, dkv, attn, dy, small, compact)
-
-
-def norm_forward(values, gain_vec):
-    row_scale = lax.rsqrt(jnp.mean(values * values, axis=-1, keepdims=True) + EPSILON)
-    normed = values * row_scale
-    return normed * gain_vec, normed, row_scale
-
-
-def norm_backward(upstream, normed, row_scale, gain_vec):
-    through = upstream * gain_vec
-    gain_grad = jnp.sum(upstream * normed, axis=0)
-    inner_mean = jnp.mean(through * normed, axis=-1, keepdims=True)
-    return row_scale * (through - normed * inner_mean), gain_grad
-
-
-def slot_index(route_ids):
-    token_rows = route_ids.shape[0]
-    expert_ids = jnp.arange(NE, dtype=jnp.int32)
-    matches = (
-        (route_ids[:, :, None] == expert_ids[None, None, :])
-        .astype(jnp.int32)
-        .reshape((token_rows * 2, NE))
+        [make((width, kv_cols + tail), jnp.bfloat16), make((2, 2, rows, cols), jnp.bfloat16)],
+        4,
+        column,
+        dq,
+        dkv,
+        attn,
+        dy,
+        small,
     )
-    before = jnp.cumsum(matches, axis=0) - 1
-    slot_pos = jnp.sum(matches * before, axis=1).reshape((token_rows, 2))
-    return jnp.where(route_ids < NE, route_ids * CAP + slot_pos, NE * CAP)
 
 
 def per_device(
@@ -983,61 +1310,46 @@
     scale = head_dim ** (-0.5)
     half_length = blocks * token_rows
     positions = 2 * half_length
-    features = w_gate.shape[2]
-    hidden_rows = w_gate.shape[1]
     copies = blocks // NE
     own_out = heads * head_dim
+    wide = heads * LANES
 
     swap = [(0, 1), (1, 0)]
     head_scalar = head_index.reshape((1,)).astype(jnp.int32)
-
-    seg_own = lax.dynamic_index_in_dim(segments, head_index, 0, keepdims=False)
-    seg_parts = jnp.concatenate([lax.rem(seg_own, 128), lax.div(seg_own, 128)]).astype(
-        jnp.bfloat16
-    )
-    seg_columns = -(-seg_parts.shape[0] // shard_rows)
-    seg_parts = jnp.pad(seg_parts, (0, seg_columns * shard_rows - seg_parts.shape[0]))
-    seg_parts = seg_parts.reshape((shard_rows, seg_columns))
+    plane_scalar = plane.reshape((1,)).astype(jnp.int32)
+
+    seg_own = lax.dynamic_index_in_dim(segments, head_index, 0, keepdims=True)
+    seg_rows = jnp.concatenate([lax.rem(seg_own, 128), lax.div(seg_own, 128)], axis=0)
+    seg_rows = jnp.pad(seg_rows, ((0, 14), (0, 0))).astype(jnp.bfloat16)
+    seg_rows = jnp.broadcast_to(seg_rows[None], (COLUMNS,) + seg_rows.shape)
+    smalls = [
+        jnp.concatenate(
+            [gain_attn[n][:, None], gain_moe[n][:, None], const_gate[n], const_vec[n]], axis=1
+        )
+        for n in range(LAYERS)
+    ]
+    smalls.append(jnp.zeros((shard_rows, LANES // 2 - 8 * LAYERS), jnp.bfloat16))
+    smalls = jnp.concatenate(smalls, axis=1)
     packs = []
     for layer in range(LAYERS):
-        split = w_qkv[layer].reshape((shard_rows, 3, COLUMNS, heads, head_dim))
-        kv_part = jnp.concatenate([split[:, 1], split[:, 2]], axis=3)
-        kv_part = kv_part.transpose((1, 0, 2, 3)).reshape((COLUMNS, shard_rows, heads * LANES))
-        query_part = split[:, 0].transpose((1, 0, 2, 3)).reshape((COLUMNS, shard_rows, own_out))
-        side = [
-            gain_attn[layer][:, None],
-            gain_moe[layer][:, None],
-            const_gate[layer],
-            const_vec[layer],
-            seg_parts,
-        ]
-        filled = own_out + 8 + seg_columns
-        side.append(jnp.zeros((shard_rows, -filled % LANES), jnp.bfloat16))
-        side = jnp.concatenate(side, axis=1)
+        parts = w_qkv[layer].reshape((shard_rows, 3, COLUMNS, heads, head_dim))
+        kv_part = jnp.concatenate([parts[:, 1], parts[:, 2]], axis=3)
+        kv_part = kv_part.transpose((1, 0, 2, 3)).reshape((COLUMNS, shard_rows, wide))
+        query_part = parts[:, 0].transpose((1, 0, 2, 3)).reshape((COLUMNS, shard_rows, own_out))
         packs.append(
             jnp.concatenate(
                 [
+                    jnp.broadcast_to(w_out[layer][None], (COLUMNS, shard_rows, width)),
                     kv_part,
-                    jnp.broadcast_to(w_out[layer][None], (COLUMNS, shard_rows, width)),
                     query_part,
-                    jnp.broadcast_to(side[None], (COLUMNS,) + side.shape),
+                    jnp.broadcast_to(smalls[None], (COLUMNS,) + smalls.shape),
                 ],
                 axis=2,
             )
         )
-    weights, column_tokens = start_gather(packs, tokens, blocks, 1)
-    weights = [pack.reshape((shards, shard_rows, -1)) for pack in weights]
-    out_at = heads * LANES
-    query_at = out_at + width
-    small_at = query_at + own_out
-
-    place = jnp.arange(own_out, dtype=jnp.int32)
-    place = lax.div(place, head_dim) * LANES + lax.rem(place, head_dim)
-    wide_place = jnp.arange(heads * LANES, dtype=jnp.int32)
-    to_low = (place[:, None] == wide_place[None, :]).astype(jnp.bfloat16)
-    to_high = (place[:, None] + head_dim == wide_place[None, :]).astype(jnp.bfloat16)
-    small_cols = own_out + LANES - own_out % LANES
-    compact = jnp.pad(to_low.T, ((0, 0), (0, small_cols - own_out)))
+    weights, column_tokens = start_gather(packs + [seg_rows], tokens, blocks, 1)
+    packs = [pack.reshape((width, -1)) for pack in weights[:LAYERS]]
+    picks, pick_gates, slot_gates, other_gates = route_tables(routes, gates)
 
     def send_experts(layer, after):
         held = lax.optimization_barrier(
@@ -1046,13 +1358,9 @@
         return held, [lax.ppermute(w, "head", swap) for w in held]
 
     own_experts, other_experts = [None] * LAYERS, [None] * LAYERS
-
-    seg_all = weights[0][:, :, small_at + 8 : small_at + 8 + seg_columns]
-    seg_all = seg_all.reshape((shards, -1))[:, : 2 * token_rows].astype(jnp.int32)
-    seg_all = seg_all[:, :token_rows] + 128 * seg_all[:, token_rows:]
-    seg_query = lax.dynamic_index_in_dim(
-        seg_all.reshape((2, COLUMNS, span, token_rows)), head_index, 0, keepdims=False
-    )
+    seg_all = weights[LAYERS][..., :2, :].astype(jnp.int32)
+    seg_all = seg_all[..., 0, :] + 128 * seg_all[..., 1, :]
+    seg_query = lax.dynamic_index_in_dim(seg_all, head_index, 0, keepdims=False)
     seg_query = lax.dynamic_index_in_dim(seg_query, rest, 1, keepdims=False)
     starts = jnp.sum(
         (seg_all.reshape((1, 1, -1)) < seg_query[:, :, None]).astype(jnp.int32), axis=2
@@ -1061,81 +1369,35 @@
         head_index * half_length
         + (jnp.arange(COLUMNS, dtype=jnp.int32) * span + rest) * token_rows
     )
-    bounds = jnp.stack(
-        [lax.div(starts[:, 0], KEYS), lax.div(bases + token_rows - 1, KEYS), bases], axis=1
-    )
+    bounds = block_bounds(starts, bases, token_rows)
     starts = starts[:, None, :]
 
-    layers = []
-    for pack in weights:
-        rows = pack.reshape((width, -1))
-        kv_w = rows[:, :out_at]
-        out_w = rows[:, out_at:query_at]
-        query_w = dot32(rows[:, query_at:small_at], to_low).astype(jnp.bfloat16)
-        small_w = rows[:, small_at : small_at + 8]
-        out_rows = lax.dynamic_slice_in_dim(out_w, plane * own_out, own_out, 0)
-        out_rows = dot32(to_high, out_rows, FIRST).astype(jnp.bfloat16)
-        layers.append((query_w, kv_w, out_w, small_w, out_rows))
-
-    def expert_buffers(layer):
-        route_ids, gate_vals = routes[layer], gates[layer]
-        slots = slot_index(route_ids)
-        named = slots[:, :, None] == jnp.arange(NE * CAP, dtype=jnp.int32)[None, None, :]
-        picks = jnp.any(named, axis=1)
-        pick_gates = jnp.sum(jnp.where(named, gate_vals[:, :, None], 0.0), axis=1)
-        return picks, pick_gates
-
-    def gated_rows(picks, pick_gates, upstream):
-        picked = jnp.dot(picks.astype(jnp.float32).T, upstream, precision=HIGHEST)
-        dz = (jnp.sum(pick_gates, axis=0)[:, None] * picked).astype(jnp.bfloat16)
-        return dz.reshape((NE, CAP, width))
-
-    upstream = cotangent.astype(jnp.float32)
-    residual = tokens.astype(jnp.float32)
+    values = tokens
+    column, small_rows = column_tokens, None
     kept = []
     for layer in range(LAYERS):
-        query_w, kv_w, out_w, small_w, out_rows = layers[layer]
-        attn_gain = small_w[:, 0].astype(jnp.float32)
-        moe_gain = small_w[:, 1].astype(jnp.float32)
-        gate_w = small_w[:, 2:6]
-        vectors = small_w[:, 6:8].astype(jnp.float32).T
-        normed_in, unit_in, scale_in = norm_forward(residual, attn_gain)
-        if layer == 0:
-            column = norm_forward(column_tokens.astype(jnp.float32), attn_gain)[0]
-            column = column.astype(jnp.bfloat16)
-        else:
-            (column,) = column_exchange([normed_in.astype(jnp.bfloat16)], [True], blocks, 3)
-        column = column.reshape((COLUMNS * token_rows, width))
-        queries = (
-            dot32(column, query_w).astype(jnp.bfloat16).astype(jnp.float32) * scale
-        ).astype(jnp.bfloat16)
-        queries = queries.reshape((COLUMNS, token_rows, heads * LANES))
-        kv_own = dot32(column, kv_w).astype(jnp.bfloat16)
-        (kv_all,) = plane_gather(
-            [kv_own.reshape((COLUMNS, token_rows, heads * LANES))], blocks, 4
-        )
-        kv_all = kv_all.reshape((positions, heads * LANES))
+        base = 8 * layer
+        last = layer + 1 == LAYERS
+        column, queries, kv_own, query_w, out_rows, small_rows = project(
+            column, packs[layer], small_rows, plane_scalar, heads, scale, layer > 0
+        )
+        (kv_all,) = plane_gather([kv_own], blocks, 4)
+        kv_all = kv_all.reshape((positions, wide))
         if layer == 0:
             own_experts[0], other_experts[0] = send_experts(0, kv_all)
-        attended = attend(bounds, queries, kv_all, starts)
-        attn_col = dot32(
-            attended.astype(jnp.bfloat16).reshape((-1, heads * LANES)), to_high, LAST
-        ).astype(jnp.bfloat16)
-        (attn,) = column_exchange(
-            [attn_col.reshape((COLUMNS, token_rows, own_out))], [False], blocks, 5, 9
-        )
-        attn = attn.transpose((1, 0, 2)).reshape((token_rows, width))
-        middle = residual + dot32(attn, out_w)
-        normed_mid, unit_mid, scale_mid = norm_forward(middle, moe_gain)
-        moe_in = normed_mid.astype(jnp.bfloat16)
-        moe_float = moe_in.astype(jnp.float32)
-        route_ids, gate_vals = routes[layer], gates[layer]
-        picks, pick_gates = expert_buffers(layer)
-        sent = dot32(picks.astype(jnp.bfloat16), moe_in, FIRST).astype(jnp.bfloat16)
-        sent = [sent.reshape((NE, CAP, width))]
-        last = layer + 1 == LAYERS
-        if last:
-            sent.append(gated_rows(picks, pick_gates, upstream))
+        attended, attn_col = attend(bounds, queries, kv_all, starts)
+        (attn,) = column_exchange([attn_col], [False], blocks, 5, 9)
+        mid, *sent = middle(
+            attn,
+            values,
+            packs[layer],
+            small_rows,
+            base,
+            picks[layer],
+            slot_gates[layer],
+            cotangent if last else None,
+        )
+        sent = [rows.reshape((NE, CAP, width)) for rows in sent]
         arrived = expert_dispatch(sent, blocks, 7 if last else 6, 24 if last else 15)
         flat_in, *dz_in = [rows.reshape((-1, width)) for rows in arrived]
         if last:
@@ -1148,101 +1410,38 @@
                 9,
                 24,
             )
-            last_grads = wgrads, dback
         else:
             own_experts[layer + 1], other_experts[layer + 1] = send_experts(layer + 1, flat_in)
             parts = expert_forward(
                 head_scalar, flat_in, own_experts[layer], other_experts[layer]
             )
             (back,) = expert_return([parts.reshape((copies, NE, CAP, width))], blocks, 8)
-        back = back.reshape((NE * CAP, width)).astype(jnp.float32)
-        ffn_out = jnp.dot(pick_gates, back, precision=HIGHEST)
-        copy_weight = jnp.sum(jnp.where(route_ids == NE + 1, gate_vals, 0.0), axis=1)
-        const_weight = jnp.stack(
-            [
-                jnp.sum(jnp.where(route_ids == NE + 2 + c, gate_vals, 0.0), axis=1)
-                for c in range(2)
-            ],
-            axis=1,
-        )
-        mixing = jax.nn.softmax(dot32(moe_in, gate_w).reshape((token_rows, 2, 2)), axis=-1)
-        const_out = jnp.sum(
-            const_weight[:, :, None]
-            * (mixing[:, :, 0:1] * moe_float[:, None, :] + mixing[:, :, 1:2] * vectors[None]),
-            axis=1,
-        )
-        residual = middle + ffn_out + copy_weight[:, None] * moe_float + const_out
         kept.append(
-            (
-                unit_in,
-                scale_in,
-                column,
-                queries,
-                kv_all,
-                attended,
-                attn_col,
-                unit_mid,
-                scale_mid,
-                moe_float,
-                picks,
-                pick_gates,
-                flat_in,
-                copy_weight,
-                const_weight,
-                mixing,
-            )
-        )
-    output = residual
-
+            (values, column, queries, kv_all, attended, attn_col, query_w, out_rows, mid, flat_in)
+        )
+        values, *normed = combine(
+            back.reshape((NE * CAP, width)),
+            pick_gates[layer],
+            mid,
+            other_gates[layer],
+            small_rows,
+            base,
+            not last,
+        )
+        if not last:
+            (column,) = column_exchange(normed, [True], blocks, 3)
+    output = values
+
+    upstream = cotangent
     shared_grads = [None] * LAYERS
     expert_grads = [None] * LAYERS
     for layer in reversed(range(LAYERS)):
-        query_w, kv_w, out_w, small_w, out_rows = layers[layer]
-        attn_gain = small_w[:, 0].astype(jnp.float32)
-        moe_gain = small_w[:, 1].astype(jnp.float32)
-        gate_w = small_w[:, 2:6].astype(jnp.float32)
-        vectors = small_w[:, 6:8].astype(jnp.float32).T
-        (
-            unit_in,
-            scale_in,
-            column,
-            queries,
-            kv_all,
-            attended,
-            attn_col,
-            unit_mid,
-            scale_mid,
-            moe_float,
-            picks,
-            pick_gates,
-            flat_in,
-            copy_weight,
-            const_weight,
-            mixing,
-        ) = kept[layer]
-        mix_grad = const_weight[:, :, None] * upstream[:, None, :]
-        alpha_grad = jnp.stack(
-            [
-                jnp.sum(mix_grad * moe_float[:, None, :], axis=-1),
-                jnp.sum(mix_grad * vectors[None], axis=-1),
-            ],
-            axis=-1,
-        )
-        logit_grad = (
-            mixing * (alpha_grad - jnp.sum(mixing * alpha_grad, axis=-1, keepdims=True))
-        ).reshape((token_rows, 4))
-        hn_grad = (
-            copy_weight[:, None] * upstream
-            + jnp.sum(mixing[:, :, 0:1] * mix_grad, axis=1)
-            + jnp.dot(logit_grad, gate_w.T, precision=HIGHEST)
-        )
-        cgate_grad = jnp.dot(moe_float.T, logit_grad, precision=HIGHEST)
-        cvec_grad = jnp.sum(mixing[:, :, 1:2] * mix_grad, axis=0).T
-
-        if layer + 1 == LAYERS:
-            wgrads, dback = last_grads
-        else:
-            (dz_in,) = expert_dispatch([gated_rows(picks, pick_gates, upstream)], blocks, 6)
+        base = 8 * layer
+        values, column, queries, kv_all, attended, attn_col, query_w, out_rows, mid, flat_in = (
+            kept[layer]
+        )
+        if layer + 1 < LAYERS:
+            (dz_in,) = expert_dispatch([dz.reshape((NE, CAP, width))], blocks, 6)
             *wgrads, dparts = expert_backward(
                 head_scalar,
                 flat_in,
@@ -1254,46 +1453,52 @@
             (dback,) = expert_return([dparts.reshape((copies, NE, CAP, width))], blocks, 8)
         got = [lax.ppermute(away, "head", swap) for away in wgrads[3:]]
         dback, got[0] = lax.optimization_barrier((dback, got[0]))
-        hn_grad = hn_grad + dot32(
-            picks.astype(jnp.bfloat16), dback.reshape((NE * CAP, width))
-        )
-        middle_grad, moe_gain_grad = norm_backward(hn_grad, unit_mid, scale_mid, moe_gain)
-        middle_grad = middle_grad + upstream
-        (dy,) = column_exchange([middle_grad.astype(jnp.bfloat16)], [True], blocks, 3)
+        dmid, dy, rows = experts_back(
+            dback.reshape((NE * CAP, width)),
+            picks[layer],
+            upstream,
+            mid,
+            other_gates[layer],
+            small_rows,
+            base,
+        )
+        (dy,) = column_exchange([dy], [True], blocks, 3)
         dy, got[1] = lax.optimization_barrier((dy, got[1]))
-        dy = dy.reshape((COLUMNS * token_rows, width))
-        dattn = dot32(dy, out_rows, LAST).astype(jnp.bfloat16)
-        dattn = dattn.reshape((COLUMNS, token_rows, heads * LANES))
-        dq, dkv_all = attend_back(bounds, queries, dattn, attended, kv_all, starts, scale)
+        dq, dkv_all = attend_back(
+            bounds, queries, dy, out_rows, attended, kv_all, starts, scale
+        )
         dkv_all, got[2] = lax.optimization_barrier((dkv_all, got[2]))
-        (dkv,) = plane_reduce(
-            [dkv_all.reshape((2, COLUMNS, span, token_rows, heads * LANES))], blocks, 10
-        )
-        dq = dq.reshape((-1, heads * LANES))
-        dkv = dkv.reshape((-1, heads * LANES))
-        dxn = (dot32(dq, query_w, LAST) + dot32(dkv, kv_w, LAST)).astype(jnp.bfloat16)
+        (dkv,) = plane_reduce([dkv_all.reshape((2, COLUMNS, span, token_rows, wide))], blocks, 10)
+        dq = dq.reshape((-1, wide))
+        dkv = dkv.reshape((-1, wide))
+        dxn = column_parts(dq, dkv, query_w, packs[layer], width)
         (dxn,) = column_exchange(
             [dxn.reshape((COLUMNS, token_rows, width))], [False], blocks, 11
         )
-        dxn = jnp.sum(dxn.astype(jnp.float32), axis=0)
-        lead_grad, attn_gain_grad = norm_backward(dxn, unit_in, scale_in, attn_gain)
-        upstream = middle_grad + lead_grad
+        before = layer > 0
+        upstream, rows, *dz = finish(
+            dxn,
+            values,
+            dmid,
+            rows,
+            small_rows,
+            base,
+            picks[layer - 1] if before else None,
+            slot_gates[layer - 1] if before else None,
+        )
+        if before:
+            (dz,) = dz
         expert_grads[layer] = [
             own + other.astype(jnp.float32) for own, other in zip(wgrads[:3], got)
         ]
-
-        small_part = jnp.concatenate(
-            [
-                jnp.zeros((width, own_out), jnp.float32),
-                attn_gain_grad[:, None],
-                moe_gain_grad[:, None],
-                cgate_grad,
-                cvec_grad,
-                jnp.zeros((width, small_cols - own_out - 8), jnp.float32),
-            ],
-            axis=1,
-        )
-        qkv_part, out_part = pack_grads(column, dq, dkv, attn_col, dy, small_part, compact)
+        qkv_part, out_part = pack_grads(
+            column.reshape((-1, width)),
+            dq,
+            dkv,
+            attn_col.reshape((-1, own_out)),
+            dy.reshape((-1, width)),
+            rows,
+        )
         shared_grads[layer] = [
             qkv_part.reshape((2, COLUMNS, span, shard_rows, -1)),
             out_part.reshape((2, 2, span, shard_rows, width // 2)),
@@ -1303,16 +1508,13 @@
     reduced = plane_reduce(packed, blocks, 12, 20)
     from_planes = column_exchange(reduced[::2], [False] * LAYERS, blocks, 13, 10)
     from_planes = jnp.stack(from_planes, axis=1).astype(jnp.float32)
-    kv_out = from_planes[..., : heads * LANES].reshape(
-        (COLUMNS, LAYERS, shard_rows, heads, 2, head_dim)
-    )
-    query_out = from_planes[..., heads * LANES : heads * LANES + own_out].reshape(
+    kv_out = from_planes[..., :wide].reshape((COLUMNS, LAYERS, shard_rows, heads, 2, head_dim))
+    query_out = from_planes[..., wide : wide + own_out].reshape(
         (COLUMNS, LAYERS, shard_rows, heads, 1, head_dim)
     )
     qkv_out = jnp.concatenate([query_out, kv_out], axis=4)
     qkv_out = qkv_out.transpose((1, 2, 4, 0, 3, 5)).reshape((LAYERS, shard_rows, 3 * width))
-    small_out = heads * LANES + own_out
-    small_out = jnp.sum(from_planes[..., small_out : small_out + 8], axis=0)
+    small_out = jnp.sum(from_planes[..., wide + own_out : wide + own_out + 8], axis=0)
     out_grads = jnp.stack(reduced[1::2]).transpose((0, 2, 1, 3))
     out_grads = out_grads.reshape((LAYERS, shard_rows, width))
     owners = [

time: 681 us -> 590 us (0.87)
  other arithmetic: 48.9 us -> 17.4 us
  local copies, waits for them, and re-layouts: 70.1 us -> 38.6 us
  matrix products: 31.3 us -> 0 us
  waiting for transfers between devices: 0.03 us -> 10.4 us
    dot_general x30 -> x0, matrix products: 31.3 us -> none  [the longest x22 22.7 us: dot32(): return lax.dot_general(a, b, dims, preferred_element_type=jnp.float32)]
    unnamed x306 -> x130, local copies, waits for them, and re-layouts: 31.6 us -> 18.3 us
    reduce_sum x20 -> x1, other arithmetic: 10.4 us -> 0.08 us  [per_device(): jnp.sum(from_planes[..., wide + own_out:wide + own_out + 8], axis=0)]
    ppermute x6, waiting for transfers between devices: 0.02 us -> 10.3 us  [send_experts(): return (held, [lax.ppermute(w, 'head', swap) for w in held])]
    pallas_call x2, Pallas kernels: 47.3 us -> 37.6 us  [attend_back(): pl.pallas_call(body, out_shape=(jax.ShapeDtypeStruct((count, rows, width)...]
    pallas_call x4 -> x17, Pallas kernels: 37.8 us -> 40.8 us  [the longest x2 23.3 us: attend(): pl.pallas_call(body, out_shape=(jax.ShapeDtypeStruct((count, rows, width)...]
  transfers between devices with their start and end apart: 13 -> 13, of which waited for: 0 -> 1; matrix products, arithmetic and copies ran while one was open for 14% -> 4% of each run, Pallas kernels for 42% -> 46%
where the time goes in v4:
time: 590 us; the launch traced here: 579 us
  Pallas kernels  496 us (84%)
  local copies, waits for them, and re-layouts  38.6 us (7%)
  other arithmetic  17.4 us (3%)
  starting transfers between devices  15.2 us (3%)
  waiting for transfers between devices  10.4 us (2%)
    pallas_call x8, Pallas kernels, column_exchange(): pl.pallas_call(body, out_shape=[jax.ShapeDtypeStruct((COLUMNS,) + slab, v...  123 us
    pallas_call x3, Pallas kernels, expert_return(): pl.pallas_call(body, out_shape=[jax.ShapeDtypeStruct(a.shape[1:], a.dtype...  54.1 us
    pallas_call x3, Pallas kernels, plane_reduce(): pl.pallas_call(body, out_shape=[jax.ShapeDtypeStruct(shape, values.dtype)...  53.5 us
    pallas_call x3, Pallas kernels, expert_dispatch(): pl.pallas_call(body, out_shape=[jax.ShapeDtypeStruct((copies,) + tuple(b....  53.3 us
    pallas_call x1, Pallas kernels, start_gather(): pl.pallas_call(body, out_shape=plane_shapes(packs, blocks) + [jax.ShapeDt...  46.8 us
    pallas_call x2, Pallas kernels, expert_backward(): pl.pallas_call(body, out_shape=[jax.ShapeDtypeStruct((hidden, features),...  41.9 us
    pallas_call x2, Pallas kernels, attend_back(): pl.pallas_call(body, out_shape=(jax.ShapeDtypeStruct((count, rows, width)...  37.6 us
    pallas_call x2, Pallas kernels, plane_gather(): pl.pallas_call(body, out_shape=plane_shapes(arrays, blocks), in_specs=[AN...  36.6 us
  transfers between devices with their start and end apart: 13, of which 1 were waited for; matrix products, arithmetic and copies ran while one was open for 4% of the time, Pallas kernels for 46%

profile of v4, /device:TPU:12, one launch (start us, length us, event | category | flops | bytes accessed | tf_op | source)
XLA Modules:
  0.0 579.4 jit_solution(7388385238059622204)
XLA Ops:
  9.9 46.8 %shard_map.221 = (bf16[2,4,4,24,1408]{4,3,2,1,0:T(8,128)(2,1)S(1)}, bf16[2,4,4,24,1408]{4,3,2,1,0:T(8,128)(2,1)}, bf16[2,4,4,16,128]{4,3,2,1,0:T(8,128)(2,1)S(1)...) custom-call(bf16[4,24,1408]{2,1,0:T(8,128)(2,1)S(1)} %concatenate.24, ...), custom_call_target="tpu_custom_call" | custom-call | bytes 122500000 | tf_op jit(solution)/shard_map/pallas_call | solution.py:277
  58.7 17.5 %shard_map.223 = bf16[2,4,4,128,384]{4,3,2,1,0:T(8,128)(2,1)S(1)} custom-call(bf16[4,128,384]{2,1,0:T(8,128)(2,1)S(1)} %get-tuple-element.106.refs_0_), custom_call_target="tpu_custom_call" | custom-call | bytes 56000000 | tf_op jit(solution)/shard_map/pallas_call | solution.py:237
  86.8 11.5 %shard_map.224 = (f32[4,128,384]{2,1,0:T(8,128)S(1)}, bf16[4,128,192]{2,1,0:T(8,128)(2,1)S(1)}) custom-call(s32[4,4]{1,0:T(4,128)S(1)} %pad_add_fusion.bounds_ref, bf16[4,128,384]{2,1,0:T(8,128)(2,1)S(1)} %copy-done.9, bf16[4096,384]{1,0:T(8,128)(2,1)S(1)} %bitcast.153, s32[4,1,128]{2,1,0:T(1,128)S(1)} %bitcast.204), custom_call_target="tpu_custom_call" | custom-call | bytes 45500000 | tf_op jit(solution)/shard_map/pallas_call | solution.py:696
  98.4 7.1 %shard_map.225.attn_ref = bf16[4,128,192]{2,1,0:T(8,128)(2,1)S(1)} custom-call(bf16[4,128,192]{2,1,0:T(8,128)(2,1)S(1)} %get-tuple-element.107.refs_0_), custom_call_target="tpu_custom_call" | custom-call | bytes 31500000 | tf_op jit(solution)/shard_map/pallas_call | solution.py:102
  106.4 13.7 %shard_map.228 = bf16[2,8,40,768]{3,2,1,0:T(8,128)(2,1)S(1)} custom-call(bf16[8,40,768]{2,1,0:T(8,128)(2,1)S(1)} %bitcast.197), custom_call_target="tpu_custom_call" | custom-call | bytes 52500000 | tf_op jit(solution)/shard_map/pallas_call | solution.py:520
  120.2 2.0 collective-permute-start.4
  122.4 10.3 %collective-permute-done.2.dx = bf16[1024,384]{1,0:T(8,128)(2,1)} collective-permute-done((bf16[1024,384]{1,0:T(8,128)(2,1)}, bf16[1024,384]{1,0:T(8,128)(2,1)}, u32[]{:S(2)}, u32[]{:S(2)}) %collective-permute-start.2) | collective-permute-done | bytes 786464 | tf_op jit(solution)/shard_map/ppermute | solution.py:1358
  132.7 7.7 %shard_map.229 = bf16[640,768]{1,0:T(8,128)(2,1)S(1)} custom-call(s32[1]{0:T(128)} %bitcast.head_ref, bf16[640,768]{1,0:T(8,128)(2,1)} %bitcast.182, bf16[1024,384]{1,0:T(8,128)(2,1)} %get-tuple-element.112.go, bf16[1024,384]{1,0:T(8,128)(2,1)} %collective-permute-done.gx, bf16[1024,384]{1,0:T(8,128)(2,1)} %get-tuple-element.113.uo, ...), custom_call_target="tpu_custom_call" | custom-call | flops 3019898880 | bytes 6684672 | tf_op jit(solution)/shard_map/pallas_call | solution.py:852
  140.4 13.6 %shard_map.230 = bf16[8,40,768]{2,1,0:T(8,128)(2,1)S(1)} custom-call(bf16[2,8,40,768]{3,2,1,0:T(8,128)(2,1)S(1)} %bitcast.190), custom_call_target="tpu_custom_call" | custom-call | bytes 52500000 | tf_op jit(solution)/shard_map/pallas_call | solution.py:590
  154.9 21.6 %shard_map.232.column_ref = bf16[4,128,768]{2,1,0:T(8,128)(2,1)S(1)} custom-call(bf16[128,768]{1,0:T(8,128)(2,1)S(1)} %get-tuple-element.118.refs_0_), custom_call_target="tpu_custom_call" | custom-call | bytes 56000000 | tf_op jit(solution)/shard_map/pallas_call | solution.py:102
  177.8 19.1 %shard_map.234 = bf16[2,4,4,128,384]{4,3,2,1,0:T(8,128)(2,1)S(1)} custom-call(bf16[4,128,384]{2,1,0:T(8,128)(2,1)S(1)} %get-tuple-element.121.refs_0_), custom_call_target="tpu_custom_call" | custom-call | bytes 56000000 | tf_op jit(solution)/shard_map/pallas_call | solution.py:237
  197.0 11.8 %shard_map.235 = (f32[4,128,384]{2,1,0:T(8,128)S(1)}, bf16[4,128,192]{2,1,0:T(8,128)(2,1)S(1)}) custom-call(s32[4,4]{1,0:T(4,128)S(1)} %pad_add_fusion.bounds_ref, bf16[4,128,384]{2,1,0:T(8,128)(2,1)S(1)} %get-tuple-element.120.q_ref, bf16[4096,384]{1,0:T(8,128)(2,1)S(1)} %bitcast.155, s32[4,1,128]{2,1,0:T(1,128)S(1)} %bitcast.205), custom_call_target="tpu_custom_call" | custom-call | bytes 45500000 | tf_op jit(solution)/shard_map/pallas_call | solution.py:696
  208.8 7.1 %shard_map.236.attn_ref = bf16[4,128,192]{2,1,0:T(8,128)(2,1)S(1)} custom-call(bf16[4,128,192]{2,1,0:T(8,128)(2,1)S(1)} %get-tuple-element.122.refs_0_), custom_call_target="tpu_custom_call" | custom-call | bytes 31500000 | tf_op jit(solution)/shard_map/pallas_call | solution.py:102
  216.9 24.8 %shard_map.238 = (bf16[2,8,40,768]{3,2,1,0:T(8,128)(2,1)S(1)}, bf16[2,8,40,768]{3,2,1,0:T(8,128)(2,1)S(1)}) custom-call(bf16[8,40,768]{2,1,0:T(8,128)(2,1)S(1)} %bitcast.195, bf16[8,40,768]{2,1,0:T(8,128)(2,1)S(1)} %bitcast.196), custom_call_target="tpu_custom_call" | custom-call | bytes 84000000 | tf_op jit(solution)/shard_map/pallas_call | solution.py:520
  244.6 21.8 %shard_map.239 = (f32[1024,384]{1,0:T(8,128)}, f32[1024,384]{1,0:T(8,128)}, f32[1024,384]{1,0:T(8,128)}, bf16[1024,384]{1,0:T(8,128)(2,1)}, bf16[1024,384]{1,0:T...) custom-call(s32[1]{0:T(128)} %bitcast.head_ref, ...), custom_call_target="tpu_custom_call" | custom-call | flops 11072962560 | bytes 15728640 | tf_op jit(solution)/shard_map/pallas_call | solution.py:918
  271.0 26.0 %shard_map.240 = (bf16[8,40,768]{2,1,0:T(8,128)(2,1)S(1)}, bf16[8,40,768]{2,1,0:T(8,128)(2,1)S(1)}) custom-call(bf16[2,8,40,768]{3,2,1,0:T(8,128)(2,1)S(1)} %bitcast.187, bf16[2,8,40,768]{3,2,1,0:T(8,128)(2,1)S(1)} %bitcast.186), custom_call_target="tpu_custom_call" | custom-call | bytes 84000000 | tf_op jit(solution)/shard_map/pallas_call | solution.py:590
  300.1 20.9 %shard_map.243.dy_ref = bf16[4,128,768]{2,1,0:T(8,128)(2,1)S(1)} custom-call(bf16[128,768]{1,0:T(8,128)(2,1)S(1)} %get-tuple-element.138.refs_0_), custom_call_target="tpu_custom_call" | custom-call | bytes 56000000 | tf_op jit(solution)/shard_map/pallas_call | solution.py:102
  321.9 18.8 %shard_map.244 = (bf16[4,128,384]{2,1,0:T(8,128)(2,1)S(1)}, bf16[4096,384]{1,0:T(8,128)(2,1)S(1)}) custom-call(s32[4,4]{1,0:T(4,128)S(1)} %copy-done.39, bf16[4,128,384]{2,1,0:T(8,128)(2,1)S(1)} %get-tuple-element.120.q_ref, bf16[4,128,768]{2,1,0:T(8,128)(2,1)S(1)} %shard_map.243.dy_ref, bf16[384,768]{1,0:T(8,128)(2,1)S(1)} %copy-done.30, ...), custom_call_target="tpu_custom_call" | custom-call | bytes 70000000 | tf_op jit(solution)/shard_map/pallas_call | solution.py:798
  344.3 18.7 %shard_map.245 = bf16[4,128,384]{2,1,0:T(8,128)(2,1)S(1)} custom-call(bf16[2,4,2,2,128,384]{5,4,3,2,1,0:T(8,128)(2,1)S(1)} %bitcast.171), custom_call_target="tpu_custom_call" | custom-call | bytes 87500000 | tf_op jit(solution)/shard_map/pallas_call | solution.py:447
  364.0 18.7 %shard_map.247.dxn_ref = bf16[4,128,768]{2,1,0:T(8,128)(2,1)S(1)} custom-call(bf16[4,128,768]{2,1,0:T(8,128)(2,1)S(1)} %bitcast.172), custom_call_target="tpu_custom_call" | custom-call | bytes 56000000 | tf_op jit(solution)/shard_map/pallas_call | solution.py:102
  383.4 14.7 %shard_map.249 = bf16[2,8,40,768]{3,2,1,0:T(8,128)(2,1)S(1)} custom-call(bf16[8,40,768]{2,1,0:T(8,128)(2,1)S(1)} %bitcast.194), custom_call_target="tpu_custom_call" | custom-call | bytes 52500000 | tf_op jit(solution)/shard_map/pallas_call | solution.py:520
  399.0 20.0 %shard_map.250 = (f32[1024,384]{1,0:T(8,128)}, f32[1024,384]{1,0:T(8,128)}, f32[1024,384]{1,0:T(8,128)}, bf16[1024,384]{1,0:T(8,128)(2,1)S(1)}, bf16[1024,384]{1...) custom-call(s32[1]{0:T(128)} %bitcast.head_ref, bf16[640,768]{1,0:T(8,128)(2,1)} %bitcast.183, ...), custom_call_target="tpu_custom_call" | custom-call | flops 11072962560 | bytes 15728640 | tf_op jit(solution)/shard_map/pallas_call | solution.py:918
  424.5 14.5 %shard_map.251 = bf16[8,40,768]{2,1,0:T(8,128)(2,1)S(1)} custom-call(bf16[2,8,40,768]{3,2,1,0:T(8,128)(2,1)S(1)} %bitcast.185), custom_call_target="tpu_custom_call" | custom-call | bytes 52500000 | tf_op jit(solution)/shard_map/pallas_call | solution.py:590
  445.4 21.2 %shard_map.253.dy_ref = bf16[4,128,768]{2,1,0:T(8,128)(2,1)S(1)} custom-call(bf16[128,768]{1,0:T(8,128)(2,1)S(1)} %get-tuple-element.155.refs_0_), custom_call_target="tpu_custom_call" | custom-call | bytes 56000000 | tf_op jit(solution)/shard_map/pallas_call | solution.py:102
  466.6 18.8 %shard_map.254 = (bf16[4,128,384]{2,1,0:T(8,128)(2,1)S(1)}, bf16[4096,384]{1,0:T(8,128)(2,1)S(1)}) custom-call(s32[4,4]{1,0:T(4,128)S(1)} %copy-done.39, bf16[4,128,384]{2,1,0:T(8,128)(2,1)S(1)} %copy-done.10, bf16[4,128,768]{2,1,0:T(8,128)(2,1)S(1)} %shard_map.253.dy_ref, bf16[384,768]{1,0:T(8,128)(2,1)S(1)} %copy-done.28, f32[4,128,384]{2,1,0:T(8,128)S(1)} %copy-done.21, ...), custom_call_target="tpu_custom_call" | custom-call | bytes 70000000 | tf_op jit(solution)/shard_map/pallas_call | solution.py:798
  485.5 18.8 %shard_map.255 = bf16[4,128,384]{2,1,0:T(8,128)(2,1)S(1)} custom-call(bf16[2,4,2,2,128,384]{5,4,3,2,1,0:T(8,128)(2,1)S(1)} %bitcast.170), custom_call_target="tpu_custom_call" | custom-call | bytes 87500000 | tf_op jit(solution)/shard_map/pallas_call | solution.py:447
  505.3 18.7 %shard_map.257.dxn_ref = bf16[4,128,768]{2,1,0:T(8,128)(2,1)S(1)} custom-call(bf16[4,128,768]{2,1,0:T(8,128)(2,1)S(1)} %bitcast.173), custom_call_target="tpu_custom_call" | custom-call | bytes 56000000 | tf_op jit(solution)/shard_map/pallas_call | solution.py:102
  526.5 16.1 %shard_map.261 = (bf16[4,24,640]{2,1,0:T(8,128)(2,1)S(1)}, bf16[2,24,384]{2,1,0:T(8,128)(2,1)S(1)}, bf16[4,24,640]{2,1,0:T(8,128)(2,1)S(1)}, bf16[2,24,384]{2,1,0:T(8,128)(2,1)S(1)}) custom-call(bf16[2,4,2,2,24,640]{5,4,3,2,1,0:T(8,128)(2,1)S(1)} %bitcast.189, bf16[2,2,2,2,24,384]{5,4,3,2,1,0:T(8,128)(2,1)S(1)} %bitcast.203, ...), custom_call_target="tpu_custom_call" | custom-call | bytes 70000000 | tf_op jit(solution)/shard_map/pallas_call | solution.py:447
  542.5 8.3 %shard_map.262 = (bf16[4,24,640]{2,1,0:T(8,128)(2,1)S(1)}, bf16[4,24,640]{2,1,0:T(8,128)(2,1)S(1)}) custom-call(bf16[4,24,640]{2,1,0:T(8,128)(2,1)S(1)} %get-tuple-element.175.refs_0_, bf16[4,24,640]{2,1,0:T(8,128)(2,1)S(1)} %get-tuple-element.176.refs_1_), custom_call_target="tpu_custom_call" | custom-call | bytes 35000000 | tf_op jit(solution)/shard_map/pallas_call | solution.py:102
  553.9 4.6 collective-permute-start.12
  560.4 2.2 reshape.250
  565.2 2.5 reshape.251
  (241 shorter events, 77.4 us)
Async XLA Ops:
  57.4 18.9 %copy-start.2 = (bf16[2,4,4,24,1408]{4,3,2,1,0:T(8,128)(2,1)}, bf16[2,4,4,24,1408]{4,3,2,1,0:T(8,128)(2,1)S(1)}, u32[]{:S(2)}) copy-start(bf16[2,4,4,24,1408]{4,3,2,1,0:T(8,128)(2,1)S(1)} %get-tuple-element.104) | copy-start | bytes 6488068
  78.3 43.9 %collective-permute-start = (bf16[1024,384]{1,0:T(8,128)(2,1)}, bf16[1024,384]{1,0:T(8,128)(2,1)}, u32[]{:S(2)}, u32[]{:S(2)}) collective-permute-start(bf16[1024,384]{1,0:T(8,128)(2,1)} %get-tuple-element.112.go), channel_id=1, source_target_pairs={{0,16},{16,0},{1,17},{17,1},{2,18},{18,2},{3,19},{19,3},{4,20},{20... | collective-permute-start | bytes 2359304 | tf_op jit(solution)/shard_map/ppermute | solution.py:1358
  78.6 43.8 %collective-permute-start.1 = (bf16[1024,384]{1,0:T(8,128)(2,1)}, bf16[1024,384]{1,0:T(8,128)(2,1)}, u32[]{:S(2)}, u32[]{:S(2)}) collective-permute-start(bf16[1024,384]{1,0:T(8,128)(2,1)} %get-tuple-element.113.uo), channel_id=1, source_target_pairs={{0,16},{16,0},{1,17},{17,1},{2,18},{18,2},{3,19},{19,3},{4,20},{20... | collective-permute-start | bytes 2359304 | tf_op jit(solution)/shard_map/ppermute | solution.py:1358
  80.4 52.4 %collective-permute-start.2 = (bf16[1024,384]{1,0:T(8,128)(2,1)}, bf16[1024,384]{1,0:T(8,128)(2,1)}, u32[]{:S(2)}, u32[]{:S(2)}) collective-permute-start(bf16[1024,384]{1,0:T(8,128)(2,1)} %get-tuple-element.114.do), channel_id=1, source_target_pairs={{0,16},{16,0},{1,17},{17,1},{2,18},{18,2},{3,19},{19,3},{4,20},{20... | collective-permute-start | bytes 2359304 | tf_op jit(solution)/shard_map/ppermute | solution.py:1358
  85.6 111.3 %copy-start.36 = (s32[4,128]{1,0:T(4,128)}, s32[4,128]{1,0:T(4,128)S(1)}, u32[]{:S(2)}) copy-start(s32[4,128]{1,0:T(4,128)S(1)} %convert_reduce_fusion) | copy-start | bytes 6148
  85.8 111.1 %copy-start.38 = (s32[4,4]{1,0:T(4,128)}, s32[4,4]{1,0:T(4,128)S(1)}, u32[]{:S(2)}) copy-start(s32[4,4]{1,0:T(4,128)S(1)} %pad_add_fusion.bounds_ref) | copy-start | bytes 196
  120.1 123.5 %collective-permute-start.3 = (bf16[1024,384]{1,0:T(8,128)(2,1)}, bf16[1024,384]{1,0:T(8,128)(2,1)S(1)}, u32[]{:S(2)}, u32[]{:S(2)}) collective-permute-start(bf16[1024,384]{1,0:T(8,128)(2,1)} %get-tuple-element.128.go), channel_id=1, source_target_pairs={{0,16},{16,0},{1,17},{17,1},{2,18},{18,2},{3,19},{19,3},{4,20},{20... | collective-permute-start | bytes 2359304 | tf_op jit(solution)/shard_map/ppermute | solution.py:1358
  120.2 123.4 %collective-permute-start.4 = (bf16[1024,384]{1,0:T(8,128)(2,1)}, bf16[1024,384]{1,0:T(8,128)(2,1)S(1)}, u32[]{:S(2)}, u32[]{:S(2)}) collective-permute-start(bf16[1024,384]{1,0:T(8,128)(2,1)} %get-tuple-element.129.uo), channel_id=1, source_target_pairs={{0,16},{16,0},{1,17},{17,1},{2,18},{18,2},{3,19},{19,3},{4,20},{20... | collective-permute-start | bytes 2359304 | tf_op jit(solution)/shard_map/ppermute | solution.py:1358
  122.3 121.4 %collective-permute-start.5 = (bf16[1024,384]{1,0:T(8,128)(2,1)S(1)}, bf16[1024,384]{1,0:T(8,128)(2,1)S(1)}, u32[]{:S(2)}, u32[]{:S(2)}) collective-permute-start(bf16[1024,384]{1,0:T(8,128)(2,1)S(1)} %copy-done.53), channel_id=1, source_target_pairs={{0,16},{16,0},{1,17},{17,1},{2,18},{18,2},{3,19},{19,3},{4,20},{20... | collective-permute-start | bytes 2359304 | tf_op jit(solution)/shard_map/ppermute | solution.py:1358
  140.4 36.1 %copy-start.4 = (bf16[2,4,4,24,1408]{4,3,2,1,0:T(8,128)(2,1)S(1)}, bf16[2,4,4,24,1408]{4,3,2,1,0:T(8,128)(2,1)}, u32[]{:S(2)}) copy-start(bf16[2,4,4,24,1408]{4,3,2,1,0:T(8,128)(2,1)} %get-tuple-element.119) | copy-start | bytes 6488068
  177.8 19.1 %copy-start.29 = (bf16[384,768]{1,0:T(8,128)(2,1)}, bf16[384,768]{1,0:T(8,128)(2,1)S(1)}, u32[]{:S(2)}) copy-start(bf16[384,768]{1,0:T(8,128)(2,1)S(1)} %get-tuple-element.141.w_ref) | copy-start | bytes 1769476
  177.8 19.1 %copy-start.33 = (bf16[768,384]{1,0:T(8,128)(2,1)}, bf16[768,384]{1,0:T(8,128)(2,1)S(1)}, u32[]{:S(2)}) copy-start(bf16[768,384]{1,0:T(8,128)(2,1)S(1)} %get-tuple-element.147.w_ref) | copy-start | bytes 1769476
  196.9 18.9 %copy-start.24 = (bf16[128,768]{1,0:T(8,128)(2,1)S(1)}, bf16[128,768]{1,0:T(8,128)(2,1)}, u32[]{:S(2)}) copy-start(bf16[128,768]{1,0:T(8,128)(2,1)} %up_ref.1) | copy-start | bytes 589828
  266.4 32.2 %collective-permute-start.6 = (bf16[1024,384]{1,0:T(8,128)(2,1)}, bf16[1024,384]{1,0:T(8,128)(2,1)S(1)}, u32[]{:S(2)}, u32[]{:S(2)}) collective-permute-start(bf16[1024,384]{1,0:T(8,128)(2,1)} %get-tuple-element.136), channel_id=1, source_target_pairs={{0,16},{16,0},{1,17},{17,1},{2,18},{18,2},{3,19},{19,3},{4,20},{20... | collective-permute-start | bytes 2359304 | tf_op jit(solution)/shard_map/ppermute | solution.py:1454
  266.5 54.5 %collective-permute-start.7 = (bf16[1024,384]{1,0:T(8,128)(2,1)S(1)}, bf16[1024,384]{1,0:T(8,128)(2,1)S(1)}, u32[]{:S(2)}, u32[]{:S(2)}) collective-permute-start(bf16[1024,384]{1,0:T(8,128)(2,1)S(1)} %get-tuple-element.139), channel_id=1, source_target_pairs={{0,16},{16,0},{1,17},{17,1},{2,18},{18,2},{3,19},{19,3},{4,20},{20... | collective-permute-start | bytes 2359304 | tf_op jit(solution)/shard_map/ppermute | solution.py:1454
  268.5 73.9 %collective-permute-start.8 = (bf16[1024,384]{1,0:T(8,128)(2,1)S(1)}, bf16[1024,384]{1,0:T(8,128)(2,1)}, u32[]{:S(2)}, u32[]{:S(2)}) collective-permute-start(bf16[1024,384]{1,0:T(8,128)(2,1)S(1)} %get-tuple-element.145), channel_id=1, source_target_pairs={{0,16},{16,0},{1,17},{17,1},{2,18},{18,2},{3,19},{19,3},{4,20},{20... | collective-permute-start | bytes 2359304 | tf_op jit(solution)/shard_map/ppermute | solution.py:1454
  297.0 24.9 %copy-start.23 = (f32[4,128,384]{2,1,0:T(8,128)S(1)}, f32[4,128,384]{2,1,0:T(8,128)}, u32[]{:S(2)}) copy-start(f32[4,128,384]{2,1,0:T(8,128)} %copy-done.22) | copy-start | bytes 2359300
  297.0 24.8 %copy-start.30 = (bf16[384,768]{1,0:T(8,128)(2,1)S(1)}, bf16[384,768]{1,0:T(8,128)(2,1)}, u32[]{:S(2)}) copy-start(bf16[384,768]{1,0:T(8,128)(2,1)} %copy-done.29) | copy-start | bytes 1769476
  297.0 24.8 %copy-start.37 = (s32[4,128]{1,0:T(4,128)S(1)}, s32[4,128]{1,0:T(4,128)}, u32[]{:S(2)}) copy-start(s32[4,128]{1,0:T(4,128)} %copy-done.36) | copy-start | bytes 6148
  297.1 24.8 %copy-start.39 = (s32[4,4]{1,0:T(4,128)S(1)}, s32[4,4]{1,0:T(4,128)}, u32[]{:S(2)}) copy-start(s32[4,4]{1,0:T(4,128)} %copy-done.38) | copy-start | bytes 196
  298.6 22.3 %copy-start.58 = (bf16[1024,384]{1,0:T(8,128)(2,1)}, bf16[1024,384]{1,0:T(8,128)(2,1)S(1)}, u32[]{:S(2)}) copy-start(bf16[1024,384]{1,0:T(8,128)(2,1)S(1)} %collective-permute-done.6) | copy-start | bytes 2359300
  399.0 24.0 %copy-start.52 = (f32[1024,384]{1,0:T(8,128)S(1)}, f32[1024,384]{1,0:T(8,128)}, u32[]{:S(2)}) copy-start(f32[1024,384]{1,0:T(8,128)} %get-tuple-element.183) | copy-start | bytes 4718596
  419.1 24.9 %collective-permute-start.9 = (bf16[1024,384]{1,0:T(8,128)(2,1)S(1)}, bf16[1024,384]{1,0:T(8,128)(2,1)}, u32[]{:S(2)}, u32[]{:S(2)}) collective-permute-start(bf16[1024,384]{1,0:T(8,128)(2,1)S(1)} %get-tuple-element.152), channel_id=1, source_target_pairs={{0,16},{16,0},{1,17},{17,1},{2,18},{18,2},{3,19},{19,3},{4,20},{20... | collective-permute-start | bytes 2359304 | tf_op jit(solution)/shard_map/ppermute | solution.py:1454
  421.0 45.5 %collective-permute-start.10 = (bf16[1024,384]{1,0:T(8,128)(2,1)S(1)}, bf16[1024,384]{1,0:T(8,128)(2,1)}, u32[]{:S(2)}, u32[]{:S(2)}) collective-permute-start(bf16[1024,384]{1,0:T(8,128)(2,1)S(1)} %get-tuple-element.156), channel_id=1, source_target_pairs={{0,16},{16,0},{1,17},{17,1},{2,18},{18,2},{3,19},{19,3},{4,20},{20... | collective-permute-start | bytes 2359304 | tf_op jit(solution)/shard_map/ppermute | solution.py:1454
  421.2 64.3 %collective-permute-start.11 = (bf16[1024,384]{1,0:T(8,128)(2,1)S(1)}, bf16[1024,384]{1,0:T(8,128)(2,1)S(1)}, u32[]{:S(2)}, u32[]{:S(2)}) collective-permute-start(bf16[1024,384]{1,0:T(8,128)(2,1)S(1)} %get-tuple-element.162), channel_id=1, source_target_pairs={{0,16},{16,0},{1,17},{17,1},{2,18},{18,2},{3,19},{19,3},{4,20},{20... | collective-permute-start | bytes 2359304 | tf_op jit(solution)/shard_map/ppermute | solution.py:1454
  443.9 22.7 %copy-start.10 = (bf16[4,128,384]{2,1,0:T(8,128)(2,1)S(1)}, bf16[4,128,384]{2,1,0:T(8,128)(2,1)}, u32[]{:S(2)}) copy-start(bf16[4,128,384]{2,1,0:T(8,128)(2,1)} %copy-done.8) | copy-start | bytes 1179652
  443.9 22.7 %copy-start.21 = (f32[4,128,384]{2,1,0:T(8,128)S(1)}, f32[4,128,384]{2,1,0:T(8,128)}, u32[]{:S(2)}) copy-start(f32[4,128,384]{2,1,0:T(8,128)} %copy-done.20) | copy-start | bytes 2359300
  443.9 22.7 %copy-start.28 = (bf16[384,768]{1,0:T(8,128)(2,1)S(1)}, bf16[384,768]{1,0:T(8,128)(2,1)}, u32[]{:S(2)}) copy-start(bf16[384,768]{1,0:T(8,128)(2,1)} %copy-done.27) | copy-start | bytes 1769476
  485.5 18.8 %copy-start.54 = (bf16[1024,384]{1,0:T(8,128)(2,1)}, bf16[1024,384]{1,0:T(8,128)(2,1)S(1)}, u32[]{:S(2)}) copy-start(bf16[1024,384]{1,0:T(8,128)(2,1)S(1)} %collective-permute-done.11) | copy-start | bytes 2359300
  505.3 19.8 %copy-start.12 = (bf16[4,128,192]{2,1,0:T(8,128)(2,1)S(1)}, bf16[4,128,192]{2,1,0:T(8,128)(2,1)}, u32[]{:S(2)}) copy-start(bf16[4,128,192]{2,1,0:T(8,128)(2,1)} %copy-done.11) | copy-start | bytes 589828
  505.3 19.7 %copy-start.26 = (bf16[4,128,768]{2,1,0:T(8,128)(2,1)S(1)}, bf16[4,128,768]{2,1,0:T(8,128)(2,1)}, u32[]{:S(2)}) copy-start(bf16[4,128,768]{2,1,0:T(8,128)(2,1)} %copy-done.25) | copy-start | bytes 2359300
  553.9 24.6 %collective-permute-start.12 = (bf16[2,24,768]{2,1,0:T(8,128)(2,1)S(1)}, bf16[2,24,768]{2,1,0:T(8,128)(2,1)S(1)}, u32[]{:S(2)}, u32[]{:S(2)}) collective-permute-start(bf16[2,24,768]{2,1,0:T(8,128)(2,1)S(1)} %bitcast.212), channel_id=1, source_target_pairs={{0,0},{1,1},{2,2},{3,3},{4,8},{5,9},{6,10},{7,11},{8,16},{9,17},{1... | collective-permute-start | bytes 221192 | tf_op jit(solution)/shard_map/ppermute | solution.py:1526
  (44 other events, 300.3 us)

commit v5 on v4

--- a/solution.py
+++ b/solution.py
@@ -17,11 +17,19 @@
 VMEM_BYTES = 48 * 1024 * 1024
 
 
-def greet(peers):
+def greet(peers, line=()):
     barrier = pltpu.get_barrier_semaphore()
+    count = len(peers)
     for peer in peers:
         pl.semaphore_signal(barrier, inc=1, device_id=peer, device_id_type=MESH)
-    pl.semaphore_wait(barrier, len(peers))
+    for there, peer in line:
+
+        @pl.when(there)
+        def _():
+            pl.semaphore_signal(barrier, inc=1, device_id=peer, device_id_type=MESH)
+
+        count = count + there.astype(jnp.int32)
+    pl.semaphore_wait(barrier, count)
 
 
 def remote(src, dst, send_sem, recv_sem, peer):
@@ -53,6 +61,67 @@
     plane, rest = lax.div(blk, span), lax.rem(blk, span)
     planes = [lax.rem(plane + d, COLUMNS) for d in range(COLUMNS)]
     return plane, planes, [(head, p * span + rest) for p in planes]
+
+
+class Chain:
+    def __init__(self, source, dst, send_sems, recv_sems, blocks):
+        span = blocks // COLUMNS
+        head, blk = lax.axis_index("head"), lax.axis_index("blk")
+        plane, rest = lax.div(blk, span), lax.rem(blk, span)
+        self.source, self.dst, self.plane = source, dst, plane
+        self.send_sems, self.recv_sems = send_sems, recv_sems
+        after = jnp.minimum(plane + 1, COLUMNS - 1)
+        before = jnp.maximum(plane - 1, 0)
+        self.line = [
+            (plane < COLUMNS - 1, (head, after * span + rest)),
+            (plane > 0, (head, before * span + rest)),
+        ]
+        lower = plane < COLUMNS // 2
+        self.slabs = [
+            plane,
+            plane + 1 - 2 * lax.rem(plane, 2),
+            jnp.where(lower, 2, 1),
+            jnp.where(lower, 3, 0),
+        ]
+
+    def copy(self, k, way):
+        slab = self.slabs[k]
+        place = self.dst.at[slab]
+        return remote(
+            self.source if k == 0 else place,
+            place,
+            self.send_sems.at[k, way],
+            self.recv_sems.at[slab],
+            self.line[way][1],
+        )
+
+    def onward(self, k):
+        if k == 0:
+            return [self.line[0][0], self.line[1][0]]
+        from_before = self.slabs[k] < self.plane
+        return [
+            from_before & self.line[0][0],
+            jnp.logical_not(from_before) & self.line[1][0],
+        ]
+
+    def pass_on(self, k):
+        for way, there in enumerate(self.onward(k)):
+
+            @pl.when(there)
+            def _():
+                self.copy(k, way).start()
+
+    def arrive(self, k):
+        self.copy(k, 0).wait_recv()
+        self.pass_on(k)
+
+    def finish(self):
+        for k in range(COLUMNS):
+            for way, there in enumerate(self.onward(k)):
+
+                @pl.when(there)
+                def _():
+                    self.copy(k, way).wait_send()
 
 
 def column_start(src, gather, dst, own_sem, send_sems, recv_sems, where):
@@ -113,6 +182,29 @@
     )(*arrays)
 
 
+def column_gather(values, blocks, collective_id, cost=14):
+    def body(src, dst, own_sem, send_sems, recv_sems):
+        chain = Chain(src, dst, send_sems, recv_sems, blocks)
+        greet([], chain.line)
+        chain.pass_on(0)
+        own = pltpu.make_async_copy(src, dst.at[chain.plane], own_sem)
+        own.start()
+        for k in range(1, COLUMNS):
+            chain.arrive(k)
+        own.wait()
+        chain.finish()
+
+    return pl.pallas_call(
+        body,
+        out_shape=jax.ShapeDtypeStruct((COLUMNS,) + tuple(values.shape), values.dtype),
+        in_specs=[ANY],
+        out_specs=ANY,
+        scratch_shapes=[DMA, DMA((COLUMNS, 2)), DMA((COLUMNS,))],
+        compiler_params=comm_params(collective_id),
+        cost_estimate=lasting(cost),
+    )(values)
+
+
 def plane_place(blocks):
     span = blocks // COLUMNS
     width = span // 2
@@ -128,86 +220,100 @@
     return head, rest, core, left, x_peers, y_peer, core_peer
 
 
-def plane_run(srcs, dsts, own_sems, send_sems, recv_sems, pass_sems, land_sems, where):
-    head, rest, core, left, x_peers, y_peer, core_peer = where
-    width, count = len(x_peers), len(srcs)
-    sends, passes = [], []
-
-    def place(n, h, dy, d):
-        half = srcs[n].shape[0] // 2
-        row = head if dy == 0 else 1 - head
-        return dsts[n].at[row, pl.ds(h * half, half), left[d] * 2 + core]
-
-    def held(n, h, dy, d):
-        half = srcs[n].shape[0] // 2
-        return srcs[n].at[pl.ds(h * half, half)] if dy == 0 and d == 0 else place(n, h, dy, d)
-
-    def send(n, h, dy, d, peer, to_dy, to_d):
+class PlaneRun:
+    def __init__(self, srcs, dsts, own_sems, send_sems, recv_sems, pass_sems, land_sems, where):
+        self.srcs, self.dsts = srcs, dsts
+        self.own_sems, self.send_sems, self.recv_sems = own_sems, send_sems, recv_sems
+        self.pass_sems, self.land_sems = pass_sems, land_sems
+        self.head, self.rest, self.core, self.left, self.x_peers, self.y_peer, self.core_peer = (
+            where
+        )
+        self.width = len(self.x_peers)
+        self.sends, self.passes, self.owns = [], [], []
+
+    def place(self, n, h, dy, d):
+        half = self.srcs[n].shape[0] // 2
+        row = self.head if dy == 0 else 1 - self.head
+        return self.dsts[n].at[row, pl.ds(h * half, half), self.left[d] * 2 + self.core]
+
+    def held(self, n, h, dy, d):
+        half = self.srcs[n].shape[0] // 2
+        if dy == 0 and d == 0:
+            return self.srcs[n].at[pl.ds(h * half, half)]
+        return self.place(n, h, dy, d)
+
+    def send(self, n, h, dy, d, peer, to_dy, to_d):
         copy = remote(
-            held(n, h, dy, d),
-            place(n, h, dy, d),
-            send_sems.at[len(sends)],
-            recv_sems.at[n, h, to_dy, to_d],
+            self.held(n, h, dy, d),
+            self.place(n, h, dy, d),
+            self.send_sems.at[len(self.sends)],
+            self.recv_sems.at[n, h, to_dy, to_d],
             peer,
         )
         copy.start()
-        sends.append(copy)
-
-    def hand_over(n, h, dy, d):
+        self.sends.append(copy)
+
+    def hand_over(self, n, h, dy, d):
         copy = remote(
-            held(n, h, dy, d),
-            place(n, h, dy, d),
-            pass_sems.at[n, h, dy, d],
-            land_sems.at[n, h, dy, d],
-            core_peer,
+            self.held(n, h, dy, d),
+            self.place(n, h, dy, d),
+            self.pass_sems.at[n, h, dy, d],
+            self.land_sems.at[n, h, dy, d],
+            self.core_peer,
         )
         copy.start()
-        passes.append(copy)
-
-    def arrived(n, h, dy, d):
-        at = place(n, h, dy, d)
-        remote(at, at, send_sems.at[0], recv_sems.at[n, h, dy, d], y_peer).wait_recv()
-
-    owns = []
-    for n in range(count):
-        own = pltpu.make_async_copy(srcs[n], dsts[n].at[head, :, rest], own_sems.at[n])
+        self.passes.append(copy)
+
+    def arrived(self, n, h, dy, d):
+        at = self.place(n, h, dy, d)
+        remote(
+            at, at, self.send_sems.at[0], self.recv_sems.at[n, h, dy, d], self.y_peer
+        ).wait_recv()
+
+    def first(self, n):
+        own = pltpu.make_async_copy(
+            self.srcs[n], self.dsts[n].at[self.head, :, self.rest], self.own_sems.at[n]
+        )
         own.start()
-        owns.append(own)
-    for n in range(count):
-        for d in range(1, width):
-            send(n, 0, 0, 0, x_peers[d], 0, d)
-        send(n, 1, 0, 0, y_peer, 1, 0)
-        send(n, 0, 0, 0, y_peer, 1, 0)
-        for d in range(1, width):
-            send(n, 1, 0, 0, x_peers[d], 0, d)
-        hand_over(n, 0, 0, 0)
-        hand_over(n, 1, 0, 0)
-    for n in range(count):
-        for d in range(1, width):
-            arrived(n, 0, 0, d)
-            send(n, 0, 0, d, y_peer, 1, d)
-            hand_over(n, 0, 0, d)
-        arrived(n, 1, 1, 0)
-        for d in range(1, width):
-            send(n, 1, 1, 0, x_peers[d], 1, d)
-        hand_over(n, 1, 1, 0)
-    for n in range(count):
-        arrived(n, 0, 1, 0)
-        hand_over(n, 0, 1, 0)
-        for d in range(1, width):
-            arrived(n, 1, 0, d)
-            hand_over(n, 1, 0, d)
-        for d in range(1, width):
-            arrived(n, 0, 1, d)
-            hand_over(n, 0, 1, d)
-            arrived(n, 1, 1, d)
-            hand_over(n, 1, 1, d)
-    for own in owns:
-        own.wait()
-    for copy in passes:
-        copy.wait()
-    for copy in sends:
-        copy.wait_send()
+        self.owns.append(own)
+        for d in range(1, self.width):
+            self.send(n, 0, 0, 0, self.x_peers[d], 0, d)
+        self.send(n, 1, 0, 0, self.y_peer, 1, 0)
+        self.send(n, 0, 0, 0, self.y_peer, 1, 0)
+        for d in range(1, self.width):
+            self.send(n, 1, 0, 0, self.x_peers[d], 0, d)
+        self.hand_over(n, 0, 0, 0)
+        self.hand_over(n, 1, 0, 0)
+
+    def second(self, n):
+        for d in range(1, self.width):
+            self.arrived(n, 0, 0, d)
+            self.send(n, 0, 0, d, self.y_peer, 1, d)
+            self.hand_over(n, 0, 0, d)
+        self.arrived(n, 1, 1, 0)
+        for d in range(1, self.width):
+            self.send(n, 1, 1, 0, self.x_peers[d], 1, d)
+        self.hand_over(n, 1, 1, 0)
+
+    def third(self, n):
+        self.arrived(n, 0, 1, 0)
+        self.hand_over(n, 0, 1, 0)
+        for d in range(1, self.width):
+            self.arrived(n, 1, 0, d)
+            self.hand_over(n, 1, 0, d)
+        for d in range(1, self.width):
+            self.arrived(n, 0, 1, d)
+            self.hand_over(n, 0, 1, d)
+            self.arrived(n, 1, 1, d)
+            self.hand_over(n, 1, 1, d)
+
+    def last(self):
+        for own in self.owns:
+            own.wait()
+        for copy in self.passes:
+            copy.wait()
+        for copy in self.sends:
+            copy.wait_send()
 
 
 def plane_scratch(count, blocks):
@@ -225,27 +331,7 @@
     ]
 
 
-def plane_gather(arrays, blocks, collective_id, cost=16):
-    count = len(arrays)
-
-    def body(*refs):
-        srcs, dsts, sems = refs[:count], refs[count : 2 * count], refs[2 * count :]
-        where = plane_place(blocks)
-        greet(where[4][1:] + [where[5], where[6]])
-        plane_run(srcs, dsts, *sems, where)
-
-    return pl.pallas_call(
-        body,
-        out_shape=plane_shapes(arrays, blocks),
-        in_specs=[ANY] * count,
-        out_specs=[ANY] * count,
-        scratch_shapes=plane_scratch(count, blocks),
-        compiler_params=comm_params(collective_id),
-        cost_estimate=lasting(cost),
-    )(*arrays)
-
-
-def start_gather(packs, tokens, blocks, collective_id, cost=35):
+def start_gather(packs, tokens, blocks, collective_id, cost=28):
     count = len(packs)
 
     def body(*refs):
@@ -255,8 +341,10 @@
         own_sems, send_sems, recv_sems, *plane_sems = refs
         column, plane = column_place(blocks), plane_place(blocks)
         greet(column[2][1:] + plane[4][1:] + [plane[5], plane[6]])
-        waits = [
-            column_start(
+        run = PlaneRun(columns[:count], wholes, *plane_sems, plane)
+
+        def begin(n):
+            return column_start(
                 srcs[n],
                 n == count,
                 columns[n],
@@ -265,12 +353,19 @@
                 recv_sems.at[n],
                 column,
             )
-            for n in range(count + 1)
-        ]
+
+        waits = [begin(0), begin(1)]
         for n in range(count):
             for copy in waits[n]:
                 copy.wait()
-        plane_run(columns[:count], wholes, *plane_sems, plane)
+            if n + 2 <= count:
+                waits.append(begin(n + 2))
+            run.first(n)
+        for n in range(count):
+            run.second(n)
+        for n in range(count):
+            run.third(n)
+        run.last()
         for copy in waits[count]:
             copy.wait()
 
@@ -291,6 +386,195 @@
         cost_estimate=lasting(cost),
     )(*packs, tokens)
     return results[:count], results[-1]
+
+
+def project_gather(source, pack, smalls, heads, scale, blocks, collective_id, cost=22):
+    span = blocks // COLUMNS
+    width = span // 2
+    chained = smalls is not None
+    rows, features = source.shape[-2:]
+    wide = heads * LANES
+    kv_at, tail_at = features, features + wide
+    tail_cols = pack.shape[1] - tail_at
+    own_out = tail_cols - LANES // 2
+    dim = LANES // 2
+    half = rows // 2
+    small_rows = 8 * LAYERS
+    links = 4 * (width - 1) + 2
+
+    def body(*refs):
+        if chained:
+            source_ref, pack_ref, small_ref = refs[:3]
+            refs = refs[3:]
+            small_out = None
+        else:
+            source_ref, pack_ref = refs[:2]
+            small_out, refs = refs[2], refs[3:]
+        column_ref, query_ref, query_w_ref, out_w_ref, kv_ref = refs[:5]
+        kv_own, own_sems, send_sems, recv_sems, pass_sems, land_sems, z_send, z_recv = refs[5:]
+        head, rest, core, left, x_peers, y_peer, core_peer = plane_place(blocks)
+        plane = lax.div(lax.axis_index("blk"), span)
+        sends, passes, owns = [], [], []
+        near = x_peers[1:] + [y_peer, core_peer]
+        if chained:
+            chain = Chain(source_ref, column_ref, z_send, z_recv, blocks)
+            slabs = chain.slabs
+            greet(near, chain.line)
+            chain.pass_on(0)
+        else:
+            slabs = list(range(COLUMNS))
+            greet(near)
+
+        tail = pack_ref[:, tail_at:]
+        low = lax.broadcasted_iota(jnp.int32, (tail_cols, wide), 0)
+        target = lax.broadcasted_iota(jnp.int32, (tail_cols, wide), 1)
+        goal = lax.div(low, dim) * LANES + lax.rem(low, dim)
+        to_low = ((goal == target) & (low < own_out)).astype(jnp.bfloat16)
+        query_w = dot32(tail, to_low).astype(jnp.bfloat16)
+        query_w_ref[...] = query_w
+        out_rows = pack_ref[pl.ds(pl.multiple_of(plane * own_out, 64), own_out), :features]
+        pieces = []
+        for h in range(heads):
+            pieces += [jnp.zeros((dim, features), jnp.bfloat16), out_rows[h * dim : (h + 1) * dim]]
+        out_w_ref[...] = jnp.concatenate(pieces, axis=0)
+        if not chained:
+            small = tail[:, tail_cols - LANES :].astype(jnp.float32).T
+            at = own_out - (tail_cols - LANES)
+            small = small[at : at + small_rows]
+            small_out[...] = small
+
+        def place(k, h, dy, d):
+            row = head if dy == 0 else 1 - head
+            return kv_ref.at[row, slabs[k], left[d] * 2 + core, pl.ds(h * half, half)]
+
+        def held(k, h, dy, d):
+            if dy == 0 and d == 0:
+                return kv_own.at[k, pl.ds(h * half, half)]
+            return place(k, h, dy, d)
+
+        def send(k, h, dy, d, peer, to_dy, to_d):
+            copy = remote(
+                held(k, h, dy, d),
+                place(k, h, dy, d),
+                send_sems.at[len(sends)],
+                recv_sems.at[k, h, to_dy, to_d],
+                peer,
+            )
+            copy.start()
+            sends.append(copy)
+
+        def hand_over(k, h, dy, d):
+            copy = remote(
+                held(k, h, dy, d),
+                place(k, h, dy, d),
+                pass_sems.at[k, h, dy, d],
+                land_sems.at[k, h, dy, d],
+                core_peer,
+            )
+            copy.start()
+            passes.append(copy)
+
+        def arrived(k, h, dy, d):
+            at = place(k, h, dy, d)
+            remote(at, at, send_sems.at[0], recv_sems.at[k, h, dy, d], y_peer).wait_recv()
+
+        def first(k):
+            slab = slabs[k]
+            if not chained:
+                x = source_ref[slab].astype(jnp.float32)
+                xn = (x * unit_scale(x) * small[0:1]).astype(jnp.bfloat16)
+                column_ref[slab] = xn
+            elif k == 0:
+                xn = source_ref[...]
+                column_ref[slab] = xn
+            else:
+                chain.arrive(k)
+                xn = column_ref[slab]
+            kv = dot32(xn, pack_ref[:, kv_at:tail_at])
+            kv_own[k] = kv.astype(jnp.bfloat16)
+            own = pltpu.make_async_copy(
+                kv_own.at[k], kv_ref.at[head, slab, rest], own_sems.at[k]
+            )
+            own.start()
+            owns.append(own)
+            for d in range(1, width):
+                send(k, 0, 0, 0, x_peers[d], 0, d)
+            send(k, 1, 0, 0, y_peer, 1, 0)
+            send(k, 0, 0, 0, y_peer, 1, 0)
+            for d in range(1, width):
+                send(k, 1, 0, 0, x_peers[d], 0, d)
+            hand_over(k, 0, 0, 0)
+            hand_over(k, 1, 0, 0)
+            query = dot32(xn, query_w).astype(jnp.bfloat16).astype(jnp.float32) * scale
+            query_ref[slab] = query.astype(jnp.bfloat16)
+
+        def second(k):
+            for d in range(1, width):
+                arrived(k, 0, 0, d)
+                send(k, 0, 0, d, y_peer, 1, d)
+                hand_over(k, 0, 0, d)
+            arrived(k, 1, 1, 0)
+            for d in range(1, width):
+                send(k, 1, 1, 0, x_peers[d], 1, d)
+            hand_over(k, 1, 1, 0)
+
+        def third(k):
+            arrived(k, 0, 1, 0)
+            hand_over(k, 0, 1, 0)
+            for d in range(1, width):
+                arrived(k, 1, 0, d)
+                hand_over(k, 1, 0, d)
+            for d in range(1, width):
+                arrived(k, 0, 1, d)
+                hand_over(k, 0, 1, d)
+                arrived(k, 1, 1, d)
+                hand_over(k, 1, 1, d)
+
+        for t in range(COLUMNS + 2):
+            if t < COLUMNS:
+                first(t)
+            if 0 <= t - 1 < COLUMNS:
+                second(t - 1)
+            if 0 <= t - 2 < COLUMNS:
+                third(t - 2)
+        for copy in owns + passes:
+            copy.wait()
+        for copy in sends:
+            copy.wait_send()
+        if chained:
+            chain.finish()
+
+    shapes = [
+        jax.ShapeDtypeStruct((COLUMNS, rows, features), jnp.bfloat16),
+        jax.ShapeDtypeStruct((COLUMNS, rows, wide), jnp.bfloat16),
+        jax.ShapeDtypeStruct((features, wide), jnp.bfloat16),
+        jax.ShapeDtypeStruct((wide, features), jnp.bfloat16),
+        jax.ShapeDtypeStruct((2, COLUMNS, span, rows, wide), jnp.bfloat16),
+    ]
+    operands = [source, pack]
+    if chained:
+        operands.append(smalls)
+    else:
+        shapes = [jax.ShapeDtypeStruct((small_rows, features), jnp.float32)] + shapes
+    results = pl.pallas_call(
+        body,
+        out_shape=shapes,
+        in_specs=[VMEM] * len(operands),
+        out_specs=[VMEM] * (len(shapes) - 1) + [ANY],
+        scratch_shapes=[
+            pltpu.VMEM((COLUMNS, rows, wide), jnp.bfloat16),
+            DMA((COLUMNS,)),
+            DMA((COLUMNS * links,)),
+            DMA((COLUMNS, 2, 2, width)),
+            DMA((COLUMNS, 2, 2, width)),
+            DMA((COLUMNS, 2, 2, width)),
+            DMA((COLUMNS, 2)),
+            DMA((COLUMNS,)),
+        ],
+        compiler_params=comm_params(collective_id),
+        cost_estimate=lasting(cost),
+    )(*operands)
+    return list(results) + [smalls] if chained else list(results[1:]) + [results[0]]
 
 
 def plane_reduce(arrays, blocks, collective_id, cost=25):
@@ -461,6 +745,203 @@
             for values in arrays
         ]
     )
+
+
+def reduce_project(dkv_all, dq, query_w, pack, blocks, collective_id, cost=26):
+    span = blocks // COLUMNS
+    width = span // 2
+    rows, wide = dkv_all.shape[3:]
+    half = rows // 2
+    features = query_w.shape[0]
+    kind = dkv_all.dtype
+
+    def body(
+        src,
+        dq_ref,
+        w_ref,
+        pack_ref,
+        dkv_ref,
+        dxn_ref,
+        core_in,
+        summed,
+        xa_in,
+        ya_out,
+        ya_in,
+        yb_in,
+        xb_out,
+        xb_in,
+        share,
+        core_send,
+        core_recv,
+        link_send,
+        link_recv,
+        z_send,
+        z_recv,
+    ):
+        head, _, core, _, x_peers, y_peer, core_peer = plane_place(blocks)
+        plane, planes, z_peers = column_place(blocks)
+        x = lax.div(lax.rem(lax.axis_index("blk"), span), 2)
+        right = [lax.rem(x + d, width) for d in range(width)]
+        greet(x_peers[1:] + [y_peer, core_peer] + z_peers[1:])
+        order = (2, 1, 3, 0)
+        copies = []
+
+        def begin(copy):
+            copy.start()
+            copies.append(copy)
+            return copy
+
+        def wide_of(ref, *at):
+            return ref[at].astype(jnp.float32)
+
+        top, low = pl.ds(0, half), pl.ds(half, half)
+        starts = [
+            begin(
+                remote(
+                    src.at[:, planes[d], :, 1 - core],
+                    core_in.at[k],
+                    core_send.at[k],
+                    core_recv.at[k],
+                    core_peer,
+                )
+            )
+            for k, d in enumerate(order)
+        ]
+        xas, yas, ybs, xbs, z_copies = {}, {}, {}, {}, []
+
+        def first(k):
+            starts[k].wait_recv()
+
+            def step(i, _):
+                yy, xx = lax.div(i, width), lax.rem(i, width)
+                total = wide_of(src, yy, planes[order[k]], xx, core) + wide_of(core_in, k, yy, xx)
+                summed[k, yy, xx] = total.astype(kind)
+                return 0
+
+            lax.fori_loop(0, 2 * width, step, 0)
+            for d in range(1, width):
+                xas[k, d] = begin(
+                    remote(
+                        summed.at[k, :, right[d], top],
+                        xa_in.at[k, d],
+                        link_send.at[k, 0, d],
+                        link_recv.at[k, 0, d],
+                        x_peers[d],
+                    )
+                )
+            ybs[k] = begin(
+                remote(
+                    summed.at[k, 1 - head, :, low],
+                    yb_in.at[k],
+                    link_send.at[k, 1, 0],
+                    link_recv.at[k, 1, 0],
+                    y_peer,
+                )
+            )
+
+        def second(k):
+            total = wide_of(summed, k, 1 - head, x, top)
+            for d in range(1, width):
+                xas[k, d].wait_recv()
+                total = total + wide_of(xa_in, k, d, 1 - head)
+            ya_out[k] = total.astype(kind)
+            yas[k] = begin(
+                remote(
+                    ya_out.at[k],
+                    ya_in.at[k],
+                    link_send.at[k, 0, 0],
+                    link_recv.at[k, 0, 0],
+                    y_peer,
+                )
+            )
+            ybs[k].wait_recv()
+            for d in range(1, width):
+                total = wide_of(summed, k, head, right[d], low) + wide_of(yb_in, k, right[d])
+                xb_out[k, d] = total.astype(kind)
+                xbs[k, d] = begin(
+                    remote(
+                        xb_out.at[k, d],
+                        xb_in.at[k, d],
+                        link_send.at[k, 1, d],
+                        link_recv.at[k, 1, d],
+                        x_peers[d],
+                    )
+                )
+
+        def third(k):
+            slab = planes[order[k]]
+            yas[k].wait_recv()
+            total = wide_of(summed, k, head, x, top) + wide_of(ya_in, k)
+            for d in range(1, width):
+                total = total + wide_of(xa_in, k, d, head)
+            dkv_ref[slab, top] = total.astype(kind)
+            total = wide_of(summed, k, head, x, low) + wide_of(yb_in, k, x)
+            for d in range(1, width):
+                xbs[k, d].wait_recv()
+                total = total + wide_of(xb_in, k, d)
+            dkv_ref[slab, low] = total.astype(kind)
+            part = (
+                dot32(dq_ref[slab], w_ref[...], LAST)
+                + dot32(dkv_ref[slab], pack_ref[:, features : features + wide], LAST)
+            ).astype(kind)
+            if order[k] == 0:
+                dxn_ref[plane] = part
+            else:
+                share[k] = part
+                z_copies.append(
+                    begin(
+                        remote(
+                            share.at[k],
+                            dxn_ref.at[plane],
+                            z_send.at[order[k]],
+                            z_recv.at[order[k]],
+                            z_peers[order[k]],
+                        )
+                    )
+                )
+
+        for t in range(COLUMNS + 2):
+            if t < COLUMNS:
+                first(t)
+            if 0 <= t - 1 < COLUMNS:
+                second(t - 1)
+            if 0 <= t - 2 < COLUMNS:
+                third(t - 2)
+        for copy in z_copies:
+            copy.wait_recv()
+        for copy in copies:
+            copy.wait_send()
+
+    tile = (rows, wide)
+    part = (half, wide)
+    return pl.pallas_call(
+        body,
+        out_shape=[
+            jax.ShapeDtypeStruct((COLUMNS,) + tile, kind),
+            jax.ShapeDtypeStruct((COLUMNS, rows, features), kind),
+        ],
+        in_specs=[VMEM] * 4,
+        out_specs=[VMEM] * 2,
+        scratch_shapes=[
+            pltpu.VMEM((COLUMNS, 2, width) + tile, kind),
+            pltpu.VMEM((COLUMNS, 2, width) + tile, kind),
+            pltpu.VMEM((COLUMNS, width, 2) + part, kind),
+            pltpu.VMEM((COLUMNS,) + part, kind),
+            pltpu.VMEM((COLUMNS,) + part, kind),
+            pltpu.VMEM((COLUMNS, width) + part, kind),
+            pltpu.VMEM((COLUMNS, width) + part, kind),
+            pltpu.VMEM((COLUMNS, width) + part, kind),
+            pltpu.VMEM((COLUMNS, rows, features), kind),
+            DMA((COLUMNS,)),
+            DMA((COLUMNS,)),
+            DMA((COLUMNS, 2, width)),
+            DMA((COLUMNS, 2, width)),
+            DMA((COLUMNS,)),
+            DMA((COLUMNS,)),
+        ],
+        compiler_params=comm_params(collective_id),
+        cost_estimate=lasting(cost),
+    )(dkv_all.reshape((2, COLUMNS, width, 2) + tile), dq, query_w, pack)
 
 
 def expert_dispatch(buffers, blocks, collective_id, cost=15):
@@ -1044,58 +1525,6 @@
     return alphas
 
 
-def project(column, pack, smalls, plane, heads, scale, normed):
-    count, rows, width = column.shape
-    own_out = pack.shape[1] - width - heads * LANES - LANES + LANES // 2
-    kv_at, tail_at = width, width + heads * LANES
-    wide = heads * LANES
-    small_rows = 8 * LAYERS
-
-    def body(plane_ref, column_ref, pack_ref, *refs):
-        if normed:
-            smalls_in, query_ref, kv_ref, query_w_ref, out_w_ref = refs
-        else:
-            xn_ref, query_ref, kv_ref, query_w_ref, out_w_ref, small_ref = refs
-        tail = pack_ref[:, tail_at:]
-        source = lax.broadcasted_iota(jnp.int32, (tail.shape[1], wide), 0)
-        target = lax.broadcasted_iota(jnp.int32, (tail.shape[1], wide), 1)
-        dim = LANES // 2
-        goal = lax.div(source, dim) * LANES + lax.rem(source, dim)
-        to_low = ((goal == target) & (source < own_out)).astype(jnp.bfloat16)
-        query_w = dot32(tail, to_low).astype(jnp.bfloat16)
-        query_w_ref[...] = query_w
-        out_rows = pack_ref[pl.ds(pl.multiple_of(plane_ref[0] * own_out, 64), own_out), :width]
-        pieces = []
-        for h in range(heads):
-            pieces += [jnp.zeros((dim, width), jnp.bfloat16), out_rows[h * dim : (h + 1) * dim]]
-        out_w_ref[...] = jnp.concatenate(pieces, axis=0)
-        if normed:
-            xn = column_ref[...].reshape((count * rows, width))
-        else:
-            small = tail[:, tail.shape[1] - LANES :].astype(jnp.float32).T
-            first = own_out - (tail.shape[1] - LANES)
-            small = small[first : first + small_rows]
-            small_ref[...] = small
-            x = column_ref[...].reshape((count * rows, width)).astype(jnp.float32)
-            xn = (x * unit_scale(x) * small[0:1]).astype(jnp.bfloat16)
-            xn_ref[...] = xn.reshape((count, rows, width))
-        query = dot32(xn, query_w).astype(jnp.bfloat16).astype(jnp.float32) * scale
-        query_ref[...] = query.astype(jnp.bfloat16).reshape((count, rows, wide))
-        kv = dot32(xn, pack_ref[:, kv_at:tail_at]).astype(jnp.bfloat16)
-        kv_ref[...] = kv.reshape((count, rows, wide))
-
-    outs = [
-        make((count, rows, wide), jnp.bfloat16),
-        make((count, rows, wide), jnp.bfloat16),
-        make((width, wide), jnp.bfloat16),
-        make((wide, width), jnp.bfloat16),
-    ]
-    if normed:
-        return [column] + alone(body, outs, 4, plane, column, pack, smalls, scalars=1) + [smalls]
-    outs = [make(column.shape, jnp.bfloat16)] + outs + [make((small_rows, width))]
-    return alone(body, outs, 4, plane, column, pack, scalars=1)
-
-
 def middle(attn, x, pack, smalls, base, picks, slot_gates, grads):
     planes, rows, part = attn.shape
     width = x.shape[1]
@@ -1229,18 +1658,6 @@
     return alone(body, outs, 3, dxn, x, dmid, rows_in, smalls, *more)
 
 
-def column_parts(dq, dkv, query_w, pack, width):
-    rows, wide = dq.shape
-
-    def body(dq_ref, dkv_ref, w_ref, pack_ref, out_ref):
-        out_ref[...] = (
-            dot32(dq_ref[...], w_ref[...], LAST)
-            + dot32(dkv_ref[...], pack_ref[:, width : width + wide], LAST)
-        ).astype(jnp.bfloat16)
-
-    return alone(body, make((rows, width), jnp.bfloat16), 2, dq, dkv, query_w, pack)
-
-
 def pack_grads(column, dq, dkv, attn, dy, small):
     width = column.shape[1]
     kv_cols, own_out = dkv.shape[1], attn.shape[1]
@@ -1316,7 +1733,6 @@
 
     swap = [(0, 1), (1, 0)]
     head_scalar = head_index.reshape((1,)).astype(jnp.int32)
-    plane_scalar = plane.reshape((1,)).astype(jnp.int32)
 
     seg_own = lax.dynamic_index_in_dim(segments, head_index, 0, keepdims=True)
     seg_rows = jnp.concatenate([lax.rem(seg_own, 128), lax.div(seg_own, 128)], axis=0)
@@ -1347,18 +1763,16 @@
                 axis=2,
             )
         )
-    weights, column_tokens = start_gather(packs + [seg_rows], tokens, blocks, 1)
-    packs = [pack.reshape((width, -1)) for pack in weights[:LAYERS]]
+    (seg_all, *packs), column_tokens = start_gather([seg_rows] + packs, tokens, blocks, 1)
+    packs = [pack.reshape((width, -1)) for pack in packs]
     picks, pick_gates, slot_gates, other_gates = route_tables(routes, gates)
 
-    def send_experts(layer, after):
-        held = lax.optimization_barrier(
-            tuple(w[layer] for w in (w_gate, w_up, w_down)) + (after,)
-        )[:3]
-        return held, [lax.ppermute(w, "head", swap) for w in held]
-
-    own_experts, other_experts = [None] * LAYERS, [None] * LAYERS
-    seg_all = weights[LAYERS][..., :2, :].astype(jnp.int32)
+    def send_expert(weight, layer, after):
+        own, _ = lax.optimization_barrier((weight[layer], after))
+        return own, lax.ppermute(own, "head", swap)
+
+    experts = [None] * LAYERS
+    seg_all = seg_all[..., :2, :].astype(jnp.int32)
     seg_all = seg_all[..., 0, :] + 128 * seg_all[..., 1, :]
     seg_query = lax.dynamic_index_in_dim(seg_all, head_index, 0, keepdims=False)
     seg_query = lax.dynamic_index_in_dim(seg_query, rest, 1, keepdims=False)
@@ -1378,13 +1792,14 @@
     for layer in range(LAYERS):
         base = 8 * layer
         last = layer + 1 == LAYERS
-        column, queries, kv_own, query_w, out_rows, small_rows = project(
-            column, packs[layer], small_rows, plane_scalar, heads, scale, layer > 0
-        )
-        (kv_all,) = plane_gather([kv_own], blocks, 4)
+        column, queries, query_w, out_rows, kv_all, small_rows = project_gather(
+            column, packs[layer], small_rows, heads, scale, blocks, 4 if layer == 0 else 2
+        )
         kv_all = kv_all.reshape((positions, wide))
         if layer == 0:
-            own_experts[0], other_experts[0] = send_experts(0, kv_all)
+            experts[layer] = [send_expert(w, layer, kv_all) for w in (w_gate, w_up, w_down)]
+        else:
+            experts[layer] += [send_expert(w, layer, kv_all) for w in (w_up, w_down)]
         attended, attn_col = attend(bounds, queries, kv_all, starts)
         (attn,) = column_exchange([attn_col], [False], blocks, 5, 9)
         mid, *sent = middle(
@@ -1402,7 +1817,7 @@
         flat_in, *dz_in = [rows.reshape((-1, width)) for rows in arrived]
         if last:
             *wgrads, dparts, parts = expert_backward(
-                head_scalar, flat_in, dz_in[0], own_experts[layer], other_experts[layer], True
+                head_scalar, flat_in, dz_in[0], *zip(*experts[layer]), True
             )
             back, dback = expert_return(
                 [rows.reshape((copies, NE, CAP, width)) for rows in (parts, dparts)],
@@ -1411,10 +1826,8 @@
                 24,
             )
         else:
-            own_experts[layer + 1], other_experts[layer + 1] = send_experts(layer + 1, flat_in)
-            parts = expert_forward(
-                head_scalar, flat_in, own_experts[layer], other_experts[layer]
-            )
+            experts[layer + 1] = [send_expert(w_gate, layer + 1, flat_in)]
+            parts = expert_forward(head_scalar, flat_in, *zip(*experts[layer]))
             (back,) = expert_return([parts.reshape((copies, NE, CAP, width))], blocks, 8)
         kept.append(
             (values, column, queries, kv_all, attended, attn_col, query_w, out_rows, mid, flat_in)
@@ -1429,7 +1842,7 @@
             not last,
         )
         if not last:
-            (column,) = column_exchange(normed, [True], blocks, 3)
+            (column,) = normed
     output = values
 
     upstream = cotangent
@@ -1446,8 +1859,7 @@
                 head_scalar,
                 flat_in,
                 dz_in.reshape((-1, width)),
-                own_experts[layer],
-                other_experts[layer],
+                *zip(*experts[layer]),
                 False,
             )
             (dback,) = expert_return([dparts.reshape((copies, NE, CAP, width))], blocks, 8)
@@ -1462,18 +1874,19 @@
             small_rows,
             base,
         )
-        (dy,) = column_exchange([dy], [True], blocks, 3)
+        dy = column_gather(dy, blocks, 3)
         dy, got[1] = lax.optimization_barrier((dy, got[1]))
         dq, dkv_all = attend_back(
             bounds, queries, dy, out_rows, attended, kv_all, starts, scale
         )
         dkv_all, got[2] = lax.optimization_barrier((dkv_all, got[2]))
-        (dkv,) = plane_reduce([dkv_all.reshape((2, COLUMNS, span, token_rows, wide))], blocks, 10)
-        dq = dq.reshape((-1, wide))
-        dkv = dkv.reshape((-1, wide))
-        dxn = column_parts(dq, dkv, query_w, packs[layer], width)
-        (dxn,) = column_exchange(
-            [dxn.reshape((COLUMNS, token_rows, width))], [False], blocks, 11
+        dkv, dxn = reduce_project(
+            dkv_all.reshape((2, COLUMNS, span, token_rows, wide)),
+            dq,
+            query_w,
+            packs[layer],
+            blocks,
+            10,
         )
         before = layer > 0
         upstream, rows, *dz = finish(
@@ -1493,8 +1906,8 @@
         ]
         qkv_part, out_part = pack_grads(
             column.reshape((-1, width)),
-            dq,
-            dkv,
+            dq.reshape((-1, wide)),
+            dkv.reshape((-1, wide)),
             attn_col.reshape((-1, own_out)),
             dy.reshape((-1, width)),
             rows,

time: 590 us -> 552 us (0.936)
  Pallas kernels: 496 us -> 460 us
    pallas_call x2 -> x6, Pallas kernels: 36.6 us -> 146 us  [the longest x2 63.3 us: reduce_project(): pl.pallas_call(body, out_shape=[jax.ShapeDtypeStruct((COLUMNS,) + tile, k...]
    pallas_call x8 -> x3, Pallas kernels: 123 us -> 25.9 us  [column_exchange(): pl.pallas_call(body, out_shape=[jax.ShapeDtypeStruct((COLUMNS,) + slab, v...]
    pallas_call x3 -> x1, Pallas kernels: 53.5 us -> 15.7 us  [plane_reduce(): pl.pallas_call(body, out_shape=[jax.ShapeDtypeStruct(shape, values.dtype)...]
    unnamed x130 -> x106, local copies, waits for them, and re-layouts: 18.3 us -> 23.6 us
    pallas_call x15 -> x11, Pallas kernels: 17.5 us -> 13.1 us  [alone(): pl.pallas_call(body, out_shape=out_shape, in_specs=specs, out_specs=jax.t...]
  transfers between devices with their start and end apart: 13 -> 13, of which waited for: 1 -> 1; matrix products, arithmetic and copies ran while one was open for 4% -> 5% of each run, Pallas kernels for 46% -> 46%
where the time goes in v5:
time: 552 us; the launch traced here: 541 us
  Pallas kernels  460 us (83%)
  local copies, waits for them, and re-layouts  38.3 us (7%)
  other arithmetic  18.3 us (3%)
  starting transfers between devices  15.3 us (3%)
  waiting for transfers between devices  6.79 us (1%)
    pallas_call x2, Pallas kernels, reduce_project(): pl.pallas_call(body, out_shape=[jax.ShapeDtypeStruct((COLUMNS,) + tile, k...  63.3 us
    pallas_call x3, Pallas kernels, expert_dispatch(): pl.pallas_call(body, out_shape=[jax.ShapeDtypeStruct((copies,) + tuple(b....  54.5 us
    pallas_call x3, Pallas kernels, expert_return(): pl.pallas_call(body, out_shape=[jax.ShapeDtypeStruct(a.shape[1:], a.dtype...  52.9 us
    pallas_call x2, Pallas kernels, project_gather(): pl.pallas_call(body, out_shape=shapes, in_specs=[VMEM] * len(operands), o...  45.3 us
    pallas_call x2, Pallas kernels, expert_backward(): pl.pallas_call(body, out_shape=[jax.ShapeDtypeStruct((hidden, features),...  41.7 us
    pallas_call x1, Pallas kernels, start_gather(): pl.pallas_call(body, out_shape=plane_shapes(packs, blocks) + [jax.ShapeDt...  41.3 us
    pallas_call x2, Pallas kernels, attend_back(): pl.pallas_call(body, out_shape=(jax.ShapeDtypeStruct((count, rows, width)...  37.6 us
    pallas_call x2, Pallas kernels, column_gather(): pl.pallas_call(body, out_shape=jax.ShapeDtypeStruct((COLUMNS,) + tuple(va...  37.2 us
  transfers between devices with their start and end apart: 13, of which 1 were waited for; matrix products, arithmetic and copies ran while one was open for 5% of the time, Pallas kernels for 46%

profile of v5, /device:TPU:12, one launch (start us, length us, event | category | flops | bytes accessed | tf_op | source)
XLA Modules:
  0.0 540.6 jit_solution(10010161715475439539)
XLA Ops:
  9.9 41.3 %shard_map.221 = (bf16[2,4,4,16,128]{4,3,2,1,0:T(8,128)(2,1)S(1)}, bf16[2,4,4,24,1408]{4,3,2,1,0:T(8,128)(2,1)S(1)}, bf16[2,4,4,24,1408]{4,3,2,1,0:T(8,128)(2,1)...) custom-call(bf16[4,16,128]{2,1,0:T(8,128)(2,1)S(1)} %broadcast_in_di, ...), custom_call_target="tpu_custom_call" | custom-call | bytes 98000000 | tf_op jit(solution)/shard_map/pallas_call | solution.py:372
  51.9 20.0 %shard_map.222 = (f32[16,768]{1,0:T(8,128)S(1)}, bf16[4,128,768]{2,1,0:T(8,128)(2,1)S(1)}, bf16[4,128,384]{2,1,0:T(8,128)(2,1)S(1)}, bf16[768,384]{1,0:T(8,128)(...) custom-call(bf16[4,128,768]{2,1,0:T(8,128)(2,1)S(1)} %get-tuple-element.108.refs_0_, ...), custom_call_target="tpu_custom_call" | custom-call | bytes 77000000 | tf_op jit(solution)/shard_map/pallas_call | solution.py:559
  82.9 1.9 copy-done.1
  84.8 11.8 %shard_map.223 = (f32[4,128,384]{2,1,0:T(8,128)S(1)}, bf16[4,128,192]{2,1,0:T(8,128)(2,1)S(1)}) custom-call(s32[4,4]{1,0:T(4,128)S(1)} %pad_add_fusion.bounds_ref, bf16[4,128,384]{2,1,0:T(8,128)(2,1)S(1)} %get-tuple-element.110.q_ref, bf16[4096,384]{1,0:T(8,128)(2,1)S(1)} %bitcast.157, s32[4,1,128]{2,1,0:T(1,128)S(1)} %bitcast.195), custom_call_target="tpu_custom_call" | custom-call | bytes 45500000 | tf_op jit(solution)/shard_map/pallas_call | solution.py:1177
  97.5 6.5 %shard_map.224.attn_ref = bf16[4,128,192]{2,1,0:T(8,128)(2,1)S(1)} custom-call(bf16[4,128,192]{2,1,0:T(8,128)(2,1)S(1)} %get-tuple-element.112.refs_0_), custom_call_target="tpu_custom_call" | custom-call | bytes 31500000 | tf_op jit(solution)/shard_map/pallas_call | solution.py:171
  104.9 13.8 %shard_map.227 = bf16[2,8,40,768]{3,2,1,0:T(8,128)(2,1)S(1)} custom-call(bf16[8,40,768]{2,1,0:T(8,128)(2,1)S(1)} %bitcast.186), custom_call_target="tpu_custom_call" | custom-call | bytes 52500000 | tf_op jit(solution)/shard_map/pallas_call | solution.py:1001
  119.7 6.8 %collective-permute-done.2.dx = bf16[1024,384]{1,0:T(8,128)(2,1)} collective-permute-done((bf16[1024,384]{1,0:T(8,128)(2,1)}, bf16[1024,384]{1,0:T(8,128)(2,1)}, u32[]{:S(2)}, u32[]{:S(2)}) %collective-permute-start.2) | collective-permute-done | bytes 786464 | tf_op jit(solution)/shard_map/ppermute | solution.py:1772
  126.4 7.7 %shard_map.228 = bf16[640,768]{1,0:T(8,128)(2,1)S(1)} custom-call(s32[1]{0:T(128)} %bitcast.head_ref, bf16[640,768]{1,0:T(8,128)(2,1)} %bitcast.170, bf16[1024,384]{1,0:T(8,128)(2,1)} %get-tuple-element.117.go, bf16[1024,384]{1,0:T(8,128)(2,1)} %collective-permute-done.gx, bf16[1024,384]{1,0:T(8,128)(2,1)} %get-tuple-element.118.uo, ...), custom_call_target="tpu_custom_call" | custom-call | flops 3019898880 | bytes 6684672 | tf_op jit(solution)/shard_map/pallas_call | solution.py:1333
  134.2 13.2 %shard_map.229 = bf16[8,40,768]{2,1,0:T(8,128)(2,1)S(1)} custom-call(bf16[2,8,40,768]{3,2,1,0:T(8,128)(2,1)S(1)} %bitcast.178), custom_call_target="tpu_custom_call" | custom-call | bytes 52500000 | tf_op jit(solution)/shard_map/pallas_call | solution.py:1071
  148.4 25.3 %shard_map.231 = (bf16[4,128,768]{2,1,0:T(8,128)(2,1)S(1)}, bf16[4,128,384]{2,1,0:T(8,128)(2,1)S(1)}, bf16[768,384]{1,0:T(8,128)(2,1)S(1)}, bf16[384,768]{1,0:T(8,128)(2,1)S(1)}, bf16[2,4,4,128,384]{4,3,2,1,0:T(8,128)(2,1)}) custom-call(bf16[128,768]{1,0:T(8,128)(2,1)S(1)} %get-tuple-element.123.refs_0_, bf16[768,1408]{1,0:T(8,128)(2,1)S(1)} %bitcast.150, ...), custom_call_target="tpu_custom_call" | custom-call | bytes 77000000 | tf_op jit(solution)/shard_map/pallas_call | solution.py:559
  178.2 1.9 copy-done.2
  180.1 11.8 %shard_map.232 = (f32[4,128,384]{2,1,0:T(8,128)S(1)}, bf16[4,128,192]{2,1,0:T(8,128)(2,1)S(1)}) custom-call(s32[4,4]{1,0:T(4,128)S(1)} %pad_add_fusion.bounds_ref, bf16[4,128,384]{2,1,0:T(8,128)(2,1)S(1)} %get-tuple-element.125.q_ref, bf16[4096,384]{1,0:T(8,128)(2,1)S(1)} %bitcast.159, s32[4,1,128]{2,1,0:T(1,128)S(1)} %bitcast.196), custom_call_target="tpu_custom_call" | custom-call | bytes 45500000 | tf_op jit(solution)/shard_map/pallas_call | solution.py:1177
  191.9 10.9 %shard_map.233.attn_ref = bf16[4,128,192]{2,1,0:T(8,128)(2,1)S(1)} custom-call(bf16[4,128,192]{2,1,0:T(8,128)(2,1)S(1)} %get-tuple-element.127.refs_0_), custom_call_target="tpu_custom_call" | custom-call | bytes 31500000 | tf_op jit(solution)/shard_map/pallas_call | solution.py:171
  203.7 24.9 %shard_map.235 = (bf16[2,8,40,768]{3,2,1,0:T(8,128)(2,1)S(1)}, bf16[2,8,40,768]{3,2,1,0:T(8,128)(2,1)S(1)}) custom-call(bf16[8,40,768]{2,1,0:T(8,128)(2,1)S(1)} %bitcast.184, bf16[8,40,768]{2,1,0:T(8,128)(2,1)S(1)} %bitcast.185), custom_call_target="tpu_custom_call" | custom-call | bytes 84000000 | tf_op jit(solution)/shard_map/pallas_call | solution.py:1001
  230.6 21.7 %shard_map.236 = (f32[1024,384]{1,0:T(8,128)}, f32[1024,384]{1,0:T(8,128)}, f32[1024,384]{1,0:T(8,128)}, bf16[1024,384]{1,0:T(8,128)(2,1)}, bf16[1024,384]{1,0:T...) custom-call(s32[1]{0:T(128)} %bitcast.head_ref, ...), custom_call_target="tpu_custom_call" | custom-call | flops 11072962560 | bytes 15728640 | tf_op jit(solution)/shard_map/pallas_call | solution.py:1399
  252.4 2.0 collective-permute-start.7
  256.9 26.0 %shard_map.237 = (bf16[8,40,768]{2,1,0:T(8,128)(2,1)S(1)}, bf16[8,40,768]{2,1,0:T(8,128)(2,1)S(1)}) custom-call(bf16[2,8,40,768]{3,2,1,0:T(8,128)(2,1)S(1)} %bitcast.175, bf16[2,8,40,768]{3,2,1,0:T(8,128)(2,1)S(1)} %bitcast.174), custom_call_target="tpu_custom_call" | custom-call | bytes 84000000 | tf_op jit(solution)/shard_map/pallas_call | solution.py:1071
  285.9 18.8 %shard_map.240.dy_ref = bf16[4,128,768]{2,1,0:T(8,128)(2,1)S(1)} custom-call(bf16[128,768]{1,0:T(8,128)(2,1)S(1)} %get-tuple-element.143.src), custom_call_target="tpu_custom_call" | custom-call | bytes 49000000 | tf_op jit(solution)/shard_map/pallas_call | solution.py:197
  304.8 18.8 %shard_map.241 = (bf16[4,128,384]{2,1,0:T(8,128)(2,1)S(1)}, bf16[4096,384]{1,0:T(8,128)(2,1)S(1)}) custom-call(s32[4,4]{1,0:T(4,128)S(1)} %pad_add_fusion.bounds_ref, bf16[4,128,384]{2,1,0:T(8,128)(2,1)S(1)} %get-tuple-element.125.q_ref, bf16[4,128,768]{2,1,0:T(8,128)(2,1)S(1)} %shard_map.240.dy_ref, bf16[384,768]{1,0:T(8,128)(2,1)S(1)} %copy-done.25, ...), custom_call_target="tpu_custom_call" | custom-call | bytes 70000000 | tf_op jit(solution)/shard_map/pallas_call | solution.py:1279
  325.3 31.5 %shard_map.242 = (bf16[4,128,384]{2,1,0:T(8,128)(2,1)S(1)}, bf16[4,128,768]{2,1,0:T(8,128)(2,1)S(1)}) custom-call(bf16[2,4,2,2,128,384]{5,4,3,2,1,0:T(8,128)(2,1)} %bitcast.163, bf16[4,128,384]{2,1,0:T(8,128)(2,1)S(1)} %get-tuple-element.151.dq_ref, bf16[768,384]{1,0:T(8,128)(2,1)S(1)} %copy-done.23, bf16[768,1408]{1,0:T(8,128)(2,1)S(1)} %bitcast.152), custom_call_target="tpu_custom_call" | custom-call | bytes 91000000 | tf_op jit(solution)/shard_map/pallas_call | solution.py:917
  357.5 15.8 %shard_map.244 = bf16[2,8,40,768]{3,2,1,0:T(8,128)(2,1)S(1)} custom-call(bf16[8,40,768]{2,1,0:T(8,128)(2,1)S(1)} %bitcast.183), custom_call_target="tpu_custom_call" | custom-call | bytes 52500000 | tf_op jit(solution)/shard_map/pallas_call | solution.py:1001
  374.3 20.0 %shard_map.245 = (f32[1024,384]{1,0:T(8,128)}, f32[1024,384]{1,0:T(8,128)}, f32[1024,384]{1,0:T(8,128)}, bf16[1024,384]{1,0:T(8,128)(2,1)S(1)}, bf16[1024,384]{1...) custom-call(s32[1]{0:T(128)} %bitcast.head_ref, bf16[640,768]{1,0:T(8,128)(2,1)} %bitcast.171, ...), custom_call_target="tpu_custom_call" | custom-call | flops 11072962560 | bytes 15728640 | tf_op jit(solution)/shard_map/pallas_call | solution.py:1399
  399.4 13.8 %shard_map.246 = bf16[8,40,768]{2,1,0:T(8,128)(2,1)S(1)} custom-call(bf16[2,8,40,768]{3,2,1,0:T(8,128)(2,1)S(1)} %bitcast.173), custom_call_target="tpu_custom_call" | custom-call | bytes 52500000 | tf_op jit(solution)/shard_map/pallas_call | solution.py:1071
  414.6 2.6 add_bitcast_fusion.2
  417.2 2.5 add_bitcast_fusion
  421.2 18.4 %shard_map.248.dy_ref = bf16[4,128,768]{2,1,0:T(8,128)(2,1)S(1)} custom-call(bf16[128,768]{1,0:T(8,128)(2,1)S(1)} %get-tuple-element.161.src), custom_call_target="tpu_custom_call" | custom-call | bytes 49000000 | tf_op jit(solution)/shard_map/pallas_call | solution.py:197
  439.6 18.8 %shard_map.249 = (bf16[4,128,384]{2,1,0:T(8,128)(2,1)S(1)}, bf16[4096,384]{1,0:T(8,128)(2,1)S(1)}) custom-call(s32[4,4]{1,0:T(4,128)S(1)} %pad_add_fusion.bounds_ref, bf16[4,128,384]{2,1,0:T(8,128)(2,1)S(1)} %get-tuple-element.110.q_ref, bf16[4,128,768]{2,1,0:T(8,128)(2,1)S(1)} %shard_map.248.dy_ref, bf16[384,768]{1,0:T(8,128)(2,1)S(1)} %copy-done.21, ...), custom_call_target="tpu_custom_call" | custom-call | bytes 70000000 | tf_op jit(solution)/shard_map/pallas_call | solution.py:1279
  460.1 31.8 %shard_map.250 = (bf16[4,128,384]{2,1,0:T(8,128)(2,1)S(1)}, bf16[4,128,768]{2,1,0:T(8,128)(2,1)S(1)}) custom-call(bf16[2,4,2,2,128,384]{5,4,3,2,1,0:T(8,128)(2,1)} %bitcast.162, bf16[4,128,384]{2,1,0:T(8,128)(2,1)S(1)} %get-tuple-element.169.dq_ref, bf16[768,384]{1,0:T(8,128)(2,1)S(1)} %get-tuple-element.170.w_ref, bf16[768,1408]{1,0:T(8,128)(2,1)S(1)} %bitcast.155), custom_call_target="tpu_custom_call" | custom-call | bytes 91000000 | tf_op jit(solution)/shard_map/pallas_call | solution.py:917
  494.5 15.7 %shard_map.254 = (bf16[4,24,640]{2,1,0:T(8,128)(2,1)S(1)}, bf16[2,24,384]{2,1,0:T(8,128)(2,1)S(1)}, bf16[4,24,640]{2,1,0:T(8,128)(2,1)S(1)}, bf16[2,24,384]{2,1,0:T(8,128)(2,1)S(1)}) custom-call(bf16[2,4,2,2,24,640]{5,4,3,2,1,0:T(8,128)(2,1)S(1)} %bitcast.177, bf16[2,2,2,2,24,384]{5,4,3,2,1,0:T(8,128)(2,1)S(1)} %bitcast.194, ...), custom_call_target="tpu_custom_call" | custom-call | bytes 70000000 | tf_op jit(solution)/shard_map/pallas_call | solution.py:731
  510.2 8.6 %shard_map.255 = (bf16[4,24,640]{2,1,0:T(8,128)(2,1)S(1)}, bf16[4,24,640]{2,1,0:T(8,128)(2,1)S(1)}) custom-call(bf16[4,24,640]{2,1,0:T(8,128)(2,1)S(1)} %get-tuple-element.185.refs_0_, bf16[4,24,640]{2,1,0:T(8,128)(2,1)S(1)} %get-tuple-element.186.refs_1_), custom_call_target="tpu_custom_call" | custom-call | bytes 35000000 | tf_op jit(solution)/shard_map/pallas_call | solution.py:171
  520.5 4.4 collective-permute-start.12
  529.1 1.9 pad_maximum_fusion
  (211 shorter events, 67.9 us)
Async XLA Ops:
  51.9 21.1 %copy-start.35 = (bf16[2,1024,384]{2,1,0:T(8,128)(2,1)S(1)}, bf16[2,1024,384]{2,1,0:T(8,128)(2,1)}, u32[]{:S(2)}) copy-start(bf16[2,1024,384]{2,1,0:T(8,128)(2,1)} %param.25) | copy-start | bytes 4718596
  72.0 3.5 copy-start.36
  72.0 47.7 %collective-permute-start = (bf16[1024,384]{1,0:T(8,128)(2,1)}, bf16[1024,384]{1,0:T(8,128)(2,1)}, u32[]{:S(2)}, u32[]{:S(2)}) collective-permute-start(bf16[1024,384]{1,0:T(8,128)(2,1)} %get-tuple-element.117.go), channel_id=1, source_target_pairs={{0,16},{16,0},{1,17},{17,1},{2,18},{18,2},{3,19},{19,3},{4,20},{20... | collective-permute-start | bytes 2359304 | tf_op jit(solution)/shard_map/ppermute | solution.py:1772
  74.3 3.6 copy-start.49
  74.3 45.4 %collective-permute-start.1 = (bf16[1024,384]{1,0:T(8,128)(2,1)}, bf16[1024,384]{1,0:T(8,128)(2,1)}, u32[]{:S(2)}, u32[]{:S(2)}) collective-permute-start(bf16[1024,384]{1,0:T(8,128)(2,1)} %get-tuple-element.118.uo), channel_id=1, source_target_pairs={{0,16},{16,0},{1,17},{17,1},{2,18},{18,2},{3,19},{19,3},{4,20},{20... | collective-permute-start | bytes 2359304 | tf_op jit(solution)/shard_map/ppermute | solution.py:1772
  76.8 49.6 %collective-permute-start.2 = (bf16[1024,384]{1,0:T(8,128)(2,1)}, bf16[1024,384]{1,0:T(8,128)(2,1)}, u32[]{:S(2)}, u32[]{:S(2)}) collective-permute-start(bf16[1024,384]{1,0:T(8,128)(2,1)} %get-tuple-element.119.do), channel_id=1, source_target_pairs={{0,16},{16,0},{1,17},{17,1},{2,18},{18,2},{3,19},{19,3},{4,20},{20... | collective-permute-start | bytes 2359304 | tf_op jit(solution)/shard_map/ppermute | solution.py:1772
  104.1 14.7 %copy-start.16 = (bf16[1024,384]{1,0:T(8,128)(2,1)S(1)}, bf16[1024,384]{1,0:T(8,128)(2,1)}, u32[]{:S(2)}) copy-start(bf16[1024,384]{1,0:T(8,128)(2,1)} %get-tuple-element.133.go) | copy-start | bytes 2359300
  118.7 7.7 %copy-start.6 = (bf16[2,8,40,768]{3,2,1,0:T(8,128)(2,1)}, bf16[2,8,40,768]{3,2,1,0:T(8,128)(2,1)S(1)}, u32[]{:S(2)}) copy-start(bf16[2,8,40,768]{3,2,1,0:T(8,128)(2,1)S(1)} %shard_map.227) | copy-start | bytes 2949124
  118.8 111.8 %collective-permute-start.3 = (bf16[1024,384]{1,0:T(8,128)(2,1)S(1)}, bf16[1024,384]{1,0:T(8,128)(2,1)S(1)}, u32[]{:S(2)}, u32[]{:S(2)}) collective-permute-start(bf16[1024,384]{1,0:T(8,128)(2,1)S(1)} %copy-done.16), channel_id=1, source_target_pairs={{0,16},{16,0},{1,17},{17,1},{2,18},{18,2},{3,19},{19,3},{4,20},{20... | collective-permute-start | bytes 2359304 | tf_op jit(solution)/shard_map/ppermute | solution.py:1772
  134.1 14.2 %copy-start = (bf16[2,4,4,24,1408]{4,3,2,1,0:T(8,128)(2,1)S(1)}, bf16[2,4,4,24,1408]{4,3,2,1,0:T(8,128)(2,1)}, u32[]{:S(2)}) copy-start(bf16[2,4,4,24,1408]{4,3,2,1,0:T(8,128)(2,1)} %get-tuple-element.124) | copy-start | bytes 6488068
  147.4 28.8 %copy-start.17 = (bf16[1024,384]{1,0:T(8,128)(2,1)S(1)}, bf16[1024,384]{1,0:T(8,128)(2,1)}, u32[]{:S(2)}) copy-start(bf16[1024,384]{1,0:T(8,128)(2,1)} %get-tuple-element.134.uo) | copy-start | bytes 2359300
  147.4 29.6 %copy-start.43 = (bf16[1024,384]{1,0:T(8,128)(2,1)S(1)}, bf16[1024,384]{1,0:T(8,128)(2,1)}, u32[]{:S(2)}) copy-start(bf16[1024,384]{1,0:T(8,128)(2,1)} %get-tuple-element.135.do) | copy-start | bytes 2359300
  176.2 54.4 %collective-permute-start.4 = (bf16[1024,384]{1,0:T(8,128)(2,1)S(1)}, bf16[1024,384]{1,0:T(8,128)(2,1)S(1)}, u32[]{:S(2)}, u32[]{:S(2)}) collective-permute-start(bf16[1024,384]{1,0:T(8,128)(2,1)S(1)} %copy-done.17), channel_id=1, source_target_pairs={{0,16},{16,0},{1,17},{17,1},{2,18},{18,2},{3,19},{19,3},{4,20},{20... | collective-permute-start | bytes 2359304 | tf_op jit(solution)/shard_map/ppermute | solution.py:1772
  177.0 53.6 %collective-permute-start.5 = (bf16[1024,384]{1,0:T(8,128)(2,1)S(1)}, bf16[1024,384]{1,0:T(8,128)(2,1)}, u32[]{:S(2)}, u32[]{:S(2)}) collective-permute-start(bf16[1024,384]{1,0:T(8,128)(2,1)S(1)} %copy-done.43), channel_id=1, source_target_pairs={{0,16},{16,0},{1,17},{17,1},{2,18},{18,2},{3,19},{19,3},{4,20},{20... | collective-permute-start | bytes 2359304 | tf_op jit(solution)/shard_map/ppermute | solution.py:1772
  180.1 22.7 %copy-start.13 = (bf16[128,768]{1,0:T(8,128)(2,1)S(1)}, bf16[128,768]{1,0:T(8,128)(2,1)}, u32[]{:S(2)}) copy-start(bf16[128,768]{1,0:T(8,128)(2,1)} %up_ref.1) | copy-start | bytes 589828
  230.6 52.3 %copy-start.26 = (f32[128,128]{1,0:T(8,128)S(1)}, f32[128,128]{1,0:T(8,128)}, u32[]{:S(2)}) copy-start(f32[128,128]{1,0:T(8,128)} %get-tuple-element.258.other_ref) | copy-start | bytes 196612
  252.3 32.1 %collective-permute-start.6 = (bf16[1024,384]{1,0:T(8,128)(2,1)}, bf16[1024,384]{1,0:T(8,128)(2,1)S(1)}, u32[]{:S(2)}, u32[]{:S(2)}) collective-permute-start(bf16[1024,384]{1,0:T(8,128)(2,1)} %get-tuple-element.141), channel_id=1, source_target_pairs={{0,16},{16,0},{1,17},{17,1},{2,18},{18,2},{3,19},{19,3},{4,20},{20... | collective-permute-start | bytes 2359304 | tf_op jit(solution)/shard_map/ppermute | solution.py:1866
  252.4 52.3 %collective-permute-start.7 = (bf16[1024,384]{1,0:T(8,128)(2,1)S(1)}, bf16[1024,384]{1,0:T(8,128)(2,1)}, u32[]{:S(2)}, u32[]{:S(2)}) collective-permute-start(bf16[1024,384]{1,0:T(8,128)(2,1)S(1)} %get-tuple-element.144), channel_id=1, source_target_pairs={{0,16},{16,0},{1,17},{17,1},{2,18},{18,2},{3,19},{19,3},{4,20},{20... | collective-permute-start | bytes 2359304 | tf_op jit(solution)/shard_map/ppermute | solution.py:1866
  254.4 70.8 %collective-permute-start.8 = (bf16[1024,384]{1,0:T(8,128)(2,1)S(1)}, bf16[1024,384]{1,0:T(8,128)(2,1)}, u32[]{:S(2)}, u32[]{:S(2)}) collective-permute-start(bf16[1024,384]{1,0:T(8,128)(2,1)S(1)} %get-tuple-element.149), channel_id=1, source_target_pairs={{0,16},{16,0},{1,17},{17,1},{2,18},{18,2},{3,19},{19,3},{4,20},{20... | collective-permute-start | bytes 2359304 | tf_op jit(solution)/shard_map/ppermute | solution.py:1866
  282.9 21.9 %copy-start.25 = (bf16[384,768]{1,0:T(8,128)(2,1)S(1)}, bf16[384,768]{1,0:T(8,128)(2,1)}, u32[]{:S(2)}) copy-start(bf16[384,768]{1,0:T(8,128)(2,1)} %copy-done.24) | copy-start | bytes 1769476
  284.5 20.3 %copy-start.46 = (bf16[1024,384]{1,0:T(8,128)(2,1)}, bf16[1024,384]{1,0:T(8,128)(2,1)S(1)}, u32[]{:S(2)}) copy-start(bf16[1024,384]{1,0:T(8,128)(2,1)S(1)} %collective-permute-done.6) | copy-start | bytes 2359300
  304.8 20.5 %copy-start.23 = (bf16[768,384]{1,0:T(8,128)(2,1)S(1)}, bf16[768,384]{1,0:T(8,128)(2,1)}, u32[]{:S(2)}) copy-start(bf16[768,384]{1,0:T(8,128)(2,1)} %copy-done.22) | copy-start | bytes 1769476
  374.3 23.6 %copy-start.42 = (f32[1024,384]{1,0:T(8,128)S(1)}, f32[1024,384]{1,0:T(8,128)}, u32[]{:S(2)}) copy-start(f32[1024,384]{1,0:T(8,128)} %get-tuple-element.193) | copy-start | bytes 4718596
  374.3 23.6 %copy-start.47 = (bf16[1024,384]{1,0:T(8,128)(2,1)S(1)}, bf16[1024,384]{1,0:T(8,128)(2,1)}, u32[]{:S(2)}) copy-start(bf16[1024,384]{1,0:T(8,128)(2,1)} %copy-done.46) | copy-start | bytes 2359300
  394.2 25.5 %collective-permute-start.9 = (bf16[1024,384]{1,0:T(8,128)(2,1)S(1)}, bf16[1024,384]{1,0:T(8,128)(2,1)}, u32[]{:S(2)}, u32[]{:S(2)}) collective-permute-start(bf16[1024,384]{1,0:T(8,128)(2,1)S(1)} %get-tuple-element.158), channel_id=1, source_target_pairs={{0,16},{16,0},{1,17},{17,1},{2,18},{18,2},{3,19},{19,3},{4,20},{20... | collective-permute-start | bytes 2359304 | tf_op jit(solution)/shard_map/ppermute | solution.py:1866
  395.8 43.8 %collective-permute-start.10 = (bf16[1024,384]{1,0:T(8,128)(2,1)S(1)}, bf16[1024,384]{1,0:T(8,128)(2,1)}, u32[]{:S(2)}, u32[]{:S(2)}) collective-permute-start(bf16[1024,384]{1,0:T(8,128)(2,1)S(1)} %get-tuple-element.162), channel_id=1, source_target_pairs={{0,16},{16,0},{1,17},{17,1},{2,18},{18,2},{3,19},{19,3},{4,20},{20... | collective-permute-start | bytes 2359304 | tf_op jit(solution)/shard_map/ppermute | solution.py:1866
  396.3 63.7 %collective-permute-start.11 = (bf16[1024,384]{1,0:T(8,128)(2,1)S(1)}, bf16[1024,384]{1,0:T(8,128)(2,1)S(1)}, u32[]{:S(2)}, u32[]{:S(2)}) collective-permute-start(bf16[1024,384]{1,0:T(8,128)(2,1)S(1)} %get-tuple-element.167), channel_id=1, source_target_pairs={{0,16},{16,0},{1,17},{17,1},{2,18},{18,2},{3,19},{19,3},{4,20},{20... | collective-permute-start | bytes 2359304 | tf_op jit(solution)/shard_map/ppermute | solution.py:1866
  399.1 14.1 %copy-start.19 = (bf16[4,128,768]{2,1,0:T(8,128)(2,1)S(1)}, bf16[4,128,768]{2,1,0:T(8,128)(2,1)}, u32[]{:S(2)}) copy-start(bf16[4,128,768]{2,1,0:T(8,128)(2,1)} %copy-done.18) | copy-start | bytes 2359300
  419.7 19.9 %copy-start.12 = (f32[4,128,384]{2,1,0:T(8,128)S(1)}, f32[4,128,384]{2,1,0:T(8,128)}, u32[]{:S(2)}) copy-start(f32[4,128,384]{2,1,0:T(8,128)} %copy-done.11) | copy-start | bytes 2359300
  419.7 19.9 %copy-start.21 = (bf16[384,768]{1,0:T(8,128)(2,1)S(1)}, bf16[384,768]{1,0:T(8,128)(2,1)}, u32[]{:S(2)}) copy-start(bf16[384,768]{1,0:T(8,128)(2,1)} %copy-done.20) | copy-start | bytes 1769476
  460.1 31.8 %copy-start.44 = (bf16[1024,384]{1,0:T(8,128)(2,1)}, bf16[1024,384]{1,0:T(8,128)(2,1)S(1)}, u32[]{:S(2)}) copy-start(bf16[1024,384]{1,0:T(8,128)(2,1)S(1)} %collective-permute-done.11) | copy-start | bytes 2359300
  520.5 19.0 %collective-permute-start.12 = (bf16[2,24,768]{2,1,0:T(8,128)(2,1)S(1)}, bf16[2,24,768]{2,1,0:T(8,128)(2,1)S(1)}, u32[]{:S(2)}, u32[]{:S(2)}) collective-permute-start(bf16[2,24,768]{2,1,0:T(8,128)(2,1)S(1)} %bitcast.203), channel_id=1, source_target_pairs={{0,0},{1,1},{2,2},{3,3},{4,8},{5,9},{6,10},{7,11},{8,16},{9,17},{1... | collective-permute-start | bytes 221192 | tf_op jit(solution)/shard_map/ppermute | solution.py:1939
  (32 other events, 49.1 us)

commit v6 on v5

--- a/solution.py
+++ b/solution.py
@@ -14,7 +14,7 @@
 ANY = pl.BlockSpec(memory_space=pl.ANY)
 VMEM = pl.BlockSpec(memory_space=pltpu.VMEM)
 DMA = pltpu.SemaphoreType.DMA
-VMEM_BYTES = 48 * 1024 * 1024
+VMEM_BYTES = 60 * 1024 * 1024
 
 
 def greet(peers, line=()):
@@ -944,145 +944,6 @@
     )(dkv_all.reshape((2, COLUMNS, width, 2) + tile), dq, query_w, pack)
 
 
-def expert_dispatch(buffers, blocks, collective_id, cost=15):
-    copies = blocks // NE
-    count = len(buffers)
-
-    def body(*refs):
-        srcs, dsts = refs[:count], refs[count : 2 * count]
-        own_sems, send_sems, recv_sems, pass_sems, land_sems = refs[2 * count :]
-        head, blk = lax.axis_index("head"), lax.axis_index("blk")
-        expert, piece = lax.div(blk, copies), lax.rem(blk, copies)
-        ahead = [lax.rem(expert + d, NE) for d in range(NE)]
-        behind = [lax.rem(expert - d + NE, NE) for d in range(NE)]
-        peers = [(head, ahead[d] * copies + piece) for d in range(NE)]
-        siblings = [(head, expert * copies + lax.rem(piece + k, copies)) for k in range(copies)]
-        greet(peers[1:] + siblings[1:])
-        sends, passes = [], []
-        for n in range(count):
-            own = pltpu.make_async_copy(
-                srcs[n].at[expert], dsts[n].at[piece, expert], own_sems.at[n]
-            )
-            own.start()
-            passes.append(own)
-        for n in range(count):
-            for d in (4, 3, 5, 2, 6, 1, 7):
-                copy = remote(
-                    srcs[n].at[ahead[d]],
-                    dsts[n].at[piece, expert],
-                    send_sems.at[n, d],
-                    recv_sems.at[n, d],
-                    peers[d],
-                )
-                copy.start()
-                sends.append(copy)
-        for n in range(count):
-            for d in (0, 1, 7, 2, 6, 3, 5, 4):
-                place = dsts[n].at[piece, behind[d]]
-                if d > 0:
-                    remote(
-                        place, place, send_sems.at[n, d], recv_sems.at[n, d], peers[d]
-                    ).wait_recv()
-                for k in range(1, copies):
-                    copy = remote(
-                        place if d > 0 else srcs[n].at[expert],
-                        place,
-                        pass_sems.at[n, k, d],
-                        land_sems.at[n, k, d],
-                        siblings[k],
-                    )
-                    copy.start()
-                    passes.append(copy)
-        for copy in passes:
-            copy.wait()
-        for copy in sends:
-            copy.wait_send()
-
-    return pl.pallas_call(
-        body,
-        out_shape=[
-            jax.ShapeDtypeStruct((copies,) + tuple(b.shape), b.dtype) for b in buffers
-        ],
-        in_specs=[ANY] * count,
-        out_specs=[ANY] * count,
-        scratch_shapes=[DMA((count,))]
-        + [DMA((count, NE))] * 2
-        + [DMA((count, copies, NE))] * 2,
-        compiler_params=comm_params(collective_id),
-        cost_estimate=lasting(cost),
-    )(*buffers)
-
-
-def expert_return(arrays, blocks, collective_id, cost=15):
-    copies = blocks // NE
-    count = len(arrays)
-
-    def body(*refs):
-        srcs, dsts = refs[:count], refs[count : 2 * count]
-        sib_ins, totals = refs[2 * count : 3 * count], refs[3 * count : 4 * count]
-        own_sems, send_sems, recv_sems, pass_sems, land_sems = refs[4 * count :]
-        head, blk = lax.axis_index("head"), lax.axis_index("blk")
-        expert, piece = lax.div(blk, copies), lax.rem(blk, copies)
-        ahead = [lax.rem(expert + d, NE) for d in range(NE)]
-        peers = [(head, ahead[d] * copies + piece) for d in range(NE)]
-        places = [lax.rem(piece + k, copies) for k in range(copies)]
-        siblings = [(head, expert * copies + places[k]) for k in range(copies)]
-        greet(peers[1:] + siblings[1:])
-        order = (4, 3, 5, 2, 6, 1, 7, 0)
-        passes, sends = {}, []
-        for n in range(count):
-            for d in order:
-                for k in range(1, copies):
-                    copy = remote(
-                        srcs[n].at[places[k], ahead[d]],
-                        sib_ins[n].at[k, ahead[d]],
-                        pass_sems.at[n, k, d],
-                        land_sems.at[n, k, d],
-                        siblings[k],
-                    )
-                    copy.start()
-                    passes[n, k, d] = copy
-        for n in range(count):
-            for d in order:
-                value = srcs[n][piece, ahead[d]].astype(jnp.float32)
-                for k in range(1, copies):
-                    passes[n, k, d].wait_recv()
-                    value = value + sib_ins[n][k, ahead[d]].astype(jnp.float32)
-                totals[n][ahead[d]] = value.astype(arrays[n].dtype)
-                if d > 0:
-                    copy = remote(
-                        totals[n].at[ahead[d]],
-                        dsts[n].at[expert],
-                        send_sems.at[n, d],
-                        recv_sems.at[n, d],
-                        peers[d],
-                    )
-                else:
-                    copy = pltpu.make_async_copy(
-                        totals[n].at[expert], dsts[n].at[expert], own_sems.at[n]
-                    )
-                copy.start()
-                sends.append(copy)
-        for copy in sends:
-            copy.wait()
-        for copy in passes.values():
-            copy.wait_send()
-
-    return pl.pallas_call(
-        body,
-        out_shape=[jax.ShapeDtypeStruct(a.shape[1:], a.dtype) for a in arrays],
-        in_specs=[VMEM] * count,
-        out_specs=[ANY] * count,
-        scratch_shapes=[pltpu.VMEM(a.shape, a.dtype) for a in arrays]
-        + [pltpu.VMEM(a.shape[1:], a.dtype) for a in arrays]
-        + [DMA((count,))]
-        + [DMA((count, NE))] * 2
-        + [DMA((count, copies, NE))] * 2,
-        compiler_params=comm_params(collective_id),
-        cost_estimate=lasting(cost),
-    )(*arrays)
-
-
 NEGATIVE = -1e30
 EPSILON = 1e-06
 KEYS = 1024
@@ -1301,120 +1162,350 @@
     )(bounds, queries, dy, out_rows, kept, kv_all, starts)
 
 
-def expert_forward(head, rows_in, own, other):
-    count, width = rows_in.shape
+def experts_exchange(sent, saved, own, other, blocks, collective_id, forward, backward, cost):
+    copies = blocks // NE
+    half = NE // 2
+    slots, width = sent[0].shape[1:]
     hidden, features = own[0].shape
     tile = min(hidden, 256)
-    steps = hidden // tile
-
-    def body(head_ref, x_ref, go, gx, uo, ux, do, dx, out_ref, acc_ref):
-        i = pl.program_id(0)
-        mine = pl.ds(pl.multiple_of(head_ref[0] * features, LANES), features)
-        rest = pl.ds(pl.multiple_of((1 - head_ref[0]) * features, LANES), features)
-        xo, xx = x_ref[:, mine], x_ref[:, rest]
-        gate = dot32(xo, go[...], LAST) + dot32(xx, gx[...], LAST)
-        up = dot32(xo, uo[...], LAST) + dot32(xx, ux[...], LAST)
-        act = (jax.nn.silu(gate) * up).astype(jnp.bfloat16)
-
-        @pl.when(i == 0)
-        def _():
-            acc_ref[...] = jnp.zeros_like(acc_ref)
-
-        acc_ref[:, mine] += dot32(act, do[...])
-        acc_ref[:, rest] += dot32(act, dx[...])
-
-        @pl.when(i == steps - 1)
-        def _():
-            out_ref[...] = acc_ref[...].astype(jnp.bfloat16)
-
-    whole = pl.BlockSpec((count, width), lambda i, h: (0, 0))
-    piece = pl.BlockSpec((tile, features), lambda i, h: (i, 0))
-    weights = [w for pair in zip(own, other) for w in pair]
+    tiles = hidden // tile
+    count = len(sent)
+    homes_count = int(forward) + int(backward)
+    total_rows = copies * NE * slots
+    kind = sent[0].dtype
+    sizes = (half // 2, half // 2, half)
+    first_rows = [copies * slots * at for at in (0, half // 2, half)]
+    most_rows = copies * slots * half
+    plain = (((1,), (0,)), ((), ()))
+
+    def body(*refs):
+        refs = list(refs)
+
+        def take(n):
+            taken = refs[:n]
+            del refs[:n]
+            return taken
+
+        srcs = take(count)
+        saved_ref = take(1)[0] if not forward else None
+        weight_refs = take(6)
+        homes = take(homes_count)
+        lands = take(1) if not backward else []
+        keeps, aways = (take(3), take(3)) if backward else ([], [])
+        if backward:
+            lands = lands + take(count)
+        weights = take(6)
+        parts, sib_ins, totals = take(homes_count), take(homes_count), take(homes_count)
+        accs = take(homes_count)
+        rows_x = take(1)[0]
+        if backward:
+            rows_z, act_ref, dgate_ref, dup_ref, keep_ref, away_ref = take(6)
+            if not forward:
+                gate_ref, up_ref = take(2)
+            out_sems = take(1)[0]
+        load_sems, own_sems, send_sems, recv_sems, pass_sems, land_sems = take(6)
+        home_own, home_send, home_recv, part_send, part_recv = take(5)
+
+        head, blk = lax.axis_index("head"), lax.axis_index("blk")
+        expert, piece = lax.div(blk, copies), lax.rem(blk, copies)
+        near = lax.div(expert, half) * half
+        far = half - near
+        places = [lax.rem(piece + k, copies) for k in range(copies)]
+        siblings = [(head, expert * copies + places[k]) for k in range(copies)]
+        others = [lax.rem(expert + d, NE) for d in range(NE)]
+        greet([(head, e * copies + piece) for e in others[1:]] + siblings[1:])
+        mine = pl.ds(pl.multiple_of(head * features, LANES), features)
+        rest = pl.ds(pl.multiple_of((1 - head) * features, LANES), features)
+        steps = [(far, sizes[0]), (far + sizes[0], sizes[1]), (near, sizes[2])]
+
+        def sending(n, e):
+            return remote(
+                srcs[n].at[e],
+                lands[n].at[piece, expert],
+                send_sems.at[n, e],
+                recv_sems.at[n, expert],
+                (head, e * copies + piece),
+            )
+
+        owns = []
+        for n in range(count):
+            copy = pltpu.make_async_copy(
+                srcs[n].at[expert], lands[n].at[piece, expert], own_sems.at[n]
+            )
+            copy.start()
+            owns.append(copy)
+        def each(t, copy_of, arrays, act):
+            first, size = steps[t]
+            for j in range(size):
+                for n in range(arrays):
+                    if t < 2:
+                        act(copy_of(n, first + j))
+                    else:
+
+                        @pl.when(first + j != expert)
+                        def _():
+                            act(copy_of(n, first + j))
+
+        def send(t):
+            each(t, sending, count, lambda copy: copy.start())
+
+        def sent_out(t):
+            each(t, sending, count, lambda copy: copy.wait_send())
+
+        for t in range(3):
+            send(t)
+        loads = []
+        for n in range(6):
+            copy = pltpu.make_async_copy(weight_refs[n], weights[n], load_sems.at[n])
+            copy.start()
+            loads.append(copy)
+        go, gx, uo, ux, do, dx = weights
+        passes, exchanges = [], {}
+
+        def arrive(t):
+            first, size = steps[t]
+            waits = []
+            if t == 2:
+                for copy in owns:
+                    copy.wait()
+            for j in range(size):
+                e = first + j
+                for n in range(count):
+                    place = lands[n].at[piece, e]
+
+                    @pl.when(e != expert)
+                    def _():
+                        remote(
+                            place, place, send_sems.at[n, e], recv_sems.at[n, e], siblings[0]
+                        ).wait_recv()
+
+                    for k in range(1, copies):
+                        copy = remote(
+                            place,
+                            place,
+                            pass_sems.at[n, k, e],
+                            land_sems.at[n, k, e],
+                            siblings[k],
+                        )
+                        copy.start()
+                        waits.append(copy)
+            for copy in waits:
+                copy.wait_recv()
+            passes.extend(waits)
+
+        def flat(ref, t):
+            first, size = steps[t]
+            value = ref[:, pl.ds(first, size)].astype(jnp.float32)
+            return value.reshape((copies * size * slots, width)).astype(kind)
+
+        def span_of(t):
+            return slice(first_rows[t], first_rows[t] + copies * steps[t][1] * slots)
+
+        def gate_up(t, j):
+            at = pl.ds(pl.multiple_of(j * tile, tile), tile)
+            xo, xx = rows_x[span_of(t), mine], rows_x[span_of(t), rest]
+            gate = dot32(xo, go[at], LAST) + dot32(xx, gx[at], LAST)
+            return gate, dot32(xo, uo[at], LAST) + dot32(xx, ux[at], LAST)
+
+        def early(t):
+            rows_x[span_of(t)] = flat(saved_ref, t)
+            size = copies * steps[t][1] * slots
+
+            def step(j, _):
+                at = pl.ds(pl.multiple_of(j * tile, tile), tile)
+                gate_ref[:size, at], up_ref[:size, at] = gate_up(t, j)
+                return 0
+
+            lax.fori_loop(0, tiles, step, 0)
+
+        def work(t):
+            size = copies * steps[t][1] * slots
+            span = span_of(t)
+            if forward:
+                rows_x[span] = flat(lands[0], t)
+            if backward:
+                rows_z[span] = flat(lands[-1], t)
+            for acc in accs:
+                acc[:size] = jnp.zeros((size, width), jnp.float32)
+
+            def step(j, _):
+                at = pl.ds(pl.multiple_of(j * tile, tile), tile)
+                if forward:
+                    gate, up = gate_up(t, j)
+                else:
+                    gate, up = gate_ref[:size, at], up_ref[:size, at]
+                sigmoid = jax.nn.sigmoid(gate)
+                silu = gate * sigmoid
+                act = (silu * up).astype(kind)
+                if forward:
+                    accs[0][:size, mine] += dot32(act, do[at])
+                    accs[0][:size, rest] += dot32(act, dx[at])
+                if backward:
+                    zo, zx = rows_z[span, mine], rows_z[span, rest]
+                    dact = dot32(zo, do[at], LAST) + dot32(zx, dx[at], LAST)
+                    dgate = (dact * up * sigmoid * (1.0 + gate * (1.0 - sigmoid))).astype(kind)
+                    dup = (dact * silu).astype(kind)
+                    act_ref[span, at] = act
+                    dgate_ref[span, at] = dgate
+                    dup_ref[span, at] = dup
+                    accs[-1][:size, mine] += dot32(dgate, go[at]) + dot32(dup, uo[at])
+                    accs[-1][:size, rest] += dot32(dgate, gx[at]) + dot32(dup, ux[at])
+                return 0
+
+            lax.fori_loop(0, tiles, step, 0)
+            first, size_e = steps[t]
+            for n in range(homes_count):
+                value = accs[n][:size].reshape((copies, size_e, slots, width))
+                parts[n][:, pl.ds(first, size_e)] = value.astype(kind)
+                for j in range(size_e):
+                    for k in range(1, copies):
+                        copy = remote(
+                            parts[n].at[places[k], first + j],
+                            sib_ins[n].at[k - 1, first + j],
+                            part_send.at[n, k, first + j],
+                            part_recv.at[n, k, first + j],
+                            siblings[k],
+                        )
+                        copy.start()
+                        exchanges[n, t, j, k] = copy
+
+        def homeward(n, e):
+            return remote(
+                totals[n].at[e],
+                homes[n].at[expert],
+                home_send.at[n, e],
+                home_recv.at[n, expert],
+                (head, e * copies + piece),
+            )
+
+        def give_back(t):
+            first, size = steps[t]
+            for j in range(size):
+                e = first + j
+                for n in range(homes_count):
+                    value = parts[n][piece, e].astype(jnp.float32)
+                    for k in range(1, copies):
+                        exchanges[n, t, j, k].wait_recv()
+                        value = value + sib_ins[n][k - 1, e].astype(jnp.float32)
+                    totals[n][e] = value.astype(kind)
+                    if t < 2:
+                        homeward(n, e).start()
+                    else:
+
+                        @pl.when(e != expert)
+                        def _():
+                            homeward(n, e).start()
+
+        for copy in loads:
+            copy.wait()
+        if not forward:
+            early(0)
+        for t in range(len(steps)):
+            arrive(t)
+            work(t)
+            if t > 0:
+                give_back(t - 1)
+            if not forward and t + 1 < len(steps):
+                early(t + 1)
+        give_back(len(steps) - 1)
+        stays = []
+        for n in range(homes_count):
+            copy = pltpu.make_async_copy(
+                totals[n].at[expert], homes[n].at[expert], home_own.at[n]
+            )
+            copy.start()
+            stays.append(copy)
+
+        if backward:
+
+            def saving(n, j, which):
+                at = pl.ds(pl.multiple_of(j * tile, tile), tile)
+                src, dst = ((keep_ref, keeps), (away_ref, aways))[which]
+                return pltpu.make_async_copy(src.at[n, at], dst[n].at[at], out_sems.at[n, j, which])
+
+            def grads(j, _):
+                at = pl.ds(pl.multiple_of(j * tile, tile), tile)
+                for n, (left, right) in enumerate(
+                    ((dgate_ref, rows_x), (dup_ref, rows_x), (act_ref, rows_z))
+                ):
+                    value = left[:, at]
+                    away_ref[n, at] = dot32(value, right[:, rest], FIRST).astype(kind)
+                    saving(n, j, 1).start()
+                    keep_ref[n, at] = dot32(value, right[:, mine], FIRST)
+                    saving(n, j, 0).start()
+                return 0
+
+            lax.fori_loop(0, tiles, grads, 0)
+
+        for n in range(homes_count):
+            for e in others[1:]:
+                place = homes[n].at[e]
+                remote(
+                    place, place, home_send.at[n, e], home_recv.at[n, e], siblings[0]
+                ).wait_recv()
+        for t in range(len(steps)):
+            sent_out(t)
+            each(t, homeward, homes_count, lambda copy: copy.wait_send())
+        for copy in passes + list(exchanges.values()):
+            copy.wait_send()
+        for copy in stays:
+            copy.wait()
+        if backward:
+
+            def settle(j, _):
+                for n in range(3):
+                    saving(n, j, 0).wait()
+                    saving(n, j, 1).wait()
+                return 0
+
+            lax.fori_loop(0, tiles, settle, 0)
+
+    slab = (copies, NE, slots, width)
+    shapes = [make((NE, slots, width), kind)] * homes_count
+    specs = [ANY] * homes_count
+    if not backward:
+        shapes.append(make(slab, kind))
+        specs.append(VMEM)
+    else:
+        shapes += [make((hidden, features))] * 3 + [make((hidden, features), kind)] * 3
+        specs += [ANY] * 6
+    scratch = []
+    if backward:
+        scratch += [pltpu.VMEM(slab, kind)] * count
+    scratch += [pltpu.VMEM((hidden, features), kind)] * 6
+    scratch += [pltpu.VMEM(slab, kind)] * homes_count
+    scratch += [pltpu.VMEM((copies - 1,) + slab[1:], kind)] * homes_count
+    scratch += [pltpu.VMEM((NE, slots, width), kind)] * homes_count
+    scratch += [pltpu.VMEM((most_rows, width), jnp.float32)] * homes_count
+    scratch.append(pltpu.VMEM((total_rows, width), kind))
+    if backward:
+        scratch.append(pltpu.VMEM((total_rows, width), kind))
+        scratch += [pltpu.VMEM((total_rows, hidden), kind)] * 3
+        scratch.append(pltpu.VMEM((3, hidden, features), jnp.float32))
+        scratch.append(pltpu.VMEM((3, hidden, features), kind))
+        if not forward:
+            scratch += [pltpu.VMEM((most_rows, hidden), jnp.float32)] * 2
+        scratch.append(DMA((3, tiles, 2)))
+    scratch += [DMA((6,)), DMA((count,)), DMA((count, NE)), DMA((count, NE))]
+    scratch += [DMA((count, copies, NE))] * 2
+    scratch += [DMA((homes_count,)), DMA((homes_count, NE)), DMA((homes_count, NE))]
+    scratch += [DMA((homes_count, copies, NE))] * 2
+    operands = list(sent)
+    in_specs = [ANY] * count
+    if not forward:
+        operands.append(saved)
+        in_specs.append(VMEM)
+    operands += [w for pair in zip(own, other) for w in pair]
+    in_specs += [ANY] * 6
     return pl.pallas_call(
         body,
-        out_shape=jax.ShapeDtypeStruct((count, width), jnp.bfloat16),
-        grid_spec=pltpu.PrefetchScalarGridSpec(
-            num_scalar_prefetch=1,
-            grid=(steps,),
-            in_specs=[whole] + [piece] * 6,
-            out_specs=whole,
-            scratch_shapes=[pltpu.VMEM((count, width), jnp.float32)],
-        ),
-        compiler_params=pltpu.CompilerParams(vmem_limit_bytes=VMEM_BYTES),
-        cost_estimate=pl.CostEstimate(
-            flops=6 * count * width * hidden,
-            bytes_accessed=6 * hidden * features * 2 + 4 * count * width,
-            transcendentals=count * hidden,
-        ),
-    )(head, rows_in, *weights)
-
-
-def expert_backward(head, rows_in, grads_in, own, other, with_parts):
-    count, width = rows_in.shape
-    hidden, features = own[0].shape
-    tile = min(hidden, 256)
-    steps = hidden // tile
-    sums = 2 if with_parts else 1
-
-    def body(head_ref, x_ref, z_ref, go, gx, uo, ux, do, dx, *outs):
-        keeps, sends, totals, accs = outs[:3], outs[3:6], outs[6 : 6 + sums], outs[6 + sums :]
-        i = pl.program_id(0)
-        mine = pl.ds(pl.multiple_of(head_ref[0] * features, LANES), features)
-        rest = pl.ds(pl.multiple_of((1 - head_ref[0]) * features, LANES), features)
-        xo, xx = x_ref[:, mine], x_ref[:, rest]
-        zo, zx = z_ref[:, mine], z_ref[:, rest]
-        gate = dot32(xo, go[...], LAST) + dot32(xx, gx[...], LAST)
-        up = dot32(xo, uo[...], LAST) + dot32(xx, ux[...], LAST)
-        dact = dot32(zo, do[...], LAST) + dot32(zx, dx[...], LAST)
-        sigmoid = jax.nn.sigmoid(gate)
-        silu = gate * sigmoid
-        act = (silu * up).astype(jnp.bfloat16)
-        dgate = (dact * up * sigmoid * (1.0 + gate * (1.0 - sigmoid))).astype(jnp.bfloat16)
-        dup = (dact * silu).astype(jnp.bfloat16)
-
-        @pl.when(i == 0)
-        def _():
-            for acc in accs:
-                acc[...] = jnp.zeros_like(acc)
-
-        accs[0][:, mine] += dot32(dgate, go[...]) + dot32(dup, uo[...])
-        accs[0][:, rest] += dot32(dgate, gx[...]) + dot32(dup, ux[...])
-        if with_parts:
-            accs[1][:, mine] += dot32(act, do[...])
-            accs[1][:, rest] += dot32(act, dx[...])
-        for n, (left, mine_in, rest_in) in enumerate(
-            ((dgate, xo, xx), (dup, xo, xx), (act, zo, zx))
-        ):
-            keeps[n][...] = dot32(left, mine_in, FIRST)
-            sends[n][...] = dot32(left, rest_in, FIRST).astype(jnp.bfloat16)
-
-        @pl.when(i == steps - 1)
-        def _():
-            for total, acc in zip(totals, accs):
-                total[...] = acc[...].astype(jnp.bfloat16)
-
-    whole = pl.BlockSpec((count, width), lambda i, h: (0, 0))
-    piece = pl.BlockSpec((tile, features), lambda i, h: (i, 0))
-    weights = [w for pair in zip(own, other) for w in pair]
-    return pl.pallas_call(
-        body,
-        out_shape=[jax.ShapeDtypeStruct((hidden, features), jnp.float32)] * 3
-        + [jax.ShapeDtypeStruct((hidden, features), jnp.bfloat16)] * 3
-        + [jax.ShapeDtypeStruct((count, width), jnp.bfloat16)] * sums,
-        grid_spec=pltpu.PrefetchScalarGridSpec(
-            num_scalar_prefetch=1,
-            grid=(steps,),
-            in_specs=[whole, whole] + [piece] * 6,
-            out_specs=[piece] * 6 + [whole] * sums,
-            scratch_shapes=[pltpu.VMEM((count, width), jnp.float32)] * sums,
-        ),
-        compiler_params=pltpu.CompilerParams(vmem_limit_bytes=VMEM_BYTES),
-        cost_estimate=pl.CostEstimate(
-            flops=22 * count * width * hidden,
-            bytes_accessed=15 * hidden * features * 2 + 8 * count * width,
-            transcendentals=count * hidden,
-        ),
-    )(head, rows_in, grads_in, *weights)
+        out_shape=shapes,
+        in_specs=in_specs,
+        out_specs=specs,
+        scratch_shapes=scratch,
+        compiler_params=comm_params(collective_id),
+        cost_estimate=lasting(cost),
+    )(*operands)
 
 
 def split(values, terms=2):
@@ -1727,12 +1818,10 @@
     scale = head_dim ** (-0.5)
     half_length = blocks * token_rows
     positions = 2 * half_length
-    copies = blocks // NE
     own_out = heads * head_dim
     wide = heads * LANES
 
     swap = [(0, 1), (1, 0)]
-    head_scalar = head_index.reshape((1,)).astype(jnp.int32)
 
     seg_own = lax.dynamic_index_in_dim(segments, head_index, 0, keepdims=True)
     seg_rows = jnp.concatenate([lax.rem(seg_own, 128), lax.div(seg_own, 128)], axis=0)
@@ -1771,7 +1860,7 @@
         own, _ = lax.optimization_barrier((weight[layer], after))
         return own, lax.ppermute(own, "head", swap)
 
-    experts = [None] * LAYERS
+    experts = [[send_expert(w_gate, 0, tokens)]] + [None] * (LAYERS - 1)
     seg_all = seg_all[..., :2, :].astype(jnp.int32)
     seg_all = seg_all[..., 0, :] + 128 * seg_all[..., 1, :]
     seg_query = lax.dynamic_index_in_dim(seg_all, head_index, 0, keepdims=False)
@@ -1797,9 +1886,9 @@
         )
         kv_all = kv_all.reshape((positions, wide))
         if layer == 0:
-            experts[layer] = [send_expert(w, layer, kv_all) for w in (w_gate, w_up, w_down)]
+            experts[layer] += [send_expert(w, layer, kv_all) for w in (w_up, w_down)]
         else:
-            experts[layer] += [send_expert(w, layer, kv_all) for w in (w_up, w_down)]
+            experts[layer].append(send_expert(w_down, layer, kv_all))
         attended, attn_col = attend(bounds, queries, kv_all, starts)
         (attn,) = column_exchange([attn_col], [False], blocks, 5, 9)
         mid, *sent = middle(
@@ -1813,24 +1902,18 @@
             cotangent if last else None,
         )
         sent = [rows.reshape((NE, CAP, width)) for rows in sent]
-        arrived = expert_dispatch(sent, blocks, 7 if last else 6, 24 if last else 15)
-        flat_in, *dz_in = [rows.reshape((-1, width)) for rows in arrived]
         if last:
-            *wgrads, dparts, parts = expert_backward(
-                head_scalar, flat_in, dz_in[0], *zip(*experts[layer]), True
+            back, dback, *wgrads = experts_exchange(
+                sent, None, *zip(*experts[layer]), blocks, 7, True, True, 55
             )
-            back, dback = expert_return(
-                [rows.reshape((copies, NE, CAP, width)) for rows in (parts, dparts)],
-                blocks,
-                9,
-                24,
+            rows_in = None
+        else:
+            experts[layer + 1] = [send_expert(w, layer + 1, sent[0]) for w in (w_gate, w_up)]
+            back, rows_in = experts_exchange(
+                sent, None, *zip(*experts[layer]), blocks, 6, True, False, 28
             )
-        else:
-            experts[layer + 1] = [send_expert(w_gate, layer + 1, flat_in)]
-            parts = expert_forward(head_scalar, flat_in, *zip(*experts[layer]))
-            (back,) = expert_return([parts.reshape((copies, NE, CAP, width))], blocks, 8)
         kept.append(
-            (values, column, queries, kv_all, attended, attn_col, query_w, out_rows, mid, flat_in)
+            (values, column, queries, kv_all, attended, attn_col, query_w, out_rows, mid, rows_in)
         )
         values, *normed = combine(
             back.reshape((NE * CAP, width)),
@@ -1850,21 +1933,22 @@
     expert_grads = [None] * LAYERS
     for layer in reversed(range(LAYERS)):
         base = 8 * layer
-        values, column, queries, kv_all, attended, attn_col, query_w, out_rows, mid, flat_in = (
+        values, column, queries, kv_all, attended, attn_col, query_w, out_rows, mid, rows_in = (
             kept[layer]
         )
         if layer + 1 < LAYERS:
-            (dz_in,) = expert_dispatch([dz.reshape((NE, CAP, width))], blocks, 6)
-            *wgrads, dparts = expert_backward(
-                head_scalar,
-                flat_in,
-                dz_in.reshape((-1, width)),
+            dback, *wgrads = experts_exchange(
+                [dz.reshape((NE, CAP, width))],
+                rows_in,
                 *zip(*experts[layer]),
+                blocks,
+                8,
                 False,
+                True,
+                36,
             )
-            (dback,) = expert_return([dparts.reshape((copies, NE, CAP, width))], blocks, 8)
+            dback, held[2] = lax.optimization_barrier((dback, held[2]))
         got = [lax.ppermute(away, "head", swap) for away in wgrads[3:]]
-        dback, got[0] = lax.optimization_barrier((dback, got[0]))
         dmid, dy, rows = experts_back(
             dback.reshape((NE * CAP, width)),
             picks[layer],
@@ -1875,11 +1959,11 @@
             base,
         )
         dy = column_gather(dy, blocks, 3)
-        dy, got[1] = lax.optimization_barrier((dy, got[1]))
+        dy, got[0] = lax.optimization_barrier((dy, got[0]))
         dq, dkv_all = attend_back(
             bounds, queries, dy, out_rows, attended, kv_all, starts, scale
         )
-        dkv_all, got[2] = lax.optimization_barrier((dkv_all, got[2]))
+        dkv_all, got[1] = lax.optimization_barrier((dkv_all, got[1]))
         dkv, dxn = reduce_project(
             dkv_all.reshape((2, COLUMNS, span, token_rows, wide)),
             dq,
@@ -1889,6 +1973,8 @@
             10,
         )
         before = layer > 0
+        if not before:
+            dxn, got[2] = lax.optimization_barrier((dxn, got[2]))
         upstream, rows, *dz = finish(
             dxn,
             values,
@@ -1901,9 +1987,8 @@
         )
         if before:
             (dz,) = dz
-        expert_grads[layer] = [
-            own + other.astype(jnp.float32) for own, other in zip(wgrads[:3], got)
-        ]
+        expert_grads[layer] = wgrads[:3], got
+        held = got
         qkv_part, out_part = pack_grads(
             column.reshape((-1, width)),
             dq.reshape((-1, wide)),
@@ -1937,7 +2022,10 @@
         for r in range(span)
     ]
     out_grads = lax.ppermute(out_grads, ("head", "blk"), owners).astype(jnp.float32)
-    stacked = [jnp.stack(group) for group in zip(*expert_grads)]
+    stacked = [
+        jnp.stack([owns[n] + gots[n].astype(jnp.float32) for owns, gots in expert_grads])
+        for n in range(3)
+    ]
     return (
         output,
         upstream,

time: 552 us -> 559 us (1.013)
  Pallas kernels: 460 us -> 479 us
  local copies, waits for them, and re-layouts: 38.3 us -> 31.1 us
  waiting for transfers between devices: 6.79 us -> 0.03 us
    pallas_call x9 -> x3, Pallas kernels: 157 us -> 132 us  [experts_exchange(): pl.pallas_call(body, out_shape=shapes, in_specs=in_specs, out_specs=specs...]
    pallas_call x11, Pallas kernels: 13.1 us -> 36.7 us  [alone(): pl.pallas_call(body, out_shape=out_shape, in_specs=specs, out_specs=jax.t...]
    unnamed x106 -> x66, local copies, waits for them, and re-layouts: 23.6 us -> 5.83 us
    pallas_call x2, Pallas kernels: 37.2 us -> 29.3 us  [column_gather(): pl.pallas_call(body, out_shape=jax.ShapeDtypeStruct((COLUMNS,) + tuple(va...]
    ppermute x6, waiting for transfers between devices: 6.77 us -> 0.02 us  [send_expert(): return (own, lax.ppermute(own, 'head', swap))]
    pallas_call x2, Pallas kernels: 23.6 us -> 29.6 us  [attend(): pl.pallas_call(body, out_shape=(jax.ShapeDtypeStruct((count, rows, width)...]
  transfers between devices with their start and end apart: 13 -> 13, of which waited for: 1 -> 0; matrix products, arithmetic and copies ran while one was open for 5% -> 8% of each run, Pallas kernels for 46% -> 71%
where the time goes in v6:
time: 559 us; the launch traced here: 550 us
  Pallas kernels  479 us (86%)
  local copies, waits for them, and re-layouts  31.1 us (6%)
  other arithmetic  22.8 us (4%)
  starting transfers between devices  15.7 us (3%)
    pallas_call x3, Pallas kernels, experts_exchange(): pl.pallas_call(body, out_shape=shapes, in_specs=in_specs, out_specs=specs...  132 us
    pallas_call x2, Pallas kernels, reduce_project(): pl.pallas_call(body, out_shape=[jax.ShapeDtypeStruct((COLUMNS,) + tile, k...  67.4 us
    pallas_call x2, Pallas kernels, project_gather(): pl.pallas_call(body, out_shape=shapes, in_specs=[VMEM] * len(operands), o...  49.4 us
    pallas_call x1, Pallas kernels, start_gather(): pl.pallas_call(body, out_shape=plane_shapes(packs, blocks) + [jax.ShapeDt...  45.6 us
    pallas_call x2, Pallas kernels, attend_back(): pl.pallas_call(body, out_shape=(jax.ShapeDtypeStruct((count, rows, width)...  42.6 us
    pallas_call x11, Pallas kernels, alone(): pl.pallas_call(body, out_shape=out_shape, in_specs=specs, out_specs=jax.t...  36.7 us
    pallas_call x2, Pallas kernels, attend(): pl.pallas_call(body, out_shape=(jax.ShapeDtypeStruct((count, rows, width)...  29.6 us
    pallas_call x2, Pallas kernels, column_gather(): pl.pallas_call(body, out_shape=jax.ShapeDtypeStruct((COLUMNS,) + tuple(va...  29.3 us
  transfers between devices with their start and end apart: 13, of which 0 were waited for; matrix products, arithmetic and copies ran while one was open for 8% of the time, Pallas kernels for 71%

profile of v6, /device:TPU:12, one launch (start us, length us, event | category | flops | bytes accessed | tf_op | source)
XLA Modules:
  0.0 550.0 jit_solution(9467338996953664724)
XLA Ops:
  0.7 2.5 slice_bitcast_fusion.2
  10.8 45.6 %shard_map.221 = (bf16[2,4,4,16,128]{4,3,2,1,0:T(8,128)(2,1)}, bf16[2,4,4,24,1408]{4,3,2,1,0:T(8,128)(2,1)}, bf16[2,4,4,24,1408]{4,3,2,1,0:T(8,128)(2,1)}, bf16[...) custom-call(bf16[4,16,128]{2,1,0:T(8,128)(2,1)} %broadcast_in_dim.16, ...), custom_call_target="tpu_custom_call" | custom-call | bytes 98000000 | tf_op jit(solution)/shard_map/pallas_call | solution.py:372
  56.4 23.3 %shard_map.222 = (f32[16,768]{1,0:T(8,128)}, bf16[4,128,768]{2,1,0:T(8,128)(2,1)}, bf16[4,128,384]{2,1,0:T(8,128)(2,1)}, bf16[768,384]{1,0:T(8,128)(2,1)}, bf16[...) custom-call(bf16[4,128,768]{2,1,0:T(8,128)(2,1)} %get-tuple-element.106.refs_0_, bf16[768,1408]{1,0:T(8,128)(2,1)} %bitcast.144), custom_call_target="tpu_custom_call" | custom-call | bytes 77000000 | tf_op jit(solution)/shard_map/pallas_call | solution.py:559
  85.9 2.9 shard_map.225
  93.1 15.1 %shard_map.223 = (f32[4,128,384]{2,1,0:T(8,128)}, bf16[4,128,192]{2,1,0:T(8,128)(2,1)}) custom-call(s32[4,4]{1,0:T(4,128)} %pad_add_fusion.bounds_ref, bf16[4,128,384]{2,1,0:T(8,128)(2,1)} %get-tuple-element.108.q_ref, bf16[4096,384]{1,0:T(8,128)(2,1)} %bitcast.147, s32[4,1,128]{2,1,0:T(1,128)} %bitcast.179), custom_call_target="tpu_custom_call" | custom-call | bytes 45500000 | tf_op jit(solution)/shard_map/pallas_call | solution.py:1038
  108.2 6.8 %shard_map.224.attn_ref = bf16[4,128,192]{2,1,0:T(8,128)(2,1)} custom-call(bf16[4,128,192]{2,1,0:T(8,128)(2,1)} %get-tuple-element.110.refs_0_), custom_call_target="tpu_custom_call" | custom-call | bytes 31500000 | tf_op jit(solution)/shard_map/pallas_call | solution.py:171
  115.7 3.6 shard_map.226
  123.6 32.9 %shard_map.227 = (bf16[8,40,768]{2,1,0:T(8,128)(2,1)}, bf16[2,8,40,768]{3,2,1,0:T(8,128)(2,1)}) custom-call(bf16[8,40,768]{2,1,0:T(8,128)(2,1)} %bitcast.167, bf16[1024,384]{1,0:T(8,128)(2,1)} %copy-done, bf16[1024,384]{1,0:T(8,128)(2,1)} %copy-done.4, bf16[1024,384]{1,0:T(8,128)(2,1)} %copy-done.1, ...), custom_call_target="tpu_custom_call" | custom-call | bytes 98000000 | tf_op jit(solution)/shard_map/pallas_call | solution.py:1500
  156.5 3.0 shard_map.228
  159.5 26.2 %shard_map.229 = (bf16[4,128,768]{2,1,0:T(8,128)(2,1)}, bf16[4,128,384]{2,1,0:T(8,128)(2,1)}, bf16[768,384]{1,0:T(8,128)(2,1)}, bf16[384,768]{1,0:T(8,128)(2,1)}, bf16[2,4,4,128,384]{4,3,2,1,0:T(8,128)(2,1)}) custom-call(bf16[128,768]{1,0:T(8,128)(2,1)} %get-tuple-element.122.refs_0_, bf16[768,1408]{1,0:T(8,128)(2,1)} %bitcast.141, ...), custom_call_target="tpu_custom_call" | custom-call | bytes 77000000 | tf_op jit(solution)/shard_map/pallas_call | solution.py:559
  187.3 14.6 %shard_map.230 = (f32[4,128,384]{2,1,0:T(8,128)}, bf16[4,128,192]{2,1,0:T(8,128)(2,1)}) custom-call(s32[4,4]{1,0:T(4,128)} %pad_add_fusion.bounds_ref, bf16[4,128,384]{2,1,0:T(8,128)(2,1)} %get-tuple-element.124.q_ref, bf16[4096,384]{1,0:T(8,128)(2,1)} %bitcast.149, s32[4,1,128]{2,1,0:T(1,128)} %bitcast.180), custom_call_target="tpu_custom_call" | custom-call | bytes 45500000 | tf_op jit(solution)/shard_map/pallas_call | solution.py:1038
  201.9 12.2 %shard_map.231.attn_ref = bf16[4,128,192]{2,1,0:T(8,128)(2,1)} custom-call(bf16[4,128,192]{2,1,0:T(8,128)(2,1)} %get-tuple-element.126.refs_0_), custom_call_target="tpu_custom_call" | custom-call | bytes 31500000 | tf_op jit(solution)/shard_map/pallas_call | solution.py:171
  214.1 3.7 shard_map.232
  218.7 56.1 %shard_map.233 = (bf16[8,40,768]{2,1,0:T(8,128)(2,1)}, bf16[8,40,768]{2,1,0:T(8,128)(2,1)}, f32[1024,384]{1,0:T(8,128)}, f32[1024,384]{1,0:T(8,128)}, f32[1024,3...) custom-call(bf16[8,40,768]{2,1,0:T(8,128)(2,1)} %bitcast.173, ...), custom_call_target="tpu_custom_call" | custom-call | bytes 192500000 | tf_op jit(solution)/shard_map/pallas_call | solution.py:1500
  277.0 3.5 shard_map.235
  280.5 14.7 %shard_map.236.dy_ref = bf16[4,128,768]{2,1,0:T(8,128)(2,1)} custom-call(bf16[128,768]{1,0:T(8,128)(2,1)} %get-tuple-element.136.src), custom_call_target="tpu_custom_call" | custom-call | bytes 49000000 | tf_op jit(solution)/shard_map/pallas_call | solution.py:197
  295.2 2.8 shard_map.234
  298.0 21.4 %shard_map.237 = (bf16[4,128,384]{2,1,0:T(8,128)(2,1)}, bf16[4096,384]{1,0:T(8,128)(2,1)}) custom-call(s32[4,4]{1,0:T(4,128)} %pad_add_fusion.bounds_ref, bf16[4,128,384]{2,1,0:T(8,128)(2,1)} %get-tuple-element.124.q_ref, bf16[4,128,768]{2,1,0:T(8,128)(2,1)} %shard_map.236.dy_ref, bf16[384,768]{1,0:T(8,128)(2,1)} %get-tuple-element.139.w_ref, ...), custom_call_target="tpu_custom_call" | custom-call | bytes 70000000 | tf_op jit(solution)/shard_map/pallas_call | solution.py:1140
  319.4 33.9 %shard_map.238 = (bf16[4,128,384]{2,1,0:T(8,128)(2,1)}, bf16[4,128,768]{2,1,0:T(8,128)(2,1)}) custom-call(bf16[2,4,2,2,128,384]{5,4,3,2,1,0:T(8,128)(2,1)} %bitcast.154, bf16[4,128,384]{2,1,0:T(8,128)(2,1)} %get-tuple-element.144.dq_ref, bf16[768,384]{1,0:T(8,128)(2,1)} %get-tuple-element.145.w_ref, bf16[768,1408]{1,0:T(8,128)(2,1)} %bitcast.143), custom_call_target="tpu_custom_call" | custom-call | bytes 91000000 | tf_op jit(solution)/shard_map/pallas_call | solution.py:917
  353.3 2.9 shard_map.239
  356.3 43.3 %shard_map.240 = (bf16[8,40,768]{2,1,0:T(8,128)(2,1)}, f32[1024,384]{1,0:T(8,128)}, f32[1024,384]{1,0:T(8,128)}, f32[1024,384]{1,0:T(8,128)}, bf16[1024,384]{1,0...) custom-call(bf16[8,40,768]{2,1,0:T(8,128)(2,1)} %bitcast.168, ...), custom_call_target="tpu_custom_call" | custom-call | bytes 126000000 | tf_op jit(solution)/shard_map/pallas_call | solution.py:1500
  404.2 3.5 shard_map.241
  407.7 14.6 %shard_map.242.dy_ref = bf16[4,128,768]{2,1,0:T(8,128)(2,1)} custom-call(bf16[128,768]{1,0:T(8,128)(2,1)} %get-tuple-element.155.src), custom_call_target="tpu_custom_call" | custom-call | bytes 49000000 | tf_op jit(solution)/shard_map/pallas_call | solution.py:197
  422.4 4.2 shard_map.247
  426.5 2.5 add_bitcast_fusion.2
  430.4 21.2 %shard_map.243 = (bf16[4,128,384]{2,1,0:T(8,128)(2,1)}, bf16[4096,384]{1,0:T(8,128)(2,1)}) custom-call(s32[4,4]{1,0:T(4,128)} %pad_add_fusion.bounds_ref, bf16[4,128,384]{2,1,0:T(8,128)(2,1)} %get-tuple-element.108.q_ref, bf16[4,128,768]{2,1,0:T(8,128)(2,1)} %shard_map.242.dy_ref, bf16[384,768]{1,0:T(8,128)(2,1)} %get-tuple-element.158.w_ref, ...), custom_call_target="tpu_custom_call" | custom-call | bytes 70000000 | tf_op jit(solution)/shard_map/pallas_call | solution.py:1140
  451.6 33.6 %shard_map.244 = (bf16[4,128,384]{2,1,0:T(8,128)(2,1)}, bf16[4,128,768]{2,1,0:T(8,128)(2,1)}) custom-call(bf16[2,4,2,2,128,384]{5,4,3,2,1,0:T(8,128)(2,1)} %bitcast.153, bf16[4,128,384]{2,1,0:T(8,128)(2,1)} %get-tuple-element.163.dq_ref, bf16[768,384]{1,0:T(8,128)(2,1)} %get-tuple-element.164.w_ref, bf16[768,1408]{1,0:T(8,128)(2,1)} %bitcast.146), custom_call_target="tpu_custom_call" | custom-call | bytes 91000000 | tf_op jit(solution)/shard_map/pallas_call | solution.py:917
  487.6 4.1 shard_map.246
  491.7 18.0 %shard_map.248 = (bf16[4,24,640]{2,1,0:T(8,128)(2,1)}, bf16[2,24,384]{2,1,0:T(8,128)(2,1)}, bf16[4,24,640]{2,1,0:T(8,128)(2,1)}, bf16[2,24,384]{2,1,0:T(8,128)(2,1)}) custom-call(bf16[2,4,2,2,24,640]{5,4,3,2,1,0:T(8,128)(2,1)} %bitcast.160, bf16[2,2,2,2,24,384]{5,4,3,2,1,0:T(8,128)(2,1)} %bitcast.178, bf16[2,4,2,2,24,640]{5,4,3,2,1,0:T(8,128)(2,1)} %bitcast.159, ...), custom_call_target="tpu_custom_call" | custom-call | bytes 70000000 | tf_op jit(solution)/shard_map/pallas_call | solution.py:731
  509.7 8.9 %shard_map.249 = (bf16[4,24,640]{2,1,0:T(8,128)(2,1)}, bf16[4,24,640]{2,1,0:T(8,128)(2,1)}) custom-call(bf16[4,24,640]{2,1,0:T(8,128)(2,1)} %get-tuple-element.181.refs_0_, bf16[4,24,640]{2,1,0:T(8,128)(2,1)} %get-tuple-element.182.refs_1_), custom_call_target="tpu_custom_call" | custom-call | bytes 35000000 | tf_op jit(solution)/shard_map/pallas_call | solution.py:171
  524.6 4.1 collective-permute-start.12
  534.5 2.5 reshape.203
  (165 shorter events, 60.6 us)
Async XLA Ops:
  0.6 3.0 copy-start.27
  0.7 3.0 copy-start.29
  0.7 3.1 copy-start.26
  0.7 3.8 copy-start.21
  0.7 3.9 copy-start.18
  3.2 119.6 %collective-permute-start = (bf16[1024,384]{1,0:T(8,128)(2,1)S(1)}, bf16[1024,384]{1,0:T(8,128)(2,1)S(1)}, u32[]{:S(2)}, u32[]{:S(2)}) collective-permute-start(bf16[1024,384]{1,0:T(8,128)(2,1)S(1)} %get-tuple-element.115.refs_1_.refs_2_), channel_id=1, source_target_pairs={{0,16},{16,0},{1,17},{17,1},{2,18},{18,2},{3,19},{19,3},{4,20},{20... | collective-permute-start | bytes 2359304 | tf_op jit(solution)/shard_map/ppermute | solution.py:1861
  8.4 71.3 %copy-start.1 = (bf16[1024,384]{1,0:T(8,128)(2,1)}, bf16[1024,384]{1,0:T(8,128)(2,1)S(1)}, u32[]{:S(2)}) copy-start(bf16[1024,384]{1,0:T(8,128)(2,1)S(1)} %get-tuple-element.116.refs_3_.refs_4_) | copy-start | bytes 2359300
  79.7 4.6 copy-start.24
  79.7 5.4 copy-start.25
  79.7 43.0 %collective-permute-start.1 = (bf16[1024,384]{1,0:T(8,128)(2,1)S(1)}, bf16[1024,384]{1,0:T(8,128)(2,1)}, u32[]{:S(2)}, u32[]{:S(2)}) collective-permute-start(bf16[1024,384]{1,0:T(8,128)(2,1)S(1)} %get-tuple-element.116.refs_3_.refs_4_), channel_id=1, source_target_pairs={{0,16},{16,0},{1,17},{17,1},{2,18},{18,2},{3,19},{19,3},{4,20},{20... | collective-permute-start | bytes 2359304 | tf_op jit(solution)/shard_map/ppermute | solution.py:1861
  83.4 24.8 %copy-start.2 = (bf16[1024,384]{1,0:T(8,128)(2,1)}, bf16[1024,384]{1,0:T(8,128)(2,1)S(1)}, u32[]{:S(2)}) copy-start(bf16[1024,384]{1,0:T(8,128)(2,1)S(1)} %get-tuple-element.117.refs_5_.refs_6_) | copy-start | bytes 2359300
  83.4 39.4 %collective-permute-start.2 = (bf16[1024,384]{1,0:T(8,128)(2,1)S(1)}, bf16[1024,384]{1,0:T(8,128)(2,1)}, u32[]{:S(2)}, u32[]{:S(2)}) collective-permute-start(bf16[1024,384]{1,0:T(8,128)(2,1)S(1)} %get-tuple-element.117.refs_5_.refs_6_), channel_id=1, source_target_pairs={{0,16},{16,0},{1,17},{17,1},{2,18},{18,2},{3,19},{19,3},{4,20},{20... | collective-permute-start | bytes 2359304 | tf_op jit(solution)/shard_map/ppermute | solution.py:1861
  93.1 21.9 %copy-start.17 = (f32[2,320,128]{2,1,0:T(8,128)S(1)}, f32[2,320,128]{2,1,0:T(8,128)}, u32[]{:S(2)}) copy-start(f32[2,320,128]{2,1,0:T(8,128)} %get-tuple-element.113) | copy-start | bytes 983044
  115.7 5.6 %copy-start.19 = (f32[2,128,128]{2,1,0:T(8,128)S(1)}, f32[2,128,128]{2,1,0:T(8,128)}, u32[]{:S(2)}) copy-start(f32[2,128,128]{2,1,0:T(8,128)} %get-tuple-element.121) | copy-start | bytes 393220
  115.7 6.3 %copy-start.16 = (f32[2,128,320]{2,1,0:T(8,128)S(1)}, f32[2,128,320]{2,1,0:T(8,128)}, u32[]{:S(2)}) copy-start(f32[2,128,320]{2,1,0:T(8,128)} %get-tuple-element.119) | copy-start | bytes 983044
  119.3 98.5 %collective-permute-start.3 = (bf16[1024,384]{1,0:T(8,128)(2,1)}, bf16[1024,384]{1,0:T(8,128)(2,1)}, u32[]{:S(2)}, u32[]{:S(2)}) collective-permute-start(bf16[1024,384]{1,0:T(8,128)(2,1)} %get-tuple-element.130.refs_2_), channel_id=1, source_target_pairs={{0,16},{16,0},{1,17},{17,1},{2,18},{18,2},{3,19},{19,3},{4,20},{20... | collective-permute-start | bytes 2359304 | tf_op jit(solution)/shard_map/ppermute | solution.py:1861
  119.3 98.5 %collective-permute-start.4 = (bf16[1024,384]{1,0:T(8,128)(2,1)}, bf16[1024,384]{1,0:T(8,128)(2,1)}, u32[]{:S(2)}, u32[]{:S(2)}) collective-permute-start(bf16[1024,384]{1,0:T(8,128)(2,1)} %get-tuple-element.131.refs_4_), channel_id=1, source_target_pairs={{0,16},{16,0},{1,17},{17,1},{2,18},{18,2},{3,19},{19,3},{4,20},{20... | collective-permute-start | bytes 2359304 | tf_op jit(solution)/shard_map/ppermute | solution.py:1861
  156.5 29.2 %copy-start.5 = (bf16[1024,384]{1,0:T(8,128)(2,1)S(1)}, bf16[1024,384]{1,0:T(8,128)(2,1)}, u32[]{:S(2)}) copy-start(bf16[1024,384]{1,0:T(8,128)(2,1)} %get-tuple-element.132.refs_6_) | copy-start | bytes 2359300
  185.7 32.1 %collective-permute-start.5 = (bf16[1024,384]{1,0:T(8,128)(2,1)S(1)}, bf16[1024,384]{1,0:T(8,128)(2,1)S(1)}, u32[]{:S(2)}, u32[]{:S(2)}) collective-permute-start(bf16[1024,384]{1,0:T(8,128)(2,1)S(1)} %copy-done.5), channel_id=1, source_target_pairs={{0,16},{16,0},{1,17},{17,1},{2,18},{18,2},{3,19},{19,3},{4,20},{20... | collective-permute-start | bytes 2359304 | tf_op jit(solution)/shard_map/ppermute | solution.py:1861
  274.8 23.2 %collective-permute-start.6 = (bf16[1024,384]{1,0:T(8,128)(2,1)}, bf16[1024,384]{1,0:T(8,128)(2,1)S(1)}, u32[]{:S(2)}, u32[]{:S(2)}) collective-permute-start(bf16[1024,384]{1,0:T(8,128)(2,1)} %get-tuple-element.137), channel_id=1, source_target_pairs={{0,16},{16,0},{1,17},{17,1},{2,18},{18,2},{3,19},{19,3},{4,20},{20... | collective-permute-start | bytes 2359304 | tf_op jit(solution)/shard_map/ppermute | solution.py:1951
  274.9 44.5 %collective-permute-start.7 = (bf16[1024,384]{1,0:T(8,128)(2,1)}, bf16[1024,384]{1,0:T(8,128)(2,1)S(1)}, u32[]{:S(2)}, u32[]{:S(2)}) collective-permute-start(bf16[1024,384]{1,0:T(8,128)(2,1)} %get-tuple-element.142), channel_id=1, source_target_pairs={{0,16},{16,0},{1,17},{17,1},{2,18},{18,2},{3,19},{19,3},{4,20},{20... | collective-permute-start | bytes 2359304 | tf_op jit(solution)/shard_map/ppermute | solution.py:1951
  276.9 127.3 %collective-permute-start.8 = (bf16[1024,384]{1,0:T(8,128)(2,1)}, bf16[1024,384]{1,0:T(8,128)(2,1)}, u32[]{:S(2)}, u32[]{:S(2)}) collective-permute-start(bf16[1024,384]{1,0:T(8,128)(2,1)} %get-tuple-element.152), channel_id=1, source_target_pairs={{0,16},{16,0},{1,17},{17,1},{2,18},{18,2},{3,19},{19,3},{4,20},{20... | collective-permute-start | bytes 2359304 | tf_op jit(solution)/shard_map/ppermute | solution.py:1951
  298.0 21.4 %copy-start.12 = (bf16[1024,384]{1,0:T(8,128)(2,1)}, bf16[1024,384]{1,0:T(8,128)(2,1)S(1)}, u32[]{:S(2)}) copy-start(bf16[1024,384]{1,0:T(8,128)(2,1)S(1)} %collective-permute-done.6) | copy-start | bytes 2359300
  319.4 33.9 %copy-start.11 = (bf16[1024,384]{1,0:T(8,128)(2,1)}, bf16[1024,384]{1,0:T(8,128)(2,1)S(1)}, u32[]{:S(2)}) copy-start(bf16[1024,384]{1,0:T(8,128)(2,1)S(1)} %collective-permute-done.7) | copy-start | bytes 2359300
  356.3 46.6 %copy-start.10 = (f32[1024,384]{1,0:T(8,128)S(1)}, f32[1024,384]{1,0:T(8,128)}, u32[]{:S(2)}) copy-start(f32[1024,384]{1,0:T(8,128)} %get-tuple-element.189) | copy-start | bytes 4718596
  399.6 30.8 %collective-permute-start.9 = (bf16[1024,384]{1,0:T(8,128)(2,1)}, bf16[1024,384]{1,0:T(8,128)(2,1)}, u32[]{:S(2)}, u32[]{:S(2)}) collective-permute-start(bf16[1024,384]{1,0:T(8,128)(2,1)} %get-tuple-element.156), channel_id=1, source_target_pairs={{0,16},{16,0},{1,17},{17,1},{2,18},{18,2},{3,19},{19,3},{4,20},{20... | collective-permute-start | bytes 2359304 | tf_op jit(solution)/shard_map/ppermute | solution.py:1951
  400.9 50.7 %collective-permute-start.10 = (bf16[1024,384]{1,0:T(8,128)(2,1)}, bf16[1024,384]{1,0:T(8,128)(2,1)}, u32[]{:S(2)}, u32[]{:S(2)}) collective-permute-start(bf16[1024,384]{1,0:T(8,128)(2,1)} %get-tuple-element.161), channel_id=1, source_target_pairs={{0,16},{16,0},{1,17},{17,1},{2,18},{18,2},{3,19},{19,3},{4,20},{20... | collective-permute-start | bytes 2359304 | tf_op jit(solution)/shard_map/ppermute | solution.py:1951
  401.7 83.5 %collective-permute-start.11 = (bf16[1024,384]{1,0:T(8,128)(2,1)}, bf16[1024,384]{1,0:T(8,128)(2,1)}, u32[]{:S(2)}, u32[]{:S(2)}) collective-permute-start(bf16[1024,384]{1,0:T(8,128)(2,1)} %get-tuple-element.166), channel_id=1, source_target_pairs={{0,16},{16,0},{1,17},{17,1},{2,18},{18,2},{3,19},{19,3},{4,20},{20... | collective-permute-start | bytes 2359304 | tf_op jit(solution)/shard_map/ppermute | solution.py:1951
  422.3 4.2 copy-start.9
  509.7 14.2 %copy-start.22 = (bf16[2,24,384]{2,1,0:T(8,128)(2,1)S(1)}, bf16[2,24,384]{2,1,0:T(8,128)(2,1)}, u32[]{:S(2)}) copy-start(bf16[2,24,384]{2,1,0:T(8,128)(2,1)} %get-tuple-element.185) | copy-start | bytes 110596
  509.7 14.2 %copy-start.23 = (bf16[2,24,384]{2,1,0:T(8,128)(2,1)S(1)}, bf16[2,24,384]{2,1,0:T(8,128)(2,1)}, u32[]{:S(2)}) copy-start(bf16[2,24,384]{2,1,0:T(8,128)(2,1)} %get-tuple-element.186) | copy-start | bytes 110596
  524.6 23.7 %collective-permute-start.12 = (bf16[2,24,768]{2,1,0:T(8,128)(2,1)}, bf16[2,24,768]{2,1,0:T(8,128)(2,1)}, u32[]{:S(2)}, u32[]{:S(2)}) collective-permute-start(bf16[2,24,768]{2,1,0:T(8,128)(2,1)} %bitcast.84), channel_id=1, source_target_pairs={{0,0},{1,1},{2,2},{3,3},{4,8},{5,9},{6,10},{7,11},{8,16},{9,17},{1... | collective-permute-start | bytes 221192 | tf_op jit(solution)/shard_map/ppermute | solution.py:2024
  (12 other events, 21.1 us)

commit v7 on v6

--- a/solution.py
+++ b/solution.py
@@ -13,8 +13,14 @@
 MESH = pl.DeviceIdType.MESH
 ANY = pl.BlockSpec(memory_space=pl.ANY)
 VMEM = pl.BlockSpec(memory_space=pltpu.VMEM)
+HBM = pl.BlockSpec(memory_space=pltpu.HBM)
 DMA = pltpu.SemaphoreType.DMA
 VMEM_BYTES = 60 * 1024 * 1024
+SPARE_BYTES = 4 * 1024 * 1024
+
+
+def make(shape, kind=jnp.float32):
+    return jax.ShapeDtypeStruct(tuple(shape), kind)
 
 
 def greet(peers, line=()):
@@ -43,9 +49,24 @@
     )
 
 
-def comm_params(collective_id):
+def room(things, spare=SPARE_BYTES):
+    total = spare
+    for thing in things:
+        if hasattr(thing, "dtype") and hasattr(thing, "shape"):
+            if not jnp.issubdtype(thing.dtype, jnp.number):
+                continue
+            size = jnp.dtype(thing.dtype).itemsize
+            for extent in thing.shape:
+                size *= extent
+            total += size
+    return min(total, VMEM_BYTES)
+
+
+def comm_params(collective_id, things=(), spare=SPARE_BYTES):
     return pltpu.CompilerParams(
-        collective_id=collective_id, has_side_effects=True, vmem_limit_bytes=VMEM_BYTES
+        collective_id=collective_id,
+        has_side_effects=True,
+        vmem_limit_bytes=room(things, spare),
     )
 
 
@@ -205,6 +226,84 @@
     )(values)
 
 
+def final_exchange(shares, rows, blocks, collective_id, cost=9):
+    span = blocks // COLUMNS
+    count = len(shares)
+    total = 2 * count
+
+    def body(*refs):
+        srcs, dsts = refs[:total], refs[total : 2 * total]
+        own_sems, send_sems, recv_sems, row_send, row_recv = refs[2 * total :]
+        where = column_place(blocks)
+        head, blk = lax.axis_index("head"), lax.axis_index("blk")
+        plane, rest = lax.div(blk, span), lax.rem(blk, span)
+        flat = head * blocks + blk
+        goal = (plane * 2 + head) * span + rest
+        from_plane = lax.div(flat, span)
+        origin = (lax.rem(from_plane, 2), lax.div(from_plane, 2) * span + lax.rem(flat, span))
+        goal_place = (lax.div(goal, blocks), lax.rem(goal, blocks))
+        away = goal != flat
+        greet(where[2][1:], [(away, goal_place), (away, origin)])
+        copies = []
+        for n in range(count):
+            copies += column_start(
+                srcs[n],
+                False,
+                dsts[n],
+                own_sems.at[n],
+                send_sems.at[n],
+                recv_sems.at[n],
+                where,
+            )
+
+        def row_copy(n):
+            return remote(
+                srcs[n], dsts[n], row_send.at[n - count], row_recv.at[n - count], goal_place
+            )
+
+        def row_stay(n):
+            return pltpu.make_async_copy(srcs[n], dsts[n], own_sems.at[n])
+
+        for n in range(count, total):
+
+            @pl.when(away)
+            def _():
+                row_copy(n).start()
+
+            @pl.when(jnp.logical_not(away))
+            def _():
+                row_stay(n).start()
+
+        for copy in copies:
+            copy.wait()
+        for n in range(count, total):
+
+            @pl.when(away)
+            def _():
+                row_copy(n).wait()
+
+            @pl.when(jnp.logical_not(away))
+            def _():
+                row_stay(n).wait()
+
+    arrays = list(shares) + list(rows)
+    return pl.pallas_call(
+        body,
+        out_shape=[make(values.shape, values.dtype) for values in arrays],
+        in_specs=[ANY] * total,
+        out_specs=[ANY] * total,
+        scratch_shapes=[
+            DMA((total,)),
+            DMA((count, COLUMNS)),
+            DMA((count, COLUMNS)),
+            DMA((count,)),
+            DMA((count,)),
+        ],
+        compiler_params=comm_params(collective_id),
+        cost_estimate=lasting(cost),
+    )(*arrays)
+
+
 def plane_place(blocks):
     span = blocks // COLUMNS
     width = span // 2
@@ -338,15 +437,19 @@
         srcs, refs = refs[: count + 1], refs[count + 1 :]
         wholes, refs = refs[:count], refs[count:]
         columns, refs = refs[: count + 1], refs[count + 1 :]
-        own_sems, send_sems, recv_sems, *plane_sems = refs
+        own_sems, send_sems, recv_sems, chain_send, chain_recv, *plane_sems = refs
         column, plane = column_place(blocks), plane_place(blocks)
         greet(column[2][1:] + plane[4][1:] + [plane[5], plane[6]])
         run = PlaneRun(columns[:count], wholes, *plane_sems, plane)
+        chain = Chain(srcs[count], columns[count], chain_send, chain_recv, blocks)
+        stay = pltpu.make_async_copy(
+            srcs[count], columns[count].at[chain.plane], own_sems.at[count]
+        )
 
         def begin(n):
             return column_start(
                 srcs[n],
-                n == count,
+                False,
                 columns[n],
                 own_sems.at[n],
                 send_sems.at[n],
@@ -358,16 +461,26 @@
         for n in range(count):
             for copy in waits[n]:
                 copy.wait()
-            if n + 2 <= count:
+            if n + 2 < count:
                 waits.append(begin(n + 2))
+            elif n + 2 == count:
+                chain.pass_on(0)
+                stay.start()
             run.first(n)
-        for n in range(count):
+        run.second(0)
+        run.second(1)
+        chain.arrive(1)
+        for n in range(2, count):
             run.second(n)
-        for n in range(count):
+        run.third(0)
+        run.third(1)
+        chain.arrive(2)
+        for n in range(2, count):
             run.third(n)
+        chain.arrive(3)
         run.last()
-        for copy in waits[count]:
-            copy.wait()
+        stay.wait()
+        chain.finish()
 
     results = pl.pallas_call(
         body,
@@ -378,8 +491,10 @@
         out_specs=[ANY] * (2 * count + 1),
         scratch_shapes=[
             DMA((count + 1,)),
-            DMA((count + 1, COLUMNS)),
-            DMA((count + 1, COLUMNS)),
+            DMA((count, COLUMNS)),
+            DMA((count, COLUMNS)),
+            DMA((COLUMNS, 2)),
+            DMA((COLUMNS,)),
         ]
         + plane_scratch(count, blocks),
         compiler_params=comm_params(collective_id),
@@ -410,8 +525,9 @@
         else:
             source_ref, pack_ref = refs[:2]
             small_out, refs = refs[2], refs[3:]
-        column_ref, query_ref, query_w_ref, out_w_ref, kv_ref = refs[:5]
-        kv_own, own_sems, send_sems, recv_sems, pass_sems, land_sems, z_send, z_recv = refs[5:]
+        column_out, query_ref, query_w_out, out_w_out, kv_ref = refs[:5]
+        column_ref, query_w_ref, out_w_ref, kv_own, own_sems, send_sems, recv_sems = refs[5:12]
+        pass_sems, land_sems, z_send, z_recv, keep_sems = refs[12:]
         head, rest, core, left, x_peers, y_peer, core_peer = plane_place(blocks)
         plane = lax.div(lax.axis_index("blk"), span)
         sends, passes, owns = [], [], []
@@ -426,17 +542,6 @@
             greet(near)
 
         tail = pack_ref[:, tail_at:]
-        low = lax.broadcasted_iota(jnp.int32, (tail_cols, wide), 0)
-        target = lax.broadcasted_iota(jnp.int32, (tail_cols, wide), 1)
-        goal = lax.div(low, dim) * LANES + lax.rem(low, dim)
-        to_low = ((goal == target) & (low < own_out)).astype(jnp.bfloat16)
-        query_w = dot32(tail, to_low).astype(jnp.bfloat16)
-        query_w_ref[...] = query_w
-        out_rows = pack_ref[pl.ds(pl.multiple_of(plane * own_out, 64), own_out), :features]
-        pieces = []
-        for h in range(heads):
-            pieces += [jnp.zeros((dim, features), jnp.bfloat16), out_rows[h * dim : (h + 1) * dim]]
-        out_w_ref[...] = jnp.concatenate(pieces, axis=0)
         if not chained:
             small = tail[:, tail_cols - LANES :].astype(jnp.float32).T
             at = own_out - (tail_cols - LANES)
@@ -505,8 +610,6 @@
                 send(k, 1, 0, 0, x_peers[d], 0, d)
             hand_over(k, 0, 0, 0)
             hand_over(k, 1, 0, 0)
-            query = dot32(xn, query_w).astype(jnp.bfloat16).astype(jnp.float32) * scale
-            query_ref[slab] = query.astype(jnp.bfloat16)
 
         def second(k):
             for d in range(1, width):
@@ -530,9 +633,39 @@
                 arrived(k, 1, 1, d)
                 hand_over(k, 1, 1, d)
 
+        def queries():
+            low = lax.broadcasted_iota(jnp.int32, (tail_cols, wide), 0)
+            target = lax.broadcasted_iota(jnp.int32, (tail_cols, wide), 1)
+            goal = lax.div(low, dim) * LANES + lax.rem(low, dim)
+            to_low = ((goal == target) & (low < own_out)).astype(jnp.bfloat16)
+            query_w = dot32(tail, to_low).astype(jnp.bfloat16)
+            query_w_ref[...] = query_w
+            out_rows = pack_ref[pl.ds(pl.multiple_of(plane * own_out, 64), own_out), :features]
+            pieces = []
+            for h in range(heads):
+                pieces += [jnp.zeros((dim, features), jnp.bfloat16), out_rows[h * dim : (h + 1) * dim]]
+            out_w_ref[...] = jnp.concatenate(pieces, axis=0)
+            for k in range(COLUMNS):
+                slab = slabs[k]
+                query = dot32(column_ref[slab], query_w).astype(jnp.bfloat16)
+                query = query.astype(jnp.float32) * scale
+                query_ref[slab] = query.astype(jnp.bfloat16)
+            for n, (src, dst) in enumerate(
+                (
+                    (column_ref, column_out),
+                    (query_w_ref, query_w_out),
+                    (out_w_ref, out_w_out),
+                )
+            ):
+                copy = pltpu.make_async_copy(src, dst, keep_sems.at[n])
+                copy.start()
+                owns.append(copy)
+
         for t in range(COLUMNS + 2):
             if t < COLUMNS:
                 first(t)
+            elif t == COLUMNS:
+                queries()
             if 0 <= t - 1 < COLUMNS:
                 second(t - 1)
             if 0 <= t - 2 < COLUMNS:
@@ -560,8 +693,11 @@
         body,
         out_shape=shapes,
         in_specs=[VMEM] * len(operands),
-        out_specs=[VMEM] * (len(shapes) - 1) + [ANY],
+        out_specs=([] if chained else [VMEM]) + [HBM, VMEM, HBM, HBM, ANY],
         scratch_shapes=[
+            pltpu.VMEM((COLUMNS, rows, features), jnp.bfloat16),
+            pltpu.VMEM((features, wide), jnp.bfloat16),
+            pltpu.VMEM((wide, features), jnp.bfloat16),
             pltpu.VMEM((COLUMNS, rows, wide), jnp.bfloat16),
             DMA((COLUMNS,)),
             DMA((COLUMNS * links,)),
@@ -570,8 +706,13 @@
             DMA((COLUMNS, 2, 2, width)),
             DMA((COLUMNS, 2)),
             DMA((COLUMNS,)),
+            DMA((3,)),
         ],
-        compiler_params=comm_params(collective_id),
+        compiler_params=comm_params(
+            collective_id,
+            operands + shapes[:-1] + [make((COLUMNS, rows, wide), jnp.bfloat16)],
+            3 * SPARE_BYTES,
+        ),
         cost_estimate=lasting(cost),
     )(*operands)
     return list(results) + [smalls] if chained else list(results[1:]) + [results[0]]
@@ -737,7 +878,9 @@
         out_specs=[VMEM] * count,
         scratch_shapes=scratch
         + [DMA((count, 2)), DMA((count, 2)), DMA((count, 2, width)), DMA((count, 2, width))],
-        compiler_params=comm_params(collective_id),
+        compiler_params=comm_params(
+            collective_id, scratch + 2 * [make(a.shape, a.dtype) for a in arrays]
+        ),
         cost_estimate=lasting(cost),
     )(
         *[
@@ -795,22 +938,29 @@
             return ref[at].astype(jnp.float32)
 
         top, low = pl.ds(0, half), pl.ds(half, half)
-        starts = [
-            begin(
-                remote(
-                    src.at[:, planes[d], :, 1 - core],
-                    core_in.at[k],
-                    core_send.at[k],
-                    core_recv.at[k],
-                    core_peer,
+        starts = []
+
+        def cross(k):
+            starts.append(
+                begin(
+                    remote(
+                        src.at[:, planes[order[k]], :, 1 - core],
+                        core_in.at[k],
+                        core_send.at[k],
+                        core_recv.at[k],
+                        core_peer,
+                    )
                 )
             )
-            for k, d in enumerate(order)
-        ]
+
+        cross(0)
+        cross(1)
         xas, yas, ybs, xbs, z_copies = {}, {}, {}, {}, []
 
         def first(k):
             starts[k].wait_recv()
+            if k + 2 < COLUMNS:
+                cross(k + 2)
 
             def step(i, _):
                 yy, xx = lax.div(i, width), lax.rem(i, width)
@@ -914,24 +1064,25 @@
 
     tile = (rows, wide)
     part = (half, wide)
+    scratch = [
+        pltpu.VMEM((COLUMNS, 2, width) + tile, kind),
+        pltpu.VMEM((COLUMNS, 2, width) + tile, kind),
+        pltpu.VMEM((COLUMNS, width, 2) + part, kind),
+        pltpu.VMEM((COLUMNS,) + part, kind),
+        pltpu.VMEM((COLUMNS,) + part, kind),
+        pltpu.VMEM((COLUMNS, width) + part, kind),
+        pltpu.VMEM((COLUMNS, width) + part, kind),
+        pltpu.VMEM((COLUMNS, width) + part, kind),
+        pltpu.VMEM((COLUMNS, rows, features), kind),
+    ]
+    shapes = [make((COLUMNS,) + tile, kind), make((COLUMNS, rows, features), kind)]
     return pl.pallas_call(
         body,
-        out_shape=[
-            jax.ShapeDtypeStruct((COLUMNS,) + tile, kind),
-            jax.ShapeDtypeStruct((COLUMNS, rows, features), kind),
-        ],
+        out_shape=shapes,
         in_specs=[VMEM] * 4,
         out_specs=[VMEM] * 2,
-        scratch_shapes=[
-            pltpu.VMEM((COLUMNS, 2, width) + tile, kind),
-            pltpu.VMEM((COLUMNS, 2, width) + tile, kind),
-            pltpu.VMEM((COLUMNS, width, 2) + part, kind),
-            pltpu.VMEM((COLUMNS,) + part, kind),
-            pltpu.VMEM((COLUMNS,) + part, kind),
-            pltpu.VMEM((COLUMNS, width) + part, kind),
-            pltpu.VMEM((COLUMNS, width) + part, kind),
-            pltpu.VMEM((COLUMNS, width) + part, kind),
-            pltpu.VMEM((COLUMNS, rows, features), kind),
+        scratch_shapes=scratch
+        + [
             DMA((COLUMNS,)),
             DMA((COLUMNS,)),
             DMA((COLUMNS, 2, width)),
@@ -939,7 +1090,9 @@
             DMA((COLUMNS,)),
             DMA((COLUMNS,)),
         ],
-        compiler_params=comm_params(collective_id),
+        compiler_params=comm_params(
+            collective_id, scratch + shapes + [dkv_all, dq, query_w, pack]
+        ),
         cost_estimate=lasting(cost),
     )(dkv_all.reshape((2, COLUMNS, width, 2) + tile), dq, query_w, pack)
 
@@ -1054,7 +1207,9 @@
                 pl.BlockSpec((1, rows, width // 2), lambda i, b: (i, 0, 0)),
             ),
         ),
-        compiler_params=pltpu.CompilerParams(vmem_limit_bytes=VMEM_BYTES),
+        compiler_params=pltpu.CompilerParams(
+            vmem_limit_bytes=room([kv_all] * 2, 4 * SPARE_BYTES)
+        ),
         cost_estimate=lasting(13),
     )(bounds, queries, kv_all, starts)
 
@@ -1157,16 +1312,20 @@
             out_specs=(block, whole),
             scratch_shapes=[pltpu.VMEM((total_keys, wide), jnp.float32)],
         ),
-        compiler_params=pltpu.CompilerParams(vmem_limit_bytes=VMEM_BYTES),
+        compiler_params=pltpu.CompilerParams(
+            vmem_limit_bytes=room([make((total_keys, wide), jnp.bfloat16)] * 6, 5 * SPARE_BYTES)
+        ),
         cost_estimate=lasting(20),
     )(bounds, queries, dy, out_rows, kept, kv_all, starts)
 
 
-def experts_exchange(sent, saved, own, other, blocks, collective_id, forward, backward, cost):
+def experts_exchange(
+    sent, saved, own, other, layer, blocks, collective_id, forward, backward, cost
+):
     copies = blocks // NE
     half = NE // 2
     slots, width = sent[0].shape[1:]
-    hidden, features = own[0].shape
+    hidden, features = other[0].shape
     tile = min(hidden, 256)
     tiles = hidden // tile
     count = len(sent)
@@ -1190,10 +1349,9 @@
         saved_ref = take(1)[0] if not forward else None
         weight_refs = take(6)
         homes = take(homes_count)
-        lands = take(1) if not backward else []
+        arrived_ref = take(1)[0] if not backward else None
         keeps, aways = (take(3), take(3)) if backward else ([], [])
-        if backward:
-            lands = lands + take(count)
+        lands = take(count)
         weights = take(6)
         parts, sib_ins, totals = take(homes_count), take(homes_count), take(homes_count)
         accs = take(homes_count)
@@ -1204,7 +1362,7 @@
                 gate_ref, up_ref = take(2)
             out_sems = take(1)[0]
         load_sems, own_sems, send_sems, recv_sems, pass_sems, land_sems = take(6)
-        home_own, home_send, home_recv, part_send, part_recv = take(5)
+        home_own, home_send, home_recv, part_send, part_recv, arrived_sem = take(6)
 
         head, blk = lax.axis_index("head"), lax.axis_index("blk")
         expert, piece = lax.div(blk, copies), lax.rem(blk, copies)
@@ -1256,7 +1414,8 @@
             send(t)
         loads = []
         for n in range(6):
-            copy = pltpu.make_async_copy(weight_refs[n], weights[n], load_sems.at[n])
+            weight = weight_refs[n] if n % 2 else weight_refs[n].at[layer]
+            copy = pltpu.make_async_copy(weight, weights[n], load_sems.at[n])
             copy.start()
             loads.append(copy)
         go, gx, uo, ux, do, dx = weights
@@ -1431,12 +1590,16 @@
                     value = left[:, at]
                     away_ref[n, at] = dot32(value, right[:, rest], FIRST).astype(kind)
                     saving(n, j, 1).start()
-                    keep_ref[n, at] = dot32(value, right[:, mine], FIRST)
+                    keep_ref[n, at] = dot32(value, right[:, mine], FIRST).astype(kind)
                     saving(n, j, 0).start()
                 return 0
 
             lax.fori_loop(0, tiles, grads, 0)
 
+        if not backward:
+            copy = pltpu.make_async_copy(lands[0], arrived_ref, arrived_sem)
+            copy.start()
+            stays.append(copy)
         for n in range(homes_count):
             for e in others[1:]:
                 place = homes[n].at[e]
@@ -1465,13 +1628,11 @@
     specs = [ANY] * homes_count
     if not backward:
         shapes.append(make(slab, kind))
-        specs.append(VMEM)
+        specs.append(HBM)
     else:
-        shapes += [make((hidden, features))] * 3 + [make((hidden, features), kind)] * 3
-        specs += [ANY] * 6
-    scratch = []
-    if backward:
-        scratch += [pltpu.VMEM(slab, kind)] * count
+        shapes += [make((hidden, features), kind)] * 6
+        specs += [HBM] * 6
+    scratch = [pltpu.VMEM(slab, kind)] * count
     scratch += [pltpu.VMEM((hidden, features), kind)] * 6
     scratch += [pltpu.VMEM(slab, kind)] * homes_count
     scratch += [pltpu.VMEM((copies - 1,) + slab[1:], kind)] * homes_count
@@ -1481,29 +1642,32 @@
     if backward:
         scratch.append(pltpu.VMEM((total_rows, width), kind))
         scratch += [pltpu.VMEM((total_rows, hidden), kind)] * 3
-        scratch.append(pltpu.VMEM((3, hidden, features), jnp.float32))
-        scratch.append(pltpu.VMEM((3, hidden, features), kind))
+        scratch += [pltpu.VMEM((3, hidden, features), kind)] * 2
         if not forward:
             scratch += [pltpu.VMEM((most_rows, hidden), jnp.float32)] * 2
         scratch.append(DMA((3, tiles, 2)))
     scratch += [DMA((6,)), DMA((count,)), DMA((count, NE)), DMA((count, NE))]
     scratch += [DMA((count, copies, NE))] * 2
     scratch += [DMA((homes_count,)), DMA((homes_count, NE)), DMA((homes_count, NE))]
-    scratch += [DMA((homes_count, copies, NE))] * 2
+    scratch += [DMA((homes_count, copies, NE))] * 2 + [DMA]
     operands = list(sent)
     in_specs = [ANY] * count
     if not forward:
         operands.append(saved)
         in_specs.append(VMEM)
     operands += [w for pair in zip(own, other) for w in pair]
-    in_specs += [ANY] * 6
+    in_specs += [HBM] * 6
     return pl.pallas_call(
         body,
         out_shape=shapes,
         in_specs=in_specs,
         out_specs=specs,
         scratch_shapes=scratch,
-        compiler_params=comm_params(collective_id),
+        compiler_params=comm_params(
+            collective_id,
+            scratch + ([saved] if not forward else []),
+            (11 if backward else 2) * SPARE_BYTES,
+        ),
         cost_estimate=lasting(cost),
     )(*operands)
 
@@ -1535,14 +1699,12 @@
         out_shape=out_shape,
         in_specs=specs,
         out_specs=jax.tree.map(lambda _: VMEM, out_shape),
-        compiler_params=pltpu.CompilerParams(vmem_limit_bytes=VMEM_BYTES),
+        compiler_params=pltpu.CompilerParams(
+            vmem_limit_bytes=room(list(operands) + jax.tree.leaves(out_shape), 2 * SPARE_BYTES)
+        ),
         cost_estimate=lasting(cost),
     )(*operands)
     return list(results) if isinstance(out_shape, (list, tuple)) else results
-
-
-def make(shape, kind=jnp.float32):
-    return jax.ShapeDtypeStruct(tuple(shape), kind)
 
 
 def route_tables(routes, gates):
@@ -1749,6 +1911,33 @@
     return alone(body, outs, 3, dxn, x, dmid, rows_in, smalls, *more)
 
 
+def sum_expert_grads(owns, gots):
+    layers, kinds = len(owns), len(owns[0])
+    hidden, features = owns[0][0].shape
+    tile = min(hidden, 256)
+
+    def body(*refs):
+        outs = refs[2 * layers * kinds :]
+        for n in range(kinds):
+            for layer in range(layers):
+                own, got = refs[2 * (layer * kinds + n) : 2 * (layer * kinds + n) + 2]
+                outs[n][layer] = own[...].astype(jnp.float32) + got[...].astype(jnp.float32)
+
+    piece = pl.BlockSpec((tile, features), lambda i: (i, 0))
+    operands = [
+        w for layer in range(layers) for pair in zip(owns[layer], gots[layer]) for w in pair
+    ]
+    return pl.pallas_call(
+        body,
+        out_shape=[make((layers, hidden, features))] * kinds,
+        grid=(hidden // tile,),
+        in_specs=[piece] * len(operands),
+        out_specs=[pl.BlockSpec((layers, tile, features), lambda i: (0, i, 0))] * kinds,
+        compiler_params=pltpu.CompilerParams(vmem_limit_bytes=VMEM_BYTES),
+        cost_estimate=lasting(7),
+    )(*operands)
+
+
 def pack_grads(column, dq, dkv, attn, dy, small):
     width = column.shape[1]
     kv_cols, own_out = dkv.shape[1], attn.shape[1]
@@ -1857,8 +2046,10 @@
     picks, pick_gates, slot_gates, other_gates = route_tables(routes, gates)
 
     def send_expert(weight, layer, after):
-        own, _ = lax.optimization_barrier((weight[layer], after))
-        return own, lax.ppermute(own, "head", swap)
+        away, _ = lax.optimization_barrier((weight[layer], after))
+        return lax.ppermute(away, "head", swap)
+
+    own_experts = (w_gate, w_up, w_down)
 
     experts = [[send_expert(w_gate, 0, tokens)]] + [None] * (LAYERS - 1)
     seg_all = seg_all[..., :2, :].astype(jnp.int32)
@@ -1904,13 +2095,13 @@
         sent = [rows.reshape((NE, CAP, width)) for rows in sent]
         if last:
             back, dback, *wgrads = experts_exchange(
-                sent, None, *zip(*experts[layer]), blocks, 7, True, True, 55
+                sent, None, own_experts, experts[layer], layer, blocks, 7, True, True, 55
             )
             rows_in = None
         else:
             experts[layer + 1] = [send_expert(w, layer + 1, sent[0]) for w in (w_gate, w_up)]
             back, rows_in = experts_exchange(
-                sent, None, *zip(*experts[layer]), blocks, 6, True, False, 28
+                sent, None, own_experts, experts[layer], layer, blocks, 6, True, False, 28
             )
         kept.append(
             (values, column, queries, kv_all, attended, attn_col, query_w, out_rows, mid, rows_in)
@@ -1940,7 +2131,9 @@
             dback, *wgrads = experts_exchange(
                 [dz.reshape((NE, CAP, width))],
                 rows_in,
-                *zip(*experts[layer]),
+                own_experts,
+                experts[layer],
+                layer,
                 blocks,
                 8,
                 False,
@@ -2004,7 +2197,8 @@
 
     packed = [part for layer in range(LAYERS) for part in shared_grads[layer]]
     reduced = plane_reduce(packed, blocks, 12, 20)
-    from_planes = column_exchange(reduced[::2], [False] * LAYERS, blocks, 13, 10)
+    exchanged = final_exchange(reduced[::2], reduced[1::2], blocks, 13)
+    from_planes, out_grads = exchanged[:LAYERS], exchanged[LAYERS:]
     from_planes = jnp.stack(from_planes, axis=1).astype(jnp.float32)
     kv_out = from_planes[..., :wide].reshape((COLUMNS, LAYERS, shard_rows, heads, 2, head_dim))
     query_out = from_planes[..., wide : wide + own_out].reshape(
@@ -2013,19 +2207,9 @@
     qkv_out = jnp.concatenate([query_out, kv_out], axis=4)
     qkv_out = qkv_out.transpose((1, 2, 4, 0, 3, 5)).reshape((LAYERS, shard_rows, 3 * width))
     small_out = jnp.sum(from_planes[..., wide + own_out : wide + own_out + 8], axis=0)
-    out_grads = jnp.stack(reduced[1::2]).transpose((0, 2, 1, 3))
+    out_grads = jnp.stack(out_grads).astype(jnp.float32).transpose((0, 2, 1, 3))
     out_grads = out_grads.reshape((LAYERS, shard_rows, width))
-    owners = [
-        (y * blocks + z * span + r, (z * 2 + y) * span + r)
-        for y in range(2)
-        for z in range(COLUMNS)
-        for r in range(span)
-    ]
-    out_grads = lax.ppermute(out_grads, ("head", "blk"), owners).astype(jnp.float32)
-    stacked = [
-        jnp.stack([owns[n] + gots[n].astype(jnp.float32) for owns, gots in expert_grads])
-        for n in range(3)
-    ]
+    stacked = sum_expert_grads(*zip(*expert_grads))
     return (
         output,
         upstream,

time: 559 us -> 496 us (0.89)
  Pallas kernels: 479 us -> 441 us
  other arithmetic: 22.8 us -> 2.82 us
    pallas_call x2 -> x4, Pallas kernels: 67.4 us -> 92.3 us  [the longest x2 74.6 us: reduce_project(): pl.pallas_call(body, out_shape=shapes, in_specs=[VMEM] * 4, out_specs=[VM...]
    pallas_call x11, Pallas kernels: 36.7 us -> 13 us  [alone(): pl.pallas_call(body, out_shape=out_shape, in_specs=specs, out_specs=jax.t...]
    another operation x10 -> x1, other arithmetic: 15.2 us -> 0.01 us  [the longest x9 15.2 us: per_device(): jnp.stack([owns[n] + gots[n].astype(jnp.float32) for owns, gots in expert...]
    unnamed x66 -> x182, local copies, waits for them, and re-layouts: 5.83 us -> 20 us
    pallas_call x2, Pallas kernels: 42.6 us -> 33.9 us  [attend_back(): pl.pallas_call(body, out_shape=(jax.ShapeDtypeStruct((count, rows, width)...]
    pallas_call x2, Pallas kernels: 49.4 us -> 41.3 us  [project_gather(): pl.pallas_call(body, out_shape=shapes, in_specs=[VMEM] * len(operands), o...]
    pallas_call x1, Pallas kernels: 45.6 us -> 38.5 us  [start_gather(): pl.pallas_call(body, out_shape=plane_shapes(packs, blocks) + [jax.ShapeDt...]
    pallas_call x2, Pallas kernels: 29.6 us -> 23.1 us  [attend(): pl.pallas_call(body, out_shape=(jax.ShapeDtypeStruct((count, rows, width)...]
  transfers between devices with their start and end apart: 13 -> 12, of which waited for: 0 -> 2; matrix products, arithmetic and copies ran while one was open for 8% -> 2% of each run, Pallas kernels for 71% -> 71%
where the time goes in v7:
time: 496 us; the launch traced here: 491 us
  Pallas kernels  441 us (89%)
  local copies, waits for them, and re-layouts  32.8 us (7%)
  starting transfers between devices  11.2 us (2%)
    pallas_call x3, Pallas kernels, experts_exchange(): pl.pallas_call(body, out_shape=shapes, in_specs=in_specs, out_specs=specs...  134 us
    pallas_call x2, Pallas kernels, reduce_project(): pl.pallas_call(body, out_shape=shapes, in_specs=[VMEM] * 4, out_specs=[VM...  74.6 us
    pallas_call x2, Pallas kernels, project_gather(): pl.pallas_call(body, out_shape=shapes, in_specs=[VMEM] * len(operands), o...  41.3 us
    pallas_call x1, Pallas kernels, start_gather(): pl.pallas_call(body, out_shape=plane_shapes(packs, blocks) + [jax.ShapeDt...  38.5 us
    pallas_call x2, Pallas kernels, attend_back(): pl.pallas_call(body, out_shape=(jax.ShapeDtypeStruct((count, rows, width)...  33.9 us
    pallas_call x2, Pallas kernels, column_gather(): pl.pallas_call(body, out_shape=jax.ShapeDtypeStruct((COLUMNS,) + tuple(va...  28 us
    pallas_call x2, Pallas kernels, attend(): pl.pallas_call(body, out_shape=(jax.ShapeDtypeStruct((count, rows, width)...  23.1 us
    pallas_call x2, Pallas kernels, column_exchange(): pl.pallas_call(body, out_shape=[jax.ShapeDtypeStruct((COLUMNS,) + slab, v...  21.9 us
  transfers between devices with their start and end apart: 12, of which 2 were waited for; matrix products, arithmetic and copies ran while one was open for 2% of the time, Pallas kernels for 71%

profile of v7, /device:TPU:12, one launch (start us, length us, event | category | flops | bytes accessed | tf_op | source)
XLA Modules:
  0.0 491.4 jit_solution(3345910450888322273)
XLA Ops:
  0.7 2.8 slice_bitcast_fusion.2
  8.1 38.5 %shard_map.221 = (bf16[2,4,4,16,128]{4,3,2,1,0:T(8,128)(2,1)S(1)}, bf16[2,4,4,24,1408]{4,3,2,1,0:T(8,128)(2,1)S(1)}, bf16[2,4,4,24,1408]{4,3,2,1,0:T(8,128)(2,1)...) custom-call(bf16[4,16,128]{2,1,0:T(8,128)(2,1)S(1)} %broadcast_in_di, ...), custom_call_target="tpu_custom_call" | custom-call | bytes 98000000 | tf_op jit(solution)/shard_map/pallas_call | solution.py:485
  48.6 18.7 %shard_map.222 = (f32[16,768]{1,0:T(8,128)S(1)}, bf16[4,128,768]{2,1,0:T(8,128)(2,1)S(1)}, bf16[4,128,384]{2,1,0:T(8,128)(2,1)S(1)}, bf16[768,384]{1,0:T(8,128)(...) custom-call(bf16[4,128,768]{2,1,0:T(8,128)(2,1)S(1)} %get-tuple-element.111.refs_0_, ...), custom_call_target="tpu_custom_call" | custom-call | bytes 77000000 | tf_op jit(solution)/shard_map/pallas_call | solution.py:692
  69.0 1.7 collective-permute-start.1
  70.6 1.4 slice_bitcast_fusion
  78.2 1.9 copy-done.11
  80.1 11.5 %shard_map.223 = (f32[4,128,384]{2,1,0:T(8,128)S(1)}, bf16[4,128,192]{2,1,0:T(8,128)(2,1)S(1)}) custom-call(s32[4,4]{1,0:T(4,128)S(1)} %pad_add_fusion.bounds_ref, bf16[4,128,384]{2,1,0:T(8,128)(2,1)S(1)} %get-tuple-element.113.q_ref, bf16[4096,384]{1,0:T(8,128)(2,1)S(1)} %bitcast.135, s32[4,1,128]{2,1,0:T(1,128)S(1)} %bitcast.167), custom_call_target="tpu_custom_call" | custom-call | bytes 45500000 | tf_op jit(solution)/shard_map/pallas_call | solution.py:1191
  91.7 10.0 %shard_map.224.attn_ref = bf16[4,128,192]{2,1,0:T(8,128)(2,1)S(1)} custom-call(bf16[4,128,192]{2,1,0:T(8,128)(2,1)S(1)} %get-tuple-element.115.refs_0_), custom_call_target="tpu_custom_call" | custom-call | bytes 31500000 | tf_op jit(solution)/shard_map/pallas_call | solution.py:192
  102.7 2.0 collective-permute-start.4
  106.6 35.3 %shard_map.227 = (bf16[8,40,768]{2,1,0:T(8,128)(2,1)S(1)}, bf16[2,8,40,768]{3,2,1,0:T(8,128)(2,1)S(1)}) custom-call(bf16[8,40,768]{2,1,0:T(8,128)(2,1)S(1)} %bitcast.162, bf16[2,1024,384]{2,1,0:T(8,128)(2,1)S(1)} %copy-done, bf16[1024,384]{1,0:T(8,128)(2,1)S(1)} %collective-permute-done.refs_2_.refs_3_, bf16[2,1024,384]{2,1,0:T(8,128)(2,1)S(1)} %copy-done.1, ...), custom_call_target="tpu_custom_call" | custom-call | bytes 98000000 | tf_op jit(solution)/shard_map/pallas_call | solution.py:1660
  142.9 22.7 %shard_map.229 = (bf16[4,128,768]{2,1,0:T(8,128)(2,1)S(1)}, bf16[4,128,384]{2,1,0:T(8,128)(2,1)S(1)}, bf16[768,384]{1,0:T(8,128)(2,1)S(1)}, bf16[384,768]{1,0:T(8,128)(2,1)S(1)}, bf16[2,4,4,128,384]{4,3,2,1,0:T(8,128)(2,1)S(1)}) custom-call(bf16[128,768]{1,0:T(8,128)(2,1)S(1)} %get-tuple-element.127.refs_0_, bf16[768,1408]{1,0:T(8,128)(2,1)S(1)} %bitcast.129, ...), custom_call_target="tpu_custom_call" | custom-call | bytes 77000000 | tf_op jit(solution)/shard_map/pallas_call | solution.py:692
  169.0 11.5 %shard_map.230 = (f32[4,128,384]{2,1,0:T(8,128)S(1)}, bf16[4,128,192]{2,1,0:T(8,128)(2,1)S(1)}) custom-call(s32[4,4]{1,0:T(4,128)S(1)} %pad_add_fusion.bounds_ref, bf16[4,128,384]{2,1,0:T(8,128)(2,1)S(1)} %get-tuple-element.129.q_ref, bf16[4096,384]{1,0:T(8,128)(2,1)S(1)} %bitcast.137, s32[4,1,128]{2,1,0:T(1,128)S(1)} %bitcast.168), custom_call_target="tpu_custom_call" | custom-call | bytes 45500000 | tf_op jit(solution)/shard_map/pallas_call | solution.py:1191
  180.5 11.9 %shard_map.231.attn_ref = bf16[4,128,192]{2,1,0:T(8,128)(2,1)S(1)} custom-call(bf16[4,128,192]{2,1,0:T(8,128)(2,1)S(1)} %get-tuple-element.131.refs_0_), custom_call_target="tpu_custom_call" | custom-call | bytes 31500000 | tf_op jit(solution)/shard_map/pallas_call | solution.py:192
  196.5 56.3 %shard_map.233 = (bf16[8,40,768]{2,1,0:T(8,128)(2,1)}, bf16[8,40,768]{2,1,0:T(8,128)(2,1)}, bf16[1024,384]{1,0:T(8,128)(2,1)}, bf16[1024,384]{1,0:T(8,128)(2,1)}...) custom-call(bf16[8,40,768]{2,1,0:T(8,128)(2,1)} %bitcast.154, ...), custom_call_target="tpu_custom_call" | custom-call | bytes 192500000 | tf_op jit(solution)/shard_map/pallas_call | solution.py:1660
  252.9 2.0 collective-permute-start.7
  256.0 1.4 shard_map.235
  257.4 14.6 %shard_map.236.dy_ref = bf16[4,128,768]{2,1,0:T(8,128)(2,1)S(1)} custom-call(bf16[128,768]{1,0:T(8,128)(2,1)S(1)} %get-tuple-element.141.src), custom_call_target="tpu_custom_call" | custom-call | bytes 49000000 | tf_op jit(solution)/shard_map/pallas_call | solution.py:218
  274.5 16.9 %shard_map.237 = (bf16[4,128,384]{2,1,0:T(8,128)(2,1)S(1)}, bf16[4096,384]{1,0:T(8,128)(2,1)S(1)}) custom-call(s32[4,4]{1,0:T(4,128)S(1)} %pad_add_fusion.bounds_ref, bf16[4,128,384]{2,1,0:T(8,128)(2,1)S(1)} %copy-done.28, bf16[4,128,768]{2,1,0:T(8,128)(2,1)S(1)} %shard_map.236.dy_ref, bf16[384,768]{1,0:T(8,128)(2,1)S(1)} %copy-done.56, ...), custom_call_target="tpu_custom_call" | custom-call | bytes 70000000 | tf_op jit(solution)/shard_map/pallas_call | solution.py:1295
  291.5 38.7 %shard_map.238 = (bf16[4,128,384]{2,1,0:T(8,128)(2,1)S(1)}, bf16[4,128,768]{2,1,0:T(8,128)(2,1)S(1)}) custom-call(bf16[2,4,2,2,128,384]{5,4,3,2,1,0:T(8,128)(2,1)S(1)} %bitcast.142, bf16[4,128,384]{2,1,0:T(8,128)(2,1)S(1)} %get-tuple-element.149.dq_ref, bf16[768,384]{1,0:T(8,128)(2,1)S(1)} %copy-done.54, bf16[768,1408]{1,0:T(8,128)(2,1)S(1)} %bitcast.131), custom_call_target="tpu_custom_call" | custom-call | bytes 91000000 | tf_op jit(solution)/shard_map/pallas_call | solution.py:1079
  331.7 42.4 %shard_map.240 = (bf16[8,40,768]{2,1,0:T(8,128)(2,1)}, bf16[1024,384]{1,0:T(8,128)(2,1)}, bf16[1024,384]{1,0:T(8,128)(2,1)}, bf16[1024,384]{1,0:T(8,128)(2,1)}, ...) custom-call(bf16[8,40,768]{2,1,0:T(8,128)(2,1)} %bitcast.157, ...), custom_call_target="tpu_custom_call" | custom-call | bytes 126000000 | tf_op jit(solution)/shard_map/pallas_call | solution.py:1660
  374.6 1.6 collective-permute-start.10
  376.6 1.6 shard_map.234
  379.2 1.4 shard_map.241
  380.7 13.4 %shard_map.242.dy_ref = bf16[4,128,768]{2,1,0:T(8,128)(2,1)S(1)} custom-call(bf16[128,768]{1,0:T(8,128)(2,1)S(1)} %get-tuple-element.160.src), custom_call_target="tpu_custom_call" | custom-call | bytes 49000000 | tf_op jit(solution)/shard_map/pallas_call | solution.py:218
  394.2 1.4 shard_map.247
  396.6 16.9 %shard_map.243 = (bf16[4,128,384]{2,1,0:T(8,128)(2,1)S(1)}, bf16[4096,384]{1,0:T(8,128)(2,1)S(1)}) custom-call(s32[4,4]{1,0:T(4,128)S(1)} %pad_add_fusion.bounds_ref, bf16[4,128,384]{2,1,0:T(8,128)(2,1)S(1)} %copy-done.20, bf16[4,128,768]{2,1,0:T(8,128)(2,1)S(1)} %shard_map.242.dy_ref, bf16[384,768]{1,0:T(8,128)(2,1)S(1)} %copy-done.52, ...), custom_call_target="tpu_custom_call" | custom-call | bytes 70000000 | tf_op jit(solution)/shard_map/pallas_call | solution.py:1295
  414.4 36.0 %shard_map.244 = (bf16[4,128,384]{2,1,0:T(8,128)(2,1)S(1)}, bf16[4,128,768]{2,1,0:T(8,128)(2,1)S(1)}) custom-call(bf16[2,4,2,2,128,384]{5,4,3,2,1,0:T(8,128)(2,1)S(1)} %bitcast.141, bf16[4,128,384]{2,1,0:T(8,128)(2,1)S(1)} %get-tuple-element.168.dq_ref, bf16[768,384]{1,0:T(8,128)(2,1)S(1)} %copy-done.50, bf16[768,1408]{1,0:T(8,128)(2,1)S(1)} %bitcast.134), custom_call_target="tpu_custom_call" | custom-call | bytes 91000000 | tf_op jit(solution)/shard_map/pallas_call | solution.py:1079
  451.5 1.5 shard_map.246
  453.0 14.9 %shard_map.248 = (bf16[4,24,640]{2,1,0:T(8,128)(2,1)S(1)}, bf16[2,24,384]{2,1,0:T(8,128)(2,1)S(1)}, bf16[4,24,640]{2,1,0:T(8,128)(2,1)S(1)}, bf16[2,24,384]{2,1,0:T(8,128)(2,1)S(1)}) custom-call(bf16[2,4,2,2,24,640]{5,4,3,2,1,0:T(8,128)(2,1)S(1)} %bitcast.148, bf16[2,2,2,2,24,384]{5,4,3,2,1,0:T(8,128)(2,1)S(1)} %bitcast.166, ...), custom_call_target="tpu_custom_call" | custom-call | bytes 70000000 | tf_op jit(solution)/shard_map/pallas_call | solution.py:872
  467.9 9.9 %shard_map.249 = (bf16[4,24,640]{2,1,0:T(8,128)(2,1)S(1)}, bf16[4,24,640]{2,1,0:T(8,128)(2,1)S(1)}, bf16[2,24,384]{2,1,0:T(8,128)(2,1)S(1)}, bf16[2,24,384]{2,1,0:T(8,128)(2,1)S(1)}) custom-call(bf16[4,24,640]{2,1,0:T(8,128)(2,1)S(1)} %get-tuple-element.186.refs_0_, bf16[4,24,640]{2,1,0:T(8,128)(2,1)S(1)} %get-tuple-element.187.refs_1_, ...), custom_call_target="tpu_custom_call" | custom-call | bytes 31500000 | tf_op jit(solution)/shard_map/pallas_call | solution.py:290
  482.0 1.4 reshape.206
  483.4 7.8 %shard_map.250 = (f32[2,1024,384]{2,1,0:T(8,128)}, f32[2,1024,384]{2,1,0:T(8,128)}, f32[2,1024,384]{2,1,0:T(8,128)}) custom-call(bf16[1024,384]{1,0:T(8,128)(2,1)} %get-tuple-element.194.refs_0_, bf16[1024,384]{1,0:T(8,128)(2,1)} %copy-done.71, bf16[1024,384]{1,0:T(8,128)(2,1)} %get-tuple-element.196.refs_2_, bf16[1024,384]{1,0:T(8,128)(2,1)} %copy-done.72, ...), custom_call_target="tpu_custom_call" | custom-call | bytes 24500000 | tf_op jit(solution)/shard_map/pallas_call | solution.py:1930
  (270 shorter events, 39.2 us)
Async XLA Ops:
  3.5 102.6 %collective-permute-start = (bf16[1024,384]{1,0:T(8,128)(2,1)}, bf16[1024,384]{1,0:T(8,128)(2,1)S(1)}, u32[]{:S(2)}, u32[]{:S(2)}) collective-permute-start(bf16[1024,384]{1,0:T(8,128)(2,1)} %get-tuple-element.120), channel_id=1, source_target_pairs={{0,16},{16,0},{1,17},{17,1},{2,18},{18,2},{3,19},{19,3},{4,20},{20... | collective-permute-start | bytes 2359304 | tf_op jit(solution)/shard_map/ppermute | solution.py:2050
  8.1 62.6 %copy-start.2 = (bf16[2,1024,384]{2,1,0:T(8,128)(2,1)S(1)}, bf16[2,1024,384]{2,1,0:T(8,128)(2,1)}, u32[]{:S(2)}) copy-start(bf16[2,1024,384]{2,1,0:T(8,128)(2,1)} %refs_6_.3) | copy-start | bytes 4718596
  69.0 37.1 %collective-permute-start.1 = (bf16[1024,384]{1,0:T(8,128)(2,1)}, bf16[1024,384]{1,0:T(8,128)(2,1)}, u32[]{:S(2)}, u32[]{:S(2)}) collective-permute-start(bf16[1024,384]{1,0:T(8,128)(2,1)} %get-tuple-element.121), channel_id=1, source_target_pairs={{0,16},{16,0},{1,17},{17,1},{2,18},{18,2},{3,19},{19,3},{4,20},{20... | collective-permute-start | bytes 2359304 | tf_op jit(solution)/shard_map/ppermute | solution.py:2050
  72.0 34.6 %collective-permute-start.2 = (bf16[1024,384]{1,0:T(8,128)(2,1)}, bf16[1024,384]{1,0:T(8,128)(2,1)}, u32[]{:S(2)}, u32[]{:S(2)}) collective-permute-start(bf16[1024,384]{1,0:T(8,128)(2,1)} %get-tuple-element.122), channel_id=1, source_target_pairs={{0,16},{16,0},{1,17},{17,1},{2,18},{18,2},{3,19},{19,3},{4,20},{20... | collective-permute-start | bytes 2359304 | tf_op jit(solution)/shard_map/ppermute | solution.py:2050
  76.1 116.4 %copy-start.36 = (bf16[128,320]{1,0:T(8,128)(2,1)}, bf16[128,320]{1,0:T(8,128)(2,1)S(1)}, u32[]{:S(2)}) copy-start(bf16[128,320]{1,0:T(8,128)(2,1)S(1)} %get-tuple-element.262.picks_ref) | copy-start | bytes 245764
  101.7 40.2 %copy-start.29 = (f32[320,128]{1,0:T(8,128)}, f32[320,128]{1,0:T(8,128)S(1)}, u32[]{:S(2)}) copy-start(f32[320,128]{1,0:T(8,128)S(1)} %get-tuple-element.253.gates_ref.refs_1_) | copy-start | bytes 491524
  102.6 39.3 %copy-start.21 = (f32[128,768]{1,0:T(8,128)}, f32[128,768]{1,0:T(8,128)S(1)}, u32[]{:S(2)}) copy-start(f32[128,768]{1,0:T(8,128)S(1)} %get-tuple-element.125.mid_ref) | copy-start | bytes 1179652
  102.6 92.4 %collective-permute-start.3 = (bf16[1024,384]{1,0:T(8,128)(2,1)S(1)}, bf16[1024,384]{1,0:T(8,128)(2,1)S(1)}, u32[]{:S(2)}, u32[]{:S(2)}) collective-permute-start(bf16[1024,384]{1,0:T(8,128)(2,1)S(1)} %copy-done.74), channel_id=1, source_target_pairs={{0,16},{16,0},{1,17},{17,1},{2,18},{18,2},{3,19},{19,3},{4,20},{20... | collective-permute-start | bytes 2359304 | tf_op jit(solution)/shard_map/ppermute | solution.py:2050
  102.7 92.3 %collective-permute-start.4 = (bf16[1024,384]{1,0:T(8,128)(2,1)S(1)}, bf16[1024,384]{1,0:T(8,128)(2,1)S(1)}, u32[]{:S(2)}, u32[]{:S(2)}) collective-permute-start(bf16[1024,384]{1,0:T(8,128)(2,1)S(1)} %copy-done.75), channel_id=1, source_target_pairs={{0,16},{16,0},{1,17},{17,1},{2,18},{18,2},{3,19},{19,3},{4,20},{20... | collective-permute-start | bytes 2359304 | tf_op jit(solution)/shard_map/ppermute | solution.py:2050
  142.8 49.6 %copy-start.25 = (f32[128,768]{1,0:T(8,128)}, f32[128,768]{1,0:T(8,128)S(1)}, u32[]{:S(2)}) copy-start(f32[128,768]{1,0:T(8,128)S(1)} %get-tuple-element.132.x_ref) | copy-start | bytes 1179652
  168.1 27.0 %collective-permute-start.5 = (bf16[1024,384]{1,0:T(8,128)(2,1)S(1)}, bf16[1024,384]{1,0:T(8,128)(2,1)S(1)}, u32[]{:S(2)}, u32[]{:S(2)}) collective-permute-start(bf16[1024,384]{1,0:T(8,128)(2,1)S(1)} %copy-done.76), channel_id=1, source_target_pairs={{0,16},{16,0},{1,17},{17,1},{2,18},{18,2},{3,19},{19,3},{4,20},{20... | collective-permute-start | bytes 2359304 | tf_op jit(solution)/shard_map/ppermute | solution.py:2050
  195.0 59.9 %copy-start.23 = (f32[128,768]{1,0:T(8,128)}, f32[128,768]{1,0:T(8,128)S(1)}, u32[]{:S(2)}) copy-start(f32[128,768]{1,0:T(8,128)S(1)} %get-tuple-element.139.mid_ref) | copy-start | bytes 1179652
  196.5 58.5 %copy-start.37 = (bf16[128,320]{1,0:T(8,128)(2,1)S(1)}, bf16[128,320]{1,0:T(8,128)(2,1)}, u32[]{:S(2)}) copy-start(bf16[128,320]{1,0:T(8,128)(2,1)} %copy-done.36) | copy-start | bytes 245764
  196.5 58.5 %copy-start.43 = (bf16[128,768]{1,0:T(8,128)(2,1)S(1)}, bf16[128,768]{1,0:T(8,128)(2,1)}, u32[]{:S(2)}) copy-start(bf16[128,768]{1,0:T(8,128)(2,1)} %up_ref.1) | copy-start | bytes 589828
  196.5 58.5 %copy-start.59 = (f32[128,128]{1,0:T(8,128)S(1)}, f32[128,128]{1,0:T(8,128)}, u32[]{:S(2)}) copy-start(f32[128,128]{1,0:T(8,128)} %get-tuple-element.264.other_ref) | copy-start | bytes 196612
  252.8 20.7 %collective-permute-start.6 = (bf16[1024,384]{1,0:T(8,128)(2,1)}, bf16[1024,384]{1,0:T(8,128)(2,1)S(1)}, u32[]{:S(2)}, u32[]{:S(2)}) collective-permute-start(bf16[1024,384]{1,0:T(8,128)(2,1)} %get-tuple-element.142), channel_id=1, source_target_pairs={{0,16},{16,0},{1,17},{17,1},{2,18},{18,2},{3,19},{19,3},{4,20},{20... | collective-permute-start | bytes 2359304 | tf_op jit(solution)/shard_map/ppermute | solution.py:2144
  252.9 38.5 %collective-permute-start.7 = (bf16[1024,384]{1,0:T(8,128)(2,1)}, bf16[1024,384]{1,0:T(8,128)(2,1)S(1)}, u32[]{:S(2)}, u32[]{:S(2)}) collective-permute-start(bf16[1024,384]{1,0:T(8,128)(2,1)} %get-tuple-element.147), channel_id=1, source_target_pairs={{0,16},{16,0},{1,17},{17,1},{2,18},{18,2},{3,19},{19,3},{4,20},{20... | collective-permute-start | bytes 2359304 | tf_op jit(solution)/shard_map/ppermute | solution.py:2144
  272.0 106.2 %collective-permute-start.8 = (bf16[1024,384]{1,0:T(8,128)(2,1)}, bf16[1024,384]{1,0:T(8,128)(2,1)}, u32[]{:S(2)}, u32[]{:S(2)}) collective-permute-start(bf16[1024,384]{1,0:T(8,128)(2,1)} %get-tuple-element.157), channel_id=1, source_target_pairs={{0,16},{16,0},{1,17},{17,1},{2,18},{18,2},{3,19},{19,3},{4,20},{20... | collective-permute-start | bytes 2359304 | tf_op jit(solution)/shard_map/ppermute | solution.py:2144
  291.4 38.7 %copy-start.17 = (bf16[4,128,384]{2,1,0:T(8,128)(2,1)}, bf16[4,128,384]{2,1,0:T(8,128)(2,1)S(1)}, u32[]{:S(2)}) copy-start(bf16[4,128,384]{2,1,0:T(8,128)(2,1)S(1)} %get-tuple-element.149.dq_ref) | copy-start | bytes 1179652
  291.4 38.7 %copy-start.70 = (bf16[1024,384]{1,0:T(8,128)(2,1)}, bf16[1024,384]{1,0:T(8,128)(2,1)S(1)}, u32[]{:S(2)}) copy-start(bf16[1024,384]{1,0:T(8,128)(2,1)S(1)} %collective-permute-done.7.refs_9_) | copy-start | bytes 2359300
  291.5 38.7 %copy-start.26 = (f32[128,768]{1,0:T(8,128)S(1)}, f32[128,768]{1,0:T(8,128)}, u32[]{:S(2)}) copy-start(f32[128,768]{1,0:T(8,128)} %copy-done.25) | copy-start | bytes 1179652
  291.5 38.7 %copy-start.30 = (f32[320,128]{1,0:T(8,128)S(1)}, f32[320,128]{1,0:T(8,128)}, u32[]{:S(2)}) copy-start(f32[320,128]{1,0:T(8,128)} %copy-done.29) | copy-start | bytes 491524
  331.7 45.0 %copy-start.24 = (f32[128,768]{1,0:T(8,128)S(1)}, f32[128,768]{1,0:T(8,128)}, u32[]{:S(2)}) copy-start(f32[128,768]{1,0:T(8,128)} %copy-done.23) | copy-start | bytes 1179652
  331.7 45.0 %copy-start.44 = (f32[128,320]{1,0:T(8,128)S(1)}, f32[128,320]{1,0:T(8,128)}, u32[]{:S(2)}) copy-start(f32[128,320]{1,0:T(8,128)} %get-tuple-element.250.weights_ref) | copy-start | bytes 491524
  331.7 45.0 %copy-start.60 = (f32[128,128]{1,0:T(8,128)S(1)}, f32[128,128]{1,0:T(8,128)}, u32[]{:S(2)}) copy-start(f32[128,128]{1,0:T(8,128)} %get-tuple-element.264.other_ref) | copy-start | bytes 196612
  331.7 45.0 %copy-start.62 = (bf16[8,40,768]{2,1,0:T(8,128)(2,1)S(1)}, bf16[8,40,768]{2,1,0:T(8,128)(2,1)}, u32[]{:S(2)}) copy-start(bf16[8,40,768]{2,1,0:T(8,128)(2,1)} %get-tuple-element.138) | copy-start | bytes 1474564
  331.7 46.5 %copy-start.22 = (f32[128,768]{1,0:T(8,128)S(1)}, f32[128,768]{1,0:T(8,128)}, u32[]{:S(2)}) copy-start(f32[128,768]{1,0:T(8,128)} %copy-done.21) | copy-start | bytes 1179652
  331.7 46.5 %copy-start.58 = (f32[128,128]{1,0:T(8,128)S(1)}, f32[128,128]{1,0:T(8,128)}, u32[]{:S(2)}) copy-start(f32[128,128]{1,0:T(8,128)} %copy-done.57) | copy-start | bytes 196612
  374.2 21.5 %collective-permute-start.9 = (bf16[1024,384]{1,0:T(8,128)(2,1)}, bf16[1024,384]{1,0:T(8,128)(2,1)S(1)}, u32[]{:S(2)}, u32[]{:S(2)}) collective-permute-start(bf16[1024,384]{1,0:T(8,128)(2,1)} %get-tuple-element.161), channel_id=1, source_target_pairs={{0,16},{16,0},{1,17},{17,1},{2,18},{18,2},{3,19},{19,3},{4,20},{20... | collective-permute-start | bytes 2359304 | tf_op jit(solution)/shard_map/ppermute | solution.py:2144
  374.6 38.9 %collective-permute-start.10 = (bf16[1024,384]{1,0:T(8,128)(2,1)}, bf16[1024,384]{1,0:T(8,128)(2,1)S(1)}, u32[]{:S(2)}, u32[]{:S(2)}) collective-permute-start(bf16[1024,384]{1,0:T(8,128)(2,1)} %get-tuple-element.166), channel_id=1, source_target_pairs={{0,16},{16,0},{1,17},{17,1},{2,18},{18,2},{3,19},{19,3},{4,20},{20... | collective-permute-start | bytes 2359304 | tf_op jit(solution)/shard_map/ppermute | solution.py:2144
  376.2 74.2 %collective-permute-start.11 = (bf16[1024,384]{1,0:T(8,128)(2,1)}, bf16[1024,384]{1,0:T(8,128)(2,1)S(1)}, u32[]{:S(2)}, u32[]{:S(2)}) collective-permute-start(bf16[1024,384]{1,0:T(8,128)(2,1)} %get-tuple-element.171), channel_id=1, source_target_pairs={{0,16},{16,0},{1,17},{17,1},{2,18},{18,2},{3,19},{19,3},{4,20},{20... | collective-permute-start | bytes 2359304 | tf_op jit(solution)/shard_map/ppermute | solution.py:2144
  414.4 37.1 %copy-start.32 = (bf16[4,128,192]{2,1,0:T(8,128)(2,1)S(1)}, bf16[4,128,192]{2,1,0:T(8,128)(2,1)}, u32[]{:S(2)}) copy-start(bf16[4,128,192]{2,1,0:T(8,128)(2,1)} %copy-done.31) | copy-start | bytes 589828
  (69 other events, 811.8 us)

commit v8 on v7

--- a/solution.py
+++ b/solution.py
@@ -678,11 +678,11 @@
             chain.finish()
 
     shapes = [
-        jax.ShapeDtypeStruct((COLUMNS, rows, features), jnp.bfloat16),
-        jax.ShapeDtypeStruct((COLUMNS, rows, wide), jnp.bfloat16),
-        jax.ShapeDtypeStruct((features, wide), jnp.bfloat16),
-        jax.ShapeDtypeStruct((wide, features), jnp.bfloat16),
-        jax.ShapeDtypeStruct((2, COLUMNS, span, rows, wide), jnp.bfloat16),
+        pltpu.HBM((COLUMNS, rows, features), jnp.bfloat16),
+        make((COLUMNS, rows, wide), jnp.bfloat16),
+        pltpu.HBM((features, wide), jnp.bfloat16),
+        pltpu.HBM((wide, features), jnp.bfloat16),
+        make((2, COLUMNS, span, rows, wide), jnp.bfloat16),
     ]
     operands = [source, pack]
     if chained:
@@ -710,7 +710,9 @@
         ],
         compiler_params=comm_params(
             collective_id,
-            operands + shapes[:-1] + [make((COLUMNS, rows, wide), jnp.bfloat16)],
+            operands
+            + [make(shape.shape, shape.dtype) for shape in shapes[:-1]]
+            + [make((COLUMNS, rows, wide), jnp.bfloat16)],
             3 * SPARE_BYTES,
         ),
         cost_estimate=lasting(cost),
@@ -1320,8 +1322,21 @@
 
 
 def experts_exchange(
-    sent, saved, own, other, layer, blocks, collective_id, forward, backward, cost
+    sent,
+    saved,
+    own,
+    other,
+    layer,
+    blocks,
+    collective_id,
+    forward,
+    backward,
+    cost,
+    ahead=None,
+    cross=(),
 ):
+    fetch = other[2] is None
+    other = [w for w in other if w is not None]
     copies = blocks // NE
     half = NE // 2
     slots, width = sent[0].shape[1:]
@@ -1347,10 +1362,15 @@
 
         srcs = take(count)
         saved_ref = take(1)[0] if not forward else None
-        weight_refs = take(6)
+        weight_refs = take(3 + len(other))
+        ahead_ref = take(1)[0] if ahead is not None else None
+        cross_refs = take(len(cross))
         homes = take(homes_count)
         arrived_ref = take(1)[0] if not backward else None
+        fetched_ref = take(1)[0] if fetch and not backward else None
+        next_ref = take(1)[0] if ahead is not None else None
         keeps, aways = (take(3), take(3)) if backward else ([], [])
+        crossed = take(len(cross))
         lands = take(count)
         weights = take(6)
         parts, sib_ins, totals = take(homes_count), take(homes_count), take(homes_count)
@@ -1363,6 +1383,7 @@
             out_sems = take(1)[0]
         load_sems, own_sems, send_sems, recv_sems, pass_sems, land_sems = take(6)
         home_own, home_send, home_recv, part_send, part_recv, arrived_sem = take(6)
+        swap_send, swap_recv = take(2)
 
         head, blk = lax.axis_index("head"), lax.axis_index("blk")
         expert, piece = lax.div(blk, copies), lax.rem(blk, copies)
@@ -1371,7 +1392,8 @@
         places = [lax.rem(piece + k, copies) for k in range(copies)]
         siblings = [(head, expert * copies + places[k]) for k in range(copies)]
         others = [lax.rem(expert + d, NE) for d in range(NE)]
-        greet([(head, e * copies + piece) for e in others[1:]] + siblings[1:])
+        swaps = [(1 - head, blk)] if fetch or ahead is not None or cross else []
+        greet([(head, e * copies + piece) for e in others[1:]] + siblings[1:] + swaps)
         mine = pl.ds(pl.multiple_of(head * features, LANES), features)
         rest = pl.ds(pl.multiple_of((1 - head) * features, LANES), features)
         steps = [(far, sizes[0]), (far + sizes[0], sizes[1]), (near, sizes[2])]
@@ -1412,8 +1434,42 @@
 
         for t in range(3):
             send(t)
+        crossing = []
+        if fetch:
+            crossing.append(
+                remote(
+                    weight_refs[4].at[layer],
+                    weights[5],
+                    swap_send.at[0],
+                    swap_recv.at[0],
+                    swaps[0],
+                )
+            )
+        if ahead is not None:
+            crossing.append(
+                remote(
+                    ahead_ref.at[layer + 1],
+                    next_ref,
+                    swap_send.at[1],
+                    swap_recv.at[1],
+                    swaps[0],
+                )
+            )
+        for n in range(len(cross)):
+            crossing.append(
+                remote(
+                    cross_refs[n],
+                    crossed[n],
+                    swap_send.at[2 + n],
+                    swap_recv.at[2 + n],
+                    swaps[0],
+                )
+            )
+        for n, copy in enumerate(crossing):
+            if ahead is None or n == 0:
+                copy.start()
         loads = []
-        for n in range(6):
+        for n in range(3 + len(other)):
             weight = weight_refs[n] if n % 2 else weight_refs[n].at[layer]
             copy = pltpu.make_async_copy(weight, weights[n], load_sems.at[n])
             copy.start()
@@ -1561,6 +1617,10 @@
             early(0)
         for t in range(len(steps)):
             arrive(t)
+            if t == 0 and fetch:
+                crossing[0].wait_recv()
+                if ahead is not None:
+                    crossing[1].start()
             work(t)
             if t > 0:
                 give_back(t - 1)
@@ -1600,6 +1660,10 @@
             copy = pltpu.make_async_copy(lands[0], arrived_ref, arrived_sem)
             copy.start()
             stays.append(copy)
+            if fetch:
+                copy = pltpu.make_async_copy(weights[5], fetched_ref, load_sems.at[5])
+                copy.start()
+                stays.append(copy)
         for n in range(homes_count):
             for e in others[1:]:
                 place = homes[n].at[e]
@@ -1613,6 +1677,10 @@
             copy.wait_send()
         for copy in stays:
             copy.wait()
+        for copy in crossing[int(fetch) :]:
+            copy.wait_recv()
+        for copy in crossing:
+            copy.wait_send()
         if backward:
 
             def settle(j, _):
@@ -1627,11 +1695,14 @@
     shapes = [make((NE, slots, width), kind)] * homes_count
     specs = [ANY] * homes_count
     if not backward:
-        shapes.append(make(slab, kind))
+        shapes.append(pltpu.HBM(slab, kind))
         specs.append(HBM)
+        for _ in range(int(fetch) + int(ahead is not None)):
+            shapes.append(pltpu.HBM((hidden, features), kind))
+            specs.append(HBM)
     else:
-        shapes += [make((hidden, features), kind)] * 6
-        specs += [HBM] * 6
+        shapes += [pltpu.HBM((hidden, features), kind)] * (6 + len(cross))
+        specs += [HBM] * (6 + len(cross))
     scratch = [pltpu.VMEM(slab, kind)] * count
     scratch += [pltpu.VMEM((hidden, features), kind)] * 6
     scratch += [pltpu.VMEM(slab, kind)] * homes_count
@@ -1649,14 +1720,18 @@
     scratch += [DMA((6,)), DMA((count,)), DMA((count, NE)), DMA((count, NE))]
     scratch += [DMA((count, copies, NE))] * 2
     scratch += [DMA((homes_count,)), DMA((homes_count, NE)), DMA((homes_count, NE))]
-    scratch += [DMA((homes_count, copies, NE))] * 2 + [DMA]
+    scratch += [DMA((homes_count, copies, NE))] * 2 + [DMA] + [DMA((2 + len(cross),))] * 2
     operands = list(sent)
     in_specs = [ANY] * count
     if not forward:
         operands.append(saved)
         in_specs.append(VMEM)
-    operands += [w for pair in zip(own, other) for w in pair]
-    in_specs += [HBM] * 6
+    for n in range(3):
+        operands += [own[n]] + other[n : n + 1]
+    if ahead is not None:
+        operands.append(ahead)
+    operands += list(cross)
+    in_specs += [HBM] * (len(operands) - len(in_specs))
     return pl.pallas_call(
         body,
         out_shape=shapes,
@@ -2139,9 +2214,15 @@
                 False,
                 True,
                 36,
-            )
-            dback, held[2] = lax.optimization_barrier((dback, held[2]))
-        got = [lax.ppermute(away, "head", swap) for away in wgrads[3:]]
+                None,
+                waiting,
+            )
+            expert_grads[layer + 1][1][1:] = wgrads[6:]
+        before = layer > 0
+        if before:
+            got, waiting = [lax.ppermute(wgrads[3], "head", swap)], wgrads[4:6]
+        else:
+            got = [lax.ppermute(away, "head", swap) for away in wgrads[3:5]]
         dmid, dy, rows = experts_back(
             dback.reshape((NE * CAP, width)),
             picks[layer],
@@ -2156,7 +2237,8 @@
         dq, dkv_all = attend_back(
             bounds, queries, dy, out_rows, attended, kv_all, starts, scale
         )
-        dkv_all, got[1] = lax.optimization_barrier((dkv_all, got[1]))
+        if not before:
+            dkv_all, got[1] = lax.optimization_barrier((dkv_all, got[1]))
         dkv, dxn = reduce_project(
             dkv_all.reshape((2, COLUMNS, span, token_rows, wide)),
             dq,
@@ -2165,9 +2247,6 @@
             blocks,
             10,
         )
-        before = layer > 0
-        if not before:
-            dxn, got[2] = lax.optimization_barrier((dxn, got[2]))
         upstream, rows, *dz = finish(
             dxn,
             values,
@@ -2181,7 +2260,6 @@
         if before:
             (dz,) = dz
         expert_grads[layer] = wgrads[:3], got
-        held = got
         qkv_part, out_part = pack_grads(
             column.reshape((-1, width)),
             dq.reshape((-1, wide)),
@@ -2197,6 +2275,8 @@
 
     packed = [part for layer in range(LAYERS) for part in shared_grads[layer]]
     reduced = plane_reduce(packed, blocks, 12, 20)
+    away, _ = lax.optimization_barrier((wgrads[5], reduced[0]))
+    expert_grads[0][1].append(lax.ppermute(away, "head", swap))
     exchanged = final_exchange(reduced[::2], reduced[1::2], blocks, 13)
     from_planes, out_grads = exchanged[:LAYERS], exchanged[LAYERS:]
     from_planes = jnp.stack(from_planes, axis=1).astype(jnp.float32)

time: 496 us -> 481 us (0.970)
  Pallas kernels: 441 us -> 428 us
    pallas_call x2, Pallas kernels: 74.6 us -> 58.3 us  [reduce_project(): pl.pallas_call(body, out_shape=shapes, in_specs=[VMEM] * 4, out_specs=[VM...]
    unnamed x182 -> x170, local copies, waits for them, and re-layouts: 20 us -> 15.4 us
  transfers between devices with their start and end apart: 12 -> 10, of which waited for: 2 -> 4; matrix products, arithmetic and copies ran while one was open for 2% -> 3% of each run, Pallas kernels for 71% -> 48%
where the time goes in v8:
time: 481 us; the launch traced here: 474 us
  Pallas kernels  428 us (89%)
  local copies, waits for them, and re-layouts  28.3 us (6%)
  starting transfers between devices  8.99 us (2%)
    pallas_call x3, Pallas kernels, experts_exchange(): pl.pallas_call(body, out_shape=shapes, in_specs=in_specs, out_specs=specs...  135 us
    pallas_call x2, Pallas kernels, reduce_project(): pl.pallas_call(body, out_shape=shapes, in_specs=[VMEM] * 4, out_specs=[VM...  58.3 us
    pallas_call x2, Pallas kernels, project_gather(): pl.pallas_call(body, out_shape=shapes, in_specs=[VMEM] * len(operands), o...  41.2 us
    pallas_call x1, Pallas kernels, start_gather(): pl.pallas_call(body, out_shape=plane_shapes(packs, blocks) + [jax.ShapeDt...  38.5 us
    pallas_call x2, Pallas kernels, attend_back(): pl.pallas_call(body, out_shape=(jax.ShapeDtypeStruct((count, rows, width)...  33.8 us
    pallas_call x2, Pallas kernels, column_gather(): pl.pallas_call(body, out_shape=jax.ShapeDtypeStruct((COLUMNS,) + tuple(va...  29.3 us
    pallas_call x2, Pallas kernels, attend(): pl.pallas_call(body, out_shape=(jax.ShapeDtypeStruct((count, rows, width)...  23.1 us
    pallas_call x2, Pallas kernels, column_exchange(): pl.pallas_call(body, out_shape=[jax.ShapeDtypeStruct((COLUMNS,) + slab, v...  21.6 us
  transfers between devices with their start and end apart: 10, of which 4 were waited for; matrix products, arithmetic and copies ran while one was open for 3% of the time, Pallas kernels for 48%

profile of v8, /device:TPU:12, one launch (start us, length us, event | category | flops | bytes accessed | tf_op | source)
XLA Modules:
  0.0 474.3 jit_solution(2955176939462575177)
XLA Ops:
  0.7 2.8 slice_bitcast_fusion.2
  8.1 38.5 %shard_map.221 = (bf16[2,4,4,16,128]{4,3,2,1,0:T(8,128)(2,1)S(1)}, bf16[2,4,4,24,1408]{4,3,2,1,0:T(8,128)(2,1)S(1)}, bf16[2,4,4,24,1408]{4,3,2,1,0:T(8,128)(2,1)...) custom-call(bf16[4,16,128]{2,1,0:T(8,128)(2,1)S(1)} %broadcast_in_di, ...), custom_call_target="tpu_custom_call" | custom-call | bytes 98000000 | tf_op jit(solution)/shard_map/pallas_call | solution.py:485
  47.9 18.7 %shard_map.222 = (f32[16,768]{1,0:T(8,128)S(1)}, bf16[4,128,768]{2,1,0:T(8,128)(2,1)}, bf16[4,128,384]{2,1,0:T(8,128)(2,1)S(1)}, bf16[768,384]{1,0:T(8,128)(2,1)...) custom-call(bf16[4,128,768]{2,1,0:T(8,128)(2,1)S(1)} %get-tuple-element.108.refs_0_, ...), custom_call_target="tpu_custom_call" | custom-call | bytes 77000000 | tf_op jit(solution)/shard_map/pallas_call | solution.py:692
  66.7 1.5 collective-permute-start.1
  68.2 1.4 slice_bitcast_fusion
  74.2 1.9 copy-done.11
  76.1 11.5 %shard_map.223 = (f32[4,128,384]{2,1,0:T(8,128)S(1)}, bf16[4,128,192]{2,1,0:T(8,128)(2,1)S(1)}) custom-call(s32[4,4]{1,0:T(4,128)S(1)} %pad_add_fusion.bounds_ref, bf16[4,128,384]{2,1,0:T(8,128)(2,1)S(1)} %get-tuple-element.110.q_ref, bf16[4096,384]{1,0:T(8,128)(2,1)S(1)} %bitcast.135, s32[4,1,128]{2,1,0:T(1,128)S(1)} %bitcast.167), custom_call_target="tpu_custom_call" | custom-call | bytes 45500000 | tf_op jit(solution)/shard_map/pallas_call | solution.py:1193
  87.7 9.8 %shard_map.224.attn_ref = bf16[4,128,192]{2,1,0:T(8,128)(2,1)S(1)} custom-call(bf16[4,128,192]{2,1,0:T(8,128)(2,1)S(1)} %get-tuple-element.112.refs_0_), custom_call_target="tpu_custom_call" | custom-call | bytes 31500000 | tf_op jit(solution)/shard_map/pallas_call | solution.py:192
  98.5 2.0 collective-permute-start.4
  101.9 2.4 collective-permute-done.2.refs_6_.refs_7_
  104.3 35.1 %shard_map.227 = (bf16[8,40,768]{2,1,0:T(8,128)(2,1)S(1)}, bf16[2,8,40,768]{3,2,1,0:T(8,128)(2,1)}) custom-call(bf16[8,40,768]{2,1,0:T(8,128)(2,1)S(1)} %bitcast.162, bf16[2,1024,384]{2,1,0:T(8,128)(2,1)S(1)} %copy-done, bf16[1024,384]{1,0:T(8,128)(2,1)S(1)} %collective-permute-done.refs_2_.refs_3_, bf16[2,1024,384]{2,1,0:T(8,128)(2,1)S(1)} %copy-done.1, ...), custom_call_target="tpu_custom_call" | custom-call | bytes 98000000 | tf_op jit(solution)/shard_map/pallas_call | solution.py:1735
  140.4 22.5 %shard_map.229 = (bf16[4,128,768]{2,1,0:T(8,128)(2,1)}, bf16[4,128,384]{2,1,0:T(8,128)(2,1)S(1)}, bf16[768,384]{1,0:T(8,128)(2,1)}, bf16[384,768]{1,0:T(8,128)(2,1)}, bf16[2,4,4,128,384]{4,3,2,1,0:T(8,128)(2,1)S(1)}) custom-call(bf16[128,768]{1,0:T(8,128)(2,1)S(1)} %get-tuple-element.124.refs_0_, bf16[768,1408]{1,0:T(8,128)(2,1)S(1)} %bitcast.129, ...), custom_call_target="tpu_custom_call" | custom-call | bytes 77000000 | tf_op jit(solution)/shard_map/pallas_call | solution.py:692
  164.0 11.5 %shard_map.230 = (f32[4,128,384]{2,1,0:T(8,128)S(1)}, bf16[4,128,192]{2,1,0:T(8,128)(2,1)S(1)}) custom-call(s32[4,4]{1,0:T(4,128)S(1)} %pad_add_fusion.bounds_ref, bf16[4,128,384]{2,1,0:T(8,128)(2,1)S(1)} %get-tuple-element.126.q_ref, bf16[4096,384]{1,0:T(8,128)(2,1)S(1)} %bitcast.137, s32[4,1,128]{2,1,0:T(1,128)S(1)} %bitcast.168), custom_call_target="tpu_custom_call" | custom-call | bytes 45500000 | tf_op jit(solution)/shard_map/pallas_call | solution.py:1193
  175.6 11.8 %shard_map.231.attn_ref = bf16[4,128,192]{2,1,0:T(8,128)(2,1)S(1)} custom-call(bf16[4,128,192]{2,1,0:T(8,128)(2,1)S(1)} %get-tuple-element.128.refs_0_), custom_call_target="tpu_custom_call" | custom-call | bytes 31500000 | tf_op jit(solution)/shard_map/pallas_call | solution.py:192
  191.4 56.4 %shard_map.233 = (bf16[8,40,768]{2,1,0:T(8,128)(2,1)}, bf16[8,40,768]{2,1,0:T(8,128)(2,1)}, bf16[1024,384]{1,0:T(8,128)(2,1)}, bf16[1024,384]{1,0:T(8,128)(2,1)}...) custom-call(bf16[8,40,768]{2,1,0:T(8,128)(2,1)} %bitcast.154, ...), custom_call_target="tpu_custom_call" | custom-call | bytes 192500000 | tf_op jit(solution)/shard_map/pallas_call | solution.py:1735
  249.1 1.4 shard_map.235
  250.5 15.8 %shard_map.236.dy_ref = bf16[4,128,768]{2,1,0:T(8,128)(2,1)S(1)} custom-call(bf16[128,768]{1,0:T(8,128)(2,1)S(1)} %get-tuple-element.138.src), custom_call_target="tpu_custom_call" | custom-call | bytes 49000000 | tf_op jit(solution)/shard_map/pallas_call | solution.py:218
  268.2 16.9 %shard_map.237 = (bf16[4,128,384]{2,1,0:T(8,128)(2,1)S(1)}, bf16[4096,384]{1,0:T(8,128)(2,1)S(1)}) custom-call(s32[4,4]{1,0:T(4,128)S(1)} %pad_add_fusion.bounds_ref, bf16[4,128,384]{2,1,0:T(8,128)(2,1)S(1)} %copy-done.28, bf16[4,128,768]{2,1,0:T(8,128)(2,1)S(1)} %shard_map.236.dy_ref, bf16[384,768]{1,0:T(8,128)(2,1)S(1)} %copy-done.49, ...), custom_call_target="tpu_custom_call" | custom-call | bytes 70000000 | tf_op jit(solution)/shard_map/pallas_call | solution.py:1297
  285.2 28.8 %shard_map.238 = (bf16[4,128,384]{2,1,0:T(8,128)(2,1)S(1)}, bf16[4,128,768]{2,1,0:T(8,128)(2,1)S(1)}) custom-call(bf16[2,4,2,2,128,384]{5,4,3,2,1,0:T(8,128)(2,1)S(1)} %bitcast.142, bf16[4,128,384]{2,1,0:T(8,128)(2,1)S(1)} %get-tuple-element.144.dq_ref, bf16[768,384]{1,0:T(8,128)(2,1)S(1)} %copy-done.48, bf16[768,1408]{1,0:T(8,128)(2,1)S(1)} %bitcast.131), custom_call_target="tpu_custom_call" | custom-call | bytes 91000000 | tf_op jit(solution)/shard_map/pallas_call | solution.py:1081
  316.3 43.3 %shard_map.240 = (bf16[8,40,768]{2,1,0:T(8,128)(2,1)}, bf16[1024,384]{1,0:T(8,128)(2,1)}, bf16[1024,384]{1,0:T(8,128)(2,1)}, bf16[1024,384]{1,0:T(8,128)(2,1)}, ...) custom-call(bf16[8,40,768]{2,1,0:T(8,128)(2,1)} %bitcast.156, ...), custom_call_target="tpu_custom_call" | custom-call | bytes 126000000 | tf_op jit(solution)/shard_map/pallas_call | solution.py:1735
  359.6 1.4 collective-permute-start.7
  363.7 1.4 shard_map.241
  365.2 13.5 %shard_map.242.dy_ref = bf16[4,128,768]{2,1,0:T(8,128)(2,1)S(1)} custom-call(bf16[128,768]{1,0:T(8,128)(2,1)S(1)} %get-tuple-element.155.src), custom_call_target="tpu_custom_call" | custom-call | bytes 49000000 | tf_op jit(solution)/shard_map/pallas_call | solution.py:218
  378.7 1.4 shard_map.247
  381.3 16.9 %shard_map.243 = (bf16[4,128,384]{2,1,0:T(8,128)(2,1)S(1)}, bf16[4096,384]{1,0:T(8,128)(2,1)S(1)}) custom-call(s32[4,4]{1,0:T(4,128)S(1)} %pad_add_fusion.bounds_ref, bf16[4,128,384]{2,1,0:T(8,128)(2,1)S(1)} %copy-done.20, bf16[4,128,768]{2,1,0:T(8,128)(2,1)S(1)} %shard_map.242.dy_ref, bf16[384,768]{1,0:T(8,128)(2,1)S(1)} %copy-done.47, ...), custom_call_target="tpu_custom_call" | custom-call | bytes 70000000 | tf_op jit(solution)/shard_map/pallas_call | solution.py:1297
  398.3 29.5 %shard_map.244 = (bf16[4,128,384]{2,1,0:T(8,128)(2,1)S(1)}, bf16[4,128,768]{2,1,0:T(8,128)(2,1)S(1)}) custom-call(bf16[2,4,2,2,128,384]{5,4,3,2,1,0:T(8,128)(2,1)S(1)} %bitcast.141, bf16[4,128,384]{2,1,0:T(8,128)(2,1)S(1)} %get-tuple-element.163.dq_ref, bf16[768,384]{1,0:T(8,128)(2,1)S(1)} %copy-done.46, bf16[768,1408]{1,0:T(8,128)(2,1)S(1)} %bitcast.134), custom_call_target="tpu_custom_call" | custom-call | bytes 91000000 | tf_op jit(solution)/shard_map/pallas_call | solution.py:1081
  428.9 1.4 shard_map.246
  430.4 15.7 %shard_map.248 = (bf16[4,24,640]{2,1,0:T(8,128)(2,1)S(1)}, bf16[2,24,384]{2,1,0:T(8,128)(2,1)S(1)}, bf16[4,24,640]{2,1,0:T(8,128)(2,1)S(1)}, bf16[2,24,384]{2,1,0:T(8,128)(2,1)S(1)}) custom-call(bf16[2,4,2,2,24,640]{5,4,3,2,1,0:T(8,128)(2,1)S(1)} %bitcast.148, bf16[2,2,2,2,24,384]{5,4,3,2,1,0:T(8,128)(2,1)S(1)} %bitcast.166, ...), custom_call_target="tpu_custom_call" | custom-call | bytes 70000000 | tf_op jit(solution)/shard_map/pallas_call | solution.py:874
  446.9 1.6 shard_map.234
  448.4 11.3 %shard_map.249 = (bf16[4,24,640]{2,1,0:T(8,128)(2,1)S(1)}, bf16[4,24,640]{2,1,0:T(8,128)(2,1)S(1)}, bf16[2,24,384]{2,1,0:T(8,128)(2,1)S(1)}, bf16[2,24,384]{2,1,0:T(8,128)(2,1)S(1)}) custom-call(bf16[4,24,640]{2,1,0:T(8,128)(2,1)S(1)} %get-tuple-element.179.refs_0_, bf16[4,24,640]{2,1,0:T(8,128)(2,1)S(1)} %get-tuple-element.180.refs_1_, ...), custom_call_target="tpu_custom_call" | custom-call | bytes 31500000 | tf_op jit(solution)/shard_map/pallas_call | solution.py:290
  463.2 1.4 reshape.206
  466.3 7.8 %shard_map.250 = (f32[2,1024,384]{2,1,0:T(8,128)}, f32[2,1024,384]{2,1,0:T(8,128)}, f32[2,1024,384]{2,1,0:T(8,128)}) custom-call(bf16[1024,384]{1,0:T(8,128)(2,1)} %get-tuple-element.187.refs_0_, bf16[1024,384]{1,0:T(8,128)(2,1)} %copy-done.64, bf16[1024,384]{1,0:T(8,128)(2,1)} %get-tuple-element.189.refs_2_, bf16[1024,384]{1,0:T(8,128)(2,1)} %copy-done.65, ...), custom_call_target="tpu_custom_call" | custom-call | bytes 24500000 | tf_op jit(solution)/shard_map/pallas_call | solution.py:2005
  (254 shorter events, 34.7 us)
Async XLA Ops:
  3.5 98.4 %collective-permute-start = (bf16[1024,384]{1,0:T(8,128)(2,1)}, bf16[1024,384]{1,0:T(8,128)(2,1)S(1)}, u32[]{:S(2)}, u32[]{:S(2)}) collective-permute-start(bf16[1024,384]{1,0:T(8,128)(2,1)} %get-tuple-element.117), channel_id=1, source_target_pairs={{0,16},{16,0},{1,17},{17,1},{2,18},{18,2},{3,19},{19,3},{4,20},{20... | collective-permute-start | bytes 2359304 | tf_op jit(solution)/shard_map/ppermute | solution.py:2125
  8.1 60.1 %copy-start.2 = (bf16[2,1024,384]{2,1,0:T(8,128)(2,1)S(1)}, bf16[2,1024,384]{2,1,0:T(8,128)(2,1)}, u32[]{:S(2)}) copy-start(bf16[2,1024,384]{2,1,0:T(8,128)(2,1)} %refs_6_.3) | copy-start | bytes 4718596
  66.7 35.2 %collective-permute-start.1 = (bf16[1024,384]{1,0:T(8,128)(2,1)}, bf16[1024,384]{1,0:T(8,128)(2,1)}, u32[]{:S(2)}, u32[]{:S(2)}) collective-permute-start(bf16[1024,384]{1,0:T(8,128)(2,1)} %get-tuple-element.118), channel_id=1, source_target_pairs={{0,16},{16,0},{1,17},{17,1},{2,18},{18,2},{3,19},{19,3},{4,20},{20... | collective-permute-start | bytes 2359304 | tf_op jit(solution)/shard_map/ppermute | solution.py:2125
  69.5 34.7 %collective-permute-start.2 = (bf16[1024,384]{1,0:T(8,128)(2,1)}, bf16[1024,384]{1,0:T(8,128)(2,1)}, u32[]{:S(2)}, u32[]{:S(2)}) collective-permute-start(bf16[1024,384]{1,0:T(8,128)(2,1)} %get-tuple-element.119), channel_id=1, source_target_pairs={{0,16},{16,0},{1,17},{17,1},{2,18},{18,2},{3,19},{19,3},{4,20},{20... | collective-permute-start | bytes 2359304 | tf_op jit(solution)/shard_map/ppermute | solution.py:2125
  72.0 115.3 %copy-start.35 = (bf16[128,320]{1,0:T(8,128)(2,1)}, bf16[128,320]{1,0:T(8,128)(2,1)S(1)}, u32[]{:S(2)}) copy-start(bf16[128,320]{1,0:T(8,128)(2,1)S(1)} %get-tuple-element.256.picks_ref) | copy-start | bytes 245764
  98.4 41.0 %copy-start.23 = (f32[128,768]{1,0:T(8,128)}, f32[128,768]{1,0:T(8,128)S(1)}, u32[]{:S(2)}) copy-start(f32[128,768]{1,0:T(8,128)S(1)} %get-tuple-element.122.mid_ref) | copy-start | bytes 1179652
  98.4 91.6 %collective-permute-start.3 = (bf16[1024,384]{1,0:T(8,128)(2,1)S(1)}, bf16[1024,384]{1,0:T(8,128)(2,1)S(1)}, u32[]{:S(2)}, u32[]{:S(2)}) collective-permute-start(bf16[1024,384]{1,0:T(8,128)(2,1)S(1)} %copy-done.67), channel_id=1, source_target_pairs={{0,16},{16,0},{1,17},{17,1},{2,18},{18,2},{3,19},{19,3},{4,20},{20... | collective-permute-start | bytes 2359304 | tf_op jit(solution)/shard_map/ppermute | solution.py:2125
  98.5 91.5 %collective-permute-start.4 = (bf16[1024,384]{1,0:T(8,128)(2,1)S(1)}, bf16[1024,384]{1,0:T(8,128)(2,1)S(1)}, u32[]{:S(2)}, u32[]{:S(2)}) collective-permute-start(bf16[1024,384]{1,0:T(8,128)(2,1)S(1)} %copy-done.68), channel_id=1, source_target_pairs={{0,16},{16,0},{1,17},{17,1},{2,18},{18,2},{3,19},{19,3},{4,20},{20... | collective-permute-start | bytes 2359304 | tf_op jit(solution)/shard_map/ppermute | solution.py:2125
  101.2 38.3 %copy-start.52 = (f32[128,128]{1,0:T(8,128)}, f32[128,128]{1,0:T(8,128)S(1)}, u32[]{:S(2)}) copy-start(f32[128,128]{1,0:T(8,128)S(1)} %get-tuple-element.259.other_ref) | copy-start | bytes 196612
  101.9 37.5 %copy-start.13 = (bf16[1024,384]{1,0:T(8,128)(2,1)}, bf16[1024,384]{1,0:T(8,128)(2,1)S(1)}, u32[]{:S(2)}) copy-start(bf16[1024,384]{1,0:T(8,128)(2,1)S(1)} %collective-permute-done.refs_2_.refs_3_) | copy-start | bytes 2359300
  104.3 36.1 %copy-start.5 = (bf16[2,4,4,24,1408]{4,3,2,1,0:T(8,128)(2,1)S(1)}, bf16[2,4,4,24,1408]{4,3,2,1,0:T(8,128)(2,1)}, u32[]{:S(2)}) copy-start(bf16[2,4,4,24,1408]{4,3,2,1,0:T(8,128)(2,1)} %copy-done.4) | copy-start | bytes 6488068
  140.4 47.0 %copy-start.25 = (f32[128,768]{1,0:T(8,128)}, f32[128,768]{1,0:T(8,128)S(1)}, u32[]{:S(2)}) copy-start(f32[128,768]{1,0:T(8,128)S(1)} %get-tuple-element.129.x_ref) | copy-start | bytes 1179652
  163.0 27.1 %collective-permute-start.5 = (bf16[1024,384]{1,0:T(8,128)(2,1)S(1)}, bf16[1024,384]{1,0:T(8,128)(2,1)S(1)}, u32[]{:S(2)}, u32[]{:S(2)}) collective-permute-start(bf16[1024,384]{1,0:T(8,128)(2,1)S(1)} %copy-done.69), channel_id=1, source_target_pairs={{0,16},{16,0},{1,17},{17,1},{2,18},{18,2},{3,19},{19,3},{4,20},{20... | collective-permute-start | bytes 2359304 | tf_op jit(solution)/shard_map/ppermute | solution.py:2125
  190.0 57.9 %copy-start.21 = (f32[128,768]{1,0:T(8,128)}, f32[128,768]{1,0:T(8,128)S(1)}, u32[]{:S(2)}) copy-start(f32[128,768]{1,0:T(8,128)S(1)} %get-tuple-element.136.mid_ref) | copy-start | bytes 1179652
  191.4 56.5 %copy-start.36 = (bf16[128,320]{1,0:T(8,128)(2,1)S(1)}, bf16[128,320]{1,0:T(8,128)(2,1)}, u32[]{:S(2)}) copy-start(bf16[128,320]{1,0:T(8,128)(2,1)} %copy-done.35) | copy-start | bytes 245764
  191.4 56.5 %copy-start.42 = (bf16[128,768]{1,0:T(8,128)(2,1)S(1)}, bf16[128,768]{1,0:T(8,128)(2,1)}, u32[]{:S(2)}) copy-start(bf16[128,768]{1,0:T(8,128)(2,1)} %up_ref.1) | copy-start | bytes 589828
  191.4 56.5 %copy-start.50 = (f32[128,128]{1,0:T(8,128)S(1)}, f32[128,128]{1,0:T(8,128)}, u32[]{:S(2)}) copy-start(f32[128,128]{1,0:T(8,128)} %get-tuple-element.258.other_ref) | copy-start | bytes 196612
  247.8 19.5 %collective-permute-start.6 = (bf16[1024,384]{1,0:T(8,128)(2,1)}, bf16[1024,384]{1,0:T(8,128)(2,1)S(1)}, u32[]{:S(2)}, u32[]{:S(2)}) collective-permute-start(bf16[1024,384]{1,0:T(8,128)(2,1)} %get-tuple-element.139), channel_id=1, source_target_pairs={{0,16},{16,0},{1,17},{17,1},{2,18},{18,2},{3,19},{19,3},{4,20},{20... | collective-permute-start | bytes 2359304 | tf_op jit(solution)/shard_map/ppermute | solution.py:2223
  285.2 28.9 %copy-start.17 = (bf16[4,128,384]{2,1,0:T(8,128)(2,1)}, bf16[4,128,384]{2,1,0:T(8,128)(2,1)S(1)}, u32[]{:S(2)}) copy-start(bf16[4,128,384]{2,1,0:T(8,128)(2,1)S(1)} %get-tuple-element.144.dq_ref) | copy-start | bytes 1179652
  285.2 28.9 %copy-start.26 = (f32[128,768]{1,0:T(8,128)S(1)}, f32[128,768]{1,0:T(8,128)}, u32[]{:S(2)}) copy-start(f32[128,768]{1,0:T(8,128)} %copy-done.25) | copy-start | bytes 1179652
  285.2 28.9 %copy-start.30 = (f32[320,128]{1,0:T(8,128)S(1)}, f32[320,128]{1,0:T(8,128)}, u32[]{:S(2)}) copy-start(f32[320,128]{1,0:T(8,128)} %copy-done.29) | copy-start | bytes 491524
  316.3 45.4 %copy-start.24 = (f32[128,768]{1,0:T(8,128)S(1)}, f32[128,768]{1,0:T(8,128)}, u32[]{:S(2)}) copy-start(f32[128,768]{1,0:T(8,128)} %copy-done.23) | copy-start | bytes 1179652
  316.3 45.4 %copy-start.53 = (f32[128,128]{1,0:T(8,128)S(1)}, f32[128,128]{1,0:T(8,128)}, u32[]{:S(2)}) copy-start(f32[128,128]{1,0:T(8,128)} %copy-done.52) | copy-start | bytes 196612
  316.3 62.4 %copy-start.45 = (bf16[4,128,768]{2,1,0:T(8,128)(2,1)S(1)}, bf16[4,128,768]{2,1,0:T(8,128)(2,1)}, u32[]{:S(2)}) copy-start(bf16[4,128,768]{2,1,0:T(8,128)(2,1)} %get-tuple-element.174) | copy-start | bytes 2359300
  316.3 65.0 %copy-start.47 = (bf16[384,768]{1,0:T(8,128)(2,1)S(1)}, bf16[384,768]{1,0:T(8,128)(2,1)}, u32[]{:S(2)}) copy-start(bf16[384,768]{1,0:T(8,128)(2,1)} %get-tuple-element.158.w_ref) | copy-start | bytes 1769476
  359.6 20.8 %collective-permute-start.7 = (bf16[1024,384]{1,0:T(8,128)(2,1)}, bf16[1024,384]{1,0:T(8,128)(2,1)S(1)}, u32[]{:S(2)}, u32[]{:S(2)}) collective-permute-start(bf16[1024,384]{1,0:T(8,128)(2,1)} %get-tuple-element.156), channel_id=1, source_target_pairs={{0,16},{16,0},{1,17},{17,1},{2,18},{18,2},{3,19},{19,3},{4,20},{20... | collective-permute-start | bytes 2359304 | tf_op jit(solution)/shard_map/ppermute | solution.py:2225
  361.0 37.2 %collective-permute-start.8 = (bf16[1024,384]{1,0:T(8,128)(2,1)}, bf16[1024,384]{1,0:T(8,128)(2,1)S(1)}, u32[]{:S(2)}, u32[]{:S(2)}) collective-permute-start(bf16[1024,384]{1,0:T(8,128)(2,1)} %get-tuple-element.161), channel_id=1, source_target_pairs={{0,16},{16,0},{1,17},{17,1},{2,18},{18,2},{3,19},{19,3},{4,20},{20... | collective-permute-start | bytes 2359304 | tf_op jit(solution)/shard_map/ppermute | solution.py:2225
  398.2 29.6 %copy-start.65 = (bf16[1024,384]{1,0:T(8,128)(2,1)}, bf16[1024,384]{1,0:T(8,128)(2,1)S(1)}, u32[]{:S(2)}) copy-start(bf16[1024,384]{1,0:T(8,128)(2,1)S(1)} %collective-permute-done.8.refs_3_) | copy-start | bytes 2359300
  398.3 29.6 %copy-start.16 = (bf16[128,768]{1,0:T(8,128)(2,1)S(1)}, bf16[128,768]{1,0:T(8,128)(2,1)}, u32[]{:S(2)}) copy-start(bf16[128,768]{1,0:T(8,128)(2,1)} %x_ref.3) | copy-start | bytes 589828
  398.3 30.6 %copy-start.32 = (bf16[4,128,192]{2,1,0:T(8,128)(2,1)S(1)}, bf16[4,128,192]{2,1,0:T(8,128)(2,1)}, u32[]{:S(2)}) copy-start(bf16[4,128,192]{2,1,0:T(8,128)(2,1)} %copy-done.31) | copy-start | bytes 589828
  398.3 30.6 %copy-start.44 = (bf16[4,128,768]{2,1,0:T(8,128)(2,1)S(1)}, bf16[4,128,768]{2,1,0:T(8,128)(2,1)}, u32[]{:S(2)}) copy-start(bf16[4,128,768]{2,1,0:T(8,128)(2,1)} %get-tuple-element.169) | copy-start | bytes 2359300
  446.1 19.3 %collective-permute-start.9 = (bf16[1024,384]{1,0:T(8,128)(2,1)S(1)}, bf16[1024,384]{1,0:T(8,128)(2,1)S(1)}, u32[]{:S(2)}, u32[]{:S(2)}) collective-permute-start(bf16[1024,384]{1,0:T(8,128)(2,1)S(1)} %copy-done.82), channel_id=1, source_target_pairs={{0,16},{16,0},{1,17},{17,1},{2,18},{18,2},{3,19},{19,3},{4,20},{20... | collective-permute-start | bytes 2359304 | tf_op jit(solution)/shard_map/ppermute | solution.py:2279
  (61 other events, 633.9 us)

commit v9 on v8

--- a/solution.py
+++ b/solution.py
@@ -1093,7 +1093,7 @@
             DMA((COLUMNS,)),
         ],
         compiler_params=comm_params(
-            collective_id, scratch + shapes + [dkv_all, dq, query_w, pack]
+            collective_id, scratch + shapes + [dkv_all, dq, query_w, pack], 7 * SPARE_BYTES
         ),
         cost_estimate=lasting(cost),
     )(dkv_all.reshape((2, COLUMNS, width, 2) + tile), dq, query_w, pack)

time: 481 us -> 478 us (level)
    unnamed x170 -> x166, local copies, waits for them, and re-layouts: 15.4 us -> 12.8 us
where the time goes in v9:
time: 478 us; the launch traced here: 471 us
  Pallas kernels  427 us (89%)
  local copies, waits for them, and re-layouts  25.7 us (5%)
  starting transfers between devices  9.07 us (2%)
    pallas_call x3, Pallas kernels, experts_exchange(): pl.pallas_call(body, out_shape=shapes, in_specs=in_specs, out_specs=specs...  135 us
    pallas_call x2, Pallas kernels, reduce_project(): pl.pallas_call(body, out_shape=shapes, in_specs=[VMEM] * 4, out_specs=[VM...  57.3 us
    pallas_call x2, Pallas kernels, project_gather(): pl.pallas_call(body, out_shape=shapes, in_specs=[VMEM] * len(operands), o...  41.2 us
    pallas_call x1, Pallas kernels, start_gather(): pl.pallas_call(body, out_shape=plane_shapes(packs, blocks) + [jax.ShapeDt...  38.4 us
    pallas_call x2, Pallas kernels, attend_back(): pl.pallas_call(body, out_shape=(jax.ShapeDtypeStruct((count, rows, width)...  33.8 us
    pallas_call x2, Pallas kernels, column_gather(): pl.pallas_call(body, out_shape=jax.ShapeDtypeStruct((COLUMNS,) + tuple(va...  29.3 us
    pallas_call x2, Pallas kernels, attend(): pl.pallas_call(body, out_shape=(jax.ShapeDtypeStruct((count, rows, width)...  23.1 us
    pallas_call x2, Pallas kernels, column_exchange(): pl.pallas_call(body, out_shape=[jax.ShapeDtypeStruct((COLUMNS,) + slab, v...  21.5 us
  transfers between devices with their start and end apart: 10, of which 4 were waited for; matrix products, arithmetic and copies ran while one was open for 3% of the time, Pallas kernels for 48%

profile of v9, /device:TPU:12, one launch (start us, length us, event | category | flops | bytes accessed | tf_op | source)
XLA Modules:
  0.0 471.5 jit_solution(8442832989022185979)
XLA Ops:
  0.7 2.7 slice_bitcast_fusion.2
  6.3 1.4 slice_bitcast_fusion.1
  8.1 38.4 %shard_map.221 = (bf16[2,4,4,16,128]{4,3,2,1,0:T(8,128)(2,1)S(1)}, bf16[2,4,4,24,1408]{4,3,2,1,0:T(8,128)(2,1)S(1)}, bf16[2,4,4,24,1408]{4,3,2,1,0:T(8,128)(2,1)...) custom-call(bf16[4,16,128]{2,1,0:T(8,128)(2,1)S(1)} %broadcast_in_di, ...), custom_call_target="tpu_custom_call" | custom-call | bytes 98000000 | tf_op jit(solution)/shard_map/pallas_call | solution.py:485
  47.9 18.7 %shard_map.222 = (f32[16,768]{1,0:T(8,128)S(1)}, bf16[4,128,768]{2,1,0:T(8,128)(2,1)}, bf16[4,128,384]{2,1,0:T(8,128)(2,1)S(1)}, bf16[768,384]{1,0:T(8,128)(2,1)...) custom-call(bf16[4,128,768]{2,1,0:T(8,128)(2,1)S(1)} %get-tuple-element.108.refs_0_, ...), custom_call_target="tpu_custom_call" | custom-call | bytes 77000000 | tf_op jit(solution)/shard_map/pallas_call | solution.py:692
  66.6 1.5 collective-permute-start.1
  74.1 1.9 copy-done.11
  76.0 11.5 %shard_map.223 = (f32[4,128,384]{2,1,0:T(8,128)S(1)}, bf16[4,128,192]{2,1,0:T(8,128)(2,1)S(1)}) custom-call(s32[4,4]{1,0:T(4,128)S(1)} %pad_add_fusion.bounds_ref, bf16[4,128,384]{2,1,0:T(8,128)(2,1)S(1)} %get-tuple-element.110.q_ref, bf16[4096,384]{1,0:T(8,128)(2,1)S(1)} %bitcast.135, s32[4,1,128]{2,1,0:T(1,128)S(1)} %bitcast.167), custom_call_target="tpu_custom_call" | custom-call | bytes 45500000 | tf_op jit(solution)/shard_map/pallas_call | solution.py:1193
  87.6 9.8 %shard_map.224.attn_ref = bf16[4,128,192]{2,1,0:T(8,128)(2,1)S(1)} custom-call(bf16[4,128,192]{2,1,0:T(8,128)(2,1)S(1)} %get-tuple-element.112.refs_0_), custom_call_target="tpu_custom_call" | custom-call | bytes 31500000 | tf_op jit(solution)/shard_map/pallas_call | solution.py:192
  98.5 2.0 collective-permute-start.4
  101.8 2.4 collective-permute-done.2.refs_6_.refs_7_
  104.2 35.1 %shard_map.227 = (bf16[8,40,768]{2,1,0:T(8,128)(2,1)S(1)}, bf16[2,8,40,768]{3,2,1,0:T(8,128)(2,1)}) custom-call(bf16[8,40,768]{2,1,0:T(8,128)(2,1)S(1)} %bitcast.162, bf16[2,1024,384]{2,1,0:T(8,128)(2,1)S(1)} %copy-done, bf16[1024,384]{1,0:T(8,128)(2,1)S(1)} %collective-permute-done.refs_2_.refs_3_, bf16[2,1024,384]{2,1,0:T(8,128)(2,1)S(1)} %copy-done.1, ...), custom_call_target="tpu_custom_call" | custom-call | bytes 98000000 | tf_op jit(solution)/shard_map/pallas_call | solution.py:1735
  140.4 22.5 %shard_map.229 = (bf16[4,128,768]{2,1,0:T(8,128)(2,1)}, bf16[4,128,384]{2,1,0:T(8,128)(2,1)S(1)}, bf16[768,384]{1,0:T(8,128)(2,1)}, bf16[384,768]{1,0:T(8,128)(2,1)}, bf16[2,4,4,128,384]{4,3,2,1,0:T(8,128)(2,1)S(1)}) custom-call(bf16[128,768]{1,0:T(8,128)(2,1)S(1)} %get-tuple-element.124.refs_0_, bf16[768,1408]{1,0:T(8,128)(2,1)S(1)} %bitcast.129, ...), custom_call_target="tpu_custom_call" | custom-call | bytes 77000000 | tf_op jit(solution)/shard_map/pallas_call | solution.py:692
  164.1 11.5 %shard_map.230 = (f32[4,128,384]{2,1,0:T(8,128)S(1)}, bf16[4,128,192]{2,1,0:T(8,128)(2,1)S(1)}) custom-call(s32[4,4]{1,0:T(4,128)S(1)} %pad_add_fusion.bounds_ref, bf16[4,128,384]{2,1,0:T(8,128)(2,1)S(1)} %get-tuple-element.126.q_ref, bf16[4096,384]{1,0:T(8,128)(2,1)S(1)} %bitcast.137, s32[4,1,128]{2,1,0:T(1,128)S(1)} %bitcast.168), custom_call_target="tpu_custom_call" | custom-call | bytes 45500000 | tf_op jit(solution)/shard_map/pallas_call | solution.py:1193
  175.7 11.7 %shard_map.231.attn_ref = bf16[4,128,192]{2,1,0:T(8,128)(2,1)S(1)} custom-call(bf16[4,128,192]{2,1,0:T(8,128)(2,1)S(1)} %get-tuple-element.128.refs_0_), custom_call_target="tpu_custom_call" | custom-call | bytes 31500000 | tf_op jit(solution)/shard_map/pallas_call | solution.py:192
  191.4 56.4 %shard_map.233 = (bf16[8,40,768]{2,1,0:T(8,128)(2,1)}, bf16[8,40,768]{2,1,0:T(8,128)(2,1)}, bf16[1024,384]{1,0:T(8,128)(2,1)}, bf16[1024,384]{1,0:T(8,128)(2,1)}...) custom-call(bf16[8,40,768]{2,1,0:T(8,128)(2,1)} %bitcast.154, ...), custom_call_target="tpu_custom_call" | custom-call | bytes 192500000 | tf_op jit(solution)/shard_map/pallas_call | solution.py:1735
  249.0 1.4 shard_map.235
  250.4 15.8 %shard_map.236.dy_ref = bf16[4,128,768]{2,1,0:T(8,128)(2,1)S(1)} custom-call(bf16[128,768]{1,0:T(8,128)(2,1)S(1)} %get-tuple-element.138.src), custom_call_target="tpu_custom_call" | custom-call | bytes 49000000 | tf_op jit(solution)/shard_map/pallas_call | solution.py:218
  267.3 16.9 %shard_map.237 = (bf16[4,128,384]{2,1,0:T(8,128)(2,1)S(1)}, bf16[4096,384]{1,0:T(8,128)(2,1)S(1)}) custom-call(s32[4,4]{1,0:T(4,128)S(1)} %pad_add_fusion.bounds_ref, bf16[4,128,384]{2,1,0:T(8,128)(2,1)S(1)} %copy-done.28, bf16[4,128,768]{2,1,0:T(8,128)(2,1)S(1)} %shard_map.236.dy_ref, bf16[384,768]{1,0:T(8,128)(2,1)S(1)} %copy-done.49, ...), custom_call_target="tpu_custom_call" | custom-call | bytes 70000000 | tf_op jit(solution)/shard_map/pallas_call | solution.py:1297
  284.3 28.8 %shard_map.238 = (bf16[4,128,384]{2,1,0:T(8,128)(2,1)S(1)}, bf16[4,128,768]{2,1,0:T(8,128)(2,1)S(1)}) custom-call(bf16[2,4,2,2,128,384]{5,4,3,2,1,0:T(8,128)(2,1)S(1)} %bitcast.142, bf16[4,128,384]{2,1,0:T(8,128)(2,1)S(1)} %get-tuple-element.144.dq_ref, bf16[768,384]{1,0:T(8,128)(2,1)S(1)} %copy-done.48, bf16[768,1408]{1,0:T(8,128)(2,1)S(1)} %bitcast.131), custom_call_target="tpu_custom_call" | custom-call | bytes 91000000 | tf_op jit(solution)/shard_map/pallas_call | solution.py:1081
  314.6 43.2 %shard_map.240 = (bf16[8,40,768]{2,1,0:T(8,128)(2,1)}, bf16[1024,384]{1,0:T(8,128)(2,1)}, bf16[1024,384]{1,0:T(8,128)(2,1)}, bf16[1024,384]{1,0:T(8,128)(2,1)}, ...) custom-call(bf16[8,40,768]{2,1,0:T(8,128)(2,1)} %bitcast.156, ...), custom_call_target="tpu_custom_call" | custom-call | bytes 126000000 | tf_op jit(solution)/shard_map/pallas_call | solution.py:1735
  357.8 1.4 collective-permute-start.7
  361.0 1.4 shard_map.241
  362.4 13.5 %shard_map.242.dy_ref = bf16[4,128,768]{2,1,0:T(8,128)(2,1)S(1)} custom-call(bf16[128,768]{1,0:T(8,128)(2,1)S(1)} %get-tuple-element.155.src), custom_call_target="tpu_custom_call" | custom-call | bytes 49000000 | tf_op jit(solution)/shard_map/pallas_call | solution.py:218
  375.9 1.4 shard_map.247
  379.5 16.9 %shard_map.243 = (bf16[4,128,384]{2,1,0:T(8,128)(2,1)S(1)}, bf16[4096,384]{1,0:T(8,128)(2,1)S(1)}) custom-call(s32[4,4]{1,0:T(4,128)S(1)} %pad_add_fusion.bounds_ref, bf16[4,128,384]{2,1,0:T(8,128)(2,1)S(1)} %copy-done.20, bf16[4,128,768]{2,1,0:T(8,128)(2,1)S(1)} %shard_map.242.dy_ref, bf16[384,768]{1,0:T(8,128)(2,1)S(1)} %copy-done.47, ...), custom_call_target="tpu_custom_call" | custom-call | bytes 70000000 | tf_op jit(solution)/shard_map/pallas_call | solution.py:1297
  396.5 28.5 %shard_map.244 = (bf16[4,128,384]{2,1,0:T(8,128)(2,1)S(1)}, bf16[4,128,768]{2,1,0:T(8,128)(2,1)S(1)}) custom-call(bf16[2,4,2,2,128,384]{5,4,3,2,1,0:T(8,128)(2,1)S(1)} %bitcast.141, bf16[4,128,384]{2,1,0:T(8,128)(2,1)S(1)} %get-tuple-element.163.dq_ref, bf16[768,384]{1,0:T(8,128)(2,1)S(1)} %copy-done.46, bf16[768,1408]{1,0:T(8,128)(2,1)S(1)} %bitcast.134), custom_call_target="tpu_custom_call" | custom-call | bytes 91000000 | tf_op jit(solution)/shard_map/pallas_call | solution.py:1081
  426.1 1.4 shard_map.246
  427.6 15.7 %shard_map.248 = (bf16[4,24,640]{2,1,0:T(8,128)(2,1)S(1)}, bf16[2,24,384]{2,1,0:T(8,128)(2,1)S(1)}, bf16[4,24,640]{2,1,0:T(8,128)(2,1)S(1)}, bf16[2,24,384]{2,1,0:T(8,128)(2,1)S(1)}) custom-call(bf16[2,4,2,2,24,640]{5,4,3,2,1,0:T(8,128)(2,1)S(1)} %bitcast.148, bf16[2,2,2,2,24,384]{5,4,3,2,1,0:T(8,128)(2,1)S(1)} %bitcast.166, ...), custom_call_target="tpu_custom_call" | custom-call | bytes 70000000 | tf_op jit(solution)/shard_map/pallas_call | solution.py:874
  444.0 1.6 shard_map.234
  445.6 11.3 %shard_map.249 = (bf16[4,24,640]{2,1,0:T(8,128)(2,1)S(1)}, bf16[4,24,640]{2,1,0:T(8,128)(2,1)S(1)}, bf16[2,24,384]{2,1,0:T(8,128)(2,1)S(1)}, bf16[2,24,384]{2,1,0:T(8,128)(2,1)S(1)}) custom-call(bf16[4,24,640]{2,1,0:T(8,128)(2,1)S(1)} %get-tuple-element.179.refs_0_, bf16[4,24,640]{2,1,0:T(8,128)(2,1)S(1)} %get-tuple-element.180.refs_1_, ...), custom_call_target="tpu_custom_call" | custom-call | bytes 31500000 | tf_op jit(solution)/shard_map/pallas_call | solution.py:290
  460.3 1.4 reshape.206
  463.5 7.8 %shard_map.250 = (f32[2,1024,384]{2,1,0:T(8,128)}, f32[2,1024,384]{2,1,0:T(8,128)}, f32[2,1024,384]{2,1,0:T(8,128)}) custom-call(bf16[1024,384]{1,0:T(8,128)(2,1)} %get-tuple-element.187.refs_0_, bf16[1024,384]{1,0:T(8,128)(2,1)} %copy-done.62, bf16[1024,384]{1,0:T(8,128)(2,1)} %get-tuple-element.189.refs_2_, bf16[1024,384]{1,0:T(8,128)(2,1)} %copy-done.63, ...), custom_call_target="tpu_custom_call" | custom-call | bytes 24500000 | tf_op jit(solution)/shard_map/pallas_call | solution.py:2005
  (250 shorter events, 33.2 us)
Async XLA Ops:
  3.5 98.4 %collective-permute-start = (bf16[1024,384]{1,0:T(8,128)(2,1)}, bf16[1024,384]{1,0:T(8,128)(2,1)S(1)}, u32[]{:S(2)}, u32[]{:S(2)}) collective-permute-start(bf16[1024,384]{1,0:T(8,128)(2,1)} %get-tuple-element.117), channel_id=1, source_target_pairs={{0,16},{16,0},{1,17},{17,1},{2,18},{18,2},{3,19},{19,3},{4,20},{20... | collective-permute-start | bytes 2359304 | tf_op jit(solution)/shard_map/ppermute | solution.py:2125
  8.1 60.0 %copy-start.2 = (bf16[2,1024,384]{2,1,0:T(8,128)(2,1)S(1)}, bf16[2,1024,384]{2,1,0:T(8,128)(2,1)}, u32[]{:S(2)}) copy-start(bf16[2,1024,384]{2,1,0:T(8,128)(2,1)} %refs_6_.3) | copy-start | bytes 4718596
  66.6 35.2 %collective-permute-start.1 = (bf16[1024,384]{1,0:T(8,128)(2,1)}, bf16[1024,384]{1,0:T(8,128)(2,1)}, u32[]{:S(2)}, u32[]{:S(2)}) collective-permute-start(bf16[1024,384]{1,0:T(8,128)(2,1)} %get-tuple-element.118), channel_id=1, source_target_pairs={{0,16},{16,0},{1,17},{17,1},{2,18},{18,2},{3,19},{19,3},{4,20},{20... | collective-permute-start | bytes 2359304 | tf_op jit(solution)/shard_map/ppermute | solution.py:2125
  69.5 34.7 %collective-permute-start.2 = (bf16[1024,384]{1,0:T(8,128)(2,1)}, bf16[1024,384]{1,0:T(8,128)(2,1)}, u32[]{:S(2)}, u32[]{:S(2)}) collective-permute-start(bf16[1024,384]{1,0:T(8,128)(2,1)} %get-tuple-element.119), channel_id=1, source_target_pairs={{0,16},{16,0},{1,17},{17,1},{2,18},{18,2},{3,19},{19,3},{4,20},{20... | collective-permute-start | bytes 2359304 | tf_op jit(solution)/shard_map/ppermute | solution.py:2125
  72.0 115.4 %copy-start.35 = (bf16[128,320]{1,0:T(8,128)(2,1)}, bf16[128,320]{1,0:T(8,128)(2,1)S(1)}, u32[]{:S(2)}) copy-start(bf16[128,320]{1,0:T(8,128)(2,1)S(1)} %get-tuple-element.256.picks_ref) | copy-start | bytes 245764
  98.4 41.0 %copy-start.23 = (f32[128,768]{1,0:T(8,128)}, f32[128,768]{1,0:T(8,128)S(1)}, u32[]{:S(2)}) copy-start(f32[128,768]{1,0:T(8,128)S(1)} %get-tuple-element.122.mid_ref) | copy-start | bytes 1179652
  98.4 91.6 %collective-permute-start.3 = (bf16[1024,384]{1,0:T(8,128)(2,1)S(1)}, bf16[1024,384]{1,0:T(8,128)(2,1)S(1)}, u32[]{:S(2)}, u32[]{:S(2)}) collective-permute-start(bf16[1024,384]{1,0:T(8,128)(2,1)S(1)} %copy-done.65), channel_id=1, source_target_pairs={{0,16},{16,0},{1,17},{17,1},{2,18},{18,2},{3,19},{19,3},{4,20},{20... | collective-permute-start | bytes 2359304 | tf_op jit(solution)/shard_map/ppermute | solution.py:2125
  98.5 91.5 %collective-permute-start.4 = (bf16[1024,384]{1,0:T(8,128)(2,1)S(1)}, bf16[1024,384]{1,0:T(8,128)(2,1)S(1)}, u32[]{:S(2)}, u32[]{:S(2)}) collective-permute-start(bf16[1024,384]{1,0:T(8,128)(2,1)S(1)} %copy-done.66), channel_id=1, source_target_pairs={{0,16},{16,0},{1,17},{17,1},{2,18},{18,2},{3,19},{19,3},{4,20},{20... | collective-permute-start | bytes 2359304 | tf_op jit(solution)/shard_map/ppermute | solution.py:2125
  101.1 38.3 %copy-start.52 = (f32[128,128]{1,0:T(8,128)}, f32[128,128]{1,0:T(8,128)S(1)}, u32[]{:S(2)}) copy-start(f32[128,128]{1,0:T(8,128)S(1)} %get-tuple-element.259.other_ref) | copy-start | bytes 196612
  101.8 37.5 %copy-start.13 = (bf16[1024,384]{1,0:T(8,128)(2,1)}, bf16[1024,384]{1,0:T(8,128)(2,1)S(1)}, u32[]{:S(2)}) copy-start(bf16[1024,384]{1,0:T(8,128)(2,1)S(1)} %collective-permute-done.refs_2_.refs_3_) | copy-start | bytes 2359300
  104.2 36.1 %copy-start.5 = (bf16[2,4,4,24,1408]{4,3,2,1,0:T(8,128)(2,1)S(1)}, bf16[2,4,4,24,1408]{4,3,2,1,0:T(8,128)(2,1)}, u32[]{:S(2)}) copy-start(bf16[2,4,4,24,1408]{4,3,2,1,0:T(8,128)(2,1)} %copy-done.4) | copy-start | bytes 6488068
  140.3 47.0 %copy-start.25 = (f32[128,768]{1,0:T(8,128)}, f32[128,768]{1,0:T(8,128)S(1)}, u32[]{:S(2)}) copy-start(f32[128,768]{1,0:T(8,128)S(1)} %get-tuple-element.129.x_ref) | copy-start | bytes 1179652
  162.9 27.1 %collective-permute-start.5 = (bf16[1024,384]{1,0:T(8,128)(2,1)S(1)}, bf16[1024,384]{1,0:T(8,128)(2,1)S(1)}, u32[]{:S(2)}, u32[]{:S(2)}) collective-permute-start(bf16[1024,384]{1,0:T(8,128)(2,1)S(1)} %copy-done.67), channel_id=1, source_target_pairs={{0,16},{16,0},{1,17},{17,1},{2,18},{18,2},{3,19},{19,3},{4,20},{20... | collective-permute-start | bytes 2359304 | tf_op jit(solution)/shard_map/ppermute | solution.py:2125
  190.0 57.9 %copy-start.21 = (f32[128,768]{1,0:T(8,128)}, f32[128,768]{1,0:T(8,128)S(1)}, u32[]{:S(2)}) copy-start(f32[128,768]{1,0:T(8,128)S(1)} %get-tuple-element.136.mid_ref) | copy-start | bytes 1179652
  191.4 56.5 %copy-start.36 = (bf16[128,320]{1,0:T(8,128)(2,1)S(1)}, bf16[128,320]{1,0:T(8,128)(2,1)}, u32[]{:S(2)}) copy-start(bf16[128,320]{1,0:T(8,128)(2,1)} %copy-done.35) | copy-start | bytes 245764
  191.4 56.5 %copy-start.42 = (bf16[128,768]{1,0:T(8,128)(2,1)S(1)}, bf16[128,768]{1,0:T(8,128)(2,1)}, u32[]{:S(2)}) copy-start(bf16[128,768]{1,0:T(8,128)(2,1)} %up_ref.1) | copy-start | bytes 589828
  191.4 56.5 %copy-start.50 = (f32[128,128]{1,0:T(8,128)S(1)}, f32[128,128]{1,0:T(8,128)}, u32[]{:S(2)}) copy-start(f32[128,128]{1,0:T(8,128)} %get-tuple-element.258.other_ref) | copy-start | bytes 196612
  247.8 19.5 %collective-permute-start.6 = (bf16[1024,384]{1,0:T(8,128)(2,1)}, bf16[1024,384]{1,0:T(8,128)(2,1)S(1)}, u32[]{:S(2)}, u32[]{:S(2)}) collective-permute-start(bf16[1024,384]{1,0:T(8,128)(2,1)} %get-tuple-element.139), channel_id=1, source_target_pairs={{0,16},{16,0},{1,17},{17,1},{2,18},{18,2},{3,19},{19,3},{4,20},{20... | collective-permute-start | bytes 2359304 | tf_op jit(solution)/shard_map/ppermute | solution.py:2223
  284.2 28.9 %copy-start.17 = (bf16[4,128,384]{2,1,0:T(8,128)(2,1)}, bf16[4,128,384]{2,1,0:T(8,128)(2,1)S(1)}, u32[]{:S(2)}) copy-start(bf16[4,128,384]{2,1,0:T(8,128)(2,1)S(1)} %get-tuple-element.144.dq_ref) | copy-start | bytes 1179652
  284.2 28.8 %copy-start.26 = (f32[128,768]{1,0:T(8,128)S(1)}, f32[128,768]{1,0:T(8,128)}, u32[]{:S(2)}) copy-start(f32[128,768]{1,0:T(8,128)} %copy-done.25) | copy-start | bytes 1179652
  284.3 28.8 %copy-start.30 = (f32[320,128]{1,0:T(8,128)S(1)}, f32[320,128]{1,0:T(8,128)}, u32[]{:S(2)}) copy-start(f32[320,128]{1,0:T(8,128)} %copy-done.29) | copy-start | bytes 491524
  314.6 45.4 %copy-start.24 = (f32[128,768]{1,0:T(8,128)S(1)}, f32[128,768]{1,0:T(8,128)}, u32[]{:S(2)}) copy-start(f32[128,768]{1,0:T(8,128)} %copy-done.23) | copy-start | bytes 1179652
  314.6 45.4 %copy-start.53 = (f32[128,128]{1,0:T(8,128)S(1)}, f32[128,128]{1,0:T(8,128)}, u32[]{:S(2)}) copy-start(f32[128,128]{1,0:T(8,128)} %copy-done.52) | copy-start | bytes 196612
  314.6 61.3 %copy-start.45 = (bf16[4,128,768]{2,1,0:T(8,128)(2,1)S(1)}, bf16[4,128,768]{2,1,0:T(8,128)(2,1)}, u32[]{:S(2)}) copy-start(bf16[4,128,768]{2,1,0:T(8,128)(2,1)} %get-tuple-element.174) | copy-start | bytes 2359300
  314.6 64.9 %copy-start.47 = (bf16[384,768]{1,0:T(8,128)(2,1)S(1)}, bf16[384,768]{1,0:T(8,128)(2,1)}, u32[]{:S(2)}) copy-start(bf16[384,768]{1,0:T(8,128)(2,1)} %get-tuple-element.158.w_ref) | copy-start | bytes 1769476
  357.8 20.8 %collective-permute-start.7 = (bf16[1024,384]{1,0:T(8,128)(2,1)}, bf16[1024,384]{1,0:T(8,128)(2,1)S(1)}, u32[]{:S(2)}, u32[]{:S(2)}) collective-permute-start(bf16[1024,384]{1,0:T(8,128)(2,1)} %get-tuple-element.156), channel_id=1, source_target_pairs={{0,16},{16,0},{1,17},{17,1},{2,18},{18,2},{3,19},{19,3},{4,20},{20... | collective-permute-start | bytes 2359304 | tf_op jit(solution)/shard_map/ppermute | solution.py:2225
  359.3 37.2 %collective-permute-start.8 = (bf16[1024,384]{1,0:T(8,128)(2,1)}, bf16[1024,384]{1,0:T(8,128)(2,1)S(1)}, u32[]{:S(2)}, u32[]{:S(2)}) collective-permute-start(bf16[1024,384]{1,0:T(8,128)(2,1)} %get-tuple-element.161), channel_id=1, source_target_pairs={{0,16},{16,0},{1,17},{17,1},{2,18},{18,2},{3,19},{19,3},{4,20},{20... | collective-permute-start | bytes 2359304 | tf_op jit(solution)/shard_map/ppermute | solution.py:2225
  396.5 28.6 %copy-start.63 = (bf16[1024,384]{1,0:T(8,128)(2,1)}, bf16[1024,384]{1,0:T(8,128)(2,1)S(1)}, u32[]{:S(2)}) copy-start(bf16[1024,384]{1,0:T(8,128)(2,1)S(1)} %collective-permute-done.8.refs_3_) | copy-start | bytes 2359300
  396.5 28.5 %copy-start.16 = (bf16[128,768]{1,0:T(8,128)(2,1)S(1)}, bf16[128,768]{1,0:T(8,128)(2,1)}, u32[]{:S(2)}) copy-start(bf16[128,768]{1,0:T(8,128)(2,1)} %x_ref.3) | copy-start | bytes 589828
  396.5 29.6 %copy-start.32 = (bf16[4,128,192]{2,1,0:T(8,128)(2,1)S(1)}, bf16[4,128,192]{2,1,0:T(8,128)(2,1)}, u32[]{:S(2)}) copy-start(bf16[4,128,192]{2,1,0:T(8,128)(2,1)} %copy-done.31) | copy-start | bytes 589828
  396.5 29.6 %copy-start.44 = (bf16[4,128,768]{2,1,0:T(8,128)(2,1)S(1)}, bf16[4,128,768]{2,1,0:T(8,128)(2,1)}, u32[]{:S(2)}) copy-start(bf16[4,128,768]{2,1,0:T(8,128)(2,1)} %get-tuple-element.169) | copy-start | bytes 2359300
  443.3 19.3 %collective-permute-start.9 = (bf16[1024,384]{1,0:T(8,128)(2,1)S(1)}, bf16[1024,384]{1,0:T(8,128)(2,1)S(1)}, u32[]{:S(2)}, u32[]{:S(2)}) collective-permute-start(bf16[1024,384]{1,0:T(8,128)(2,1)S(1)} %copy-done.80), channel_id=1, source_target_pairs={{0,16},{16,0},{1,17},{17,1},{2,18},{18,2},{3,19},{19,3},{4,20},{20... | collective-permute-start | bytes 2359304 | tf_op jit(solution)/shard_map/ppermute | solution.py:2279
  (59 other events, 646.0 us)

commit v10 on v9

--- a/solution.py
+++ b/solution.py
@@ -10,6 +10,7 @@
 LAYERS = 2
 CAP = 40
 COLUMNS = 4
+PIECES = 2
 MESH = pl.DeviceIdType.MESH
 ANY = pl.BlockSpec(memory_space=pl.ANY)
 VMEM = pl.BlockSpec(memory_space=pltpu.VMEM)
@@ -105,14 +106,16 @@
             jnp.where(lower, 3, 0),
         ]
 
-    def copy(self, k, way):
+    def copy(self, k, way, piece):
         slab = self.slabs[k]
-        place = self.dst.at[slab]
+        rows = self.dst.shape[1] // PIECES
+        part = pl.ds(piece * rows, rows)
+        place = self.dst.at[slab, part]
         return remote(
-            self.source if k == 0 else place,
+            self.source.at[part] if k == 0 else place,
             place,
-            self.send_sems.at[k, way],
-            self.recv_sems.at[slab],
+            self.send_sems.at[k, way, piece],
+            self.recv_sems.at[slab, piece],
             self.line[way][1],
         )
 
@@ -125,24 +128,27 @@
             jnp.logical_not(from_before) & self.line[1][0],
         ]
 
-    def pass_on(self, k):
-        for way, there in enumerate(self.onward(k)):
-
-            @pl.when(there)
-            def _():
-                self.copy(k, way).start()
+    def pass_on(self, k, pieces=range(PIECES)):
+        for piece in pieces:
+            for way, there in enumerate(self.onward(k)):
+
+                @pl.when(there)
+                def _():
+                    self.copy(k, way, piece).start()
 
     def arrive(self, k):
-        self.copy(k, 0).wait_recv()
-        self.pass_on(k)
+        for piece in range(PIECES):
+            self.copy(k, 0, piece).wait_recv()
+            self.pass_on(k, [piece])
 
     def finish(self):
         for k in range(COLUMNS):
-            for way, there in enumerate(self.onward(k)):
-
-                @pl.when(there)
-                def _():
-                    self.copy(k, way).wait_send()
+            for piece in range(PIECES):
+                for way, there in enumerate(self.onward(k)):
+
+                    @pl.when(there)
+                    def _():
+                        self.copy(k, way, piece).wait_send()
 
 
 def column_start(src, gather, dst, own_sem, send_sems, recv_sems, where):
@@ -220,7 +226,7 @@
         out_shape=jax.ShapeDtypeStruct((COLUMNS,) + tuple(values.shape), values.dtype),
         in_specs=[ANY],
         out_specs=ANY,
-        scratch_shapes=[DMA, DMA((COLUMNS, 2)), DMA((COLUMNS,))],
+        scratch_shapes=[DMA, DMA((COLUMNS, 2, PIECES)), DMA((COLUMNS, PIECES))],
         compiler_params=comm_params(collective_id),
         cost_estimate=lasting(cost),
     )(values)
@@ -493,8 +499,8 @@
             DMA((count + 1,)),
             DMA((count, COLUMNS)),
             DMA((count, COLUMNS)),
-            DMA((COLUMNS, 2)),
-            DMA((COLUMNS,)),
+            DMA((COLUMNS, 2, PIECES)),
+            DMA((COLUMNS, PIECES)),
         ]
         + plane_scratch(count, blocks),
         compiler_params=comm_params(collective_id),
@@ -704,8 +710,8 @@
             DMA((COLUMNS, 2, 2, width)),
             DMA((COLUMNS, 2, 2, width)),
             DMA((COLUMNS, 2, 2, width)),
-            DMA((COLUMNS, 2)),
-            DMA((COLUMNS,)),
+            DMA((COLUMNS, 2, PIECES)),
+            DMA((COLUMNS, PIECES)),
             DMA((3,)),
         ],
         compiler_params=comm_params(

time: 478 us -> 479 us (level)
  transfers between devices with their start and end apart: 10 -> 10, of which waited for: 4 -> 3; matrix products, arithmetic and copies ran while one was open for 3% -> 3% of each run, Pallas kernels for 48% -> 48%
where the time goes in v10:
time: 479 us; the launch traced here: 472 us
  Pallas kernels  426 us (89%)
  local copies, waits for them, and re-layouts  25.7 us (5%)
  starting transfers between devices  9.01 us (2%)
  waiting for transfers between devices  6.08 us (1%)
    pallas_call x3, Pallas kernels, experts_exchange(): pl.pallas_call(body, out_shape=shapes, in_specs=in_specs, out_specs=specs...  135 us
    pallas_call x2, Pallas kernels, reduce_project(): pl.pallas_call(body, out_shape=shapes, in_specs=[VMEM] * 4, out_specs=[VM...  57 us
    pallas_call x2, Pallas kernels, project_gather(): pl.pallas_call(body, out_shape=shapes, in_specs=[VMEM] * len(operands), o...  41.4 us
    pallas_call x1, Pallas kernels, start_gather(): pl.pallas_call(body, out_shape=plane_shapes(packs, blocks) + [jax.ShapeDt...  38.5 us
    pallas_call x2, Pallas kernels, attend_back(): pl.pallas_call(body, out_shape=(jax.ShapeDtypeStruct((count, rows, width)...  33.8 us
    pallas_call x2, Pallas kernels, column_gather(): pl.pallas_call(body, out_shape=jax.ShapeDtypeStruct((COLUMNS,) + tuple(va...  27.7 us
    pallas_call x2, Pallas kernels, attend(): pl.pallas_call(body, out_shape=(jax.ShapeDtypeStruct((count, rows, width)...  23.1 us
    pallas_call x2, Pallas kernels, column_exchange(): pl.pallas_call(body, out_shape=[jax.ShapeDtypeStruct((COLUMNS,) + slab, v...  21.5 us
  transfers between devices with their start and end apart: 10, of which 3 were waited for; matrix products, arithmetic and copies ran while one was open for 3% of the time, Pallas kernels for 48%

profile of v10, /device:TPU:12, one launch (start us, length us, event | category | flops | bytes accessed | tf_op | source)
XLA Modules:
  0.0 471.8 jit_solution(416901231903208013)
XLA Ops:
  0.7 2.7 slice_bitcast_fusion.2
  8.1 38.5 %shard_map.221 = (bf16[2,4,4,16,128]{4,3,2,1,0:T(8,128)(2,1)S(1)}, bf16[2,4,4,24,1408]{4,3,2,1,0:T(8,128)(2,1)S(1)}, bf16[2,4,4,24,1408]{4,3,2,1,0:T(8,128)(2,1)...) custom-call(bf16[4,16,128]{2,1,0:T(8,128)(2,1)S(1)} %broadcast_in_di, ...), custom_call_target="tpu_custom_call" | custom-call | bytes 98000000 | tf_op jit(solution)/shard_map/pallas_call | solution.py:491
  48.0 18.8 %shard_map.222 = (f32[16,768]{1,0:T(8,128)S(1)}, bf16[4,128,768]{2,1,0:T(8,128)(2,1)}, bf16[4,128,384]{2,1,0:T(8,128)(2,1)S(1)}, bf16[768,384]{1,0:T(8,128)(2,1)...) custom-call(bf16[4,128,768]{2,1,0:T(8,128)(2,1)S(1)} %get-tuple-element.108.refs_0_, ...), custom_call_target="tpu_custom_call" | custom-call | bytes 77000000 | tf_op jit(solution)/shard_map/pallas_call | solution.py:698
  66.8 1.5 collective-permute-start.1
  74.3 1.9 copy-done.11
  76.2 11.5 %shard_map.223 = (f32[4,128,384]{2,1,0:T(8,128)S(1)}, bf16[4,128,192]{2,1,0:T(8,128)(2,1)S(1)}) custom-call(s32[4,4]{1,0:T(4,128)S(1)} %pad_add_fusion.bounds_ref, bf16[4,128,384]{2,1,0:T(8,128)(2,1)S(1)} %get-tuple-element.110.q_ref, bf16[4096,384]{1,0:T(8,128)(2,1)S(1)} %bitcast.135, s32[4,1,128]{2,1,0:T(1,128)S(1)} %bitcast.167), custom_call_target="tpu_custom_call" | custom-call | bytes 45500000 | tf_op jit(solution)/shard_map/pallas_call | solution.py:1199
  87.8 9.8 %shard_map.224.attn_ref = bf16[4,128,192]{2,1,0:T(8,128)(2,1)S(1)} custom-call(bf16[4,128,192]{2,1,0:T(8,128)(2,1)S(1)} %get-tuple-element.112.refs_0_), custom_call_target="tpu_custom_call" | custom-call | bytes 31500000 | tf_op jit(solution)/shard_map/pallas_call | solution.py:198
  98.7 2.0 collective-permute-start.4
  102.1 2.4 collective-permute-done.2.refs_6_.refs_7_
  104.4 35.1 %shard_map.227 = (bf16[8,40,768]{2,1,0:T(8,128)(2,1)S(1)}, bf16[2,8,40,768]{3,2,1,0:T(8,128)(2,1)}) custom-call(bf16[8,40,768]{2,1,0:T(8,128)(2,1)S(1)} %bitcast.162, bf16[2,1024,384]{2,1,0:T(8,128)(2,1)S(1)} %copy-done, bf16[1024,384]{1,0:T(8,128)(2,1)S(1)} %collective-permute-done.refs_2_.refs_3_, bf16[2,1024,384]{2,1,0:T(8,128)(2,1)S(1)} %copy-done.1, ...), custom_call_target="tpu_custom_call" | custom-call | bytes 98000000 | tf_op jit(solution)/shard_map/pallas_call | solution.py:1741
  140.6 22.7 %shard_map.229 = (bf16[4,128,768]{2,1,0:T(8,128)(2,1)}, bf16[4,128,384]{2,1,0:T(8,128)(2,1)S(1)}, bf16[768,384]{1,0:T(8,128)(2,1)}, bf16[384,768]{1,0:T(8,128)(2,1)}, bf16[2,4,4,128,384]{4,3,2,1,0:T(8,128)(2,1)S(1)}) custom-call(bf16[128,768]{1,0:T(8,128)(2,1)S(1)} %get-tuple-element.124.refs_0_, bf16[768,1408]{1,0:T(8,128)(2,1)S(1)} %bitcast.129, ...), custom_call_target="tpu_custom_call" | custom-call | bytes 77000000 | tf_op jit(solution)/shard_map/pallas_call | solution.py:698
  164.4 11.5 %shard_map.230 = (f32[4,128,384]{2,1,0:T(8,128)S(1)}, bf16[4,128,192]{2,1,0:T(8,128)(2,1)S(1)}) custom-call(s32[4,4]{1,0:T(4,128)S(1)} %pad_add_fusion.bounds_ref, bf16[4,128,384]{2,1,0:T(8,128)(2,1)S(1)} %get-tuple-element.126.q_ref, bf16[4096,384]{1,0:T(8,128)(2,1)S(1)} %bitcast.137, s32[4,1,128]{2,1,0:T(1,128)S(1)} %bitcast.168), custom_call_target="tpu_custom_call" | custom-call | bytes 45500000 | tf_op jit(solution)/shard_map/pallas_call | solution.py:1199
  175.9 11.7 %shard_map.231.attn_ref = bf16[4,128,192]{2,1,0:T(8,128)(2,1)S(1)} custom-call(bf16[4,128,192]{2,1,0:T(8,128)(2,1)S(1)} %get-tuple-element.128.refs_0_), custom_call_target="tpu_custom_call" | custom-call | bytes 31500000 | tf_op jit(solution)/shard_map/pallas_call | solution.py:198
  191.7 56.4 %shard_map.233 = (bf16[8,40,768]{2,1,0:T(8,128)(2,1)}, bf16[8,40,768]{2,1,0:T(8,128)(2,1)}, bf16[1024,384]{1,0:T(8,128)(2,1)}, bf16[1024,384]{1,0:T(8,128)(2,1)}...) custom-call(bf16[8,40,768]{2,1,0:T(8,128)(2,1)} %bitcast.154, ...), custom_call_target="tpu_custom_call" | custom-call | bytes 192500000 | tf_op jit(solution)/shard_map/pallas_call | solution.py:1741
  250.8 14.6 %shard_map.236.dy_ref = bf16[4,128,768]{2,1,0:T(8,128)(2,1)S(1)} custom-call(bf16[128,768]{1,0:T(8,128)(2,1)S(1)} %get-tuple-element.138.src), custom_call_target="tpu_custom_call" | custom-call | bytes 49000000 | tf_op jit(solution)/shard_map/pallas_call | solution.py:224
  265.4 2.1 collective-permute-done.6.refs_7_
  267.6 16.9 %shard_map.237 = (bf16[4,128,384]{2,1,0:T(8,128)(2,1)S(1)}, bf16[4096,384]{1,0:T(8,128)(2,1)S(1)}) custom-call(s32[4,4]{1,0:T(4,128)S(1)} %pad_add_fusion.bounds_ref, bf16[4,128,384]{2,1,0:T(8,128)(2,1)S(1)} %copy-done.28, bf16[4,128,768]{2,1,0:T(8,128)(2,1)S(1)} %shard_map.236.dy_ref, bf16[384,768]{1,0:T(8,128)(2,1)S(1)} %copy-done.49, ...), custom_call_target="tpu_custom_call" | custom-call | bytes 70000000 | tf_op jit(solution)/shard_map/pallas_call | solution.py:1303
  284.6 28.8 %shard_map.238 = (bf16[4,128,384]{2,1,0:T(8,128)(2,1)S(1)}, bf16[4,128,768]{2,1,0:T(8,128)(2,1)S(1)}) custom-call(bf16[2,4,2,2,128,384]{5,4,3,2,1,0:T(8,128)(2,1)S(1)} %bitcast.142, bf16[4,128,384]{2,1,0:T(8,128)(2,1)S(1)} %get-tuple-element.144.dq_ref, bf16[768,384]{1,0:T(8,128)(2,1)S(1)} %copy-done.48, bf16[768,1408]{1,0:T(8,128)(2,1)S(1)} %bitcast.131), custom_call_target="tpu_custom_call" | custom-call | bytes 91000000 | tf_op jit(solution)/shard_map/pallas_call | solution.py:1087
  314.9 43.5 %shard_map.240 = (bf16[8,40,768]{2,1,0:T(8,128)(2,1)}, bf16[1024,384]{1,0:T(8,128)(2,1)}, bf16[1024,384]{1,0:T(8,128)(2,1)}, bf16[1024,384]{1,0:T(8,128)(2,1)}, ...) custom-call(bf16[8,40,768]{2,1,0:T(8,128)(2,1)} %bitcast.156, ...), custom_call_target="tpu_custom_call" | custom-call | bytes 126000000 | tf_op jit(solution)/shard_map/pallas_call | solution.py:1741
  358.5 1.4 collective-permute-start.7
  361.6 1.4 shard_map.241
  363.1 13.1 %shard_map.242.dy_ref = bf16[4,128,768]{2,1,0:T(8,128)(2,1)S(1)} custom-call(bf16[128,768]{1,0:T(8,128)(2,1)S(1)} %get-tuple-element.155.src), custom_call_target="tpu_custom_call" | custom-call | bytes 49000000 | tf_op jit(solution)/shard_map/pallas_call | solution.py:224
  376.2 1.4 shard_map.247
  377.6 1.6 collective-permute-done.7.refs_1_
  380.2 16.9 %shard_map.243 = (bf16[4,128,384]{2,1,0:T(8,128)(2,1)S(1)}, bf16[4096,384]{1,0:T(8,128)(2,1)S(1)}) custom-call(s32[4,4]{1,0:T(4,128)S(1)} %pad_add_fusion.bounds_ref, bf16[4,128,384]{2,1,0:T(8,128)(2,1)S(1)} %copy-done.20, bf16[4,128,768]{2,1,0:T(8,128)(2,1)S(1)} %shard_map.242.dy_ref, bf16[384,768]{1,0:T(8,128)(2,1)S(1)} %copy-done.47, ...), custom_call_target="tpu_custom_call" | custom-call | bytes 70000000 | tf_op jit(solution)/shard_map/pallas_call | solution.py:1303
  397.1 28.1 %shard_map.244 = (bf16[4,128,384]{2,1,0:T(8,128)(2,1)S(1)}, bf16[4,128,768]{2,1,0:T(8,128)(2,1)S(1)}) custom-call(bf16[2,4,2,2,128,384]{5,4,3,2,1,0:T(8,128)(2,1)S(1)} %bitcast.141, bf16[4,128,384]{2,1,0:T(8,128)(2,1)S(1)} %get-tuple-element.163.dq_ref, bf16[768,384]{1,0:T(8,128)(2,1)S(1)} %copy-done.46, bf16[768,1408]{1,0:T(8,128)(2,1)S(1)} %bitcast.134), custom_call_target="tpu_custom_call" | custom-call | bytes 91000000 | tf_op jit(solution)/shard_map/pallas_call | solution.py:1087
  426.4 1.4 shard_map.246
  427.8 15.7 %shard_map.248 = (bf16[4,24,640]{2,1,0:T(8,128)(2,1)S(1)}, bf16[2,24,384]{2,1,0:T(8,128)(2,1)S(1)}, bf16[4,24,640]{2,1,0:T(8,128)(2,1)S(1)}, bf16[2,24,384]{2,1,0:T(8,128)(2,1)S(1)}) custom-call(bf16[2,4,2,2,24,640]{5,4,3,2,1,0:T(8,128)(2,1)S(1)} %bitcast.148, bf16[2,2,2,2,24,384]{5,4,3,2,1,0:T(8,128)(2,1)S(1)} %bitcast.166, ...), custom_call_target="tpu_custom_call" | custom-call | bytes 70000000 | tf_op jit(solution)/shard_map/pallas_call | solution.py:880
  444.3 1.6 shard_map.234
  445.9 11.4 %shard_map.249 = (bf16[4,24,640]{2,1,0:T(8,128)(2,1)S(1)}, bf16[4,24,640]{2,1,0:T(8,128)(2,1)S(1)}, bf16[2,24,384]{2,1,0:T(8,128)(2,1)S(1)}, bf16[2,24,384]{2,1,0:T(8,128)(2,1)S(1)}) custom-call(bf16[4,24,640]{2,1,0:T(8,128)(2,1)S(1)} %get-tuple-element.179.refs_0_, bf16[4,24,640]{2,1,0:T(8,128)(2,1)S(1)} %get-tuple-element.180.refs_1_, ...), custom_call_target="tpu_custom_call" | custom-call | bytes 31500000 | tf_op jit(solution)/shard_map/pallas_call | solution.py:296
  460.7 1.4 reshape.206
  463.8 7.8 %shard_map.250 = (f32[2,1024,384]{2,1,0:T(8,128)}, f32[2,1024,384]{2,1,0:T(8,128)}, f32[2,1024,384]{2,1,0:T(8,128)}) custom-call(bf16[1024,384]{1,0:T(8,128)(2,1)} %get-tuple-element.187.refs_0_, bf16[1024,384]{1,0:T(8,128)(2,1)} %copy-done.62, bf16[1024,384]{1,0:T(8,128)(2,1)} %get-tuple-element.189.refs_2_, bf16[1024,384]{1,0:T(8,128)(2,1)} %copy-done.63, ...), custom_call_target="tpu_custom_call" | custom-call | bytes 24500000 | tf_op jit(solution)/shard_map/pallas_call | solution.py:2011
  (250 shorter events, 33.6 us)
Async XLA Ops:
  3.5 98.6 %collective-permute-start = (bf16[1024,384]{1,0:T(8,128)(2,1)}, bf16[1024,384]{1,0:T(8,128)(2,1)S(1)}, u32[]{:S(2)}, u32[]{:S(2)}) collective-permute-start(bf16[1024,384]{1,0:T(8,128)(2,1)} %get-tuple-element.117), channel_id=1, source_target_pairs={{0,16},{16,0},{1,17},{17,1},{2,18},{18,2},{3,19},{19,3},{4,20},{20... | collective-permute-start | bytes 2359304 | tf_op jit(solution)/shard_map/ppermute | solution.py:2131
  8.1 60.3 %copy-start.2 = (bf16[2,1024,384]{2,1,0:T(8,128)(2,1)S(1)}, bf16[2,1024,384]{2,1,0:T(8,128)(2,1)}, u32[]{:S(2)}) copy-start(bf16[2,1024,384]{2,1,0:T(8,128)(2,1)} %refs_6_.3) | copy-start | bytes 4718596
  66.8 35.2 %collective-permute-start.1 = (bf16[1024,384]{1,0:T(8,128)(2,1)}, bf16[1024,384]{1,0:T(8,128)(2,1)}, u32[]{:S(2)}, u32[]{:S(2)}) collective-permute-start(bf16[1024,384]{1,0:T(8,128)(2,1)} %get-tuple-element.118), channel_id=1, source_target_pairs={{0,16},{16,0},{1,17},{17,1},{2,18},{18,2},{3,19},{19,3},{4,20},{20... | collective-permute-start | bytes 2359304 | tf_op jit(solution)/shard_map/ppermute | solution.py:2131
  69.7 34.7 %collective-permute-start.2 = (bf16[1024,384]{1,0:T(8,128)(2,1)}, bf16[1024,384]{1,0:T(8,128)(2,1)}, u32[]{:S(2)}, u32[]{:S(2)}) collective-permute-start(bf16[1024,384]{1,0:T(8,128)(2,1)} %get-tuple-element.119), channel_id=1, source_target_pairs={{0,16},{16,0},{1,17},{17,1},{2,18},{18,2},{3,19},{19,3},{4,20},{20... | collective-permute-start | bytes 2359304 | tf_op jit(solution)/shard_map/ppermute | solution.py:2131
  72.2 115.5 %copy-start.35 = (bf16[128,320]{1,0:T(8,128)(2,1)}, bf16[128,320]{1,0:T(8,128)(2,1)S(1)}, u32[]{:S(2)}) copy-start(bf16[128,320]{1,0:T(8,128)(2,1)S(1)} %get-tuple-element.256.picks_ref) | copy-start | bytes 245764
  98.6 41.0 %copy-start.23 = (f32[128,768]{1,0:T(8,128)}, f32[128,768]{1,0:T(8,128)S(1)}, u32[]{:S(2)}) copy-start(f32[128,768]{1,0:T(8,128)S(1)} %get-tuple-element.122.mid_ref) | copy-start | bytes 1179652
  98.6 91.7 %collective-permute-start.3 = (bf16[1024,384]{1,0:T(8,128)(2,1)S(1)}, bf16[1024,384]{1,0:T(8,128)(2,1)S(1)}, u32[]{:S(2)}, u32[]{:S(2)}) collective-permute-start(bf16[1024,384]{1,0:T(8,128)(2,1)S(1)} %copy-done.65), channel_id=1, source_target_pairs={{0,16},{16,0},{1,17},{17,1},{2,18},{18,2},{3,19},{19,3},{4,20},{20... | collective-permute-start | bytes 2359304 | tf_op jit(solution)/shard_map/ppermute | solution.py:2131
  98.7 91.6 %collective-permute-start.4 = (bf16[1024,384]{1,0:T(8,128)(2,1)S(1)}, bf16[1024,384]{1,0:T(8,128)(2,1)S(1)}, u32[]{:S(2)}, u32[]{:S(2)}) collective-permute-start(bf16[1024,384]{1,0:T(8,128)(2,1)S(1)} %copy-done.66), channel_id=1, source_target_pairs={{0,16},{16,0},{1,17},{17,1},{2,18},{18,2},{3,19},{19,3},{4,20},{20... | collective-permute-start | bytes 2359304 | tf_op jit(solution)/shard_map/ppermute | solution.py:2131
  101.3 38.3 %copy-start.52 = (f32[128,128]{1,0:T(8,128)}, f32[128,128]{1,0:T(8,128)S(1)}, u32[]{:S(2)}) copy-start(f32[128,128]{1,0:T(8,128)S(1)} %get-tuple-element.259.other_ref) | copy-start | bytes 196612
  102.1 37.5 %copy-start.13 = (bf16[1024,384]{1,0:T(8,128)(2,1)}, bf16[1024,384]{1,0:T(8,128)(2,1)S(1)}, u32[]{:S(2)}) copy-start(bf16[1024,384]{1,0:T(8,128)(2,1)S(1)} %collective-permute-done.refs_2_.refs_3_) | copy-start | bytes 2359300
  104.4 36.1 %copy-start.5 = (bf16[2,4,4,24,1408]{4,3,2,1,0:T(8,128)(2,1)S(1)}, bf16[2,4,4,24,1408]{4,3,2,1,0:T(8,128)(2,1)}, u32[]{:S(2)}) copy-start(bf16[2,4,4,24,1408]{4,3,2,1,0:T(8,128)(2,1)} %copy-done.4) | copy-start | bytes 6488068
  140.6 47.1 %copy-start.25 = (f32[128,768]{1,0:T(8,128)}, f32[128,768]{1,0:T(8,128)S(1)}, u32[]{:S(2)}) copy-start(f32[128,768]{1,0:T(8,128)S(1)} %get-tuple-element.129.x_ref) | copy-start | bytes 1179652
  163.3 27.0 %collective-permute-start.5 = (bf16[1024,384]{1,0:T(8,128)(2,1)S(1)}, bf16[1024,384]{1,0:T(8,128)(2,1)S(1)}, u32[]{:S(2)}, u32[]{:S(2)}) collective-permute-start(bf16[1024,384]{1,0:T(8,128)(2,1)S(1)} %copy-done.67), channel_id=1, source_target_pairs={{0,16},{16,0},{1,17},{17,1},{2,18},{18,2},{3,19},{19,3},{4,20},{20... | collective-permute-start | bytes 2359304 | tf_op jit(solution)/shard_map/ppermute | solution.py:2131
  190.3 57.9 %copy-start.21 = (f32[128,768]{1,0:T(8,128)}, f32[128,768]{1,0:T(8,128)S(1)}, u32[]{:S(2)}) copy-start(f32[128,768]{1,0:T(8,128)S(1)} %get-tuple-element.136.mid_ref) | copy-start | bytes 1179652
  191.7 56.5 %copy-start.36 = (bf16[128,320]{1,0:T(8,128)(2,1)S(1)}, bf16[128,320]{1,0:T(8,128)(2,1)}, u32[]{:S(2)}) copy-start(bf16[128,320]{1,0:T(8,128)(2,1)} %copy-done.35) | copy-start | bytes 245764
  191.7 56.5 %copy-start.42 = (bf16[128,768]{1,0:T(8,128)(2,1)S(1)}, bf16[128,768]{1,0:T(8,128)(2,1)}, u32[]{:S(2)}) copy-start(bf16[128,768]{1,0:T(8,128)(2,1)} %up_ref.1) | copy-start | bytes 589828
  191.7 56.6 %copy-start.50 = (f32[128,128]{1,0:T(8,128)S(1)}, f32[128,128]{1,0:T(8,128)}, u32[]{:S(2)}) copy-start(f32[128,128]{1,0:T(8,128)} %get-tuple-element.258.other_ref) | copy-start | bytes 196612
  248.1 19.4 %collective-permute-start.6 = (bf16[1024,384]{1,0:T(8,128)(2,1)}, bf16[1024,384]{1,0:T(8,128)(2,1)S(1)}, u32[]{:S(2)}, u32[]{:S(2)}) collective-permute-start(bf16[1024,384]{1,0:T(8,128)(2,1)} %get-tuple-element.139), channel_id=1, source_target_pairs={{0,16},{16,0},{1,17},{17,1},{2,18},{18,2},{3,19},{19,3},{4,20},{20... | collective-permute-start | bytes 2359304 | tf_op jit(solution)/shard_map/ppermute | solution.py:2229
  284.5 28.9 %copy-start.17 = (bf16[4,128,384]{2,1,0:T(8,128)(2,1)}, bf16[4,128,384]{2,1,0:T(8,128)(2,1)S(1)}, u32[]{:S(2)}) copy-start(bf16[4,128,384]{2,1,0:T(8,128)(2,1)S(1)} %get-tuple-element.144.dq_ref) | copy-start | bytes 1179652
  284.6 28.9 %copy-start.26 = (f32[128,768]{1,0:T(8,128)S(1)}, f32[128,768]{1,0:T(8,128)}, u32[]{:S(2)}) copy-start(f32[128,768]{1,0:T(8,128)} %copy-done.25) | copy-start | bytes 1179652
  284.6 28.9 %copy-start.30 = (f32[320,128]{1,0:T(8,128)S(1)}, f32[320,128]{1,0:T(8,128)}, u32[]{:S(2)}) copy-start(f32[320,128]{1,0:T(8,128)} %copy-done.29) | copy-start | bytes 491524
  314.9 45.7 %copy-start.24 = (f32[128,768]{1,0:T(8,128)S(1)}, f32[128,768]{1,0:T(8,128)}, u32[]{:S(2)}) copy-start(f32[128,768]{1,0:T(8,128)} %copy-done.23) | copy-start | bytes 1179652
  314.9 45.7 %copy-start.53 = (f32[128,128]{1,0:T(8,128)S(1)}, f32[128,128]{1,0:T(8,128)}, u32[]{:S(2)}) copy-start(f32[128,128]{1,0:T(8,128)} %copy-done.52) | copy-start | bytes 196612
  314.9 61.2 %copy-start.45 = (bf16[4,128,768]{2,1,0:T(8,128)(2,1)S(1)}, bf16[4,128,768]{2,1,0:T(8,128)(2,1)}, u32[]{:S(2)}) copy-start(bf16[4,128,768]{2,1,0:T(8,128)(2,1)} %get-tuple-element.174) | copy-start | bytes 2359300
  314.9 65.2 %copy-start.47 = (bf16[384,768]{1,0:T(8,128)(2,1)S(1)}, bf16[384,768]{1,0:T(8,128)(2,1)}, u32[]{:S(2)}) copy-start(bf16[384,768]{1,0:T(8,128)(2,1)} %get-tuple-element.158.w_ref) | copy-start | bytes 1769476
  358.5 20.8 %collective-permute-start.7 = (bf16[1024,384]{1,0:T(8,128)(2,1)}, bf16[1024,384]{1,0:T(8,128)(2,1)S(1)}, u32[]{:S(2)}, u32[]{:S(2)}) collective-permute-start(bf16[1024,384]{1,0:T(8,128)(2,1)} %get-tuple-element.156), channel_id=1, source_target_pairs={{0,16},{16,0},{1,17},{17,1},{2,18},{18,2},{3,19},{19,3},{4,20},{20... | collective-permute-start | bytes 2359304 | tf_op jit(solution)/shard_map/ppermute | solution.py:2231
  359.9 37.2 %collective-permute-start.8 = (bf16[1024,384]{1,0:T(8,128)(2,1)}, bf16[1024,384]{1,0:T(8,128)(2,1)S(1)}, u32[]{:S(2)}, u32[]{:S(2)}) collective-permute-start(bf16[1024,384]{1,0:T(8,128)(2,1)} %get-tuple-element.161), channel_id=1, source_target_pairs={{0,16},{16,0},{1,17},{17,1},{2,18},{18,2},{3,19},{19,3},{4,20},{20... | collective-permute-start | bytes 2359304 | tf_op jit(solution)/shard_map/ppermute | solution.py:2231
  397.1 28.2 %copy-start.63 = (bf16[1024,384]{1,0:T(8,128)(2,1)}, bf16[1024,384]{1,0:T(8,128)(2,1)S(1)}, u32[]{:S(2)}) copy-start(bf16[1024,384]{1,0:T(8,128)(2,1)S(1)} %collective-permute-done.8.refs_3_) | copy-start | bytes 2359300
  397.1 28.2 %copy-start.16 = (bf16[128,768]{1,0:T(8,128)(2,1)S(1)}, bf16[128,768]{1,0:T(8,128)(2,1)}, u32[]{:S(2)}) copy-start(bf16[128,768]{1,0:T(8,128)(2,1)} %x_ref.3) | copy-start | bytes 589828
  397.1 29.2 %copy-start.32 = (bf16[4,128,192]{2,1,0:T(8,128)(2,1)S(1)}, bf16[4,128,192]{2,1,0:T(8,128)(2,1)}, u32[]{:S(2)}) copy-start(bf16[4,128,192]{2,1,0:T(8,128)(2,1)} %copy-done.31) | copy-start | bytes 589828
  397.1 29.2 %copy-start.44 = (bf16[4,128,768]{2,1,0:T(8,128)(2,1)S(1)}, bf16[4,128,768]{2,1,0:T(8,128)(2,1)}, u32[]{:S(2)}) copy-start(bf16[4,128,768]{2,1,0:T(8,128)(2,1)} %get-tuple-element.169) | copy-start | bytes 2359300
  443.5 19.4 %collective-permute-start.9 = (bf16[1024,384]{1,0:T(8,128)(2,1)S(1)}, bf16[1024,384]{1,0:T(8,128)(2,1)S(1)}, u32[]{:S(2)}, u32[]{:S(2)}) collective-permute-start(bf16[1024,384]{1,0:T(8,128)(2,1)S(1)} %copy-done.80), channel_id=1, source_target_pairs={{0,16},{16,0},{1,17},{17,1},{2,18},{18,2},{3,19},{19,3},{4,20},{20... | collective-permute-start | bytes 2359304 | tf_op jit(solution)/shard_map/ppermute | solution.py:2285
  (59 other events, 645.8 us)
